TPU v7x, 512 devices: a whole 4x8x8 slice. The times are simulated.
512 devices in a mesh: row: 16 (over y_lo, x, core), col: 32 (over y_hi, z).
Axes of the slice: x: 4, y: 8 (y_hi: 4, y_lo: 2; y = y_hi * 2 + y_lo), z: 8, core: 2. Of those that a mesh axis runs over, the one named last changes fastest.
Arguments:
- obj: float32 [2, 2048, 4096], P(None, 'row', 'col'), may hold values from -5 to 5
- probe: float32 [2, 2, 128, 128], replicated, may hold values from -5 to 5
- measured: float32 [16, 32, 2, 8, 128, 128], P('row', 'col'), may hold values from 0.05 to 4
- offsets: int32 [16, 32, 2, 8, 2], P('row', 'col'), may hold values from -64 to 64, as said below
Outputs:
- new_obj: float32 [2, 2048, 4096], P(None, 'row', 'col')
- new_probe: float32 [2, 2, 128, 128], replicated
- probe_gradient: float32 [2, 2, 128, 128], replicated
Inputs may be any that keep to these rules, and one draw needn't show every extreme that they name: `offsets`: window starts are relative to the device's own tile of 128 pixels, so a window may reach up to 64 pixels into neighbouring tiles; both extremes occur in every draw.
All inputs are finite; a program needn't handle non-finite values.
Results may differ from a plain program's by a relative error of at most 0.0003.
Values sent between devices are 32-bit elements; how exact they have to be, the bound alone decides.
No kernel may reach another device: no remote copies, remote signals or barrier semaphores. Data moves between devices by JAX's collectives and lax.ppermute only.
A program may use at most 64 MiB of HBM per device.

v0:
```python
import math

import jax
import jax.numpy as jnp
from jax import lax
from jax.sharding import PartitionSpec as P


def with_halo(block, sides, width):
    for axis, dim in sides:
        count = lax.axis_size(axis)
        forward = [(i, i + 1) for i in range(count - 1)]
        backward = [(target, source) for source, target in forward]
        low = lax.ppermute(
            lax.slice_in_dim(block, block.shape[dim] - width, None, axis=dim), axis, forward
        )
        high = lax.ppermute(lax.slice_in_dim(block, 0, width, axis=dim), axis, backward)
        block = jnp.concatenate([low, block, high], axis=dim)
    return block


def passed_along(block, axis, distance):
    devices = range(lax.axis_size(axis))
    route = [(i - distance, i) for i in devices if i - distance in devices]
    return lax.ppermute(block, axis, route)


def tables(size):
    index = jnp.arange(size, dtype=jnp.int32)
    product = index[:, None] * index[None, :] % size
    angle = 2.0 * math.pi / size * product.astype(jnp.float32)
    scale = 1.0 / math.sqrt(size)
    return (jnp.cos(angle) * scale, -jnp.sin(angle) * scale)


def transform(real_in, imag_in, lookup_real, lookup_imaginary):
    best = lax.Precision.HIGHEST

    def left(matrix, field):
        return jnp.einsum("kn,...nw->...kw", matrix, field, precision=best)

    def right(field, matrix):
        return jnp.einsum("...kn,nw->...kw", field, matrix, precision=best)

    first_r = left(lookup_real, real_in) - left(lookup_imaginary, imag_in)
    first_i = left(lookup_real, imag_in) + left(lookup_imaginary, real_in)
    out_r = right(first_r, lookup_real) - right(first_i, lookup_imaginary)
    out_i = right(first_r, lookup_imaginary) + right(first_i, lookup_real)
    return (out_r, out_i)


def cmul(ar, ai, br, bi):
    return (ar * br - ai * bi, ar * bi + ai * br)


def cmul_conj(ar, ai, br, bi):
    return (ar * br + ai * bi, ar * bi - ai * br)


def exit_residual(
    probe_real,
    probe_imaginary,
    window_real,
    window_imaginary,
    recorded_pattern,
    lookup_real,
    lookup_imaginary,
):
    psi_r, psi_i = cmul(
        probe_real[None], probe_imaginary[None], window_real[:, None], window_imaginary[:, None]
    )
    wave_r, wave_i = transform(psi_r, psi_i, lookup_real, lookup_imaginary)
    model_intensity = jnp.sum(wave_r * wave_r + wave_i * wave_i, axis=1)
    amplitude_ratio = (
        jnp.sqrt(recorded_pattern) / jnp.maximum(jnp.sqrt(model_intensity), 0.5) - 1.0
    )[:, None]
    return transform(
        wave_r * amplitude_ratio, wave_i * amplitude_ratio, lookup_real, -lookup_imaginary
    )


def fetch(field, width):
    return with_halo(field, (("row", 1), ("col", 2)), width)


def windows(padded, starts, size):
    zero = jnp.zeros((), jnp.int32)
    return jax.vmap(
        lambda s: lax.dynamic_slice(padded, (zero, s[0], s[1]), (padded.shape[0], size, size))
    )(starts)


def pass_col(strip, by):
    return passed_along(strip, "col", by)


def pass_row(strip, by):
    return passed_along(strip, "row", by)


def fold_cols(total, width):
    inner_len = total.shape[2] - 2 * width
    from_right = pass_col(total[:, :, :width], -1)
    from_left = pass_col(total[:, :, inner_len + width :], 1)
    inner = total[:, :, width : inner_len + width]
    inner = inner.at[:, :, :width].add(from_left)
    return inner.at[:, :, inner_len - width :].add(from_right)


def fold_rows(total, width):
    inner_len = total.shape[1] - 2 * width
    from_below = pass_row(total[:, :width, :], -1)
    from_above = pass_row(total[:, inner_len + width :, :], 1)
    inner = total[:, width : inner_len + width, :]
    inner = inner.at[:, :width, :].add(from_above)
    return inner.at[:, inner_len - width :, :].add(from_below)


def step_total(values):
    return lax.psum(values, ("row", "col"))


def per_device(obj, probe, measured, offsets):
    size = probe.shape[-1]
    half = size // 2
    tile = obj.shape[-1]
    lookup_real, lookup_imaginary = tables(size)
    probe_real, probe_imaginary = (probe[0], probe[1])
    obj_pair = obj
    padded = fetch(obj_pair, half)
    count = offsets.shape[2]
    gradient = None
    for scan_batch in range(count):
        starts = offsets[0, 0, scan_batch] + half
        recorded_pattern = measured[0, 0, scan_batch]
        object_window = windows(padded, starts, size)
        window_real, window_imaginary = (object_window[:, 0], object_window[:, 1])
        residual_real, residual_imaginary = exit_residual(
            probe_real,
            probe_imaginary,
            window_real,
            window_imaginary,
            recorded_pattern,
            lookup_real,
            lookup_imaginary,
        )
        cont_r, cont_i = cmul_conj(
            probe_real[None], probe_imaginary[None], residual_real, residual_imaginary
        )
        light = jnp.sum(probe_real * probe_real + probe_imaginary * probe_imaginary, axis=0)
        cont_r = jnp.sum(cont_r, axis=1)
        cont_i = jnp.sum(cont_i, axis=1)
        blocks = jnp.stack([cont_r, cont_i, jnp.broadcast_to(light, cont_r.shape)], axis=1)
        zero = jnp.zeros((), jnp.int32)

        def place(k, total):
            start = starts[k]
            current = lax.dynamic_slice(total, (zero, start[0], start[1]), (3, size, size))
            return lax.dynamic_update_slice(total, current + blocks[k], (zero, start[0], start[1]))

        accum = jnp.zeros((3, tile + 2 * half, tile + 2 * half), jnp.float32)
        accum = lax.fori_loop(0, starts.shape[0], place, accum)
        inner = fold_rows(fold_cols(accum, half), half)
        d_obj = inner[:2] / (inner[2] + 1.0)
        num_r, num_i = cmul_conj(
            window_real[:, None], window_imaginary[:, None], residual_real, residual_imaginary
        )
        numer = jnp.stack([jnp.sum(num_r, axis=0), jnp.sum(num_i, axis=0)])
        coverage = jnp.sum(window_real * window_real + window_imaginary * window_imaginary, axis=0)
        numer, coverage = lax.psum((numer, coverage), ("row", "col"))
        d_probe = numer / (coverage + 1.0)
        gradient = numer / jnp.sqrt(coverage + 1.0)
        d_padded = fetch(d_obj, half)
        d_patch = windows(d_padded, starts, size)
        u1r, u1i = cmul(
            probe_real[None], probe_imaginary[None], d_patch[:, 0, None], d_patch[:, 1, None]
        )
        u2r, u2i = cmul(
            d_probe[0][None], d_probe[1][None], window_real[:, None], window_imaginary[:, None]
        )
        a11 = jnp.sum(u1r * u1r + u1i * u1i)
        a12 = jnp.sum(u1r * u2r + u1i * u2i)
        b_one = jnp.sum(u1r * residual_real + u1i * residual_imaginary)
        a22 = jnp.sum(u2r * u2r + u2i * u2i)
        b_two = jnp.sum(u2r * residual_real + u2i * residual_imaginary)
        totals = step_total(jnp.stack([a11, a22, a12, b_one, b_two]))
        a11, a22, a12, b_one, b_two = (totals[0], totals[1], totals[2], totals[3], totals[4])
        big_one = 1.1 * a11
        big_two = 1.1 * a22
        det = big_one * big_two - a12 * a12
        step_obj = (b_one * big_two - a12 * b_two) / det
        step_probe = (big_one * b_two - a12 * b_one) / det
        obj_pair = obj_pair + step_obj * d_obj
        probe_real = probe_real + step_probe * d_probe[0]
        probe_imaginary = probe_imaginary + step_probe * d_probe[1]
        if scan_batch + 1 < count:
            padded = fetch(obj_pair, half)
    return (obj_pair, jnp.stack([probe_real, probe_imaginary]), gradient)


def solution(mesh):
    in_specs = (
        P(None, "row", "col"),
        P(),
        P("row", "col", None, None, None, None),
        P("row", "col", None, None, None),
    )
    out_specs = (P(None, "row", "col"), P(), P())
    return jax.shard_map(
        per_device, mesh=mesh, in_specs=in_specs, out_specs=out_specs, check_vma=False
    )
```

profile of v0, /device:TPU:1, one launch (start us, length us, event | category | flops | bytes accessed | tf_op | source)
XLA Modules:
  0.0 1226.7 jit_solution(10008459181517566384)
XLA Ops:
  8.1 4.5 collective-permute-start
  12.7 5.6 collective-permute-start.1
  23.8 4.3 collective-permute-done.2
  28.0 4.1 collective-permute-done.3
  32.5 16.8 %while.40 = (s32[]{:T(128)}, f32[2,256,256]{2,1,0:T(8,128)S(1)}, s32[8,3]{0,1:T(4,128)S(1)}, f32[8,2,128,128]{3,2,1,0:T(8,128)S(1)}, s32[]{:T(128)}) while((s32[]{:T(128)}, f32[2,256,256]{2,1,0:T(8,128)S(1)}, s32[8,3]{0,1:T(4,128)S(1)}, f32[8,2,128,128]{3,2,1,0:T(8,128)S(1)}, s32[]{:T(128)}) %tuple.204), condition=%wide.while_cond.8, body=%wide.while_body.8.sunk | while | flops 2 | bytes 262261 | solution.py:89
  71.9 13.3 %fusion.107 = f32[8,2,128,128]{3,2,1,0:T(8,128)S(1)} fusion(f32[8,2,128,128]{2,3,1,0:T(8,128)S(1)} %fusion.5), kind=kOutput, calls=%fused_computation.223 | convolution fusion | flops 402898944 | bytes 2097152 | tf_op jit(solution)/shard_map/...kn,nw->...kw/dot_general | solution.py:43
  91.2 4.3 add_reduce_fusion.12
  96.9 65.6 %while.38 = (s32[]{:T(128)}, f32[3,256,256]{2,1,0:T(8,128)S(1)}, s32[8,2]{0,1:T(2,128)S(1)}, f32[8,3,128,128]{3,2,1,0:T(8,128)}, s32[]{:T(128)}, /*index=5*/s32[]{:T(128)}, s32[]{:T(128)}) while((s32[]{:T(128)}, f32[3,256,256]{2,1,0:T(8,128)S(1)}, s32[8,2]{0,1:T(2,128)S(1)}, f32[8,3,128,128]{3,2,1,0:T(8,128)}, s32[]{:T(128)}, ...), condition=%wide.region_5.6_spmd, body=%wide.region_4.5_spmd.sunk | while | flops 49160 | bytes 983237 | solution.py:162
  164.4 3.5 collective-permute-start.4
  170.7 5.4 collective-permute-done.4
  182.9 3.1 scatter-add.29
  187.0 6.8 collective-permute-start.6
  193.8 258.4 %all-reduce.7.cloned.1.call-done = (f32[2,2,128,128]{3,2,1,0:T(8,128)}, f32[128,128]{1,0:T(8,128)}) async-done(((f32[2,2,128,128]{3,2,1,0:T(8,128)}, f32[128,128]{1,0:T(8,128)}), (f32[2,2,128,128]{3,2,1,0:T(8,128)}, f32[128,128]{1,0:T(8,128)})) %all-reduce.7.cloned.1.call-update) | async-done | bytes 327696 | tf_op jit(solution)/shard_map/psum | solution.py:170
  467.8 3.3 collective-permute-start.10
  475.7 5.1 collective-permute-done.11
  482.2 21.0 %while.41 = (s32[]{:T(128)}, f32[2,256,256]{2,1,0:T(8,128)S(1)}, s32[8,3]{0,1:T(4,128)S(1)}, f32[8,2,128,128]{3,2,1,0:T(8,128)}, s32[]{:T(128)}) while((s32[]{:T(128)}, f32[2,256,256]{2,1,0:T(8,128)S(1)}, s32[8,3]{0,1:T(4,128)S(1)}, f32[8,2,128,128]{3,2,1,0:T(8,128)}, s32[]{:T(128)}) %tuple.229), condition=%wide.while_cond.9, body=%wide.while_body.9.sunk | while | flops 2 | bytes 263785 | solution.py:89
  507.5 3.2 stack.88
  510.6 104.9 %psum.44 = f32[5]{0:T(128)S(1)} all-reduce(f32[5]{0:T(128)S(1)} %stack.88), channel_id=1, replica_groups=mesh['row'=16,'col'=32] {'row','col'}, use_global_device_ids=true, to_apply=%region_16.17 | all-reduce | flops 5 | bytes 40 | tf_op jit(solution)/shard_map/psum | solution.py:120
  621.5 4.1 collective-permute-start.12
  631.3 3.3 collective-permute-start.14
  638.7 4.1 collective-permute-done.15
  643.2 16.6 %while.42 = (s32[]{:T(128)}, f32[2,256,256]{2,1,0:T(8,128)S(1)}, s32[8,3]{0,1:T(4,128)S(1)}, f32[8,2,128,128]{3,2,1,0:T(8,128)S(1)}, s32[]{:T(128)}) while((s32[]{:T(128)}, f32[2,256,256]{2,1,0:T(8,128)S(1)}, s32[8,3]{0,1:T(4,128)S(1)}, f32[8,2,128,128]{3,2,1,0:T(8,128)S(1)}, s32[]{:T(128)}) %tuple.213), condition=%wide.while_cond.10, body=%wide.while_body.10.sunk | while | flops 2 | bytes 262261 | solution.py:89
  690.5 4.3 add_reduce_fusion.4
  696.1 66.0 %while.39 = (s32[]{:T(128)}, f32[3,256,256]{2,1,0:T(8,128)S(1)}, s32[8,2]{0,1:T(2,128)S(1)}, f32[8,3,128,128]{3,2,1,0:T(8,128)}, s32[]{:T(128)}, /*index=5*/s32[]{:T(128)}, s32[]{:T(128)}) while((s32[]{:T(128)}, f32[3,256,256]{2,1,0:T(8,128)S(1)}, s32[8,2]{0,1:T(2,128)S(1)}, f32[8,3,128,128]{3,2,1,0:T(8,128)}, s32[]{:T(128)}, ...), condition=%wide.region_22.23_spmd, body=%wide.region_21.22_spmd.sunk | while | flops 49160 | bytes 983237 | solution.py:162
  764.0 3.5 collective-permute-start.16
  770.3 5.3 collective-permute-done.16
  781.8 3.1 scatter-add.35
  788.3 259.2 %all-reduce.5.cloned.1.call-done = (f32[2,2,128,128]{3,2,1,0:T(8,128)}, f32[128,128]{1,0:T(8,128)}) async-done(((f32[2,2,128,128]{3,2,1,0:T(8,128)}, f32[128,128]{1,0:T(8,128)}), (f32[2,2,128,128]{3,2,1,0:T(8,128)}, f32[128,128]{1,0:T(8,128)})) %all-reduce.5.cloned.1.call-update) | async-done | bytes 327696 | tf_op jit(solution)/shard_map/psum | solution.py:170
  1063.3 3.3 collective-permute-start.22
  1071.2 5.1 collective-permute-done.23
  1077.8 19.9 %while.43 = (s32[]{:T(128)}, f32[2,256,256]{2,1,0:T(8,128)S(1)}, s32[8,3]{0,1:T(4,128)S(1)}, f32[8,2,128,128]{3,2,1,0:T(8,128)}, s32[]{:T(128)}) while((s32[]{:T(128)}, f32[2,256,256]{2,1,0:T(8,128)S(1)}, s32[8,3]{0,1:T(4,128)S(1)}, f32[8,2,128,128]{3,2,1,0:T(8,128)}, s32[]{:T(128)}) %tuple.228), condition=%wide.while_cond.11, body=%wide.while_body.11.sunk | while | flops 2 | bytes 263785 | solution.py:89
  1105.0 104.9 %psum.47 = f32[5]{0:T(128)S(1)} all-reduce(f32[5]{0:T(128)S(1)} %stack.100), channel_id=1, replica_groups=mesh['row'=16,'col'=32] {'row','col'}, use_global_device_ids=true, to_apply=%region_33.34 | all-reduce | flops 5 | bytes 40 | tf_op jit(solution)/shard_map/psum | solution.py:120
  (374 shorter events, 305.1 us)
Async XLA Ops:
  7.2 445.0 %all-reduce.7.cloned.1.call-start = ((), (), s32[]{:S(2)}) async-start(), calls=%async_computation.1 | async-start | bytes 655360 | tf_op jit(solution)/shard_map/psum | solution.py:170
  8.1 11.8 collective-permute-start
  12.7 8.3 collective-permute-start.1
  21.1 7.0 collective-permute-start.2
  22.4 9.8 collective-permute-start.3
  164.4 11.7 collective-permute-start.4
  167.9 13.7 %collective-permute-start.5 = (f32[3,256,64]{2,1,0:T(8,128)}, f32[3,256,64]{2,1,0:T(8,128)}, u32[]{:S(2)}, u32[]{:S(2)}) collective-permute-start(f32[3,256,64]{2,1,0:T(8,128)} %get-tuple-element.385), channel_id=1, source_target_pairs={{1,0},{2,1},{3,2},{4,3},{5,4},{6,5},{7,6},{8,7},{9,8},{10,9},{11,1... | collective-permute-start | bytes 589832 | tf_op jit(solution)/shard_map/ppermute | solution.py:25
  170.7 876.9 %all-reduce.5.cloned.1.call-start = ((), (), s32[]{:S(2)}) async-start(), calls=%async_computation | async-start | bytes 655360 | tf_op jit(solution)/shard_map/psum | solution.py:170
  187.0 269.3 %collective-permute-start.6 = (f32[3,64,128]{2,1,0:T(8,128)S(1)}, f32[3,64,128]{2,1,0:T(8,128)S(1)}, u32[]{:S(2)}, u32[]{:S(2)}) collective-permute-start(f32[3,64,128]{2,1,0:T(8,128)S(1)} %get-tuple-element.392), channel_id=1, source_target_pairs={{0,32},{32,64},{64,96},{96,128},{128,160},{160,192},{192,224},{224... | collective-permute-start | bytes 294920 | tf_op jit(solution)/shard_map/ppermute | solution.py:25
  454.1 5.9 collective-permute-start.7
  460.1 4.4 collective-permute-start.8
  462.0 5.6 collective-permute-start.9
  464.5 171.4 %copy-start.5 = (f32[2,2,128,128]{3,2,1,0:T(8,128)}, f32[2,2,128,128]{3,2,1,0:T(8,128)S(1)}, u32[]{:S(2)}) copy-start(f32[2,2,128,128]{3,2,1,0:T(8,128)S(1)} %broadcast_divide_fusion.2) | copy-start | bytes 786436
  467.8 7.9 collective-permute-start.10
  471.0 9.7 collective-permute-start.11
  504.8 116.6 %copy-start.21 = (f32[2,128,128]{2,1,0:T(8,128)S(1)}, f32[2,128,128]{2,1,0:T(8,128)}, u32[]{:S(2)}) copy-start(f32[2,128,128]{2,1,0:T(8,128)} %param.24) | copy-start | bytes 393220
  621.5 8.6 collective-permute-start.12
  625.6 5.6 collective-permute-start.13
  631.3 7.4 collective-permute-start.14
  634.6 8.2 collective-permute-start.15
  764.0 11.5 collective-permute-start.16
  767.5 13.0 %collective-permute-start.17 = (f32[3,256,64]{2,1,0:T(8,128)}, f32[3,256,64]{2,1,0:T(8,128)}, u32[]{:S(2)}, u32[]{:S(2)}) collective-permute-start(f32[3,256,64]{2,1,0:T(8,128)} %get-tuple-element.383), channel_id=1, source_target_pairs={{1,0},{2,1},{3,2},{4,3},{5,4},{6,5},{7,6},{8,7},{9,8},{10,9},{11,1... | collective-permute-start | bytes 589832 | tf_op jit(solution)/shard_map/ppermute | solution.py:25
  785.9 265.7 %collective-permute-start.18 = (f32[3,64,128]{2,1,0:T(8,128)S(1)}, f32[3,64,128]{2,1,0:T(8,128)S(1)}, u32[]{:S(2)}, u32[]{:S(2)}) collective-permute-start(f32[3,64,128]{2,1,0:T(8,128)S(1)} %get-tuple-element.390), channel_id=1, source_target_pairs={{0,32},{32,64},{64,96},{96,128},{128,160},{160,192},{192,224},{224... | collective-permute-start | bytes 294920 | tf_op jit(solution)/shard_map/ppermute | solution.py:25
  1049.4 5.9 collective-permute-start.19
  1055.4 5.3 collective-permute-start.20
  1057.4 5.8 collective-permute-start.21
  1063.3 7.9 collective-permute-start.22
  1066.6 9.7 collective-permute-start.23
  1099.2 118.1 %copy-start.6 = (f32[2,2,128,128]{3,2,1,0:T(8,128)S(1)}, f32[2,2,128,128]{3,2,1,0:T(8,128)}, u32[]{:S(2)}) copy-start(f32[2,2,128,128]{3,2,1,0:T(8,128)} %copy-done.5) | copy-start | bytes 786436
  1099.2 118.2 %copy-start.16 = (f32[2,2,128,128]{3,2,1,0:T(8,128)S(1)}, f32[2,2,128,128]{3,2,1,0:T(8,128)}, u32[]{:S(2)}) copy-start(f32[2,2,128,128]{3,2,1,0:T(8,128)} %copy-done.15) | copy-start | bytes 786436
  1099.2 118.9 %copy-start.14 = (f32[2,128,128]{2,1,0:T(8,128)S(1)}, f32[2,128,128]{2,1,0:T(8,128)}, u32[]{:S(2)}) copy-start(f32[2,128,128]{2,1,0:T(8,128)} %copy-done.13) | copy-start | bytes 393220
  1099.2 118.9 %copy-start.20 = (f32[3,128,128]{2,1,0:T(8,128)S(1)}, f32[3,128,128]{2,1,0:T(8,128)}, u32[]{:S(2)}) copy-start(f32[3,128,128]{2,1,0:T(8,128)} %copy-done.19) | copy-start | bytes 589828
  (26 other events, 462.8 us)
Sparse Core Ops, SparseCore 0:
  170.8 281.3 all-reduce.6
  770.4 277.0 all-reduce.4
where the time goes:
time: 1240 us; the launch traced here: 1230 us
  waiting for transfers between devices  574 us (46%)
  blocking collectives  210 us (17%)
  local copies, waits for them, and re-layouts  166 us (13%)
  matrix products  79.9 us (6%)
  starting transfers between devices  64.5 us (5%)
  loops' own time  61 us (5%)
  other arithmetic  41.2 us (3%)
  between operations  30.8 us (2%)
    psum x2, waiting for transfers between devices, per_device(): numer, coverage = lax.psum((numer, coverage), ('row', 'col'))  518 us
    psum x2, blocking collectives, step_total(): return lax.psum(values, ('row', 'col'))  210 us
    gather x96, local copies, waits for them, and re-layouts  73.5 us
    another operation x2, loops' own time, per_device(): accum = lax.fori_loop(0, starts.shape[0], place, accum)  60.2 us
    dot_general x16, matrix products, right(): return jnp.einsum('...kn,nw->...kw', field, matrix, precision=best)  47.5 us
    dynamic_update_slice x16, local copies, waits for them, and re-layouts, place(): lax.dynamic_update_slice(total, current + blocks[k], (zero, start[0], sta...  44 us
    dot_general x16, matrix products, left(): return jnp.einsum('kn,...nw->...kw', matrix, field, precision=best)  32.4 us
    ppermute x8, waiting for transfers between devices, with_halo(): lax.ppermute(lax.slice_in_dim(block, 0, width, axis=dim), axis, backward)  25 us
  transfers between devices with their start and end apart: 26, of which 19 were waited for; matrix products, arithmetic and copies ran while one was open for 3% of the time, Pallas kernels for 0%

commit v1 on v0

v1 whole, which is shorter than its diff:
```python
import math

import jax
import jax.numpy as jnp
import numpy as np
from jax import lax
from jax.experimental import pallas as pl
from jax.experimental.pallas import tpu as pltpu
from jax.sharding import Mesh, PartitionSpec as P

SIZE = 128
HALF = 64
MODES = 2
COUNT = 8
GROUP = 2
ROW = ("yl", "x", "c")
COL = ("yh", "z")
ALL = ROW + COL
TILES = 8
VMEM_LIMIT = 48 * 1024 * 1024
F32 = jnp.float32
BF16 = jnp.bfloat16


def dft_tables():
    index = np.arange(SIZE)
    angle = 2.0 * math.pi / SIZE * (np.outer(index, index) % SIZE)
    real = np.cos(angle) / math.sqrt(SIZE)
    imag = -np.sin(angle) / math.sqrt(SIZE)
    right = np.block([[real, imag], [-imag, real]]).astype(np.float32)
    high = right.astype(jnp.bfloat16)
    low = (right - high.astype(np.float32)).astype(jnp.bfloat16)
    right3 = np.concatenate([high, high, low], axis=0)
    left3 = np.ascontiguousarray(right3.T)
    return right3, left3


def halves(x):
    high = x.astype(BF16)
    return high, (x - high.astype(F32)).astype(BF16)


def right_transform(fields, table):
    rows = []
    for real, imag in fields:
        rh, rl = halves(real)
        ih, il = halves(imag)
        rows.append(jnp.concatenate([rh, ih, rl, il, rh, ih], axis=1))
    out = jnp.dot(jnp.concatenate(rows, axis=0), table, preferred_element_type=F32)
    return [
        (out[SIZE * n : SIZE * (n + 1), :SIZE], out[SIZE * n : SIZE * (n + 1), SIZE:])
        for n in range(len(fields))
    ]


def left_transform(fields, table):
    cols = []
    for real, imag in fields:
        rh, rl = halves(real)
        ih, il = halves(imag)
        cols.append(jnp.concatenate([rh, ih, rl, il, rh, ih], axis=0))
    out = jnp.dot(table, jnp.concatenate(cols, axis=1), preferred_element_type=F32)
    return [
        (out[:SIZE, SIZE * n : SIZE * (n + 1)], out[SIZE:, SIZE * n : SIZE * (n + 1)])
        for n in range(len(fields))
    ]


def lanes():
    return lax.broadcasted_iota(jnp.int32, (SIZE, SIZE), 1)


def window(ref, lead, row, col):
    shift = lax.rem(SIZE - col, SIZE)
    first = pltpu.roll(ref[lead + (0, pl.ds(row, SIZE))], shift, 1)
    second = pltpu.roll(ref[lead + (1, pl.ds(row, SIZE))], shift, 1)
    return jnp.where(lanes() < SIZE - col, first, second)


def place(ref, plane, row, col, block):
    moved = pltpu.roll(block, lax.rem(col, SIZE), 1)
    first = lanes() >= col
    rows = pl.ds(row, SIZE)
    ref[plane, 0, rows] += jnp.where(first, moved, 0.0)
    ref[plane, 1, rows] += jnp.where(first, 0.0, moved)


def join(low, first, second):
    return jnp.where(low, pltpu.roll(first, HALF, 1), pltpu.roll(second, HALF, 1))


def pack_low(low, upper, lower):
    return jnp.where(low, upper, pltpu.roll(lower, HALF, 1))


def pack_high(low, upper, lower):
    return jnp.where(low, pltpu.roll(upper, HALF, 1), lower)


def low_lanes(rows):
    return lax.broadcasted_iota(jnp.int32, (rows, SIZE), 1) < HALF


def pad_field(above, own, below, from_left, from_right, store):
    low = low_lanes(HALF)
    for c in range(2):
        strips = (above[c], own[c, :HALF], own[c, HALF:], below[c])
        for k in range(4):
            half = slice(HALF * (k % 2), HALF * (k % 2 + 1))
            left, right = from_left[c, half], from_right[c, half]
            if k < 2:
                right = pltpu.roll(right, HALF, 1)
            else:
                left = pltpu.roll(left, HALF, 1)
            mine = pltpu.roll(strips[k], HALF, 1)
            rows = slice(HALF * k, HALF * (k + 1))
            store(c, 0, rows, jnp.where(low, left, mine))
            store(c, 1, rows, jnp.where(low, mine, right))


def pack_kernel(above, own, below, left, right):
    low = low_lanes(HALF)
    for c in range(2):
        strips = (above[c], own[c, :HALF], own[c, HALF:], below[c])
        for k in range(2):
            rows = slice(HALF * k, HALF * (k + 1))
            left[c, rows] = pack_low(low, strips[k], strips[k + 2])
            right[c, rows] = pack_high(low, strips[k], strips[k + 2])


def sweep(batch, starts, padded, probe, measured, right3, left3, top, middle, bottom, sums, accum):
    accum[...] = jnp.zeros_like(accum)
    sums[...] = jnp.zeros_like(sums)
    light = sum(probe[c, m] * probe[c, m] for c in range(2) for m in range(MODES))
    tr = right3[...]
    tl = left3[...]

    def body(step, carry):
        wins = []
        fields = []
        for g in range(GROUP):
            j = step * GROUP + g
            row, col = starts[j, 0], starts[j, 1]
            wr = window(padded, (0,), row, col)
            wi = window(padded, (1,), row, col)
            wins.append((row, col, wr, wi))
            for m in range(MODES):
                pr, pi = probe[0, m], probe[1, m]
                fields.append((pr * wr - pi * wi, pr * wi + pi * wr))
        waves = left_transform(right_transform(fields, tr), tl)
        back = []
        for g in range(GROUP):
            own = waves[g * MODES : (g + 1) * MODES]
            intensity = sum(r * r + i * i for r, i in own)
            recorded = measured[0, 0, batch, step * GROUP + g]
            ratio = jnp.sqrt(recorded) / jnp.maximum(jnp.sqrt(intensity), 0.5) - 1.0
            back += [(r * ratio, -(i * ratio)) for r, i in own]
        chis = right_transform(left_transform(back, tl), tr)
        for g in range(GROUP):
            row, col, wr, wi = wins[g]
            cr = jnp.zeros((SIZE, SIZE), F32)
            ci = jnp.zeros((SIZE, SIZE), F32)
            for m in range(MODES):
                xr, xn = chis[g * MODES + m]
                pr, pi = probe[0, m], probe[1, m]
                cr += pr * xr - pi * xn
                ci -= pr * xn + pi * xr
                sums[m] += wr * xr - wi * xn
                sums[MODES + m] -= wr * xn + wi * xr
            sums[2 * MODES] += wr * wr + wi * wi
            place(accum, 0, row, col, cr)
            place(accum, 1, row, col, ci)
            place(accum, 2, row, col, light)
        return carry

    lax.fori_loop(0, COUNT // GROUP, body, 0)
    top[...] = accum[:, :, :HALF]
    middle[...] = accum[:, :, HALF : HALF + SIZE]
    bottom[...] = accum[:, :, HALF + SIZE :]


def first_kernel(starts, above, own, below, from_left, from_right, probe, measured, right3, left3,
                 top, middle, bottom, sums, padded, accum):
    def store(c, h, rows, value):
        padded[c, h, rows] = value

    pad_field(above, own, below, from_left, from_right, store)
    sweep(0, starts, padded, probe, measured, right3, left3, top, middle, bottom, sums, accum)


def fold_kernel(middle, from_above, from_below, tile, left, right):
    low = low_lanes(HALF)
    for k in range(3):
        upper = [middle[k, h, :HALF] + from_above[k, h] for h in range(2)]
        lower = [middle[k, h, HALF:] + from_below[k, h] for h in range(2)]
        tile[k, :HALF] = join(low, *upper)
        tile[k, HALF:] = join(low, *lower)
        left[k] = pack_low(low, upper[0], lower[0])
        right[k] = pack_high(low, upper[1], lower[1])


def merge_kernel(shifts, tile, from_left, from_right, padded, sums,
                 packed, numbers, direction, product, overlap):
    low = low_lanes(HALF)
    lane = lanes()
    a11 = jnp.zeros((1, SIZE), F32)
    b1 = jnp.zeros((1, SIZE), F32)
    product[...] = jnp.zeros_like(product)
    for v in range(2):
        rows = slice(HALF * v, HALF * (v + 1))
        full = []
        for k in range(3):
            left, right = from_left[k], from_right[k]
            if v == 0:
                right = pltpu.roll(right, HALF, 1)
            else:
                left = pltpu.roll(left, HALF, 1)
            full.append(tile[k, rows] + jnp.where(low, left, right))
        gr, gi, cover = full
        inverse = 1.0 / (cover + 1.0)
        dr = gr * inverse
        di = gi * inverse
        direction[0, rows] = dr
        direction[1, rows] = di
        span = slice(HALF * (v + 1), HALF * (v + 2))
        pr = join(low, padded[0, 0, span], padded[0, 1, span])
        pi = join(low, padded[1, 0, span], padded[1, 1, span])
        inner = slice(SIZE + HALF * v, SIZE + HALF * (v + 1))
        product[0, inner] = dr * pr + di * pi
        product[1, inner] = dr * pi - di * pr
        power = dr * dr + di * di
        a11 += jnp.sum(power * cover, axis=0, keepdims=True)
        b1 += jnp.sum(power * (cover + 1.0), axis=0, keepdims=True)
    line = lax.broadcasted_iota(jnp.int32, (TILES, SIZE), 0)
    numbers[...] = jnp.where(line == 0, a11, jnp.where(line == 1, b1, 0.0))

    overlap[...] = jnp.zeros_like(overlap)

    def body(k, carry):
        down, across = shifts[k, 0], shifts[k, 1]

        @pl.when((jnp.abs(down) < SIZE) & (jnp.abs(across) < SIZE))
        def _():
            turn = lax.rem(SIZE - across, SIZE)
            source = lane + across
            inside = (source >= 0) & (source < SIZE)
            for c in range(2):
                moved = pltpu.roll(product[c, pl.ds(SIZE + down, SIZE)], turn, 1)
                overlap[c] += jnp.where(inside, moved, 0.0)

        return carry

    lax.fori_loop(0, shifts.shape[0], body, 0)

    strips = (SIZE // TILES, TILES, SIZE)
    for k in range(5):
        packed[:, k] = sums[k].reshape(strips)
    for c in range(2):
        packed[:, 5 + c] = overlap[c].reshape(strips)


def add_all(parts):
    total = parts[0]
    for k in range(1, parts.shape[0]):
        total = total + parts[k]
    return total


def scatter_kernel(parts, numbers, out):
    total = add_all(parts)
    for k in range(out.shape[0]):
        out[k, :7] = total
        out[k, 7] = numbers[...]


def reduce_kernel(parts, out):
    total = add_all(parts)
    for k in range(out.shape[0]):
        out[k] = total


def strip_kernel(place_ref, parts, probe, out):
    total = add_all(parts)
    rows = pl.ds(pl.multiple_of(place_ref[0] * TILES, TILES), TILES)
    cover = total[2 * MODES]
    inverse = 1.0 / (cover + 1.0)
    cross = jnp.zeros((TILES, SIZE), F32)
    power = jnp.zeros((TILES, SIZE), F32)
    for m in range(MODES):
        dr, di = total[m] * inverse, total[MODES + m] * inverse
        pr, pi = probe[0, m, rows], probe[1, m, rows]
        cross += (pr * dr + pi * di) * total[5] - (pr * di - pi * dr) * total[6]
        power += dr * dr + di * di
    line = lax.broadcasted_iota(jnp.int32, (TILES, SIZE), 0)
    numbers = total[7]
    for k, term in ((2, power * cover), (3, power * (cover + 1.0)), (4, cross)):
        numbers = jnp.where(line == k, jnp.sum(term, axis=0, keepdims=True), numbers)
    for k in range(out.shape[0]):
        out[k, :5] = total[:5]
        out[k, 5] = numbers


def step_sizes(totals, probe, new_probe, gradient=None):
    numbers = jnp.sum(add_all(totals.at[:, 5]), axis=1, keepdims=True)
    a11, b1, a22, b2, a12 = (numbers[k : k + 1] for k in range(5))
    a11 = 1.1 * a11
    a22 = 1.1 * a22
    det = a11 * a22 - a12 * a12
    step_obj = (b1 * a22 - a12 * b2) / det
    step_probe = (a11 * b2 - a12 * b1) / det
    cover = totals[:, 4].reshape(SIZE, SIZE) + 1.0
    scale = step_probe / cover
    for m in range(MODES):
        for c in range(2):
            numer = totals[:, MODES * c + m].reshape(SIZE, SIZE)
            new_probe[c, m] = probe[c, m] + scale * numer
            if gradient is not None:
                gradient[c, m] = numer * lax.rsqrt(cover)
    return step_obj


def next_kernel(starts, totals, padded, above, direction, below, from_left, from_right, probe,
                measured, right3, left3,
                top, middle, bottom, sums, new_padded, new_probe, accum):
    step = step_sizes(totals, probe, new_probe)

    def store(c, h, rows, value):
        new_padded[c, h, rows] = padded[c, h, rows] + step * value

    pad_field(above, direction, below, from_left, from_right, store)
    sweep(1, starts, new_padded, new_probe, measured, right3, left3, top, middle, bottom, sums, accum)


def last_kernel(totals, padded, direction, probe, new_obj, new_probe, gradient):
    step = step_sizes(totals, probe, new_probe, gradient)
    low = lanes() < HALF
    rows = slice(HALF, HALF + SIZE)
    for c in range(2):
        old = join(low, padded[c, 0, rows], padded[c, 1, rows])
        new_obj[c] = old + step * direction[c]


def shape(*dims):
    return jax.ShapeDtypeStruct(dims, F32)


def call(kernel, ins, outs, scratch=()):
    vmem = pl.BlockSpec(memory_space=pltpu.VMEM)
    smem = pl.BlockSpec(memory_space=pltpu.SMEM)
    specs = [smem if x.dtype == jnp.int32 else vmem for x in ins]
    return pl.pallas_call(
        kernel,
        in_specs=specs,
        out_specs=[vmem] * len(outs),
        out_shape=list(outs),
        scratch_shapes=list(scratch),
        compiler_params=pltpu.CompilerParams(vmem_limit_bytes=VMEM_LIMIT),
        name=kernel.__name__,
    )(*ins)


def shift(block, rows, cols):
    n_row = math.prod(lax.axis_size(a) for a in ROW)
    n_col = math.prod(lax.axis_size(a) for a in COL)
    route = [
        (r * n_col + c, (r + rows) * n_col + c + cols)
        for r in range(n_row)
        for c in range(n_col)
        if 0 <= r + rows < n_row and 0 <= c + cols < n_col
    ]
    return lax.ppermute(block, ALL, route)


def exchange(block, axes):
    return lax.all_to_all(block, axes, 0, 0, tiled=True)


def size_of(axes):
    return math.prod(lax.axis_size(a) for a in axes)


def reduce_all(packed, numbers, probe, place_in_row, direction=None):
    halo = None
    if direction is not None:
        above = shift(direction[:, HALF:], 1, 0)
        below = shift(direction[:, :HALF], -1, 0)
    part = exchange(packed, ROW)
    if direction is not None:
        part, above, below = lax.optimization_barrier((part, above, below))
        left, right = call(pack_kernel, [above, direction, below], [shape(2, SIZE, SIZE)] * 2)
        from_left = shift(right, 0, 1)
        from_right = shift(left, 0, -1)
    (part,) = call(scatter_kernel, [part, numbers], [shape(size_of(("z",)), 8, TILES, SIZE)])
    part = exchange(part, ("z",))
    if direction is not None:
        part, from_left, from_right = lax.optimization_barrier((part, from_left, from_right))
        halo = above, direction, below, from_left, from_right
    (part,) = call(reduce_kernel, [part], [shape(size_of(("yh",)), 8, TILES, SIZE)])
    part = exchange(part, ("yh",))
    (part,) = call(strip_kernel, [place_in_row, part, probe], [shape(packed.shape[0], 6, TILES, SIZE)])
    return exchange(part, ROW), halo


MARK = 1024.0


def per_device(obj, probe, measured, offsets):
    right3, left3 = (jnp.asarray(t) for t in dft_tables())
    offsets = offsets[0, 0]
    starts = offsets + HALF
    batches = offsets.shape[0]
    place_in_row = lax.axis_index(ROW).astype(jnp.int32).reshape(1)

    code = jnp.zeros((TILES * SIZE,), F32).at[: offsets.size].set(
        offsets.reshape(-1).astype(F32) + MARK)
    code = code.reshape(1, TILES, SIZE)

    def with_code(strip, more):
        return jnp.concatenate([strip, jnp.pad(more, ((0, 1), (0, 0), (0, 0)))], axis=1)

    above = shift(with_code(obj[:, HALF:], code), 1, 0)
    below = shift(with_code(obj[:, :HALF], code), -1, 0)
    codes = jnp.concatenate([above[:1, HALF:], code, below[:1, HALF:]], axis=1)
    above, below = above[:, :HALF], below[:, :HALF]
    packed_field = shape(2, SIZE, SIZE)
    left, right = call(pack_kernel, [above, obj, below], [packed_field] * 2)
    from_left = shift(with_code(right, codes), 0, 1)
    from_right = shift(with_code(left, codes), 0, -1)
    codes = jnp.stack([from_left[0, SIZE:], codes[0], from_right[0, SIZE:]])
    codes = codes.reshape(3, 3, -1)[:, :, : offsets.size].reshape((3, 3) + offsets.shape)
    away = jnp.arange(-1, 2, dtype=jnp.int32) * SIZE
    steps = jnp.stack([
        jnp.broadcast_to(away[None, :, None, None], codes.shape[:-1]),
        jnp.broadcast_to(away[:, None, None, None], codes.shape[:-1]),
    ], axis=-1)
    shifts = (codes - MARK).astype(jnp.int32) + steps
    shifts = jnp.moveaxis(shifts, 2, 0).reshape(batches, -1, 2)

    whole = 2 * SIZE
    field = shape(2, 2, whole, SIZE)
    edge = shape(3, 2, HALF, SIZE)
    middle = shape(3, 2, SIZE, SIZE)
    planes = shape(2, MODES, SIZE, SIZE)
    accum = pltpu.VMEM((3, 2, whole, SIZE), F32)

    top, middle_in, bottom, sums, padded = call(
        first_kernel,
        [starts[0], above, obj, below, from_left[:, :SIZE], from_right[:, :SIZE], probe,
         measured, right3, left3],
        [edge, middle, edge, shape(5, SIZE, SIZE), field],
        [accum],
    )

    def merge(top, middle_in, bottom, sums, padded, batch):
        from_above = shift(bottom, 1, 0)
        from_below = shift(top, -1, 0)
        side = shape(3, HALF, SIZE)
        tile, left, right = call(
            fold_kernel, [middle_in, from_above, from_below], [shape(3, SIZE, SIZE), side, side])
        left_in = shift(right, 0, 1)
        right_in = shift(left, 0, -1)
        return call(
            merge_kernel,
            [shifts[batch], tile, left_in, right_in, padded, sums],
            [shape(SIZE // TILES, 7, TILES, SIZE), shape(TILES, SIZE), shape(2, SIZE, SIZE)],
            [pltpu.VMEM((2, 3 * SIZE, SIZE), F32), pltpu.VMEM((2, SIZE, SIZE), F32)],
        )

    packed, numbers, direction = merge(top, middle_in, bottom, sums, padded, 0)
    totals, halo = reduce_all(packed, numbers, probe, place_in_row, direction)
    top, middle_in, bottom, sums, padded, probe = call(
        next_kernel,
        [starts[1], totals, padded, *halo, probe, measured, right3, left3],
        [edge, middle, edge, shape(5, SIZE, SIZE), field, planes],
        [accum],
    )
    packed, numbers, direction = merge(top, middle_in, bottom, sums, padded, 1)
    totals, _ = reduce_all(packed, numbers, probe, place_in_row)
    return tuple(call(
        last_kernel, [totals, padded, direction, probe], [shape(2, SIZE, SIZE), planes, planes]
    ))


def solution(mesh):
    parts = Mesh(mesh.devices.reshape(2, 4, 2, 4, 8), ALL)
    in_specs = (P(None, ROW, COL), P(), P(ROW, COL), P(ROW, COL))
    out_specs = (P(None, ROW, COL), P(), P())
    return jax.shard_map(
        per_device, mesh=parts, in_specs=in_specs, out_specs=out_specs, check_vma=False
    )
```

time: 1240 us -> 230 us (0.19); the launches traced: 1230 us -> 229 us
  waiting for transfers between devices: 574 us -> 49.4 us
  local copies, waits for them, and re-layouts: 166 us -> 4.33 us
  blocking collectives: 210 us -> 62.2 us
  matrix products: 79.9 us -> 0 us
  loops' own time: 61 us -> 0 us
  other arithmetic: 41.2 us -> 0.79 us
  Pallas kernels: 0 us -> 30.4 us
  between operations: 30.8 us -> 1.06 us
  starting transfers between devices: 64.5 us -> 80.9 us
    psum x2 -> x0, waiting for transfers between devices: 518 us -> none  [per_device(): numer, coverage = lax.psum((numer, coverage), ('row', 'col'))]
    psum x2 -> x0, blocking collectives: 210 us -> none  [step_total(): return lax.psum(values, ('row', 'col'))]
    dot_general x32 -> x0, matrix products: 79.9 us -> none  [the longest x16 47.5 us: right(): return jnp.einsum('...kn,nw->...kw', field, matrix, precision=best)]
    gather x96 -> x0, local copies, waits for them, and re-layouts: 73.5 us -> none
    all_to_all x0 -> x4, blocking collectives: none -> 62.2 us  [exchange(): return lax.all_to_all(block, axes, 0, 0, tiled=True)]
    another operation x6 -> x0, loops' own time: 61 us -> none  [the longest x2 60.2 us: per_device(): accum = lax.fori_loop(0, starts.shape[0], place, accum)]
    dynamic_update_slice x16 -> x0, local copies, waits for them, and re-layouts: 44 us -> none  [place(): lax.dynamic_update_slice(total, current + blocks[k], (zero, start[0], sta...]
    all_to_all x0 -> x4, starting transfers between devices: none -> 37.6 us  [exchange(): return lax.all_to_all(block, axes, 0, 0, tiled=True)]
  transfers between devices with their start and end apart: 26 -> 20, of which waited for: 19 -> 18; matrix products, arithmetic and copies ran while one was open for 3% -> 0% of each run, Pallas kernels for 0% -> 0%
where the time goes in v1:
time: 230 us; the launch traced here: 229 us
  starting transfers between devices  80.9 us (35%)
  blocking collectives  62.2 us (27%)
  waiting for transfers between devices  49.4 us (21%)
  Pallas kernels  30.4 us (13%)
  local copies, waits for them, and re-layouts  4.33 us (2%)
    all_to_all x4, blocking collectives, exchange(): return lax.all_to_all(block, axes, 0, 0, tiled=True)  62.2 us
    ppermute x16, starting transfers between devices, shift(): return lax.ppermute(block, ALL, route)  43.3 us
    all_to_all x4, starting transfers between devices, exchange(): return lax.all_to_all(block, axes, 0, 0, tiled=True)  37.6 us
    ppermute x16, waiting for transfers between devices, shift(): return lax.ppermute(block, ALL, route)  32.3 us
    pallas_call x15, Pallas kernels, call(): pl.pallas_call(kernel, in_specs=specs, out_specs=[vmem] * len(outs), out_...  30.4 us
    all_to_all x4, waiting for transfers between devices, exchange(): return lax.all_to_all(block, axes, 0, 0, tiled=True)  17.2 us
  transfers between devices with their start and end apart: 20, of which 18 were waited for; matrix products, arithmetic and copies ran while one was open for 0% of the time, Pallas kernels for 0%

profile of v1, /device:TPU:1, one launch (start us, length us, event | category | flops | bytes accessed | tf_op | source)
XLA Modules:
  0.0 229.2 jit_solution(733326400893699182)
XLA Ops:
  2.4 4.6 %collective-permute-start = (f32[2,72,128]{2,1,0:T(8,128)S(1)}, f32[2,72,128]{2,1,0:T(8,128)S(1)}, u32[]{:S(2)}, u32[]{:S(2)}) collective-permute-start(f32[2,72,128]{2,1,0:T(8,128)S(1)} %get-tuple-element.89), channel_id=1, source_target_pairs={{0,32},{1,33},{2,34},{3,35},{4,36},{5,37},{6,38},{7,39},{8,40},{9,... | collective-permute-start | bytes 221192 | tf_op jit(solution)/shard_map/ppermute | solution.py:371
  7.1 5.6 %collective-permute-start.1 = (f32[2,72,128]{2,1,0:T(8,128)S(1)}, f32[2,72,128]{2,1,0:T(8,128)S(1)}, u32[]{:S(2)}, u32[]{:S(2)}) collective-permute-start(f32[2,72,128]{2,1,0:T(8,128)S(1)} %get-tuple-element.90), channel_id=1, source_target_pairs={{32,0},{33,1},{34,2},{35,3},{36,4},{37,5},{38,6},{39,7},{40,8},{41... | collective-permute-start | bytes 221192 | tf_op jit(solution)/shard_map/ppermute | solution.py:371
  13.8 3.3 %collective-permute-start.2 = (f32[2,152,128]{2,1,0:T(8,128)S(1)}, f32[2,152,128]{2,1,0:T(8,128)S(1)}, u32[]{:S(2)}, u32[]{:S(2)}) collective-permute-start(f32[2,152,128]{2,1,0:T(8,128)S(1)} %get-tuple-element.87), channel_id=1, source_target_pairs={{0,1},{1,2},{2,3},{3,4},{4,5},{5,6},{6,7},{7,8},{8,9},{9,10},{10,1... | collective-permute-start | bytes 466952 | tf_op jit(solution)/shard_map/ppermute | solution.py:371
  19.6 4.2 %collective-permute-done.3 = f32[2,152,128]{2,1,0:T(8,128)S(1)} collective-permute-done((f32[2,152,128]{2,1,0:T(8,128)S(1)}, f32[2,152,128]{2,1,0:T(8,128)S(1)}, u32[]{:S(2)}, u32[]{:S(2)}) %collective-permute-start.3) | collective-permute-done | bytes 155680 | tf_op jit(solution)/shard_map/ppermute | solution.py:371
  24.9 8.5 %first_kernel.1 = (f32[3,2,64,128]{3,2,1,0:T(8,128)S(1)}, f32[3,2,128,128]{3,2,1,0:T(8,128)S(1)}, f32[3,2,64,128]{3,2,1,0:T(8,128)S(1)}, f32[5,128,128]{2,1,0:T(8,128)S(1)}, f32[2,2,256,128]{3,2,1,0:T(8,128)S(1)}) custom-call(s32[8,2]{1,0:T(8,128)S(1)} %copy.17.starts, f32[2,64,128]{2,1,0:T(8,128)S(1)} %slice.83.above, f32[2,128,128]{2,1,0:T(8,128)S(1)} %copy-done.4, ...), custom_call_target="tpu_custom_call" | custom-call | tf_op jit(solution)/shard_map/first_kernel/pallas_call | solution.py:351
  33.4 4.0 %collective-permute-start.4 = (f32[3,2,64,128]{3,2,1,0:T(8,128)S(1)}, f32[3,2,64,128]{3,2,1,0:T(8,128)S(1)}, u32[]{:S(2)}, u32[]{:S(2)}) collective-permute-start(f32[3,2,64,128]{3,2,1,0:T(8,128)S(1)} %get-tuple-element.51), channel_id=1, source_target_pairs={{0,32},{1,33},{2,34},{3,35},{4,36},{5,37},{6,38},{7,39},{8,40},{9,... | collective-permute-start | bytes 589832 | tf_op jit(solution)/shard_map/ppermute | solution.py:371
  37.4 1.9 collective-permute-start.5
  40.0 4.4 %collective-permute-done.5.from_below = f32[3,2,64,128]{3,2,1,0:T(8,128)S(1)} collective-permute-done((f32[3,2,64,128]{3,2,1,0:T(8,128)S(1)}, f32[3,2,64,128]{3,2,1,0:T(8,128)S(1)}, u32[]{:S(2)}, u32[]{:S(2)}) %collective-permute-start.5) | collective-permute-done | bytes 196640 | tf_op jit(solution)/shard_map/ppermute | solution.py:371
  44.6 4.0 %collective-permute-start.6 = (f32[3,64,128]{2,1,0:T(8,128)S(1)}, f32[3,64,128]{2,1,0:T(8,128)S(1)}, u32[]{:S(2)}, u32[]{:S(2)}) collective-permute-start(f32[3,64,128]{2,1,0:T(8,128)S(1)} %get-tuple-element.54), channel_id=1, source_target_pairs={{0,1},{1,2},{2,3},{3,4},{4,5},{5,6},{6,7},{7,8},{8,9},{9,10},{10,1... | collective-permute-start | bytes 294920 | tf_op jit(solution)/shard_map/ppermute | solution.py:371
  50.2 5.5 %collective-permute-done.7.from_right = f32[3,64,128]{2,1,0:T(8,128)S(1)} collective-permute-done((f32[3,64,128]{2,1,0:T(8,128)S(1)}, f32[3,64,128]{2,1,0:T(8,128)S(1)}, u32[]{:S(2)}, u32[]{:S(2)}) %collective-permute-start.7) | collective-permute-done | bytes 98336 | tf_op jit(solution)/shard_map/ppermute | solution.py:371
  55.8 4.7 %merge_kernel.2 = (f32[16,7,8,128]{3,2,1,0:T(8,128)S(1)}, f32[8,128]{1,0:T(8,128)S(1)}, f32[2,128,128]{2,1,0:T(8,128)S(1)}) custom-call(s32[72,2]{1,0:T(8,128)S(1)} %bitcast.14, f32[3,128,128]{2,1,0:T(8,128)S(1)} %get-tuple-element.53.tile, f32[3,64,128]{2,1,0:T(8,128)S(1)} %collective-permute-done.6.from_left, ...), custom_call_target="tpu_custom_call" | custom-call | tf_op jit(solution)/shard_map/merge_kernel/pallas_call | solution.py:351
  61.3 7.9 %all-to-all-start = ((f32[16,7,8,128]{3,2,1,0:T(8,128)}), f32[16,7,8,128]{3,2,1,0:T(8,128)S(1)}, u32[]{:S(2)}, u32[]{:S(2)}) async-start(f32[16,7,8,128]{3,2,1,0:T(8,128)} %copy-done.5), calls=%async_computation | async-start | bytes 917504 | tf_op jit(solution)/shard_map/all_to_all | solution.py:375
  69.2 2.0 collective-permute-start.9
  71.2 3.5 %collective-permute-start.8 = (f32[2,64,128]{2,1,0:T(8,128)S(1)}, f32[2,64,128]{2,1,0:T(8,128)S(1)}, u32[]{:S(2)}, u32[]{:S(2)}) collective-permute-start(f32[2,64,128]{2,1,0:T(8,128)S(1)} %get-tuple-element.82), channel_id=1, source_target_pairs={{0,32},{1,33},{2,34},{3,35},{4,36},{5,37},{6,38},{7,39},{8,40},{9,... | collective-permute-start | bytes 196616 | tf_op jit(solution)/shard_map/ppermute | solution.py:371
  74.8 2.2 collective-permute-done.9.below
  79.0 13.7 %all-to-all-start.1 = ((f32[8,8,8,128]{3,2,1,0:T(8,128)}), f32[8,8,8,128]{3,2,1,0:T(8,128)S(1)}, u32[]{:S(2)}, u32[]{:S(2)}) async-start(f32[8,8,8,128]{3,2,1,0:T(8,128)} %scatter_kernel.2), calls=%async_computation.1 | async-start | bytes 524288 | tf_op jit(solution)/shard_map/all_to_all | solution.py:375
  92.9 3.4 %collective-permute-start.10 = (f32[2,128,128]{2,1,0:T(8,128)S(1)}, f32[2,128,128]{2,1,0:T(8,128)S(1)}, u32[]{:S(2)}, u32[]{:S(2)}) collective-permute-start(f32[2,128,128]{2,1,0:T(8,128)S(1)} %get-tuple-element.64), channel_id=1, source_target_pairs={{0,1},{1,2},{2,3},{3,4},{4,5},{5,6},{6,7},{7,8},{8,9},{9,10},{10,1... | collective-permute-start | bytes 393224 | tf_op jit(solution)/shard_map/ppermute | solution.py:371
  97.5 3.5 %collective-permute-done.10.from_left = f32[2,128,128]{2,1,0:T(8,128)S(1)} collective-permute-done((f32[2,128,128]{2,1,0:T(8,128)S(1)}, f32[2,128,128]{2,1,0:T(8,128)S(1)}, u32[]{:S(2)}, u32[]{:S(2)}) %collective-permute-start.10) | collective-permute-done | bytes 131104 | tf_op jit(solution)/shard_map/ppermute | solution.py:371
  103.5 5.6 %all-to-all-start.2 = ((f32[4,8,8,128]{3,2,1,0:T(8,128)}), f32[4,8,8,128]{3,2,1,0:T(8,128)S(1)}, u32[]{:S(2)}, u32[]{:S(2)}) async-start(f32[4,8,8,128]{3,2,1,0:T(8,128)} %reduce_kernel.2), calls=%async_computation.2 | async-start | bytes 262144 | tf_op jit(solution)/shard_map/all_to_all | solution.py:375
  109.1 7.2 %all-to-all-done.2.parts = f32[4,8,8,128]{3,2,1,0:T(8,128)S(1)} async-done(((f32[4,8,8,128]{3,2,1,0:T(8,128)}), f32[4,8,8,128]{3,2,1,0:T(8,128)S(1)}, u32[]{:S(2)}, u32[]{:S(2)}) %all-to-all-start.2) | async-done | bytes 131104 | tf_op jit(solution)/shard_map/all_to_all | solution.py:375
  117.2 10.4 %all-to-all-start.3 = ((f32[16,6,8,128]{3,2,1,0:T(8,128)}), f32[16,6,8,128]{3,2,1,0:T(8,128)S(1)}, u32[]{:S(2)}, u32[]{:S(2)}) async-start(f32[16,6,8,128]{3,2,1,0:T(8,128)} %strip_kernel.2), calls=%async_computation.3 | async-start | bytes 786432 | tf_op jit(solution)/shard_map/all_to_all | solution.py:375
  127.6 8.3 %all-to-all-done.3.totals = f32[16,6,8,128]{3,2,1,0:T(8,128)S(1)} async-done(((f32[16,6,8,128]{3,2,1,0:T(8,128)}), f32[16,6,8,128]{3,2,1,0:T(8,128)S(1)}, u32[]{:S(2)}, u32[]{:S(2)}) %all-to-all-start.3) | async-done | bytes 393248 | tf_op jit(solution)/shard_map/all_to_all | solution.py:375
  136.8 8.5 %next_kernel.1 = (f32[3,2,64,128]{3,2,1,0:T(8,128)S(1)}, f32[3,2,128,128]{3,2,1,0:T(8,128)S(1)}, f32[3,2,64,128]{3,2,1,0:T(8,128)S(1)}, f32[5,128,128]{2,1,0:T(8...) custom-call(s32[8,2]{1,0:T(8,128)S(1)} %copy.18.starts, ...), custom_call_target="tpu_custom_call" | custom-call | tf_op jit(solution)/shard_map/next_kernel/pallas_call | solution.py:351
  145.3 1.9 collective-permute-start.12
  147.2 2.5 %collective-permute-start.13 = (f32[3,2,64,128]{3,2,1,0:T(8,128)S(1)}, f32[3,2,64,128]{3,2,1,0:T(8,128)S(1)}, u32[]{:S(2)}, u32[]{:S(2)}) collective-permute-start(f32[3,2,64,128]{3,2,1,0:T(8,128)S(1)} %get-tuple-element.71), channel_id=1, source_target_pairs={{32,0},{33,1},{34,2},{35,3},{36,4},{37,5},{38,6},{39,7},{40,8},{41... | collective-permute-start | bytes 589832 | tf_op jit(solution)/shard_map/ppermute | solution.py:371
  149.8 4.4 %collective-permute-done.13.from_below = f32[3,2,64,128]{3,2,1,0:T(8,128)S(1)} collective-permute-done((f32[3,2,64,128]{3,2,1,0:T(8,128)S(1)}, f32[3,2,64,128]{3,2,1,0:T(8,128)S(1)}, u32[]{:S(2)}, u32[]{:S(2)}) %collective-permute-start.13) | collective-permute-done | bytes 196640 | tf_op jit(solution)/shard_map/ppermute | solution.py:371
  157.3 3.7 %collective-permute-done.15.from_right = f32[3,64,128]{2,1,0:T(8,128)S(1)} collective-permute-done((f32[3,64,128]{2,1,0:T(8,128)S(1)}, f32[3,64,128]{2,1,0:T(8,128)S(1)}, u32[]{:S(2)}, u32[]{:S(2)}) %collective-permute-start.15) | collective-permute-done | bytes 98336 | tf_op jit(solution)/shard_map/ppermute | solution.py:371
  161.1 4.7 %merge_kernel.3 = (f32[16,7,8,128]{3,2,1,0:T(8,128)S(1)}, f32[8,128]{1,0:T(8,128)S(1)}, f32[2,128,128]{2,1,0:T(8,128)S(1)}) custom-call(s32[72,2]{1,0:T(8,128)S(1)} %bitcast.13, f32[3,128,128]{2,1,0:T(8,128)S(1)} %get-tuple-element.72.tile, f32[3,64,128]{2,1,0:T(8,128)S(1)} %collective-permute-done.14.from_left, ...), custom_call_target="tpu_custom_call" | custom-call | tf_op jit(solution)/shard_map/merge_kernel/pallas_call | solution.py:351
  165.8 16.9 %all_to_all.40.parts = f32[16,7,8,128]{3,2,1,0:T(8,128)S(1)} all-to-all(f32[16,7,8,128]{3,2,1,0:T(8,128)S(1)} %get-tuple-element.77), channel_id=1, replica_groups=mesh['yl'=2,'x'=4,'c'=2,'yh'=4,'z'=8] {'yl','x','c'}, dimensions={0} | all-to-all | bytes 917504 | tf_op jit(solution)/shard_map/all_to_all | solution.py:375
  182.8 19.1 %all_to_all.41.parts = f32[8,8,8,128]{3,2,1,0:T(8,128)S(1)} all-to-all(f32[8,8,8,128]{3,2,1,0:T(8,128)S(1)} %scatter_kernel.3), channel_id=1, replica_groups=mesh['yl'=2,'x'=4,'c'=2,'yh'=4,'z'=8] {'z'}, dimensions={0} | all-to-all | bytes 524288 | tf_op jit(solution)/shard_map/all_to_all | solution.py:375
  201.9 9.8 %all_to_all.42.parts = f32[4,8,8,128]{3,2,1,0:T(8,128)S(1)} all-to-all(f32[4,8,8,128]{3,2,1,0:T(8,128)S(1)} %reduce_kernel.3), channel_id=1, replica_groups=mesh['yl'=2,'x'=4,'c'=2,'yh'=4,'z'=8] {'yh'}, dimensions={0} | all-to-all | bytes 262144 | tf_op jit(solution)/shard_map/all_to_all | solution.py:375
  211.7 16.4 %all_to_all.43.totals = f32[16,6,8,128]{3,2,1,0:T(8,128)S(1)} all-to-all(f32[16,6,8,128]{3,2,1,0:T(8,128)S(1)} %strip_kernel.3), channel_id=1, replica_groups=mesh['yl'=2,'x'=4,'c'=2,'yh'=4,'z'=8] {'yl','x','c'}, dimensions={0} | all-to-all | bytes 786432 | tf_op jit(solution)/shard_map/all_to_all | solution.py:375
  (77 shorter events, 21.4 us)
Async XLA Ops:
  2.4 11.2 %copy-start.4 = (f32[2,128,128]{2,1,0:T(8,128)S(1)}, f32[2,128,128]{2,1,0:T(8,128)}, u32[]{:S(2)}) copy-start(f32[2,128,128]{2,1,0:T(8,128)} %own.3) | copy-start | bytes 393220
  2.4 10.2 %copy-start.8 = (s32[1,1,2,8,2]{3,4,2,1,0:T(2,128)S(1)}, s32[1,1,2,8,2]{3,4,2,1,0:T(2,128)}, u32[]{:S(2)}) copy-start(s32[1,1,2,8,2]{3,4,2,1,0:T(2,128)} %param.11) | copy-start | bytes 388
  2.4 10.3 %collective-permute-start = (f32[2,72,128]{2,1,0:T(8,128)S(1)}, f32[2,72,128]{2,1,0:T(8,128)S(1)}, u32[]{:S(2)}, u32[]{:S(2)}) collective-permute-start(f32[2,72,128]{2,1,0:T(8,128)S(1)} %get-tuple-element.89), channel_id=1, source_target_pairs={{0,32},{1,33},{2,34},{3,35},{4,36},{5,37},{6,38},{7,39},{8,40},{9,... | collective-permute-start | bytes 221192 | tf_op jit(solution)/shard_map/ppermute | solution.py:371
  7.1 6.5 %collective-permute-start.1 = (f32[2,72,128]{2,1,0:T(8,128)S(1)}, f32[2,72,128]{2,1,0:T(8,128)S(1)}, u32[]{:S(2)}, u32[]{:S(2)}) collective-permute-start(f32[2,72,128]{2,1,0:T(8,128)S(1)} %get-tuple-element.90), channel_id=1, source_target_pairs={{32,0},{33,1},{34,2},{35,3},{36,4},{37,5},{38,6},{39,7},{40,8},{41... | collective-permute-start | bytes 221192 | tf_op jit(solution)/shard_map/ppermute | solution.py:371
  13.6 10.4 %copy-start = (f32[1,1,2,8,128,128]{5,4,3,2,1,0:T(8,128)S(1)}, f32[1,1,2,8,128,128]{5,4,3,2,1,0:T(8,128)}, u32[]{:S(2)}) copy-start(f32[1,1,2,8,128,128]{5,4,3,2,1,0:T(8,128)} %measured.3) | copy-start | bytes 3145732
  13.7 10.2 %copy-start.3 = (bf16[768,256]{1,0:T(8,128)(2,1)S(1)}, bf16[768,256]{1,0:T(8,128)(2,1)}, u32[]{:S(2)}) copy-start(bf16[768,256]{1,0:T(8,128)(2,1)} %constant.62.clone.right3) | copy-start | bytes 1179652
  13.8 5.8 %collective-permute-start.2 = (f32[2,152,128]{2,1,0:T(8,128)S(1)}, f32[2,152,128]{2,1,0:T(8,128)S(1)}, u32[]{:S(2)}, u32[]{:S(2)}) collective-permute-start(f32[2,152,128]{2,1,0:T(8,128)S(1)} %get-tuple-element.87), channel_id=1, source_target_pairs={{0,1},{1,2},{2,3},{3,4},{4,5},{5,6},{6,7},{7,8},{8,9},{9,10},{10,1... | collective-permute-start | bytes 466952 | tf_op jit(solution)/shard_map/ppermute | solution.py:371
  17.1 6.6 %collective-permute-start.3 = (f32[2,152,128]{2,1,0:T(8,128)S(1)}, f32[2,152,128]{2,1,0:T(8,128)S(1)}, u32[]{:S(2)}, u32[]{:S(2)}) collective-permute-start(f32[2,152,128]{2,1,0:T(8,128)S(1)} %get-tuple-element.88), channel_id=1, source_target_pairs={{1,0},{2,1},{3,2},{4,3},{5,4},{6,5},{7,6},{8,7},{9,8},{10,9},{11,1... | collective-permute-start | bytes 466952 | tf_op jit(solution)/shard_map/ppermute | solution.py:371
  23.8 1.0 copy-start.2
  23.9 1.0 copy-start.1
  33.4 6.6 %collective-permute-start.4 = (f32[3,2,64,128]{3,2,1,0:T(8,128)S(1)}, f32[3,2,64,128]{3,2,1,0:T(8,128)S(1)}, u32[]{:S(2)}, u32[]{:S(2)}) collective-permute-start(f32[3,2,64,128]{3,2,1,0:T(8,128)S(1)} %get-tuple-element.51), channel_id=1, source_target_pairs={{0,32},{1,33},{2,34},{3,35},{4,36},{5,37},{6,38},{7,39},{8,40},{9,... | collective-permute-start | bytes 589832 | tf_op jit(solution)/shard_map/ppermute | solution.py:371
  37.4 7.0 %collective-permute-start.5 = (f32[3,2,64,128]{3,2,1,0:T(8,128)S(1)}, f32[3,2,64,128]{3,2,1,0:T(8,128)S(1)}, u32[]{:S(2)}, u32[]{:S(2)}) collective-permute-start(f32[3,2,64,128]{3,2,1,0:T(8,128)S(1)} %get-tuple-element.52), channel_id=1, source_target_pairs={{32,0},{33,1},{34,2},{35,3},{36,4},{37,5},{38,6},{39,7},{40,8},{41... | collective-permute-start | bytes 589832 | tf_op jit(solution)/shard_map/ppermute | solution.py:371
  44.6 5.6 %collective-permute-start.6 = (f32[3,64,128]{2,1,0:T(8,128)S(1)}, f32[3,64,128]{2,1,0:T(8,128)S(1)}, u32[]{:S(2)}, u32[]{:S(2)}) collective-permute-start(f32[3,64,128]{2,1,0:T(8,128)S(1)} %get-tuple-element.54), channel_id=1, source_target_pairs={{0,1},{1,2},{2,3},{3,4},{4,5},{5,6},{6,7},{7,8},{8,9},{9,10},{10,1... | collective-permute-start | bytes 294920 | tf_op jit(solution)/shard_map/ppermute | solution.py:371
  48.6 7.2 %collective-permute-start.7 = (f32[3,64,128]{2,1,0:T(8,128)S(1)}, f32[3,64,128]{2,1,0:T(8,128)S(1)}, u32[]{:S(2)}, u32[]{:S(2)}) collective-permute-start(f32[3,64,128]{2,1,0:T(8,128)S(1)} %get-tuple-element.55), channel_id=1, source_target_pairs={{1,0},{2,1},{3,2},{4,3},{5,4},{6,5},{7,6},{8,7},{9,8},{10,9},{11,1... | collective-permute-start | bytes 294920 | tf_op jit(solution)/shard_map/ppermute | solution.py:371
  60.5 0.8 copy-start.5
  61.3 17.0 %all-to-all-start = ((f32[16,7,8,128]{3,2,1,0:T(8,128)}), f32[16,7,8,128]{3,2,1,0:T(8,128)S(1)}, u32[]{:S(2)}, u32[]{:S(2)}) async-start(f32[16,7,8,128]{3,2,1,0:T(8,128)} %copy-done.5), calls=%async_computation | async-start | bytes 917504 | tf_op jit(solution)/shard_map/all_to_all | solution.py:375
  69.2 7.8 %collective-permute-start.9 = (f32[2,64,128]{2,1,0:T(8,128)S(1)}, f32[2,64,128]{2,1,0:T(8,128)S(1)}, u32[]{:S(2)}, u32[]{:S(2)}) collective-permute-start(f32[2,64,128]{2,1,0:T(8,128)S(1)} %get-tuple-element.81), channel_id=1, source_target_pairs={{32,0},{33,1},{34,2},{35,3},{36,4},{37,5},{38,6},{39,7},{40,8},{41... | collective-permute-start | bytes 196616 | tf_op jit(solution)/shard_map/ppermute | solution.py:371
  71.2 5.8 %collective-permute-start.8 = (f32[2,64,128]{2,1,0:T(8,128)S(1)}, f32[2,64,128]{2,1,0:T(8,128)S(1)}, u32[]{:S(2)}, u32[]{:S(2)}) collective-permute-start(f32[2,64,128]{2,1,0:T(8,128)S(1)} %get-tuple-element.82), channel_id=1, source_target_pairs={{0,32},{1,33},{2,34},{3,35},{4,36},{5,37},{6,38},{7,39},{8,40},{9,... | collective-permute-start | bytes 196616 | tf_op jit(solution)/shard_map/ppermute | solution.py:371
  79.0 23.8 %all-to-all-start.1 = ((f32[8,8,8,128]{3,2,1,0:T(8,128)}), f32[8,8,8,128]{3,2,1,0:T(8,128)S(1)}, u32[]{:S(2)}, u32[]{:S(2)}) async-start(f32[8,8,8,128]{3,2,1,0:T(8,128)} %scatter_kernel.2), calls=%async_computation.1 | async-start | bytes 524288 | tf_op jit(solution)/shard_map/all_to_all | solution.py:375
  92.9 8.2 %collective-permute-start.10 = (f32[2,128,128]{2,1,0:T(8,128)S(1)}, f32[2,128,128]{2,1,0:T(8,128)S(1)}, u32[]{:S(2)}, u32[]{:S(2)}) collective-permute-start(f32[2,128,128]{2,1,0:T(8,128)S(1)} %get-tuple-element.64), channel_id=1, source_target_pairs={{0,1},{1,2},{2,3},{3,4},{4,5},{5,6},{6,7},{7,8},{8,9},{9,10},{10,1... | collective-permute-start | bytes 393224 | tf_op jit(solution)/shard_map/ppermute | solution.py:371
  96.2 6.2 %collective-permute-start.11 = (f32[2,128,128]{2,1,0:T(8,128)S(1)}, f32[2,128,128]{2,1,0:T(8,128)S(1)}, u32[]{:S(2)}, u32[]{:S(2)}) collective-permute-start(f32[2,128,128]{2,1,0:T(8,128)S(1)} %get-tuple-element.65), channel_id=1, source_target_pairs={{1,0},{2,1},{3,2},{4,3},{5,4},{6,5},{7,6},{8,7},{9,8},{10,9},{11,1... | collective-permute-start | bytes 393224 | tf_op jit(solution)/shard_map/ppermute | solution.py:371
  102.4 1.0 copy-start.6
  103.5 12.9 %all-to-all-start.2 = ((f32[4,8,8,128]{3,2,1,0:T(8,128)}), f32[4,8,8,128]{3,2,1,0:T(8,128)S(1)}, u32[]{:S(2)}, u32[]{:S(2)}) async-start(f32[4,8,8,128]{3,2,1,0:T(8,128)} %reduce_kernel.2), calls=%async_computation.2 | async-start | bytes 262144 | tf_op jit(solution)/shard_map/all_to_all | solution.py:375
  117.2 18.7 %all-to-all-start.3 = ((f32[16,6,8,128]{3,2,1,0:T(8,128)}), f32[16,6,8,128]{3,2,1,0:T(8,128)S(1)}, u32[]{:S(2)}, u32[]{:S(2)}) async-start(f32[16,6,8,128]{3,2,1,0:T(8,128)} %strip_kernel.2), calls=%async_computation.3 | async-start | bytes 786432 | tf_op jit(solution)/shard_map/all_to_all | solution.py:375
  135.9 0.9 copy-start.7
  145.3 4.5 %collective-permute-start.12 = (f32[3,2,64,128]{3,2,1,0:T(8,128)S(1)}, f32[3,2,64,128]{3,2,1,0:T(8,128)S(1)}, u32[]{:S(2)}, u32[]{:S(2)}) collective-permute-start(f32[3,2,64,128]{3,2,1,0:T(8,128)S(1)} %get-tuple-element.70), channel_id=1, source_target_pairs={{0,32},{1,33},{2,34},{3,35},{4,36},{5,37},{6,38},{7,39},{8,40},{9,... | collective-permute-start | bytes 589832 | tf_op jit(solution)/shard_map/ppermute | solution.py:371
  147.2 7.0 %collective-permute-start.13 = (f32[3,2,64,128]{3,2,1,0:T(8,128)S(1)}, f32[3,2,64,128]{3,2,1,0:T(8,128)S(1)}, u32[]{:S(2)}, u32[]{:S(2)}) collective-permute-start(f32[3,2,64,128]{3,2,1,0:T(8,128)S(1)} %get-tuple-element.71), channel_id=1, source_target_pairs={{32,0},{33,1},{34,2},{35,3},{36,4},{37,5},{38,6},{39,7},{40,8},{41... | collective-permute-start | bytes 589832 | tf_op jit(solution)/shard_map/ppermute | solution.py:371
  154.4 2.9 %collective-permute-start.14 = (f32[3,64,128]{2,1,0:T(8,128)S(1)}, f32[3,64,128]{2,1,0:T(8,128)S(1)}, u32[]{:S(2)}, u32[]{:S(2)}) collective-permute-start(f32[3,64,128]{2,1,0:T(8,128)S(1)} %get-tuple-element.73), channel_id=1, source_target_pairs={{0,1},{1,2},{2,3},{3,4},{4,5},{5,6},{6,7},{7,8},{8,9},{9,10},{10,1... | collective-permute-start | bytes 294920 | tf_op jit(solution)/shard_map/ppermute | solution.py:371
  155.7 5.4 %collective-permute-start.15 = (f32[3,64,128]{2,1,0:T(8,128)S(1)}, f32[3,64,128]{2,1,0:T(8,128)S(1)}, u32[]{:S(2)}, u32[]{:S(2)}) collective-permute-start(f32[3,64,128]{2,1,0:T(8,128)S(1)} %get-tuple-element.74), channel_id=1, source_target_pairs={{1,0},{2,1},{3,2},{4,3},{5,4},{6,5},{7,6},{8,7},{9,8},{10,9},{11,1... | collective-permute-start | bytes 294920 | tf_op jit(solution)/shard_map/ppermute | solution.py:371

commit v2 on v1

v2 whole, which is shorter than its diff:
```python
import math
from functools import partial

import jax
import jax.numpy as jnp
import numpy as np
from jax import lax
from jax.experimental import pallas as pl
from jax.experimental.pallas import tpu as pltpu
from jax.sharding import Mesh, PartitionSpec as P

SIZE = 128
HALF = 64
MODES = 2
COUNT = 8
GROUP = 2
ROW = ("yl", "x", "c")
COL = ("yh", "z")
ALL = ROW + COL
TILES = 8
VMEM_LIMIT = 48 * 1024 * 1024
F32 = jnp.float32
BF16 = jnp.bfloat16


def dft_tables():
    index = np.arange(SIZE)
    angle = 2.0 * math.pi / SIZE * (np.outer(index, index) % SIZE)
    real = np.cos(angle) / math.sqrt(SIZE)
    imag = -np.sin(angle) / math.sqrt(SIZE)
    right = np.block([[real, imag], [-imag, real]]).astype(np.float32)
    high = right.astype(jnp.bfloat16)
    low = (right - high.astype(np.float32)).astype(jnp.bfloat16)
    right3 = np.concatenate([high, high, low], axis=0)
    left3 = np.ascontiguousarray(right3.T)
    return right3, left3


def halves(x):
    high = x.astype(BF16)
    return high, (x - high.astype(F32)).astype(BF16)


def right_transform(fields, table):
    rows = []
    for real, imag in fields:
        rh, rl = halves(real)
        ih, il = halves(imag)
        rows.append(jnp.concatenate([rh, ih, rl, il, rh, ih], axis=1))
    out = jnp.dot(jnp.concatenate(rows, axis=0), table, preferred_element_type=F32)
    return [
        (out[SIZE * n : SIZE * (n + 1), :SIZE], out[SIZE * n : SIZE * (n + 1), SIZE:])
        for n in range(len(fields))
    ]


def left_transform(fields, table):
    cols = []
    for real, imag in fields:
        rh, rl = halves(real)
        ih, il = halves(imag)
        cols.append(jnp.concatenate([rh, ih, rl, il, rh, ih], axis=0))
    out = jnp.dot(table, jnp.concatenate(cols, axis=1), preferred_element_type=F32)
    return [
        (out[:SIZE, SIZE * n : SIZE * (n + 1)], out[SIZE:, SIZE * n : SIZE * (n + 1)])
        for n in range(len(fields))
    ]


def lanes():
    return lax.broadcasted_iota(jnp.int32, (SIZE, SIZE), 1)


def window(ref, lead, row, col):
    shift = lax.rem(SIZE - col, SIZE)
    first = pltpu.roll(ref[lead + (0, pl.ds(row, SIZE))], shift, 1)
    second = pltpu.roll(ref[lead + (1, pl.ds(row, SIZE))], shift, 1)
    return jnp.where(lanes() < SIZE - col, first, second)


def place(ref, plane, row, col, block):
    moved = pltpu.roll(block, lax.rem(col, SIZE), 1)
    first = lanes() >= col
    rows = pl.ds(row, SIZE)
    ref[plane, 0, rows] += jnp.where(first, moved, 0.0)
    ref[plane, 1, rows] += jnp.where(first, 0.0, moved)


def join(low, first, second):
    return jnp.where(low, pltpu.roll(first, HALF, 1), pltpu.roll(second, HALF, 1))


def pack_low(low, upper, lower):
    return jnp.where(low, upper, pltpu.roll(lower, HALF, 1))


def pack_high(low, upper, lower):
    return jnp.where(low, pltpu.roll(upper, HALF, 1), lower)


def low_lanes(rows):
    return lax.broadcasted_iota(jnp.int32, (rows, SIZE), 1) < HALF


def bounds(edges):
    return tuple(edges[k] for k in range(4))


def inside(limits, down, across, rows=SIZE):
    row_low, row_high, col_low, col_high = limits
    line = lax.broadcasted_iota(jnp.int32, (rows, SIZE), 0) + down
    lane = lax.broadcasted_iota(jnp.int32, (rows, SIZE), 1) + across
    return (line >= row_low) & (line < row_high) & (lane >= col_low) & (lane < col_high)


def send_kernel(offsets, own, bottom, top):
    line = lax.broadcasted_iota(jnp.int32, (TILES, SIZE), 0)
    lane = lax.broadcasted_iota(jnp.int32, (TILES, SIZE), 1)
    code = jnp.zeros((TILES, SIZE), jnp.int32)
    batches, count, _ = offsets.shape
    for b in range(batches):
        for k in range(count):
            for d in range(2):
                code = jnp.where(lane == (b * count + k) * 2 + d, offsets[b, k, d], code)
    code = jnp.where(line == 0, code, 0).astype(F32)
    for c in range(2):
        bottom[c, :HALF] = own[c, HALF:]
        bottom[c, HALF:] = code
        top[c] = own[c, :HALF]


def pack_kernel(above, own, below, bottom, to_left, to_right):
    low = low_lanes(HALF)
    for c in range(2):
        strips = (above[c, :HALF], own[c, :HALF], own[c, HALF:], below[c])
        for k in range(2):
            rows = slice(HALF * k, HALF * (k + 1))
            to_left[c, rows] = pack_low(low, strips[k], strips[k + 2])
            to_right[c, rows] = pack_high(low, strips[k], strips[k + 2])
        to_right[c, SIZE : SIZE + TILES] = bottom[c, HALF:]
        to_right[c, SIZE + TILES :] = above[c, HALF:]


def sweep(batch, offsets, limits, padded, probe, measured, right3, left3,
          own, right, below, corner, sums, accum):
    accum[...] = jnp.zeros_like(accum)
    sums[...] = jnp.zeros_like(sums)
    tr = right3[...]
    tl = left3[...]

    def body(step, carry):
        wins = []
        fields = []
        for g in range(GROUP):
            j = step * GROUP + g
            row, col = offsets[batch, j, 0] + HALF, offsets[batch, j, 1] + HALF
            wr = window(padded, (0,), row, col)
            wi = window(padded, (1,), row, col)
            wins.append((row, col, wr, wi))
            for m in range(MODES):
                pr, pi = probe[0, m], probe[1, m]
                fields.append((pr * wr - pi * wi, pr * wi + pi * wr))
        waves = left_transform(right_transform(fields, tr), tl)
        back = []
        for g in range(GROUP):
            mine = waves[g * MODES : (g + 1) * MODES]
            intensity = sum(r * r + i * i for r, i in mine)
            recorded = measured[0, 0, batch, step * GROUP + g]
            ratio = jnp.sqrt(recorded) / jnp.maximum(jnp.sqrt(intensity), 0.5) - 1.0
            back += [(r * ratio, -(i * ratio)) for r, i in mine]
        chis = right_transform(left_transform(back, tl), tr)
        for g in range(GROUP):
            row, col, wr, wi = wins[g]
            cr = jnp.zeros((SIZE, SIZE), F32)
            ci = jnp.zeros((SIZE, SIZE), F32)
            for m in range(MODES):
                xr, xn = chis[g * MODES + m]
                pr, pi = probe[0, m], probe[1, m]
                cr += pr * xr - pi * xn
                ci -= pr * xn + pi * xr
                sums[m] += wr * xr - wi * xn
                sums[MODES + m] -= wr * xn + wi * xr
            sums[2 * MODES] += wr * wr + wi * wi
            place(accum, 0, row, col, cr)
            place(accum, 1, row, col, ci)
        return carry

    lax.fori_loop(0, COUNT // GROUP, body, 0)
    for v, h, out in ((0, 0, own), (0, 1, right), (1, 0, below), (1, 1, corner)):
        valid = inside(limits, v * SIZE, h * SIZE)
        for c in range(2):
            out[c] = jnp.where(valid, accum[c, h, v * SIZE : (v + 1) * SIZE], 0.0)


def first_kernel(offsets, edges, above, tile, below, from_left, from_right, probe, measured, right3, left3,
                 own_g, right_g, below_g, corner_g, sums, padded, core, accum):
    limits = bounds(edges)
    low = low_lanes(HALF)
    for c in range(2):
        strips = (above[c, :HALF], tile[c, :HALF], tile[c, HALF:], below[c])
        for k in range(4):
            half = slice(HALF * (k % 2), HALF * (k % 2 + 1))
            left, right = from_left[c, half], from_right[c, half]
            if k < 2:
                right = pltpu.roll(right, HALF, 1)
            else:
                left = pltpu.roll(left, HALF, 1)
            mine = pltpu.roll(strips[k], HALF, 1)
            rows = slice(HALF * k, HALF * (k + 1))
            first = jnp.where(low, left, mine)
            second = jnp.where(low, mine, right)
            if k < 2:
                core[c, rows] = first
            padded[c, 0, rows] = jnp.where(inside(limits, HALF * k, 0, HALF), first, 0.0)
            padded[c, 1, rows] = jnp.where(inside(limits, HALF * k, SIZE, HALF), second, 0.0)
    sweep(0, offsets, limits, padded, probe, measured, right3, left3,
          own_g, right_g, below_g, corner_g, sums, accum)


def window_classes(offsets, others, batch, limits):
    row_low, _, col_low, _ = limits
    line = lax.broadcasted_iota(jnp.int32, (SIZE, SIZE), 0)
    lane = lanes()
    count = offsets.shape[1]
    for v in range(2):
        for h in range(2):
            rows = line < SIZE - row_low if v else line >= row_low
            cols = lane < SIZE - col_low if h else lane >= col_low
            shifts = []
            for j in range(count):
                if v or h:
                    at = (batch * count + j) * 2
                    which = 2 * v + h - 1
                    row, col = others[which, at], others[which, at + 1]
                else:
                    row, col = offsets[batch, j, 0], offsets[batch, j, 1]
                shifts.append((row + HALF - v * SIZE, col + HALF - h * SIZE))
            yield rows & cols, shifts


def moved_sum(ref, lead, shifts, sign):
    lane = lanes()
    total = jnp.zeros((SIZE, SIZE), F32)
    for row, col in shifts:
        row, col = sign * row, sign * col
        moved = pltpu.roll(ref[lead + (pl.ds(SIZE + row, SIZE),)], lax.rem(2 * SIZE - col, SIZE), 1)
        source = lane + col
        total += jnp.where((source >= 0) & (source < SIZE), moved, 0.0)
    return total


def cover_kernel(batch, offsets, others, edges, probe, cover, light):
    limits = bounds(edges)
    light[...] = jnp.zeros_like(light)
    light[SIZE : 2 * SIZE] = sum(probe[c, m] * probe[c, m] for c in range(2) for m in range(MODES))
    total = jnp.zeros((SIZE, SIZE), F32)
    for mask, shifts in window_classes(offsets, others, batch, limits):
        total += jnp.where(mask, moved_sum(light, (), shifts, -1), 0.0)
    cover[...] = total


def merge_kernel(batch, offsets, others, edges, own, from_left, from_above, from_corner, cover, core, sums,
                 packed, numbers, direction, product):
    limits = bounds(edges)
    light = cover[...]
    inverse = 1.0 / (light + 1.0)
    dr, di = ((own[c] + from_left[c] + from_above[c] + from_corner[c]) * inverse for c in range(2))
    direction[0] = dr
    direction[1] = di
    power = dr * dr + di * di
    a11 = jnp.sum(power * light, axis=0, keepdims=True)
    b1 = jnp.sum(power * (light + 1.0), axis=0, keepdims=True)
    line = lax.broadcasted_iota(jnp.int32, (TILES, SIZE), 0)
    numbers[...] = jnp.where(line == 0, a11, jnp.where(line == 1, b1, 0.0))

    er = dr * core[0] + di * core[1]
    ei = dr * core[1] - di * core[0]
    for c in range(2):
        product[c, :SIZE] = jnp.zeros((SIZE, SIZE), F32)
        product[c, 2 * SIZE :] = jnp.zeros((SIZE, SIZE), F32)
    overlap = [jnp.zeros((SIZE, SIZE), F32)] * 2
    for mask, shifts in window_classes(offsets, others, batch, limits):
        product[0, SIZE : 2 * SIZE] = jnp.where(mask, er, 0.0)
        product[1, SIZE : 2 * SIZE] = jnp.where(mask, ei, 0.0)
        overlap = [overlap[c] + moved_sum(product, (c,), shifts, 1) for c in range(2)]

    strips = (SIZE // TILES, TILES, SIZE)
    for k in range(5):
        packed[:, k] = sums[k].reshape(strips)
    for c in range(2):
        packed[:, 5 + c] = overlap[c].reshape(strips)


def add_all(parts):
    total = parts[0]
    for k in range(1, parts.shape[0]):
        total = total + parts[k]
    return total


def scatter_kernel(parts, numbers, out):
    total = add_all(parts)
    for k in range(out.shape[0]):
        out[k, :7] = total
        out[k, 7] = numbers[...]


def reduce_kernel(parts, out):
    total = add_all(parts)
    for k in range(out.shape[0]):
        out[k] = total


def strip_kernel(place_ref, parts, probe, out):
    total = add_all(parts)
    rows = pl.ds(pl.multiple_of(place_ref[0] * TILES, TILES), TILES)
    cover = total[2 * MODES]
    inverse = 1.0 / (cover + 1.0)
    cross = jnp.zeros((TILES, SIZE), F32)
    power = jnp.zeros((TILES, SIZE), F32)
    for m in range(MODES):
        dr, di = total[m] * inverse, total[MODES + m] * inverse
        pr, pi = probe[0, m, rows], probe[1, m, rows]
        cross += (pr * dr + pi * di) * total[5] - (pr * di - pi * dr) * total[6]
        power += dr * dr + di * di
    line = lax.broadcasted_iota(jnp.int32, (TILES, SIZE), 0)
    numbers = total[7]
    for k, term in ((2, power * cover), (3, power * (cover + 1.0)), (4, cross)):
        numbers = jnp.where(line == k, jnp.sum(term, axis=0, keepdims=True), numbers)
    for k in range(out.shape[0]):
        out[k, :5] = total[:5]
        out[k, 5] = numbers


def step_sizes(totals, probe, new_probe, gradient=None):
    numbers = jnp.sum(add_all(totals.at[:, 5]), axis=1, keepdims=True)
    a11, b1, a22, b2, a12 = (numbers[k : k + 1] for k in range(5))
    a11 = 1.1 * a11
    a22 = 1.1 * a22
    det = a11 * a22 - a12 * a12
    step_obj = (b1 * a22 - a12 * b2) / det
    step_probe = (a11 * b2 - a12 * b1) / det
    cover = totals[:, 4].reshape(SIZE, SIZE) + 1.0
    scale = step_probe / cover
    for m in range(MODES):
        for c in range(2):
            numer = totals[:, MODES * c + m].reshape(SIZE, SIZE)
            new_probe[c, m] = probe[c, m] + scale * numer
            if gradient is not None:
                gradient[c, m] = numer * lax.rsqrt(cover)
    return step_obj


def next_kernel(offsets, edges, totals, padded, core, direction, from_below, from_right, from_corner, probe,
                measured, right3, left3,
                own_g, right_g, below_g, corner_g, sums, new_padded, new_core, new_probe, accum):
    limits = bounds(edges)
    step = step_sizes(totals, probe, new_probe)
    for v, h, part in ((0, 0, direction), (0, 1, from_right), (1, 0, from_below), (1, 1, from_corner)):
        valid = inside(limits, v * SIZE, h * SIZE)
        rows = slice(v * SIZE, (v + 1) * SIZE)
        for c in range(2):
            move = step * part[c]
            if (v, h) == (0, 0):
                new_core[c] = core[c] + move
            new_padded[c, h, rows] = padded[c, h, rows] + jnp.where(valid, move, 0.0)
    sweep(1, offsets, limits, new_padded, new_probe, measured, right3, left3,
          own_g, right_g, below_g, corner_g, sums, accum)


def last_kernel(totals, padded, direction, from_below, from_right, from_corner, probe,
                new_obj, new_probe, gradient):
    step = step_sizes(totals, probe, new_probe, gradient)
    low = low_lanes(HALF)
    for c in range(2):
        moves = (join(low, direction[c, HALF:], from_right[c]), join(low, from_below[c], from_corner[c]))
        for k in range(2):
            span = slice(HALF * (k + 1), HALF * (k + 2))
            old = join(low, padded[c, 0, span], padded[c, 1, span])
            new_obj[c, HALF * k : HALF * (k + 1)] = old + step * moves[k]


def shape(*dims):
    return jax.ShapeDtypeStruct(dims, F32)


def call(kernel, ins, outs, scratch=()):
    vmem = pl.BlockSpec(memory_space=pltpu.VMEM)
    smem = pl.BlockSpec(memory_space=pltpu.SMEM)
    specs = [smem if x.dtype == jnp.int32 else vmem for x in ins]
    return pl.pallas_call(
        kernel,
        in_specs=specs,
        out_specs=[vmem] * len(outs),
        out_shape=list(outs),
        scratch_shapes=list(scratch),
        compiler_params=pltpu.CompilerParams(vmem_limit_bytes=VMEM_LIMIT),
        name=getattr(kernel, "func", kernel).__name__,
    )(*ins)


def size_of(axes):
    return math.prod(lax.axis_size(a) for a in axes)


def shift(block, rows, cols):
    n_row, n_col = size_of(ROW), size_of(COL)
    route = [
        (r * n_col + c, (r + rows) % n_row * n_col + (c + cols) % n_col)
        for r in range(n_row)
        for c in range(n_col)
    ]
    return lax.ppermute(block, ALL, route)


def exchange(block, axes):
    return lax.all_to_all(block, axes, 0, 0, tiled=True)


def reduce_all(packed, numbers, probe, place_in_row, halo):
    part = exchange(packed, ROW)
    part, *halo = lax.optimization_barrier((part, *halo))
    (part,) = call(scatter_kernel, [part, numbers], [shape(size_of(("z",)), 8, TILES, SIZE)])
    part = exchange(part, ("z",))
    (part,) = call(reduce_kernel, [part], [shape(size_of(("yh",)), 8, TILES, SIZE)])
    part = exchange(part, ("yh",))
    (part,) = call(strip_kernel, [place_in_row, part, probe], [shape(packed.shape[0], 6, TILES, SIZE)])
    return exchange(part, ROW), halo


def per_device(obj, probe, measured, offsets):
    right3, left3 = (jnp.asarray(t) for t in dft_tables())
    offsets = offsets[0, 0]
    r, c = (lax.axis_index(axes).astype(jnp.int32) for axes in (ROW, COL))
    place_in_row = r.reshape(1)
    whole = 2 * SIZE
    edges = jnp.stack([
        jnp.where(r == 0, HALF, 0),
        jnp.where(r == size_of(ROW) - 1, whole - HALF, whole),
        jnp.where(c == 0, HALF, 0),
        jnp.where(c == size_of(COL) - 1, whole - HALF, whole),
    ]).astype(jnp.int32)
    quad = shape(2, SIZE, SIZE)
    field = shape(2, 2, whole, SIZE)
    planes = shape(2, MODES, SIZE, SIZE)
    accum = pltpu.VMEM((2, 2, whole, SIZE), F32)

    bottom, top = call(send_kernel, [offsets, obj], [shape(2, HALF + TILES, SIZE), shape(2, HALF, SIZE)])
    above = shift(bottom, 1, 0)
    below = shift(top, -1, 0)
    to_left, to_right = call(
        pack_kernel, [above, obj, below, bottom], [quad, shape(2, SIZE + 2 * TILES, SIZE)])
    from_left = shift(to_right, 0, 1)
    from_right = shift(to_left, 0, -1)
    others = jnp.concatenate(
        [from_left[0, SIZE : SIZE + 1], above[0, HALF : HALF + 1],
         from_left[0, SIZE + TILES : SIZE + TILES + 1]], axis=0)
    others = others[:, : offsets.size].astype(jnp.int32)

    *parts, sums, padded, core = call(
        first_kernel,
        [offsets, edges, above, obj, below, from_left, from_right, probe, measured, right3, left3],
        [quad] * 4 + [shape(5, SIZE, SIZE), field, quad],
        [accum],
    )

    def merge(batch, parts, sums, core, probe):
        own, right, below, corner = parts
        from_left = shift(right, 0, 1)
        from_above = shift(below, 1, 0)
        from_corner = shift(corner, 1, 1)
        (cover,) = call(
            partial(cover_kernel, batch), [offsets, others, edges, probe], [shape(SIZE, SIZE)],
            [pltpu.VMEM((3 * SIZE, SIZE), F32)])
        return call(
            partial(merge_kernel, batch),
            [offsets, others, edges, own, from_left, from_above, from_corner, cover, core, sums],
            [shape(SIZE // TILES, 7, TILES, SIZE), shape(TILES, SIZE), quad],
            [pltpu.VMEM((2, 3 * SIZE, SIZE), F32)],
        )

    packed, numbers, direction = merge(0, parts, sums, core, probe)
    halo = shift(direction, -1, 0), shift(direction, 0, -1), shift(direction, -1, -1)
    totals, halo = reduce_all(packed, numbers, probe, place_in_row, halo)
    *parts, sums, padded, core, probe = call(
        next_kernel,
        [offsets, edges, totals, padded, core, direction, *halo, probe, measured, right3, left3],
        [quad] * 4 + [shape(5, SIZE, SIZE), field, quad, planes],
        [accum],
    )
    packed, numbers, direction = merge(1, parts, sums, core, probe)
    upper, lower = direction[:, :HALF], direction[:, HALF:]
    halo = shift(upper, -1, 0), shift(lower, 0, -1), shift(upper, -1, -1)
    totals, halo = reduce_all(packed, numbers, probe, place_in_row, halo)
    return tuple(call(
        last_kernel, [totals, padded, direction, *halo, probe], [quad, planes, planes]))


def solution(mesh):
    parts = Mesh(mesh.devices.reshape(2, 4, 2, 4, 8), ALL)
    in_specs = (P(None, ROW, COL), P(), P(ROW, COL), P(ROW, COL))
    out_specs = (P(None, ROW, COL), P(), P())
    return jax.shard_map(
        per_device, mesh=parts, in_specs=in_specs, out_specs=out_specs, check_vma=False
    )
```

time: 230 us -> 239 us (1.039)
  blocking collectives: 62.2 us -> 92.4 us
  starting transfers between devices: 80.9 us -> 67.1 us
  waiting for transfers between devices: 49.4 us -> 44.3 us
  Pallas kernels: 30.4 us -> 27.3 us
    all_to_all x4 -> x6, blocking collectives: 62.2 us -> 92.4 us  [exchange(): return lax.all_to_all(block, axes, 0, 0, tiled=True)]
    all_to_all x4 -> x2, starting transfers between devices: 37.6 us -> 11.9 us  [exchange(): return lax.all_to_all(block, axes, 0, 0, tiled=True)]
    all_to_all x4 -> x2, waiting for transfers between devices: 17.2 us -> 2.02 us  [exchange(): return lax.all_to_all(block, axes, 0, 0, tiled=True)]
    ppermute x16, starting transfers between devices: 43.3 us -> 55.3 us  [shift(): return lax.ppermute(block, ALL, route)]
    ppermute x16, waiting for transfers between devices: 32.3 us -> 42.3 us  [shift(): return lax.ppermute(block, ALL, route)]
    pallas_call x15, Pallas kernels: 30.4 us -> 27.3 us  [call(): pl.pallas_call(kernel, in_specs=specs, out_specs=[vmem] * len(outs), out_...]
    unnamed x18 -> x20, local copies, waits for them, and re-layouts: 2.6 us -> 5.05 us
  transfers between devices with their start and end apart: 20 -> 18, of which waited for: 18 -> 11; matrix products, arithmetic and copies ran while one was open for 0% -> 0% of each run, Pallas kernels for 0% -> 1%
where the time goes in v2:
time: 239 us; the launch traced here: 238 us
  blocking collectives  92.4 us (39%)
  starting transfers between devices  67.1 us (28%)
  waiting for transfers between devices  44.3 us (19%)
  Pallas kernels  27.3 us (11%)
  local copies, waits for them, and re-layouts  5.83 us (2%)
    all_to_all x6, blocking collectives, exchange(): return lax.all_to_all(block, axes, 0, 0, tiled=True)  92.4 us
    ppermute x16, starting transfers between devices, shift(): return lax.ppermute(block, ALL, route)  55.3 us
    ppermute x16, waiting for transfers between devices, shift(): return lax.ppermute(block, ALL, route)  42.3 us
    pallas_call x15, Pallas kernels, call(): pl.pallas_call(kernel, in_specs=specs, out_specs=[vmem] * len(outs), out_...  27.3 us
    all_to_all x2, starting transfers between devices, exchange(): return lax.all_to_all(block, axes, 0, 0, tiled=True)  11.9 us
    unnamed x20, local copies, waits for them, and re-layouts  5.05 us
  transfers between devices with their start and end apart: 18, of which 11 were waited for; matrix products, arithmetic and copies ran while one was open for 0% of the time, Pallas kernels for 1%

profile of v2, /device:TPU:1, one launch (start us, length us, event | category | flops | bytes accessed | tf_op | source)
XLA Modules:
  0.0 238.1 jit_solution(16454135464997680452)
XLA Ops:
  3.0 8.8 %collective-permute-start.1 = (f32[2,64,128]{2,1,0:T(8,128)S(1)}, f32[2,64,128]{2,1,0:T(8,128)S(1)}, u32[]{:S(2)}, u32[]{:S(2)}) collective-permute-start(f32[2,64,128]{2,1,0:T(8,128)S(1)} %get-tuple-element.37), channel_id=1, source_target_pairs={{0,480},{1,481},{2,482},{3,483},{4,484},{5,485},{6,486},{7,487},{8... | collective-permute-start | bytes 196616 | tf_op jit(solution)/shard_map/ppermute | solution.py:413
  11.8 1.9 collective-permute-start
  16.1 10.6 %collective-permute-start.3 = (f32[2,128,128]{2,1,0:T(8,128)S(1)}, f32[2,128,128]{2,1,0:T(8,128)S(1)}, u32[]{:S(2)}, u32[]{:S(2)}) collective-permute-start(f32[2,128,128]{2,1,0:T(8,128)S(1)} %get-tuple-element.39), channel_id=1, source_target_pairs={{0,31},{1,0},{2,1},{3,2},{4,3},{5,4},{6,5},{7,6},{8,7},{9,8},{10,9... | collective-permute-start | bytes 393224 | tf_op jit(solution)/shard_map/ppermute | solution.py:413
  26.8 1.9 collective-permute-start.2
  28.7 9.7 %collective-permute-done.2.from_left = f32[2,144,128]{2,1,0:T(8,128)S(1)} collective-permute-done((f32[2,144,128]{2,1,0:T(8,128)S(1)}, f32[2,144,128]{2,1,0:T(8,128)S(1)}, u32[]{:S(2)}, u32[]{:S(2)}) %collective-permute-start.2) | collective-permute-done | bytes 147488 | tf_op jit(solution)/shard_map/ppermute | solution.py:413
  41.7 8.4 %first_kernel.1 = (f32[2,128,128]{2,1,0:T(8,128)S(1)}, f32[2,128,128]{2,1,0:T(8,128)S(1)}, f32[2,128,128]{2,1,0:T(8,128)S(1)}, f32[2,128,128]{2,1,0:T(8,128)S(1)...) custom-call(s32[2,8,2]{2,1,0:T(8,128)S(1)} %copy.15.offsets, ...), custom_call_target="tpu_custom_call" | custom-call | tf_op jit(solution)/shard_map/first_kernel/pallas_call | solution.py:391
  50.1 1.9 collective-permute-start.4
  52.0 6.0 %collective-permute-start.5 = (f32[2,128,128]{2,1,0:T(8,128)S(1)}, f32[2,128,128]{2,1,0:T(8,128)S(1)}, u32[]{:S(2)}, u32[]{:S(2)}) collective-permute-start(f32[2,128,128]{2,1,0:T(8,128)S(1)} %get-tuple-element.42), channel_id=1, source_target_pairs={{0,32},{1,33},{2,34},{3,35},{4,36},{5,37},{6,38},{7,39},{8,40},{9,... | collective-permute-start | bytes 393224 | tf_op jit(solution)/shard_map/ppermute | solution.py:413
  58.0 1.9 collective-permute-start.6
  61.4 12.8 %collective-permute-done.6.from_corner = f32[2,128,128]{2,1,0:T(8,128)S(1)} collective-permute-done((f32[2,128,128]{2,1,0:T(8,128)S(1)}, f32[2,128,128]{2,1,0:T(8,128)S(1)}, u32[]{:S(2)}, u32[]{:S(2)}) %collective-permute-start.6) | collective-permute-done | bytes 131104 | tf_op jit(solution)/shard_map/ppermute | solution.py:413
  74.1 2.8 %merge_kernel.2 = (f32[16,7,8,128]{3,2,1,0:T(8,128)}, f32[8,128]{1,0:T(8,128)S(1)}, f32[2,128,128]{2,1,0:T(8,128)S(1)}) custom-call(s32[2,8,2]{2,1,0:T(8,128)S(1)} %copy.15.offsets, s32[3,32]{1,0:T(4,128)S(1)} %slice_convert_fusion.others, s32[4]{0:T(128)S(1)} %pad_add_fusion.edges, f32[2,128,128]{2,1,0:T(8,128)S(1)} %get-tuple-element.40.own, ...), custom_call_target="tpu_custom_call" | custom-call | tf_op jit(solution)/shard_map/merge_kernel/pallas_call | solution.py:391
  77.0 6.6 %all-to-all-start = ((f32[16,7,8,128]{3,2,1,0:T(8,128)}), f32[16,7,8,128]{3,2,1,0:T(8,128)S(1)}, u32[]{:S(2)}, u32[]{:S(2)}) async-start(f32[16,7,8,128]{3,2,1,0:T(8,128)} %get-tuple-element.46), calls=%async_computation | async-start | bytes 917504 | tf_op jit(solution)/shard_map/all_to_all | solution.py:417
  85.5 1.9 collective-permute-start.8
  87.4 4.0 %collective-permute-start.7 = (f32[2,128,128]{2,1,0:T(8,128)S(1)}, f32[2,128,128]{2,1,0:T(8,128)S(1)}, u32[]{:S(2)}, u32[]{:S(2)}) collective-permute-start(f32[2,128,128]{2,1,0:T(8,128)S(1)} %get-tuple-element.47.direction), channel_id=1, source_target_pairs={{0,480},{1,481},{2,482},{3,483},{4,484},{5,485},{6,486},{7,487},{8... | collective-permute-start | bytes 393224 | tf_op jit(solution)/shard_map/ppermute | solution.py:413
  92.4 2.9 %collective-permute-done.7.from_below = f32[2,128,128]{2,1,0:T(8,128)S(1)} collective-permute-done((f32[2,128,128]{2,1,0:T(8,128)S(1)}, f32[2,128,128]{2,1,0:T(8,128)S(1)}, u32[]{:S(2)}, u32[]{:S(2)}) %collective-permute-start.7) | collective-permute-done | bytes 131104 | tf_op jit(solution)/shard_map/ppermute | solution.py:413
  96.1 12.3 %all_to_all.40.parts = f32[8,8,8,128]{3,2,1,0:T(8,128)S(1)} all-to-all(f32[8,8,8,128]{3,2,1,0:T(8,128)S(1)} %scatter_kernel.2), channel_id=1, replica_groups=mesh['yl'=2,'x'=4,'c'=2,'yh'=4,'z'=8] {'z'}, dimensions={0} | all-to-all | bytes 524288 | tf_op jit(solution)/shard_map/all_to_all | solution.py:417
  108.4 12.7 %all_to_all.41.parts = f32[4,8,8,128]{3,2,1,0:T(8,128)S(1)} all-to-all(f32[4,8,8,128]{3,2,1,0:T(8,128)S(1)} %reduce_kernel.2), channel_id=1, replica_groups=mesh['yl'=2,'x'=4,'c'=2,'yh'=4,'z'=8] {'yh'}, dimensions={0} | all-to-all | bytes 262144 | tf_op jit(solution)/shard_map/all_to_all | solution.py:417
  121.2 24.1 %all_to_all.42.totals = f32[16,6,8,128]{3,2,1,0:T(8,128)S(1)} all-to-all(f32[16,6,8,128]{3,2,1,0:T(8,128)S(1)} %strip_kernel.2), channel_id=1, replica_groups=mesh['yl'=2,'x'=4,'c'=2,'yh'=4,'z'=8] {'yl','x','c'}, dimensions={0} | all-to-all | bytes 786432 | tf_op jit(solution)/shard_map/all_to_all | solution.py:417
  145.2 8.6 %next_kernel.1 = (f32[2,128,128]{2,1,0:T(8,128)S(1)}, f32[2,128,128]{2,1,0:T(8,128)S(1)}, f32[2,128,128]{2,1,0:T(8,128)S(1)}, f32[2,128,128]{2,1,0:T(8,128)S(1)}...) custom-call(s32[2,8,2]{2,1,0:T(8,128)S(1)} %copy.15.offsets, ...), custom_call_target="tpu_custom_call" | custom-call | tf_op jit(solution)/shard_map/next_kernel/pallas_call | solution.py:391
  153.8 2.2 collective-permute-start.10
  156.0 1.9 collective-permute-start.11
  158.0 2.0 collective-permute-start.12
  161.3 3.5 %collective-permute-done.10.from_left = f32[2,128,128]{2,1,0:T(8,128)S(1)} collective-permute-done((f32[2,128,128]{2,1,0:T(8,128)S(1)}, f32[2,128,128]{2,1,0:T(8,128)S(1)}, u32[]{:S(2)}, u32[]{:S(2)}) %collective-permute-start.10) | collective-permute-done | bytes 131104 | tf_op jit(solution)/shard_map/ppermute | solution.py:413
  164.8 8.3 %collective-permute-done.12.from_corner = f32[2,128,128]{2,1,0:T(8,128)S(1)} collective-permute-done((f32[2,128,128]{2,1,0:T(8,128)S(1)}, f32[2,128,128]{2,1,0:T(8,128)S(1)}, u32[]{:S(2)}, u32[]{:S(2)}) %collective-permute-start.12) | collective-permute-done | bytes 131104 | tf_op jit(solution)/shard_map/ppermute | solution.py:413
  173.1 2.8 %merge_kernel.3 = (f32[16,7,8,128]{3,2,1,0:T(8,128)}, f32[8,128]{1,0:T(8,128)S(1)}, f32[2,128,128]{2,1,0:T(8,128)S(1)}) custom-call(s32[2,8,2]{2,1,0:T(8,128)S(1)} %copy.15.offsets, s32[3,32]{1,0:T(4,128)S(1)} %slice_convert_fusion.others, s32[4]{0:T(128)S(1)} %pad_add_fusion.edges, f32[2,128,128]{2,1,0:T(8,128)S(1)} %get-tuple-element.54.own, ...), custom_call_target="tpu_custom_call" | custom-call | tf_op jit(solution)/shard_map/merge_kernel/pallas_call | solution.py:391
  175.9 5.3 %all-to-all-start.4 = ((f32[16,7,8,128]{3,2,1,0:T(8,128)}), f32[16,7,8,128]{3,2,1,0:T(8,128)S(1)}, u32[]{:S(2)}, u32[]{:S(2)}) async-start(f32[16,7,8,128]{3,2,1,0:T(8,128)} %get-tuple-element.61), calls=%async_computation.4 | async-start | bytes 917504 | tf_op jit(solution)/shard_map/all_to_all | solution.py:417
  181.2 1.9 collective-permute-start.14
  183.1 1.9 collective-permute-start.15
  185.1 4.5 %collective-permute-start.13 = (f32[2,64,128]{2,1,0:T(8,128)S(1)}, f32[2,64,128]{2,1,0:T(8,128)S(1)}, u32[]{:S(2)}, u32[]{:S(2)}) collective-permute-start(f32[2,64,128]{2,1,0:T(8,128)S(1)} %get-tuple-element.72), channel_id=1, source_target_pairs={{0,480},{1,481},{2,482},{3,483},{4,484},{5,485},{6,486},{7,487},{8... | collective-permute-start | bytes 196616 | tf_op jit(solution)/shard_map/ppermute | solution.py:413
  193.6 12.5 %all_to_all.43.parts = f32[8,8,8,128]{3,2,1,0:T(8,128)S(1)} all-to-all(f32[8,8,8,128]{3,2,1,0:T(8,128)S(1)} %scatter_kernel.3), channel_id=1, replica_groups=mesh['yl'=2,'x'=4,'c'=2,'yh'=4,'z'=8] {'z'}, dimensions={0} | all-to-all | bytes 524288 | tf_op jit(solution)/shard_map/all_to_all | solution.py:417
  206.2 9.6 %all_to_all.44.parts = f32[4,8,8,128]{3,2,1,0:T(8,128)S(1)} all-to-all(f32[4,8,8,128]{3,2,1,0:T(8,128)S(1)} %reduce_kernel.3), channel_id=1, replica_groups=mesh['yl'=2,'x'=4,'c'=2,'yh'=4,'z'=8] {'yh'}, dimensions={0} | all-to-all | bytes 262144 | tf_op jit(solution)/shard_map/all_to_all | solution.py:417
  215.8 21.3 %all_to_all.45.totals = f32[16,6,8,128]{3,2,1,0:T(8,128)S(1)} all-to-all(f32[16,6,8,128]{3,2,1,0:T(8,128)S(1)} %strip_kernel.3), channel_id=1, replica_groups=mesh['yl'=2,'x'=4,'c'=2,'yh'=4,'z'=8] {'yl','x','c'}, dimensions={0} | all-to-all | bytes 786432 | tf_op jit(solution)/shard_map/all_to_all | solution.py:417
  (52 shorter events, 19.7 us)
Async XLA Ops:
  1.4 0.9 copy-start.7
  2.3 36.2 %copy-start.2 = (f32[2,2,128,128]{3,2,1,0:T(8,128)S(1)}, f32[2,2,128,128]{3,2,1,0:T(8,128)}, u32[]{:S(2)}) copy-start(f32[2,2,128,128]{3,2,1,0:T(8,128)} %probe.7) | copy-start | bytes 786436
  3.0 10.8 %collective-permute-start.1 = (f32[2,64,128]{2,1,0:T(8,128)S(1)}, f32[2,64,128]{2,1,0:T(8,128)S(1)}, u32[]{:S(2)}, u32[]{:S(2)}) collective-permute-start(f32[2,64,128]{2,1,0:T(8,128)S(1)} %get-tuple-element.37), channel_id=1, source_target_pairs={{0,480},{1,481},{2,482},{3,483},{4,484},{5,485},{6,486},{7,487},{8... | collective-permute-start | bytes 196616 | tf_op jit(solution)/shard_map/ppermute | solution.py:413
  11.8 3.3 %collective-permute-start = (f32[2,72,128]{2,1,0:T(8,128)S(1)}, f32[2,72,128]{2,1,0:T(8,128)S(1)}, u32[]{:S(2)}, u32[]{:S(2)}) collective-permute-start(f32[2,72,128]{2,1,0:T(8,128)S(1)} %get-tuple-element.36.bottom), channel_id=1, source_target_pairs={{0,32},{1,33},{2,34},{3,35},{4,36},{5,37},{6,38},{7,39},{8,40},{9,... | collective-permute-start | bytes 221192 | tf_op jit(solution)/shard_map/ppermute | solution.py:413
  15.1 0.9 copy-start.8
  16.0 22.5 %copy-start.9 = (f32[2,128,128]{2,1,0:T(8,128)S(1)}, f32[2,128,128]{2,1,0:T(8,128)}, u32[]{:S(2)}) copy-start(f32[2,128,128]{2,1,0:T(8,128)} %tile.1) | copy-start | bytes 393220
  16.1 12.6 %collective-permute-start.3 = (f32[2,128,128]{2,1,0:T(8,128)S(1)}, f32[2,128,128]{2,1,0:T(8,128)S(1)}, u32[]{:S(2)}, u32[]{:S(2)}) collective-permute-start(f32[2,128,128]{2,1,0:T(8,128)S(1)} %get-tuple-element.39), channel_id=1, source_target_pairs={{0,31},{1,0},{2,1},{3,2},{4,3},{5,4},{6,5},{7,6},{8,7},{9,8},{10,9... | collective-permute-start | bytes 393224 | tf_op jit(solution)/shard_map/ppermute | solution.py:413
  26.8 11.7 %collective-permute-start.2 = (f32[2,144,128]{2,1,0:T(8,128)S(1)}, f32[2,144,128]{2,1,0:T(8,128)S(1)}, u32[]{:S(2)}, u32[]{:S(2)}) collective-permute-start(f32[2,144,128]{2,1,0:T(8,128)S(1)} %get-tuple-element.38), channel_id=1, source_target_pairs={{0,1},{1,2},{2,3},{3,4},{4,5},{5,6},{6,7},{7,8},{8,9},{9,10},{10,1... | collective-permute-start | bytes 442376 | tf_op jit(solution)/shard_map/ppermute | solution.py:413
  38.5 1.2 copy-start
  39.7 1.0 copy-start.3
  40.7 1.0 copy-start.5
  50.1 11.2 %collective-permute-start.4 = (f32[2,128,128]{2,1,0:T(8,128)S(1)}, f32[2,128,128]{2,1,0:T(8,128)S(1)}, u32[]{:S(2)}, u32[]{:S(2)}) collective-permute-start(f32[2,128,128]{2,1,0:T(8,128)S(1)} %get-tuple-element.41), channel_id=1, source_target_pairs={{0,1},{1,2},{2,3},{3,4},{4,5},{5,6},{6,7},{7,8},{8,9},{9,10},{10,1... | collective-permute-start | bytes 393224 | tf_op jit(solution)/shard_map/ppermute | solution.py:413
  52.0 9.3 %collective-permute-start.5 = (f32[2,128,128]{2,1,0:T(8,128)S(1)}, f32[2,128,128]{2,1,0:T(8,128)S(1)}, u32[]{:S(2)}, u32[]{:S(2)}) collective-permute-start(f32[2,128,128]{2,1,0:T(8,128)S(1)} %get-tuple-element.42), channel_id=1, source_target_pairs={{0,32},{1,33},{2,34},{3,35},{4,36},{5,37},{6,38},{7,39},{8,40},{9,... | collective-permute-start | bytes 393224 | tf_op jit(solution)/shard_map/ppermute | solution.py:413
  58.0 16.1 %collective-permute-start.6 = (f32[2,128,128]{2,1,0:T(8,128)S(1)}, f32[2,128,128]{2,1,0:T(8,128)S(1)}, u32[]{:S(2)}, u32[]{:S(2)}) collective-permute-start(f32[2,128,128]{2,1,0:T(8,128)S(1)} %get-tuple-element.43), channel_id=1, source_target_pairs={{0,33},{1,34},{2,35},{3,36},{4,37},{5,38},{6,39},{7,40},{8,41},{9,... | collective-permute-start | bytes 393224 | tf_op jit(solution)/shard_map/ppermute | solution.py:413
  77.0 19.1 %all-to-all-start = ((f32[16,7,8,128]{3,2,1,0:T(8,128)}), f32[16,7,8,128]{3,2,1,0:T(8,128)S(1)}, u32[]{:S(2)}, u32[]{:S(2)}) async-start(f32[16,7,8,128]{3,2,1,0:T(8,128)} %get-tuple-element.46), calls=%async_computation | async-start | bytes 917504 | tf_op jit(solution)/shard_map/all_to_all | solution.py:417
  83.6 8.9 %collective-permute-start.9 = (f32[2,128,128]{2,1,0:T(8,128)S(1)}, f32[2,128,128]{2,1,0:T(8,128)S(1)}, u32[]{:S(2)}, u32[]{:S(2)}) collective-permute-start(f32[2,128,128]{2,1,0:T(8,128)S(1)} %get-tuple-element.47.direction), channel_id=1, source_target_pairs={{0,511},{1,480},{2,481},{3,482},{4,483},{5,484},{6,485},{7,486},{8... | collective-permute-start | bytes 393224 | tf_op jit(solution)/shard_map/ppermute | solution.py:413
  85.5 7.0 %collective-permute-start.8 = (f32[2,128,128]{2,1,0:T(8,128)S(1)}, f32[2,128,128]{2,1,0:T(8,128)S(1)}, u32[]{:S(2)}, u32[]{:S(2)}) collective-permute-start(f32[2,128,128]{2,1,0:T(8,128)S(1)} %get-tuple-element.47.direction), channel_id=1, source_target_pairs={{0,31},{1,0},{2,1},{3,2},{4,3},{5,4},{6,5},{7,6},{8,7},{9,8},{10,9... | collective-permute-start | bytes 393224 | tf_op jit(solution)/shard_map/ppermute | solution.py:413
  87.4 7.9 %collective-permute-start.7 = (f32[2,128,128]{2,1,0:T(8,128)S(1)}, f32[2,128,128]{2,1,0:T(8,128)S(1)}, u32[]{:S(2)}, u32[]{:S(2)}) collective-permute-start(f32[2,128,128]{2,1,0:T(8,128)S(1)} %get-tuple-element.47.direction), channel_id=1, source_target_pairs={{0,480},{1,481},{2,482},{3,483},{4,484},{5,485},{6,486},{7,487},{8... | collective-permute-start | bytes 393224 | tf_op jit(solution)/shard_map/ppermute | solution.py:413
  108.4 36.8 %copy-start.1 = (f32[1,1,2,8,128,128]{5,4,3,2,1,0:T(8,128)S(1)}, f32[1,1,2,8,128,128]{5,4,3,2,1,0:T(8,128)}, u32[]{:S(2)}) copy-start(f32[1,1,2,8,128,128]{5,4,3,2,1,0:T(8,128)} %measured.3) | copy-start | bytes 3145732
  121.1 24.1 %copy-start.4 = (bf16[256,768]{1,0:T(8,128)(2,1)S(1)}, bf16[256,768]{1,0:T(8,128)(2,1)}, u32[]{:S(2)}) copy-start(bf16[256,768]{1,0:T(8,128)(2,1)} %constant.43.clone.left3) | copy-start | bytes 1179652
  121.1 24.1 %copy-start.6 = (bf16[768,256]{1,0:T(8,128)(2,1)S(1)}, bf16[768,256]{1,0:T(8,128)(2,1)}, u32[]{:S(2)}) copy-start(bf16[768,256]{1,0:T(8,128)(2,1)} %constant.42.clone.right3) | copy-start | bytes 1179652
  153.8 11.0 %collective-permute-start.10 = (f32[2,128,128]{2,1,0:T(8,128)S(1)}, f32[2,128,128]{2,1,0:T(8,128)S(1)}, u32[]{:S(2)}, u32[]{:S(2)}) collective-permute-start(f32[2,128,128]{2,1,0:T(8,128)S(1)} %get-tuple-element.55), channel_id=1, source_target_pairs={{0,1},{1,2},{2,3},{3,4},{4,5},{5,6},{6,7},{7,8},{8,9},{9,10},{10,1... | collective-permute-start | bytes 393224 | tf_op jit(solution)/shard_map/ppermute | solution.py:413
  156.0 8.8 %collective-permute-start.11 = (f32[2,128,128]{2,1,0:T(8,128)S(1)}, f32[2,128,128]{2,1,0:T(8,128)S(1)}, u32[]{:S(2)}, u32[]{:S(2)}) collective-permute-start(f32[2,128,128]{2,1,0:T(8,128)S(1)} %get-tuple-element.56), channel_id=1, source_target_pairs={{0,32},{1,33},{2,34},{3,35},{4,36},{5,37},{6,38},{7,39},{8,40},{9,... | collective-permute-start | bytes 393224 | tf_op jit(solution)/shard_map/ppermute | solution.py:413
  158.0 15.2 %collective-permute-start.12 = (f32[2,128,128]{2,1,0:T(8,128)S(1)}, f32[2,128,128]{2,1,0:T(8,128)S(1)}, u32[]{:S(2)}, u32[]{:S(2)}) collective-permute-start(f32[2,128,128]{2,1,0:T(8,128)S(1)} %get-tuple-element.57), channel_id=1, source_target_pairs={{0,33},{1,34},{2,35},{3,36},{4,37},{5,38},{6,39},{7,40},{8,41},{9,... | collective-permute-start | bytes 393224 | tf_op jit(solution)/shard_map/ppermute | solution.py:413
  175.9 17.7 %all-to-all-start.4 = ((f32[16,7,8,128]{3,2,1,0:T(8,128)}), f32[16,7,8,128]{3,2,1,0:T(8,128)S(1)}, u32[]{:S(2)}, u32[]{:S(2)}) async-start(f32[16,7,8,128]{3,2,1,0:T(8,128)} %get-tuple-element.61), calls=%async_computation.4 | async-start | bytes 917504 | tf_op jit(solution)/shard_map/all_to_all | solution.py:417
  181.2 8.4 %collective-permute-start.14 = (f32[2,64,128]{2,1,0:T(8,128)S(1)}, f32[2,64,128]{2,1,0:T(8,128)S(1)}, u32[]{:S(2)}, u32[]{:S(2)}) collective-permute-start(f32[2,64,128]{2,1,0:T(8,128)S(1)} %get-tuple-element.71), channel_id=1, source_target_pairs={{0,31},{1,0},{2,1},{3,2},{4,3},{5,4},{6,5},{7,6},{8,7},{9,8},{10,9... | collective-permute-start | bytes 196616 | tf_op jit(solution)/shard_map/ppermute | solution.py:413
  183.1 7.9 %collective-permute-start.15 = (f32[2,64,128]{2,1,0:T(8,128)S(1)}, f32[2,64,128]{2,1,0:T(8,128)S(1)}, u32[]{:S(2)}, u32[]{:S(2)}) collective-permute-start(f32[2,64,128]{2,1,0:T(8,128)S(1)} %get-tuple-element.72), channel_id=1, source_target_pairs={{0,511},{1,480},{2,481},{3,482},{4,483},{5,484},{6,485},{7,486},{8... | collective-permute-start | bytes 196616 | tf_op jit(solution)/shard_map/ppermute | solution.py:413
  185.1 7.3 %collective-permute-start.13 = (f32[2,64,128]{2,1,0:T(8,128)S(1)}, f32[2,64,128]{2,1,0:T(8,128)S(1)}, u32[]{:S(2)}, u32[]{:S(2)}) collective-permute-start(f32[2,64,128]{2,1,0:T(8,128)S(1)} %get-tuple-element.72), channel_id=1, source_target_pairs={{0,480},{1,481},{2,482},{3,483},{4,484},{5,485},{6,486},{7,487},{8... | collective-permute-start | bytes 196616 | tf_op jit(solution)/shard_map/ppermute | solution.py:413

commit v3 on v1

--- a/solution.py
+++ b/solution.py
@@ -1,4 +1,5 @@
 import math
+from functools import partial
 
 import jax
 import jax.numpy as jnp
@@ -14,8 +15,10 @@
 COUNT = 8
 GROUP = 2
 ROW = ("yl", "x", "c")
-COL = ("yh", "z")
+COL = ("yh", "zh", "zl")
 ALL = ROW + COL
+SCATTER = ROW + ("zl",)
+REST = ("yh", "zh")
 TILES = 8
 VMEM_LIMIT = 48 * 1024 * 1024
 F32 = jnp.float32
@@ -99,6 +102,17 @@
 
 def low_lanes(rows):
     return lax.broadcasted_iota(jnp.int32, (rows, SIZE), 1) < HALF
+
+
+def bounds(edges):
+    return tuple(edges[k] for k in range(4))
+
+
+def inside(limits, down, across, rows=SIZE):
+    row_low, row_high, col_low, col_high = limits
+    line = lax.broadcasted_iota(jnp.int32, (rows, SIZE), 0) + down
+    lane = lax.broadcasted_iota(jnp.int32, (rows, SIZE), 1) + across
+    return (line >= row_low) & (line < row_high) & (lane >= col_low) & (lane < col_high)
 
 
 def pad_field(above, own, below, from_left, from_right, store):
@@ -128,10 +142,14 @@
             right[c, rows] = pack_high(low, strips[k], strips[k + 2])
 
 
-def sweep(batch, starts, padded, probe, measured, right3, left3, top, middle, bottom, sums, accum):
+def power_of(probe):
+    return sum(probe[c, m] * probe[c, m] for c in range(2) for m in range(MODES))
+
+
+def sweep(batch, offsets, padded, probe, measured, right3, left3, sums, accum):
     accum[...] = jnp.zeros_like(accum)
     sums[...] = jnp.zeros_like(sums)
-    light = sum(probe[c, m] * probe[c, m] for c in range(2) for m in range(MODES))
+    light = power_of(probe) if accum.shape[0] == 3 else None
     tr = right3[...]
     tl = left3[...]
 
@@ -140,7 +158,7 @@
         fields = []
         for g in range(GROUP):
             j = step * GROUP + g
-            row, col = starts[j, 0], starts[j, 1]
+            row, col = offsets[batch, j, 0] + HALF, offsets[batch, j, 1] + HALF
             wr = window(padded, (0,), row, col)
             wi = window(padded, (1,), row, col)
             wins.append((row, col, wr, wi))
@@ -170,22 +188,104 @@
             sums[2 * MODES] += wr * wr + wi * wi
             place(accum, 0, row, col, cr)
             place(accum, 1, row, col, ci)
-            place(accum, 2, row, col, light)
+            if light is not None:
+                place(accum, 2, row, col, light)
         return carry
 
     lax.fori_loop(0, COUNT // GROUP, body, 0)
-    top[...] = accum[:, :, :HALF]
-    middle[...] = accum[:, :, HALF : HALF + SIZE]
-    bottom[...] = accum[:, :, HALF + SIZE :]
-
-
-def first_kernel(starts, above, own, below, from_left, from_right, probe, measured, right3, left3,
-                 top, middle, bottom, sums, padded, accum):
+
+
+def first_kernel(offsets, above, own, below, from_left, from_right, probe, measured, right3, left3,
+                 top, bottom, sums, padded, accum):
     def store(c, h, rows, value):
         padded[c, h, rows] = value
 
     pad_field(above, own, below, from_left, from_right, store)
-    sweep(0, starts, padded, probe, measured, right3, left3, top, middle, bottom, sums, accum)
+    sweep(0, offsets, padded, probe, measured, right3, left3, sums, accum)
+    top[...] = accum[:, :, :SIZE]
+    bottom[...] = accum[:, :, SIZE:]
+
+
+def cover_kernel(shifts, probe, cover, total):
+    total[...] = jnp.zeros_like(total)
+    light = power_of(probe)
+    lane = lanes()
+
+    def body(k, carry):
+        row, col = shifts[k, 0] + SIZE + HALF, shifts[k, 1] + SIZE + HALF
+
+        @pl.when((row >= 0) & (row <= 3 * SIZE) & (col >= 0) & (col <= 3 * SIZE))
+        def _():
+            block = lax.div(col, SIZE)
+            turn = lax.rem(col, SIZE)
+            moved = pltpu.roll(light, turn, 1)
+            first = lane >= turn
+            rows = pl.ds(row, SIZE)
+            total[block, rows] += jnp.where(first, moved, 0.0)
+            total[block + 1, rows] += jnp.where(first, 0.0, moved)
+
+        return carry
+
+    lax.fori_loop(0, shifts.shape[0], body, 0)
+    cover[...] = total[1:3, SIZE : 3 * SIZE]
+
+
+def wide_fold_kernel(top, bottom, from_above, from_below, left, right):
+    for v, own, other in ((0, top, from_above), (1, bottom, from_below)):
+        left[v] = own[:, 0] + other[:, 0]
+        right[v] = own[:, 1] + other[:, 1]
+
+
+def pack_planes(packed, planes):
+    strips = (SIZE // TILES, TILES, SIZE)
+    upper = lax.rem(lax.broadcasted_iota(jnp.int32, (SIZE, SIZE), 0), TILES) < TILES // 2
+    for q in range(len(planes) // 2):
+        one, two = planes[2 * q], planes[2 * q + 1]
+        packed[:, 0, q] = jnp.where(upper, one, pltpu.roll(two, TILES // 2, 0)).reshape(strips)
+        packed[:, 1, q] = jnp.where(upper, pltpu.roll(one, SIZE - TILES // 2, 0), two).reshape(strips)
+
+
+def unpack_planes(packed, q):
+    upper = lax.rem(lax.broadcasted_iota(jnp.int32, (SIZE, SIZE), 0), TILES) < TILES // 2
+    one, two = (packed[:, h, q].reshape(SIZE, SIZE) for h in range(2))
+    return (jnp.where(upper, one, pltpu.roll(two, TILES // 2, 0)),
+            jnp.where(upper, pltpu.roll(one, SIZE - TILES // 2, 0), two))
+
+
+def pack_sums(packed, sums, overlap, a11, b1):
+    turn = lax.rem(lax.broadcasted_iota(jnp.int32, (SIZE, SIZE), 0), TILES // 2)
+    numbers = jnp.where(turn == 0, a11, jnp.where(turn == 1, b1, 0.0))
+    pack_planes(packed, [sums[k] for k in range(5)] + [numbers] + list(overlap))
+
+
+def wide_merge_kernel(edges, offsets, left, right, from_left, from_right, cover, padded, sums,
+                      packed, direction, product):
+    limits = bounds(edges)
+    a11 = jnp.zeros((1, SIZE), F32)
+    b1 = jnp.zeros((1, SIZE), F32)
+    for v in range(2):
+        rows = slice(v * SIZE, (v + 1) * SIZE)
+        mine_rows = lax.broadcasted_iota(jnp.int32, (SIZE, SIZE), 0) + v * SIZE
+        for h in range(2):
+            own, other = ((left, from_left), (right, from_right))[h]
+            light = cover[h, rows]
+            inverse = jnp.where(inside(limits, v * SIZE, h * SIZE), 1.0 / (light + 1.0), 0.0)
+            dr, di = ((own[v, c] + other[v, c]) * inverse for c in range(2))
+            direction[0, h, rows] = dr
+            direction[1, h, rows] = di
+            pr, pi = padded[0, h, rows], padded[1, h, rows]
+            product[0, h, rows] = dr * pr + di * pi
+            product[1, h, rows] = dr * pi - di * pr
+            across = lanes() + h * SIZE
+            mine = (mine_rows >= HALF) & (mine_rows < HALF + SIZE) & (across >= HALF) & (across < HALF + SIZE)
+            power = jnp.where(mine, dr * dr + di * di, 0.0)
+            a11 += jnp.sum(power * light, axis=0, keepdims=True)
+            b1 += jnp.sum(power * (light + 1.0), axis=0, keepdims=True)
+    overlap = [jnp.zeros((SIZE, SIZE), F32)] * 2
+    for j in range(COUNT):
+        row, col = offsets[0, j, 0] + HALF, offsets[0, j, 1] + HALF
+        overlap = [overlap[c] + window(product, (c,), row, col) for c in range(2)]
+    pack_sums(packed, sums, overlap, a11, b1)
 
 
 def fold_kernel(middle, from_above, from_below, tile, left, right):
@@ -200,7 +300,7 @@
 
 
 def merge_kernel(shifts, tile, from_left, from_right, padded, sums,
-                 packed, numbers, direction, product, overlap):
+                 packed, direction, product, overlap):
     low = low_lanes(HALF)
     lane = lanes()
     a11 = jnp.zeros((1, SIZE), F32)
@@ -231,9 +331,6 @@
         power = dr * dr + di * di
         a11 += jnp.sum(power * cover, axis=0, keepdims=True)
         b1 += jnp.sum(power * (cover + 1.0), axis=0, keepdims=True)
-    line = lax.broadcasted_iota(jnp.int32, (TILES, SIZE), 0)
-    numbers[...] = jnp.where(line == 0, a11, jnp.where(line == 1, b1, 0.0))
-
     overlap[...] = jnp.zeros_like(overlap)
 
     def body(k, carry):
@@ -252,11 +349,7 @@
 
     lax.fori_loop(0, shifts.shape[0], body, 0)
 
-    strips = (SIZE // TILES, TILES, SIZE)
-    for k in range(5):
-        packed[:, k] = sums[k].reshape(strips)
-    for c in range(2):
-        packed[:, 5 + c] = overlap[c].reshape(strips)
+    pack_sums(packed, sums, (overlap[0], overlap[1]), a11, b1)
 
 
 def add_all(parts):
@@ -266,13 +359,6 @@
     return total
 
 
-def scatter_kernel(parts, numbers, out):
-    total = add_all(parts)
-    for k in range(out.shape[0]):
-        out[k, :7] = total
-        out[k, 7] = numbers[...]
-
-
 def reduce_kernel(parts, out):
     total = add_all(parts)
     for k in range(out.shape[0]):
@@ -281,54 +367,77 @@
 
 def strip_kernel(place_ref, parts, probe, out):
     total = add_all(parts)
+    line = lax.broadcasted_iota(jnp.int32, (TILES, SIZE), 0)
+    half = TILES // 2
+    upper = line < half
+    first = place_ref[1] == 0
     rows = pl.ds(pl.multiple_of(place_ref[0] * TILES, TILES), TILES)
-    cover = total[2 * MODES]
+
+    def turned(x):
+        return pltpu.roll(x, half, 0)
+
+    def both(x, of_upper):
+        return jnp.where(upper == of_upper, x, turned(x))
+
+    def modes(c):
+        one, two = probe[c, 0, rows], probe[c, 1, rows]
+        return jnp.where(upper, jnp.where(first, one, turned(one)), jnp.where(first, turned(two), two))
+
+    pr, pi = modes(0), modes(1)
+    cover = both(total[2], True)
     inverse = 1.0 / (cover + 1.0)
-    cross = jnp.zeros((TILES, SIZE), F32)
-    power = jnp.zeros((TILES, SIZE), F32)
-    for m in range(MODES):
-        dr, di = total[m] * inverse, total[MODES + m] * inverse
-        pr, pi = probe[0, m, rows], probe[1, m, rows]
-        cross += (pr * dr + pi * di) * total[5] - (pr * di - pi * dr) * total[6]
-        power += dr * dr + di * di
-    line = lax.broadcasted_iota(jnp.int32, (TILES, SIZE), 0)
-    numbers = total[7]
-    for k, term in ((2, power * cover), (3, power * (cover + 1.0)), (4, cross)):
-        numbers = jnp.where(line == k, jnp.sum(term, axis=0, keepdims=True), numbers)
+    dr, di = total[0] * inverse, total[1] * inverse
+    cross = (pr * dr + pi * di) * both(total[3], True) - (pr * di - pi * dr) * both(total[3], False)
+    power = dr * dr + di * di
+    a22, b2, a12 = (
+        jnp.sum(x, axis=0, keepdims=True) for x in (power * cover, power * (cover + 1.0), cross))
+    a11, b1 = total[2, half : half + 1], total[2, half + 1 : half + 2]
+    low = low_lanes(1)
+    known = jnp.where(low, a11 + pltpu.roll(a11, HALF, 1), b1 + pltpu.roll(b1, HALF, 1))
+    numbers = total[2]
+    for k, term in enumerate((known, a22, b2, a12)):
+        numbers = jnp.where(line == half + k, term, numbers)
     for k in range(out.shape[0]):
-        out[k, :5] = total[:5]
-        out[k, 5] = numbers
+        out[k, 0] = total[0]
+        out[k, 1] = total[1]
+        out[k, 2] = numbers
 
 
 def step_sizes(totals, probe, new_probe, gradient=None):
-    numbers = jnp.sum(add_all(totals.at[:, 5]), axis=1, keepdims=True)
-    a11, b1, a22, b2, a12 = (numbers[k : k + 1] for k in range(5))
+    numbers = jnp.zeros((TILES, SIZE), F32)
+    for k in range(totals.shape[0]):
+        numbers += totals[k, 0, 2] + totals[k, 1, 2]
+    half = TILES // 2
+    low = low_lanes(1)
+    known, *rest = (numbers[half + k : half + k + 1] for k in range(4))
+    a22, b2, a12 = (jnp.sum(x, axis=1, keepdims=True) for x in rest)
+    share = 1.0 / (2 * totals.shape[0])
+    a11 = jnp.sum(jnp.where(low, known, 0.0), axis=1, keepdims=True) * share
+    b1 = jnp.sum(jnp.where(low, 0.0, known), axis=1, keepdims=True) * share
     a11 = 1.1 * a11
     a22 = 1.1 * a22
     det = a11 * a22 - a12 * a12
     step_obj = (b1 * a22 - a12 * b2) / det
     step_probe = (a11 * b2 - a12 * b1) / det
-    cover = totals[:, 4].reshape(SIZE, SIZE) + 1.0
+    cover, _ = unpack_planes(totals, 2)
+    cover = cover + 1.0
     scale = step_probe / cover
-    for m in range(MODES):
-        for c in range(2):
-            numer = totals[:, MODES * c + m].reshape(SIZE, SIZE)
+    for c in range(2):
+        for m, numer in enumerate(unpack_planes(totals, c)):
             new_probe[c, m] = probe[c, m] + scale * numer
             if gradient is not None:
                 gradient[c, m] = numer * lax.rsqrt(cover)
     return step_obj
 
 
-def next_kernel(starts, totals, padded, above, direction, below, from_left, from_right, probe,
-                measured, right3, left3,
+def next_kernel(offsets, totals, padded, direction, probe, measured, right3, left3,
                 top, middle, bottom, sums, new_padded, new_probe, accum):
     step = step_sizes(totals, probe, new_probe)
-
-    def store(c, h, rows, value):
-        new_padded[c, h, rows] = padded[c, h, rows] + step * value
-
-    pad_field(above, direction, below, from_left, from_right, store)
-    sweep(1, starts, new_padded, new_probe, measured, right3, left3, top, middle, bottom, sums, accum)
+    new_padded[...] = padded[...] + step * direction[...]
+    sweep(1, offsets, new_padded, new_probe, measured, right3, left3, sums, accum)
+    top[...] = accum[:, :, :HALF]
+    middle[...] = accum[:, :, HALF : HALF + SIZE]
+    bottom[...] = accum[:, :, HALF + SIZE :]
 
 
 def last_kernel(totals, padded, direction, probe, new_obj, new_probe, gradient):
@@ -355,7 +464,7 @@
         out_shape=list(outs),
         scratch_shapes=list(scratch),
         compiler_params=pltpu.CompilerParams(vmem_limit_bytes=VMEM_LIMIT),
-        name=kernel.__name__,
+        name=getattr(kernel, "func", kernel).__name__,
     )(*ins)
 
 
@@ -379,26 +488,13 @@
     return math.prod(lax.axis_size(a) for a in axes)
 
 
-def reduce_all(packed, numbers, probe, place_in_row, direction=None):
-    halo = None
-    if direction is not None:
-        above = shift(direction[:, HALF:], 1, 0)
-        below = shift(direction[:, :HALF], -1, 0)
-    part = exchange(packed, ROW)
-    if direction is not None:
-        part, above, below = lax.optimization_barrier((part, above, below))
-        left, right = call(pack_kernel, [above, direction, below], [shape(2, SIZE, SIZE)] * 2)
-        from_left = shift(right, 0, 1)
-        from_right = shift(left, 0, -1)
-    (part,) = call(scatter_kernel, [part, numbers], [shape(size_of(("z",)), 8, TILES, SIZE)])
-    part = exchange(part, ("z",))
-    if direction is not None:
-        part, from_left, from_right = lax.optimization_barrier((part, from_left, from_right))
-        halo = above, direction, below, from_left, from_right
-    (part,) = call(reduce_kernel, [part], [shape(size_of(("yh",)), 8, TILES, SIZE)])
-    part = exchange(part, ("yh",))
-    (part,) = call(strip_kernel, [place_in_row, part, probe], [shape(packed.shape[0], 6, TILES, SIZE)])
-    return exchange(part, ROW), halo
+def reduce_all(packed, probe, place_in_group):
+    group, rest = size_of(SCATTER), size_of(REST)
+    part = exchange(packed.reshape(group, 4, TILES, SIZE), SCATTER)
+    (part,) = call(reduce_kernel, [part], [shape(rest, 4, TILES, SIZE)])
+    part = exchange(part, REST)
+    (part,) = call(strip_kernel, [place_in_group, part, probe], [shape(group, 3, TILES, SIZE)])
+    return exchange(part, SCATTER).reshape(SIZE // TILES, 2, 3, TILES, SIZE)
 
 
 MARK = 1024.0
@@ -407,9 +503,16 @@
 def per_device(obj, probe, measured, offsets):
     right3, left3 = (jnp.asarray(t) for t in dft_tables())
     offsets = offsets[0, 0]
-    starts = offsets + HALF
     batches = offsets.shape[0]
-    place_in_row = lax.axis_index(ROW).astype(jnp.int32).reshape(1)
+    r, c, half = (lax.axis_index(axes).astype(jnp.int32) for axes in (ROW, COL, ("zl",)))
+    whole = 2 * SIZE
+    place_in_group = jnp.stack([r, half])
+    edges = jnp.stack([
+        jnp.where(r == 0, HALF, 0),
+        jnp.where(r == size_of(ROW) - 1, whole - HALF, whole),
+        jnp.where(c == 0, HALF, 0),
+        jnp.where(c == size_of(COL) - 1, whole - HALF, whole),
+    ]).astype(jnp.int32)
 
     code = jnp.zeros((TILES * SIZE,), F32).at[: offsets.size].set(
         offsets.reshape(-1).astype(F32) + MARK)
@@ -436,53 +539,61 @@
     shifts = (codes - MARK).astype(jnp.int32) + steps
     shifts = jnp.moveaxis(shifts, 2, 0).reshape(batches, -1, 2)
 
-    whole = 2 * SIZE
     field = shape(2, 2, whole, SIZE)
     edge = shape(3, 2, HALF, SIZE)
-    middle = shape(3, 2, SIZE, SIZE)
+    quads = shape(2, 2, SIZE, SIZE)
     planes = shape(2, MODES, SIZE, SIZE)
-    accum = pltpu.VMEM((3, 2, whole, SIZE), F32)
-
-    top, middle_in, bottom, sums, padded = call(
+    sums_shape = shape(5, SIZE, SIZE)
+    packed_shape = shape(SIZE // TILES, 2, 4, TILES, SIZE)
+
+    top, bottom, sums, padded = call(
         first_kernel,
-        [starts[0], above, obj, below, from_left[:, :SIZE], from_right[:, :SIZE], probe,
-         measured, right3, left3],
-        [edge, middle, edge, shape(5, SIZE, SIZE), field],
-        [accum],
+        [offsets, above, obj, below, from_left[:, :SIZE], from_right[:, :SIZE], probe, measured, right3, left3],
+        [quads, quads, sums_shape, field],
+        [pltpu.VMEM((2, 2, whole, SIZE), F32)],
     )
-
-    def merge(top, middle_in, bottom, sums, padded, batch):
-        from_above = shift(bottom, 1, 0)
-        from_below = shift(top, -1, 0)
-        side = shape(3, HALF, SIZE)
-        tile, left, right = call(
-            fold_kernel, [middle_in, from_above, from_below], [shape(3, SIZE, SIZE), side, side])
-        left_in = shift(right, 0, 1)
-        right_in = shift(left, 0, -1)
-        return call(
-            merge_kernel,
-            [shifts[batch], tile, left_in, right_in, padded, sums],
-            [shape(SIZE // TILES, 7, TILES, SIZE), shape(TILES, SIZE), shape(2, SIZE, SIZE)],
-            [pltpu.VMEM((2, 3 * SIZE, SIZE), F32), pltpu.VMEM((2, SIZE, SIZE), F32)],
-        )
-
-    packed, numbers, direction = merge(top, middle_in, bottom, sums, padded, 0)
-    totals, halo = reduce_all(packed, numbers, probe, place_in_row, direction)
-    top, middle_in, bottom, sums, padded, probe = call(
+    from_above = shift(bottom, 1, 0)
+    from_below = shift(top, -1, 0)
+    (cover,) = call(
+        cover_kernel, [shifts[0], probe], [shape(2, whole, SIZE)], [pltpu.VMEM((5, 4 * SIZE, SIZE), F32)])
+    left, right = call(wide_fold_kernel, [top, bottom, from_above, from_below], [quads, quads])
+    from_left = shift(right, 0, 1)
+    from_right = shift(left, 0, -1)
+    packed, direction = call(
+        wide_merge_kernel,
+        [edges, offsets, left, right, from_left, from_right, cover, padded, sums],
+        [packed_shape, field],
+        [pltpu.VMEM((2, 2, whole, SIZE), F32)],
+    )
+    totals = reduce_all(packed, probe, place_in_group)
+
+    top, middle, bottom, sums, padded, probe = call(
         next_kernel,
-        [starts[1], totals, padded, *halo, probe, measured, right3, left3],
-        [edge, middle, edge, shape(5, SIZE, SIZE), field, planes],
-        [accum],
+        [offsets, totals, padded, direction, probe, measured, right3, left3],
+        [edge, shape(3, 2, SIZE, SIZE), edge, sums_shape, field, planes],
+        [pltpu.VMEM((3, 2, whole, SIZE), F32)],
     )
-    packed, numbers, direction = merge(top, middle_in, bottom, sums, padded, 1)
-    totals, _ = reduce_all(packed, numbers, probe, place_in_row)
+    from_above = shift(bottom, 1, 0)
+    from_below = shift(top, -1, 0)
+    side = shape(3, HALF, SIZE)
+    tile, left, right = call(
+        fold_kernel, [middle, from_above, from_below], [shape(3, SIZE, SIZE), side, side])
+    from_left = shift(right, 0, 1)
+    from_right = shift(left, 0, -1)
+    packed, direction = call(
+        merge_kernel,
+        [shifts[1], tile, from_left, from_right, padded, sums],
+        [packed_shape, shape(2, SIZE, SIZE)],
+        [pltpu.VMEM((2, 3 * SIZE, SIZE), F32), pltpu.VMEM((2, SIZE, SIZE), F32)],
+    )
+    totals = reduce_all(packed, probe, place_in_group)
     return tuple(call(
         last_kernel, [totals, padded, direction, probe], [shape(2, SIZE, SIZE), planes, planes]
     ))
 
 
 def solution(mesh):
-    parts = Mesh(mesh.devices.reshape(2, 4, 2, 4, 8), ALL)
+    parts = Mesh(mesh.devices.reshape(2, 4, 2, 4, 4, 2), ALL)
     in_specs = (P(None, ROW, COL), P(), P(ROW, COL), P(ROW, COL))
     out_specs = (P(None, ROW, COL), P(), P())
     return jax.shard_map(

time: 230 us -> 223 us (0.970)
  blocking collectives: 62.2 us -> 97 us
  starting transfers between devices: 80.9 us -> 54.3 us
  waiting for transfers between devices: 49.4 us -> 26.7 us
  Pallas kernels: 30.4 us -> 34.1 us
  local copies, waits for them, and re-layouts: 4.33 us -> 7.43 us
    all_to_all x4 -> x5, blocking collectives: 62.2 us -> 97 us  [exchange(): return lax.all_to_all(block, axes, 0, 0, tiled=True)]
    all_to_all x4 -> x1, starting transfers between devices: 37.6 us -> 18.6 us  [exchange(): return lax.all_to_all(block, axes, 0, 0, tiled=True)]
    ppermute x16 -> x12, waiting for transfers between devices: 32.3 us -> 14.7 us  [shift(): return lax.ppermute(block, ALL, route)]
    ppermute x16 -> x12, starting transfers between devices: 43.3 us -> 35.7 us  [shift(): return lax.ppermute(block, ALL, route)]
    all_to_all x4 -> x1, waiting for transfers between devices: 17.2 us -> 12 us  [exchange(): return lax.all_to_all(block, axes, 0, 0, tiled=True)]
    pallas_call x15 -> x13, Pallas kernels: 30.4 us -> 34.1 us  [call(): pl.pallas_call(kernel, in_specs=specs, out_specs=[vmem] * len(outs), out_...]
  transfers between devices with their start and end apart: 20 -> 13, of which waited for: 18 -> 8; matrix products, arithmetic and copies ran while one was open for 0% -> 2% of each run, Pallas kernels for 0% -> 3%
where the time goes in v3:
time: 223 us; the launch traced here: 222 us
  blocking collectives  97 us (43%)
  starting transfers between devices  54.3 us (24%)
  Pallas kernels  34.1 us (15%)
  waiting for transfers between devices  26.7 us (12%)
  local copies, waits for them, and re-layouts  7.43 us (3%)
    all_to_all x5, blocking collectives, exchange(): return lax.all_to_all(block, axes, 0, 0, tiled=True)  97 us
    ppermute x12, starting transfers between devices, shift(): return lax.ppermute(block, ALL, route)  35.7 us
    pallas_call x13, Pallas kernels, call(): pl.pallas_call(kernel, in_specs=specs, out_specs=[vmem] * len(outs), out_...  34.1 us
    all_to_all x1, starting transfers between devices, exchange(): return lax.all_to_all(block, axes, 0, 0, tiled=True)  18.6 us
    ppermute x12, waiting for transfers between devices, shift(): return lax.ppermute(block, ALL, route)  14.7 us
    all_to_all x1, waiting for transfers between devices, exchange(): return lax.all_to_all(block, axes, 0, 0, tiled=True)  12 us
  transfers between devices with their start and end apart: 13, of which 8 were waited for; matrix products, arithmetic and copies ran while one was open for 2% of the time, Pallas kernels for 3%

profile of v3, /device:TPU:1, one launch (start us, length us, event | category | flops | bytes accessed | tf_op | source)
XLA Modules:
  0.0 222.2 jit_solution(18065814747038189609)
XLA Ops:
  1.5 0.9 fusion.3
  2.5 4.6 %collective-permute-start = (f32[2,72,128]{2,1,0:T(8,128)S(1)}, f32[2,72,128]{2,1,0:T(8,128)S(1)}, u32[]{:S(2)}, u32[]{:S(2)}) collective-permute-start(f32[2,72,128]{2,1,0:T(8,128)S(1)} %get-tuple-element.63), channel_id=1, source_target_pairs={{0,32},{1,33},{2,34},{3,35},{4,36},{5,37},{6,38},{7,39},{8,40},{9,... | collective-permute-start | bytes 221192 | tf_op jit(solution)/shard_map/ppermute | solution.py:480
  7.1 5.6 %collective-permute-start.1 = (f32[2,72,128]{2,1,0:T(8,128)S(1)}, f32[2,72,128]{2,1,0:T(8,128)S(1)}, u32[]{:S(2)}, u32[]{:S(2)}) collective-permute-start(f32[2,72,128]{2,1,0:T(8,128)S(1)} %get-tuple-element.64), channel_id=1, source_target_pairs={{32,0},{33,1},{34,2},{35,3},{36,4},{37,5},{38,6},{39,7},{40,8},{41... | collective-permute-start | bytes 221192 | tf_op jit(solution)/shard_map/ppermute | solution.py:480
  12.7 0.9 collective-permute-done.1
  13.8 3.3 %collective-permute-start.2 = (f32[2,152,128]{2,1,0:T(8,128)S(1)}, f32[2,152,128]{2,1,0:T(8,128)S(1)}, u32[]{:S(2)}, u32[]{:S(2)}) collective-permute-start(f32[2,152,128]{2,1,0:T(8,128)S(1)} %get-tuple-element.61), channel_id=1, source_target_pairs={{0,1},{1,2},{2,3},{3,4},{4,5},{5,6},{6,7},{7,8},{8,9},{9,10},{10,1... | collective-permute-start | bytes 466952 | tf_op jit(solution)/shard_map/ppermute | solution.py:480
  17.2 1.3 collective-permute-start.3
  19.6 4.2 %collective-permute-done.3 = f32[2,152,128]{2,1,0:T(8,128)S(1)} collective-permute-done((f32[2,152,128]{2,1,0:T(8,128)S(1)}, f32[2,152,128]{2,1,0:T(8,128)S(1)}, u32[]{:S(2)}, u32[]{:S(2)}) %collective-permute-start.3) | collective-permute-done | bytes 155680 | tf_op jit(solution)/shard_map/ppermute | solution.py:480
  24.5 8.4 %first_kernel.1 = (f32[2,2,128,128]{3,2,1,0:T(8,128)S(1)}, f32[2,2,128,128]{3,2,1,0:T(8,128)S(1)}, f32[5,128,128]{2,1,0:T(8,128)S(1)}, f32[2,2,256,128]{3,2,1,0:T(8,128)S(1)}) custom-call(s32[2,8,2]{2,1,0:T(8,128)S(1)} %copy.21.offsets, f32[2,64,128]{2,1,0:T(8,128)S(1)} %slice.65.above, f32[2,128,128]{2,1,0:T(8,128)S(1)} %copy-done.4, ...), custom_call_target="tpu_custom_call" | custom-call | tf_op jit(solution)/shard_map/first_kernel/pallas_call | solution.py:460
  33.6 1.9 collective-permute-start.5
  35.5 4.0 %collective-permute-start.4 = (f32[2,2,128,128]{3,2,1,0:T(8,128)S(1)}, f32[2,2,128,128]{3,2,1,0:T(8,128)}, u32[]{:S(2)}, u32[]{:S(2)}) collective-permute-start(f32[2,2,128,128]{3,2,1,0:T(8,128)S(1)} %get-tuple-element.39.bottom), channel_id=1, source_target_pairs={{0,32},{1,33},{2,34},{3,35},{4,36},{5,37},{6,38},{7,39},{8,40},{9,... | collective-permute-start | bytes 786440 | tf_op jit(solution)/shard_map/ppermute | solution.py:480
  43.8 0.9 copy-done.8
  44.8 1.0 wide_fold_kernel.1
  45.8 1.3 collective-permute-start.7
  47.1 4.6 %collective-permute-start.6 = (f32[2,2,128,128]{3,2,1,0:T(8,128)S(1)}, f32[2,2,128,128]{3,2,1,0:T(8,128)S(1)}, u32[]{:S(2)}, u32[]{:S(2)}) collective-permute-start(f32[2,2,128,128]{3,2,1,0:T(8,128)S(1)} %get-tuple-element.41.right), channel_id=1, source_target_pairs={{0,1},{1,2},{2,3},{3,4},{4,5},{5,6},{6,7},{7,8},{8,9},{9,10},{10,1... | collective-permute-start | bytes 786440 | tf_op jit(solution)/shard_map/ppermute | solution.py:480
  51.8 6.3 %cover_kernel.1.cover = f32[2,256,128]{2,1,0:T(8,128)S(1)} custom-call(s32[72,2]{1,0:T(8,128)S(1)} %bitcast.24, f32[2,2,128,128]{3,2,1,0:T(8,128)S(1)} %copy-done), custom_call_target="tpu_custom_call" | custom-call | tf_op jit(solution)/shard_map/cover_kernel/pallas_call | solution.py:460
  58.2 1.6 wide_merge_kernel.1
  59.8 24.9 %all_to_all.30.parts = f32[32,4,8,128]{3,2,1,0:T(8,128)S(1)} all-to-all(f32[32,4,8,128]{3,2,1,0:T(8,128)S(1)} %bitcast.21), channel_id=1, replica_groups=mesh['yl'=2,'x'=4,'c'=2,'yh'=4,'zh'=4,'zl'=2] {'yl','x','c','zl'}, dimensions={0} | all-to-all | bytes 1048576 | tf_op jit(solution)/shard_map/all_to_all | solution.py:484
  85.5 18.6 %all-to-all-start.1 = ((f32[16,4,8,128]{3,2,1,0:T(8,128)}), f32[16,4,8,128]{3,2,1,0:T(8,128)S(1)}, u32[]{:S(2)}, u32[]{:S(2)}) async-start(f32[16,4,8,128]{3,2,1,0:T(8,128)} %reduce_kernel.2), calls=%async_computation.1 | async-start | bytes 524288 | tf_op jit(solution)/shard_map/all_to_all | solution.py:484
  104.3 12.0 %all-to-all-done.1.parts = f32[16,4,8,128]{3,2,1,0:T(8,128)S(1)} async-done(((f32[16,4,8,128]{3,2,1,0:T(8,128)}), f32[16,4,8,128]{3,2,1,0:T(8,128)S(1)}, u32[]{:S(2)}, u32[]{:S(2)}) %all-to-all-start.1) | async-done | bytes 262176 | tf_op jit(solution)/shard_map/all_to_all | solution.py:484
  116.9 16.0 %all_to_all.31 = f32[32,3,8,128]{3,2,1,0:T(8,128)S(1)} all-to-all(f32[32,3,8,128]{3,2,1,0:T(8,128)S(1)} %strip_kernel.2), channel_id=1, replica_groups=mesh['yl'=2,'x'=4,'c'=2,'yh'=4,'zh'=4,'zl'=2] {'yl','x','c','zl'}, dimensions={0} | all-to-all | bytes 786432 | tf_op jit(solution)/shard_map/all_to_all | solution.py:484
  132.9 8.6 %next_kernel.1 = (f32[3,2,64,128]{3,2,1,0:T(8,128)S(1)}, f32[3,2,128,128]{3,2,1,0:T(8,128)S(1)}, f32[3,2,64,128]{3,2,1,0:T(8,128)S(1)}, f32[5,128,128]{2,1,0:T(8...) custom-call(s32[2,8,2]{2,1,0:T(8,128)S(1)} %copy.21.offsets, ...), custom_call_target="tpu_custom_call" | custom-call | tf_op jit(solution)/shard_map/next_kernel/pallas_call | solution.py:460
  141.5 2.7 %collective-permute-start.8 = (f32[3,2,64,128]{3,2,1,0:T(8,128)S(1)}, f32[3,2,64,128]{3,2,1,0:T(8,128)S(1)}, u32[]{:S(2)}, u32[]{:S(2)}) collective-permute-start(f32[3,2,64,128]{3,2,1,0:T(8,128)S(1)} %get-tuple-element.47), channel_id=1, source_target_pairs={{0,32},{1,33},{2,34},{3,35},{4,36},{5,37},{6,38},{7,39},{8,40},{9,... | collective-permute-start | bytes 589832 | tf_op jit(solution)/shard_map/ppermute | solution.py:480
  144.3 1.9 collective-permute-start.9
  146.9 4.4 %collective-permute-done.9.from_below = f32[3,2,64,128]{3,2,1,0:T(8,128)S(1)} collective-permute-done((f32[3,2,64,128]{3,2,1,0:T(8,128)S(1)}, f32[3,2,64,128]{3,2,1,0:T(8,128)S(1)}, u32[]{:S(2)}, u32[]{:S(2)}) %collective-permute-start.9) | collective-permute-done | bytes 196640 | tf_op jit(solution)/shard_map/ppermute | solution.py:480
  151.5 3.0 %collective-permute-start.10 = (f32[3,64,128]{2,1,0:T(8,128)S(1)}, f32[3,64,128]{2,1,0:T(8,128)S(1)}, u32[]{:S(2)}, u32[]{:S(2)}) collective-permute-start(f32[3,64,128]{2,1,0:T(8,128)S(1)} %get-tuple-element.50), channel_id=1, source_target_pairs={{0,1},{1,2},{2,3},{3,4},{4,5},{5,6},{6,7},{7,8},{8,9},{9,10},{10,1... | collective-permute-start | bytes 294920 | tf_op jit(solution)/shard_map/ppermute | solution.py:480
  154.5 1.3 collective-permute-start.11
  156.1 3.7 %collective-permute-done.11.from_right = f32[3,64,128]{2,1,0:T(8,128)S(1)} collective-permute-done((f32[3,64,128]{2,1,0:T(8,128)S(1)}, f32[3,64,128]{2,1,0:T(8,128)S(1)}, u32[]{:S(2)}, u32[]{:S(2)}) %collective-permute-start.11) | collective-permute-done | bytes 98336 | tf_op jit(solution)/shard_map/ppermute | solution.py:480
  159.8 4.6 %merge_kernel.1 = (f32[16,2,4,8,128]{4,3,2,1,0:T(8,128)S(1)}, f32[2,128,128]{2,1,0:T(8,128)S(1)}) custom-call(s32[72,2]{1,0:T(8,128)S(1)} %bitcast.23, f32[3,128,128]{2,1,0:T(8,128)S(1)} %get-tuple-element.49.tile, f32[3,64,128]{2,1,0:T(8,128)S(1)} %collective-permute-done.10.from_left, f32[3,64,128]{2,1,0:T(8,128)S(1)} %collective-permute-done.11.from_right, ...), custom_call_target="tpu_custom_call" | custom-call | tf_op jit(solution)/shard_map/merge_kernel/pallas_call | solution.py:460
  164.4 17.6 %all_to_all.32.parts = f32[32,4,8,128]{3,2,1,0:T(8,128)S(1)} all-to-all(f32[32,4,8,128]{3,2,1,0:T(8,128)S(1)} %bitcast.22), channel_id=1, replica_groups=mesh['yl'=2,'x'=4,'c'=2,'yh'=4,'zh'=4,'zl'=2] {'yl','x','c','zl'}, dimensions={0} | all-to-all | bytes 1048576 | tf_op jit(solution)/shard_map/all_to_all | solution.py:484
  182.1 22.5 %all_to_all.33.parts = f32[16,4,8,128]{3,2,1,0:T(8,128)S(1)} all-to-all(f32[16,4,8,128]{3,2,1,0:T(8,128)S(1)} %reduce_kernel.3), channel_id=1, replica_groups=mesh['yl'=2,'x'=4,'c'=2,'yh'=4,'zh'=4,'zl'=2] {'yh','zh'}, dimensions={0} | all-to-all | bytes 524288 | tf_op jit(solution)/shard_map/all_to_all | solution.py:484
  205.2 16.0 %all_to_all.34 = f32[32,3,8,128]{3,2,1,0:T(8,128)S(1)} all-to-all(f32[32,3,8,128]{3,2,1,0:T(8,128)S(1)} %strip_kernel.3), channel_id=1, replica_groups=mesh['yl'=2,'x'=4,'c'=2,'yh'=4,'zh'=4,'zl'=2] {'yl','x','c','zl'}, dimensions={0} | all-to-all | bytes 786432 | tf_op jit(solution)/shard_map/all_to_all | solution.py:484
  221.2 1.0 last_kernel.1
  (68 shorter events, 11.2 us)
Async XLA Ops:
  1.5 12.1 %copy-start.4 = (f32[2,128,128]{2,1,0:T(8,128)S(1)}, f32[2,128,128]{2,1,0:T(8,128)}, u32[]{:S(2)}) copy-start(f32[2,128,128]{2,1,0:T(8,128)} %own.3) | copy-start | bytes 393220
  2.4 22.0 %copy-start.1 = (f32[1,1,2,8,128,128]{5,4,3,2,1,0:T(8,128)S(1)}, f32[1,1,2,8,128,128]{5,4,3,2,1,0:T(8,128)}, u32[]{:S(2)}) copy-start(f32[1,1,2,8,128,128]{5,4,3,2,1,0:T(8,128)} %measured.3) | copy-start | bytes 3145732
  2.5 10.2 %collective-permute-start = (f32[2,72,128]{2,1,0:T(8,128)S(1)}, f32[2,72,128]{2,1,0:T(8,128)S(1)}, u32[]{:S(2)}, u32[]{:S(2)}) collective-permute-start(f32[2,72,128]{2,1,0:T(8,128)S(1)} %get-tuple-element.63), channel_id=1, source_target_pairs={{0,32},{1,33},{2,34},{3,35},{4,36},{5,37},{6,38},{7,39},{8,40},{9,... | collective-permute-start | bytes 221192 | tf_op jit(solution)/shard_map/ppermute | solution.py:480
  7.1 6.5 %collective-permute-start.1 = (f32[2,72,128]{2,1,0:T(8,128)S(1)}, f32[2,72,128]{2,1,0:T(8,128)S(1)}, u32[]{:S(2)}, u32[]{:S(2)}) collective-permute-start(f32[2,72,128]{2,1,0:T(8,128)S(1)} %get-tuple-element.64), channel_id=1, source_target_pairs={{32,0},{33,1},{34,2},{35,3},{36,4},{37,5},{38,6},{39,7},{40,8},{41... | collective-permute-start | bytes 221192 | tf_op jit(solution)/shard_map/ppermute | solution.py:480
  13.8 4.9 %copy-start.12 = (s32[1,1,2,8,2]{3,4,2,1,0:T(2,128)S(1)}, s32[1,1,2,8,2]{3,4,2,1,0:T(2,128)}, u32[]{:S(2)}) copy-start(s32[1,1,2,8,2]{3,4,2,1,0:T(2,128)} %param.11) | copy-start | bytes 388
  13.8 10.7 %copy-start.3 = (bf16[768,256]{1,0:T(8,128)(2,1)S(1)}, bf16[768,256]{1,0:T(8,128)(2,1)}, u32[]{:S(2)}) copy-start(bf16[768,256]{1,0:T(8,128)(2,1)} %constant.78.clone.right3) | copy-start | bytes 1179652
  13.8 10.7 %copy-start.2 = (bf16[256,768]{1,0:T(8,128)(2,1)S(1)}, bf16[256,768]{1,0:T(8,128)(2,1)}, u32[]{:S(2)}) copy-start(bf16[256,768]{1,0:T(8,128)(2,1)} %constant.79.clone.left3) | copy-start | bytes 1179652
  13.8 5.8 %collective-permute-start.2 = (f32[2,152,128]{2,1,0:T(8,128)S(1)}, f32[2,152,128]{2,1,0:T(8,128)S(1)}, u32[]{:S(2)}, u32[]{:S(2)}) collective-permute-start(f32[2,152,128]{2,1,0:T(8,128)S(1)} %get-tuple-element.61), channel_id=1, source_target_pairs={{0,1},{1,2},{2,3},{3,4},{4,5},{5,6},{6,7},{7,8},{8,9},{9,10},{10,1... | collective-permute-start | bytes 466952 | tf_op jit(solution)/shard_map/ppermute | solution.py:480
  17.2 6.6 %collective-permute-start.3 = (f32[2,152,128]{2,1,0:T(8,128)S(1)}, f32[2,152,128]{2,1,0:T(8,128)S(1)}, u32[]{:S(2)}, u32[]{:S(2)}) collective-permute-start(f32[2,152,128]{2,1,0:T(8,128)S(1)} %get-tuple-element.62), channel_id=1, source_target_pairs={{1,0},{2,1},{3,2},{4,3},{5,4},{6,5},{7,6},{8,7},{9,8},{10,9},{11,1... | collective-permute-start | bytes 466952 | tf_op jit(solution)/shard_map/ppermute | solution.py:480
  19.1 5.5 %copy-start = (f32[2,2,128,128]{3,2,1,0:T(8,128)S(1)}, f32[2,2,128,128]{3,2,1,0:T(8,128)}, u32[]{:S(2)}) copy-start(f32[2,2,128,128]{3,2,1,0:T(8,128)} %probe.7) | copy-start | bytes 786436
  19.6 4.2 %copy-start.10 = (f32[2,152,128]{2,1,0:T(8,128)}, f32[2,152,128]{2,1,0:T(8,128)S(1)}, u32[]{:S(2)}) copy-start(f32[2,152,128]{2,1,0:T(8,128)S(1)} %collective-permute-done.2) | copy-start | bytes 466948
  23.8 0.7 copy-start.11
  32.9 0.7 copy-start.5
  33.6 9.5 %collective-permute-start.5 = (f32[2,2,128,128]{3,2,1,0:T(8,128)S(1)}, f32[2,2,128,128]{3,2,1,0:T(8,128)S(1)}, u32[]{:S(2)}, u32[]{:S(2)}) collective-permute-start(f32[2,2,128,128]{3,2,1,0:T(8,128)S(1)} %get-tuple-element.38.top), channel_id=1, source_target_pairs={{32,0},{33,1},{34,2},{35,3},{36,4},{37,5},{38,6},{39,7},{40,8},{41... | collective-permute-start | bytes 786440 | tf_op jit(solution)/shard_map/ppermute | solution.py:480
  35.5 8.3 %collective-permute-start.4 = (f32[2,2,128,128]{3,2,1,0:T(8,128)S(1)}, f32[2,2,128,128]{3,2,1,0:T(8,128)}, u32[]{:S(2)}, u32[]{:S(2)}) collective-permute-start(f32[2,2,128,128]{3,2,1,0:T(8,128)S(1)} %get-tuple-element.39.bottom), channel_id=1, source_target_pairs={{0,32},{1,33},{2,34},{3,35},{4,36},{5,37},{6,38},{7,39},{8,40},{9,... | collective-permute-start | bytes 786440 | tf_op jit(solution)/shard_map/ppermute | solution.py:480
  43.1 0.7 copy-start.7
  43.8 1.0 copy-start.8
  44.8 7.0 %copy-start.9 = (s32[3,3,2,8,2]{4,3,2,1,0:T(8,128)S(1)}, s32[3,3,2,8,2]{4,3,2,1,0:T(8,128)}, u32[]{:S(2)}) copy-start(s32[3,3,2,8,2]{4,3,2,1,0:T(8,128)} %convert_element_type.18) | copy-start | bytes 3460
  45.8 12.3 %collective-permute-start.7 = (f32[2,2,128,128]{3,2,1,0:T(8,128)S(1)}, f32[2,2,128,128]{3,2,1,0:T(8,128)S(1)}, u32[]{:S(2)}, u32[]{:S(2)}) collective-permute-start(f32[2,2,128,128]{3,2,1,0:T(8,128)S(1)} %get-tuple-element.40.left), channel_id=1, source_target_pairs={{1,0},{2,1},{3,2},{4,3},{5,4},{6,5},{7,6},{8,7},{9,8},{10,9},{11,1... | collective-permute-start | bytes 786440 | tf_op jit(solution)/shard_map/ppermute | solution.py:480
  47.1 11.1 %collective-permute-start.6 = (f32[2,2,128,128]{3,2,1,0:T(8,128)S(1)}, f32[2,2,128,128]{3,2,1,0:T(8,128)S(1)}, u32[]{:S(2)}, u32[]{:S(2)}) collective-permute-start(f32[2,2,128,128]{3,2,1,0:T(8,128)S(1)} %get-tuple-element.41.right), channel_id=1, source_target_pairs={{0,1},{1,2},{2,3},{3,4},{4,5},{5,6},{6,7},{7,8},{8,9},{9,10},{10,1... | collective-permute-start | bytes 786440 | tf_op jit(solution)/shard_map/ppermute | solution.py:480
  51.8 6.4 %copy-start.6 = (f32[5,128,128]{2,1,0:T(8,128)S(1)}, f32[5,128,128]{2,1,0:T(8,128)}, u32[]{:S(2)}) copy-start(f32[5,128,128]{2,1,0:T(8,128)} %copy-done.5) | copy-start | bytes 983044
  85.5 30.7 %all-to-all-start.1 = ((f32[16,4,8,128]{3,2,1,0:T(8,128)}), f32[16,4,8,128]{3,2,1,0:T(8,128)S(1)}, u32[]{:S(2)}, u32[]{:S(2)}) async-start(f32[16,4,8,128]{3,2,1,0:T(8,128)} %reduce_kernel.2), calls=%async_computation.1 | async-start | bytes 524288 | tf_op jit(solution)/shard_map/all_to_all | solution.py:484
  141.5 5.3 %collective-permute-start.8 = (f32[3,2,64,128]{3,2,1,0:T(8,128)S(1)}, f32[3,2,64,128]{3,2,1,0:T(8,128)S(1)}, u32[]{:S(2)}, u32[]{:S(2)}) collective-permute-start(f32[3,2,64,128]{3,2,1,0:T(8,128)S(1)} %get-tuple-element.47), channel_id=1, source_target_pairs={{0,32},{1,33},{2,34},{3,35},{4,36},{5,37},{6,38},{7,39},{8,40},{9,... | collective-permute-start | bytes 589832 | tf_op jit(solution)/shard_map/ppermute | solution.py:480
  144.3 7.0 %collective-permute-start.9 = (f32[3,2,64,128]{3,2,1,0:T(8,128)S(1)}, f32[3,2,64,128]{3,2,1,0:T(8,128)S(1)}, u32[]{:S(2)}, u32[]{:S(2)}) collective-permute-start(f32[3,2,64,128]{3,2,1,0:T(8,128)S(1)} %get-tuple-element.48), channel_id=1, source_target_pairs={{32,0},{33,1},{34,2},{35,3},{36,4},{37,5},{38,6},{39,7},{40,8},{41... | collective-permute-start | bytes 589832 | tf_op jit(solution)/shard_map/ppermute | solution.py:480
  151.5 4.6 %collective-permute-start.10 = (f32[3,64,128]{2,1,0:T(8,128)S(1)}, f32[3,64,128]{2,1,0:T(8,128)S(1)}, u32[]{:S(2)}, u32[]{:S(2)}) collective-permute-start(f32[3,64,128]{2,1,0:T(8,128)S(1)} %get-tuple-element.50), channel_id=1, source_target_pairs={{0,1},{1,2},{2,3},{3,4},{4,5},{5,6},{6,7},{7,8},{8,9},{9,10},{10,1... | collective-permute-start | bytes 294920 | tf_op jit(solution)/shard_map/ppermute | solution.py:480
  154.5 5.4 %collective-permute-start.11 = (f32[3,64,128]{2,1,0:T(8,128)S(1)}, f32[3,64,128]{2,1,0:T(8,128)S(1)}, u32[]{:S(2)}, u32[]{:S(2)}) collective-permute-start(f32[3,64,128]{2,1,0:T(8,128)S(1)} %get-tuple-element.51), channel_id=1, source_target_pairs={{1,0},{2,1},{3,2},{4,3},{5,4},{6,5},{7,6},{8,7},{9,8},{10,9},{11,1... | collective-permute-start | bytes 294920 | tf_op jit(solution)/shard_map/ppermute | solution.py:480

commit v4 on v3

--- a/solution.py
+++ b/solution.py
@@ -13,14 +13,17 @@
 HALF = 64
 MODES = 2
 COUNT = 8
-GROUP = 2
+GROUP = 8
 ROW = ("yl", "x", "c")
 COL = ("yh", "zh", "zl")
 ALL = ROW + COL
 SCATTER = ROW + ("zl",)
 REST = ("yh", "zh")
+MARK = 1024
+LIST_STEP = 4
+LIST_SIZE = 9 * COUNT + 8
 TILES = 8
-VMEM_LIMIT = 48 * 1024 * 1024
+VMEM_LIMIT = 16 * 1024 * 1024
 F32 = jnp.float32
 BF16 = jnp.bfloat16
 
@@ -75,9 +78,9 @@
 
 def window(ref, lead, row, col):
     shift = lax.rem(SIZE - col, SIZE)
-    first = pltpu.roll(ref[lead + (0, pl.ds(row, SIZE))], shift, 1)
-    second = pltpu.roll(ref[lead + (1, pl.ds(row, SIZE))], shift, 1)
-    return jnp.where(lanes() < SIZE - col, first, second)
+    rows = pl.ds(row, SIZE)
+    mixed = jnp.where(lanes() >= col, ref[lead + (0, rows)], ref[lead + (1, rows)])
+    return pltpu.roll(mixed, shift, 1)
 
 
 def place(ref, plane, row, col, block):
@@ -118,7 +121,7 @@
 def pad_field(above, own, below, from_left, from_right, store):
     low = low_lanes(HALF)
     for c in range(2):
-        strips = (above[c], own[c, :HALF], own[c, HALF:], below[c])
+        strips = (above[c, :HALF], own[c, :HALF], own[c, HALF:], below[c, :HALF])
         for k in range(4):
             half = slice(HALF * (k % 2), HALF * (k % 2 + 1))
             left, right = from_left[c, half], from_right[c, half]
@@ -132,14 +135,36 @@
             store(c, 1, rows, jnp.where(low, mine, right))
 
 
-def pack_kernel(above, own, below, left, right):
+def send_kernel(offsets, own, to_below, to_above):
+    line = lax.broadcasted_iota(jnp.int32, (TILES, SIZE), 0)
+    lane = lax.broadcasted_iota(jnp.int32, (TILES, SIZE), 1)
+    code = jnp.zeros((TILES, SIZE), jnp.int32)
+    batches, count, _ = offsets.shape
+    for b in range(batches):
+        for k in range(count):
+            for d in range(2):
+                code = jnp.where(lane == (b * count + k) * 2 + d, offsets[b, k, d] + MARK, code)
+    code = jnp.where(line == 0, code, 0).astype(F32)
+    for c in range(2):
+        to_below[c, :HALF] = own[c, HALF:]
+        to_above[c, :HALF] = own[c, :HALF]
+        to_below[c, HALF:] = code
+        to_above[c, HALF:] = code
+
+
+def pack_kernel(above, own, below, mine, to_left, to_right, codes):
     low = low_lanes(HALF)
     for c in range(2):
-        strips = (above[c], own[c, :HALF], own[c, HALF:], below[c])
+        strips = (above[c, :HALF], own[c, :HALF], own[c, HALF:], below[c, :HALF])
         for k in range(2):
             rows = slice(HALF * k, HALF * (k + 1))
-            left[c, rows] = pack_low(low, strips[k], strips[k + 2])
-            right[c, rows] = pack_high(low, strips[k], strips[k + 2])
+            to_left[c, rows] = pack_low(low, strips[k], strips[k + 2])
+            to_right[c, rows] = pack_high(low, strips[k], strips[k + 2])
+    code = mine[0, HALF:] + pltpu.roll(above[0, HALF:], 1, 0) + pltpu.roll(below[0, HALF:], 2, 0)
+    for c in range(2):
+        to_left[c, SIZE:] = code
+        to_right[c, SIZE:] = code
+    codes[...] = code
 
 
 def power_of(probe):
@@ -206,28 +231,47 @@
     bottom[...] = accum[:, :, SIZE:]
 
 
-def cover_kernel(shifts, probe, cover, total):
-    total[...] = jnp.zeros_like(total)
-    light = power_of(probe)
+def offset_of(others, batch, across, down, j, d):
+    return others[TILES * across + (1, 0, 2)[down], (batch * COUNT + j) * 2 + d] - MARK
+
+
+def cover_kernel(others, probe, cover, near, light):
+    none = jnp.zeros((SIZE, SIZE), F32)
+    light[:SIZE] = none
+    light[SIZE : 2 * SIZE] = power_of(probe)
+    light[2 * SIZE :] = none
     lane = lanes()
-
-    def body(k, carry):
-        row, col = shifts[k, 0] + SIZE + HALF, shifts[k, 1] + SIZE + HALF
-
-        @pl.when((row >= 0) & (row <= 3 * SIZE) & (col >= 0) & (col <= 3 * SIZE))
-        def _():
-            block = lax.div(col, SIZE)
-            turn = lax.rem(col, SIZE)
-            moved = pltpu.roll(light, turn, 1)
-            first = lane >= turn
-            rows = pl.ds(row, SIZE)
-            total[block, rows] += jnp.where(first, moved, 0.0)
-            total[block + 1, rows] += jnp.where(first, 0.0, moved)
-
-        return carry
-
-    lax.fori_loop(0, shifts.shape[0], body, 0)
-    cover[...] = total[1:3, SIZE : 3 * SIZE]
+    for v in range(2):
+        total = [none, none]
+        for down in (v, v + 1):
+            for across in range(3):
+                for j in range(COUNT):
+                    row, col = (offset_of(others, 0, across, down, j, d) + HALF for d in range(2))
+                    row = jnp.clip(row + SIZE * (down - 1 - v), -SIZE, SIZE)
+                    col = jnp.clip(col, 0, SIZE)
+                    moved = pltpu.roll(light[pl.ds(SIZE - row, SIZE)], lax.rem(col, SIZE), 1)
+                    first = lane >= col
+                    if across >= 1:
+                        total[across - 1] = total[across - 1] + jnp.where(first, moved, 0.0)
+                    if across <= 1:
+                        total[across] = total[across] + jnp.where(first, 0.0, moved)
+        for h in range(2):
+            cover[h, v * SIZE : (v + 1) * SIZE] = total[h]
+
+    count = jnp.int32(0)
+    for down in range(3):
+        for across in range(3):
+            for j in range(COUNT):
+                row = offset_of(others, 1, across, down, j, 0) + SIZE * (down - 1)
+                col = offset_of(others, 1, across, down, j, 1) + SIZE * (across - 1)
+                near[count, 0] = row
+                near[count, 1] = col
+                reaches = (jnp.abs(row) < SIZE) & (jnp.abs(col) < SIZE)
+                count += reaches.astype(jnp.int32)
+    for k in range(LIST_STEP):
+        near[count + k, 0] = SIZE
+        near[count + k, 1] = 0
+    near[LIST_SIZE - 1, 0] = count
 
 
 def wide_fold_kernel(top, bottom, from_above, from_below, left, right):
@@ -299,7 +343,7 @@
         right[k] = pack_high(low, upper[1], lower[1])
 
 
-def merge_kernel(shifts, tile, from_left, from_right, padded, sums,
+def merge_kernel(near, tile, from_left, from_right, padded, sums,
                  packed, direction, product, overlap):
     low = low_lanes(HALF)
     lane = lanes()
@@ -333,21 +377,21 @@
         b1 += jnp.sum(power * (cover + 1.0), axis=0, keepdims=True)
     overlap[...] = jnp.zeros_like(overlap)
 
-    def body(k, carry):
-        down, across = shifts[k, 0], shifts[k, 1]
-
-        @pl.when((jnp.abs(down) < SIZE) & (jnp.abs(across) < SIZE))
-        def _():
-            turn = lax.rem(SIZE - across, SIZE)
+    def body(step, carry):
+        total = [0.0, 0.0]
+        for g in range(LIST_STEP):
+            down, across = near[step * LIST_STEP + g, 0], near[step * LIST_STEP + g, 1]
+            turn = lax.rem(2 * SIZE - across, SIZE)
             source = lane + across
-            inside = (source >= 0) & (source < SIZE)
+            valid = (source >= 0) & (source < SIZE)
             for c in range(2):
                 moved = pltpu.roll(product[c, pl.ds(SIZE + down, SIZE)], turn, 1)
-                overlap[c] += jnp.where(inside, moved, 0.0)
-
+                total[c] = total[c] + jnp.where(valid, moved, 0.0)
+        for c in range(2):
+            overlap[c] += total[c]
         return carry
 
-    lax.fori_loop(0, shifts.shape[0], body, 0)
+    lax.fori_loop(0, lax.div(near[LIST_SIZE - 1, 0] + LIST_STEP - 1, LIST_STEP), body, 0)
 
     pack_sums(packed, sums, (overlap[0], overlap[1]), a11, b1)
 
@@ -460,7 +504,7 @@
     return pl.pallas_call(
         kernel,
         in_specs=specs,
-        out_specs=[vmem] * len(outs),
+        out_specs=[smem if x.dtype == jnp.int32 else vmem for x in outs],
         out_shape=list(outs),
         scratch_shapes=list(scratch),
         compiler_params=pltpu.CompilerParams(vmem_limit_bytes=VMEM_LIMIT),
@@ -497,13 +541,9 @@
     return exchange(part, SCATTER).reshape(SIZE // TILES, 2, 3, TILES, SIZE)
 
 
-MARK = 1024.0
-
-
 def per_device(obj, probe, measured, offsets):
     right3, left3 = (jnp.asarray(t) for t in dft_tables())
     offsets = offsets[0, 0]
-    batches = offsets.shape[0]
     r, c, half = (lax.axis_index(axes).astype(jnp.int32) for axes in (ROW, COL, ("zl",)))
     whole = 2 * SIZE
     place_in_group = jnp.stack([r, half])
@@ -514,30 +554,16 @@
         jnp.where(c == size_of(COL) - 1, whole - HALF, whole),
     ]).astype(jnp.int32)
 
-    code = jnp.zeros((TILES * SIZE,), F32).at[: offsets.size].set(
-        offsets.reshape(-1).astype(F32) + MARK)
-    code = code.reshape(1, TILES, SIZE)
-
-    def with_code(strip, more):
-        return jnp.concatenate([strip, jnp.pad(more, ((0, 1), (0, 0), (0, 0)))], axis=1)
-
-    above = shift(with_code(obj[:, HALF:], code), 1, 0)
-    below = shift(with_code(obj[:, :HALF], code), -1, 0)
-    codes = jnp.concatenate([above[:1, HALF:], code, below[:1, HALF:]], axis=1)
-    above, below = above[:, :HALF], below[:, :HALF]
-    packed_field = shape(2, SIZE, SIZE)
-    left, right = call(pack_kernel, [above, obj, below], [packed_field] * 2)
-    from_left = shift(with_code(right, codes), 0, 1)
-    from_right = shift(with_code(left, codes), 0, -1)
-    codes = jnp.stack([from_left[0, SIZE:], codes[0], from_right[0, SIZE:]])
-    codes = codes.reshape(3, 3, -1)[:, :, : offsets.size].reshape((3, 3) + offsets.shape)
-    away = jnp.arange(-1, 2, dtype=jnp.int32) * SIZE
-    steps = jnp.stack([
-        jnp.broadcast_to(away[None, :, None, None], codes.shape[:-1]),
-        jnp.broadcast_to(away[:, None, None, None], codes.shape[:-1]),
-    ], axis=-1)
-    shifts = (codes - MARK).astype(jnp.int32) + steps
-    shifts = jnp.moveaxis(shifts, 2, 0).reshape(batches, -1, 2)
+    strip = shape(2, HALF + TILES, SIZE)
+    side = shape(2, SIZE + TILES, SIZE)
+    to_below, to_above = call(send_kernel, [offsets, obj], [strip, strip])
+    above = shift(to_below, 1, 0)
+    below = shift(to_above, -1, 0)
+    to_left, to_right, codes = call(
+        pack_kernel, [above, obj, below, to_below], [side, side, shape(TILES, SIZE)])
+    from_left = shift(to_right, 0, 1)
+    from_right = shift(to_left, 0, -1)
+    others = jnp.concatenate([from_left[0, SIZE:], codes, from_right[0, SIZE:]], axis=0).astype(jnp.int32)
 
     field = shape(2, 2, whole, SIZE)
     edge = shape(3, 2, HALF, SIZE)
@@ -548,14 +574,16 @@
 
     top, bottom, sums, padded = call(
         first_kernel,
-        [offsets, above, obj, below, from_left[:, :SIZE], from_right[:, :SIZE], probe, measured, right3, left3],
+        [offsets, above, obj, below, from_left, from_right, probe, measured, right3, left3],
         [quads, quads, sums_shape, field],
         [pltpu.VMEM((2, 2, whole, SIZE), F32)],
     )
     from_above = shift(bottom, 1, 0)
     from_below = shift(top, -1, 0)
-    (cover,) = call(
-        cover_kernel, [shifts[0], probe], [shape(2, whole, SIZE)], [pltpu.VMEM((5, 4 * SIZE, SIZE), F32)])
+    cover, near = call(
+        cover_kernel, [others, probe],
+        [shape(2, whole, SIZE), jax.ShapeDtypeStruct((LIST_SIZE, 2), jnp.int32)],
+        [pltpu.VMEM((3 * SIZE, SIZE), F32)])
     left, right = call(wide_fold_kernel, [top, bottom, from_above, from_below], [quads, quads])
     from_left = shift(right, 0, 1)
     from_right = shift(left, 0, -1)
@@ -582,7 +610,7 @@
     from_right = shift(left, 0, -1)
     packed, direction = call(
         merge_kernel,
-        [shifts[1], tile, from_left, from_right, padded, sums],
+        [near, tile, from_left, from_right, padded, sums],
         [packed_shape, shape(2, SIZE, SIZE)],
         [pltpu.VMEM((2, 3 * SIZE, SIZE), F32), pltpu.VMEM((2, SIZE, SIZE), F32)],
     )

time: 223 us -> 217 us (0.973)
  Pallas kernels: 34.1 us -> 25.9 us
  waiting for transfers between devices: 26.7 us -> 31.6 us
    pallas_call x13 -> x14, Pallas kernels: 34.1 us -> 25.9 us  [call(): pl.pallas_call(kernel, in_specs=specs, out_specs=[smem if x.dtype == jnp....]
    ppermute x12, waiting for transfers between devices: 14.7 us -> 19.6 us  [shift(): return lax.ppermute(block, ALL, route)]
    all_to_all x1, starting transfers between devices: 18.6 us -> 22.6 us  [exchange(): return lax.all_to_all(block, axes, 0, 0, tiled=True)]
    slice x10 -> x0, local copies, waits for them, and re-layouts: 2.38 us -> none  [the longest x2 1.42 us: per_device(): codes = jnp.stack([from_left[0, SIZE:], codes[0], from_right[0, SIZE:]])]
    unnamed x26 -> x20, local copies, waits for them, and re-layouts: 3.08 us -> 5.05 us
  transfers between devices with their start and end apart: 13 -> 13, of which waited for: 8 -> 10; matrix products, arithmetic and copies ran while one was open for 2% -> 0% of each run, Pallas kernels for 3% -> 2%
where the time goes in v4:
time: 217 us; the launch traced here: 216 us
  blocking collectives  95.7 us (44%)
  starting transfers between devices  56 us (26%)
  waiting for transfers between devices  31.6 us (15%)
  Pallas kernels  25.9 us (12%)
  local copies, waits for them, and re-layouts  5.82 us (3%)
    all_to_all x5, blocking collectives, exchange(): return lax.all_to_all(block, axes, 0, 0, tiled=True)  95.7 us
    ppermute x12, starting transfers between devices, shift(): return lax.ppermute(block, ALL, route)  33.5 us
    pallas_call x14, Pallas kernels, call(): pl.pallas_call(kernel, in_specs=specs, out_specs=[smem if x.dtype == jnp....  25.9 us
    all_to_all x1, starting transfers between devices, exchange(): return lax.all_to_all(block, axes, 0, 0, tiled=True)  22.6 us
    ppermute x12, waiting for transfers between devices, shift(): return lax.ppermute(block, ALL, route)  19.6 us
    all_to_all x1, waiting for transfers between devices, exchange(): return lax.all_to_all(block, axes, 0, 0, tiled=True)  12 us
    unnamed x20, local copies, waits for them, and re-layouts  5.05 us
  transfers between devices with their start and end apart: 13, of which 10 were waited for; matrix products, arithmetic and copies ran while one was open for 0% of the time, Pallas kernels for 2%

profile of v4, /device:TPU:1, one launch (start us, length us, event | category | flops | bytes accessed | tf_op | source)
XLA Modules:
  0.0 216.1 jit_solution(17348148454816420690)
XLA Ops:
  3.0 8.8 %collective-permute-start.1 = (f32[2,72,128]{2,1,0:T(8,128)S(1)}, f32[2,72,128]{2,1,0:T(8,128)S(1)}, u32[]{:S(2)}, u32[]{:S(2)}) collective-permute-start(f32[2,72,128]{2,1,0:T(8,128)S(1)} %get-tuple-element.30), channel_id=1, source_target_pairs={{32,0},{33,1},{34,2},{35,3},{36,4},{37,5},{38,6},{39,7},{40,8},{41... | collective-permute-start | bytes 221192 | tf_op jit(solution)/shard_map/ppermute | solution.py:524
  11.8 1.9 collective-permute-start
  13.7 1.4 collective-permute-done.above
  16.1 1.3 collective-permute-start.2
  17.5 1.3 collective-permute-start.3
  18.8 1.9 collective-permute-done.2.from_left
  20.7 3.9 %collective-permute-done.3.from_right = f32[2,136,128]{2,1,0:T(8,128)S(1)} collective-permute-done((f32[2,136,128]{2,1,0:T(8,128)S(1)}, f32[2,136,128]{2,1,0:T(8,128)S(1)}, u32[]{:S(2)}, u32[]{:S(2)}) %collective-permute-start.3) | collective-permute-done | bytes 139296 | tf_op jit(solution)/shard_map/ppermute | solution.py:524
  24.7 1.2 copy-done
  27.9 6.5 %first_kernel.1 = (f32[2,2,128,128]{3,2,1,0:T(8,128)S(1)}, f32[2,2,128,128]{3,2,1,0:T(8,128)S(1)}, f32[5,128,128]{2,1,0:T(8,128)S(1)}, f32[2,2,256,128]{3,2,1,0:T(8,128)S(1)}) custom-call(s32[2,8,2]{2,1,0:T(8,128)S(1)} %copy.9.offsets, f32[2,72,128]{2,1,0:T(8,128)S(1)} %collective-permute-done.above, f32[2,128,128]{2,1,0:T(8,128)S(1)} %copy-done.9, ...), custom_call_target="tpu_custom_call" | custom-call | tf_op jit(solution)/shard_map/first_kernel/pallas_call | solution.py:504
  34.4 2.7 %collective-permute-start.5 = (f32[2,2,128,128]{3,2,1,0:T(8,128)S(1)}, f32[2,2,128,128]{3,2,1,0:T(8,128)S(1)}, u32[]{:S(2)}, u32[]{:S(2)}) collective-permute-start(f32[2,2,128,128]{3,2,1,0:T(8,128)S(1)} %get-tuple-element.35.top), channel_id=1, source_target_pairs={{32,0},{33,1},{34,2},{35,3},{36,4},{37,5},{38,6},{39,7},{40,8},{41... | collective-permute-start | bytes 786440 | tf_op jit(solution)/shard_map/ppermute | solution.py:524
  37.1 3.3 %collective-permute-start.4 = (f32[2,2,128,128]{3,2,1,0:T(8,128)S(1)}, f32[2,2,128,128]{3,2,1,0:T(8,128)S(1)}, u32[]{:S(2)}, u32[]{:S(2)}) collective-permute-start(f32[2,2,128,128]{3,2,1,0:T(8,128)S(1)} %get-tuple-element.36.bottom), channel_id=1, source_target_pairs={{0,32},{1,33},{2,34},{3,35},{4,36},{5,37},{6,38},{7,39},{8,40},{9,... | collective-permute-start | bytes 786440 | tf_op jit(solution)/shard_map/ppermute | solution.py:524
  40.4 2.0 collective-permute-done.5.from_below
  42.4 1.2 collective-permute-done.4.from_above
  43.7 1.3 collective-permute-start.7
  45.0 4.0 %collective-permute-start.6 = (f32[2,2,128,128]{3,2,1,0:T(8,128)S(1)}, f32[2,2,128,128]{3,2,1,0:T(8,128)S(1)}, u32[]{:S(2)}, u32[]{:S(2)}) collective-permute-start(f32[2,2,128,128]{3,2,1,0:T(8,128)S(1)} %get-tuple-element.38.right), channel_id=1, source_target_pairs={{0,1},{1,2},{2,3},{3,4},{4,5},{5,6},{6,7},{7,8},{8,9},{9,10},{10,1... | collective-permute-start | bytes 786440 | tf_op jit(solution)/shard_map/ppermute | solution.py:524
  49.0 4.0 %cover_kernel.1 = (f32[2,256,128]{2,1,0:T(8,128)S(1)}, s32[80,2]{1,0:T(8,128)S(1)}) custom-call(s32[24,128]{1,0:T(8,128)S(1)} %maximum_convert_fusion.others, f32[2,2,128,128]{3,2,1,0:T(8,128)S(1)} %copy-done.2), custom_call_target="tpu_custom_call" | custom-call | tf_op jit(solution)/shard_map/cover_kernel/pallas_call | solution.py:504
  53.1 1.3 wide_merge_kernel.1
  54.4 23.9 %all_to_all.30.parts = f32[32,4,8,128]{3,2,1,0:T(8,128)S(1)} all-to-all(f32[32,4,8,128]{3,2,1,0:T(8,128)S(1)} %bitcast.17), channel_id=1, replica_groups=mesh['yl'=2,'x'=4,'c'=2,'yh'=4,'zh'=4,'zl'=2] {'yl','x','c','zl'}, dimensions={0} | all-to-all | bytes 1048576 | tf_op jit(solution)/shard_map/all_to_all | solution.py:528
  79.1 22.6 %all-to-all-start.1 = ((f32[16,4,8,128]{3,2,1,0:T(8,128)}), f32[16,4,8,128]{3,2,1,0:T(8,128)S(1)}, u32[]{:S(2)}, u32[]{:S(2)}) async-start(f32[16,4,8,128]{3,2,1,0:T(8,128)} %reduce_kernel.2), calls=%async_computation.1 | async-start | bytes 524288 | tf_op jit(solution)/shard_map/all_to_all | solution.py:528
  101.8 12.0 %all-to-all-done.1.parts = f32[16,4,8,128]{3,2,1,0:T(8,128)S(1)} async-done(((f32[16,4,8,128]{3,2,1,0:T(8,128)}), f32[16,4,8,128]{3,2,1,0:T(8,128)S(1)}, u32[]{:S(2)}, u32[]{:S(2)}) %all-to-all-start.1) | async-done | bytes 262176 | tf_op jit(solution)/shard_map/all_to_all | solution.py:528
  114.4 16.1 %all_to_all.31 = f32[32,3,8,128]{3,2,1,0:T(8,128)S(1)} all-to-all(f32[32,3,8,128]{3,2,1,0:T(8,128)S(1)} %strip_kernel.2), channel_id=1, replica_groups=mesh['yl'=2,'x'=4,'c'=2,'yh'=4,'zh'=4,'zl'=2] {'yl','x','c','zl'}, dimensions={0} | all-to-all | bytes 786432 | tf_op jit(solution)/shard_map/all_to_all | solution.py:528
  130.6 6.9 %next_kernel.1 = (f32[3,2,64,128]{3,2,1,0:T(8,128)S(1)}, f32[3,2,128,128]{3,2,1,0:T(8,128)S(1)}, f32[3,2,64,128]{3,2,1,0:T(8,128)S(1)}, f32[5,128,128]{2,1,0:T(8...) custom-call(s32[2,8,2]{2,1,0:T(8,128)S(1)} %copy.9.offsets, ...), custom_call_target="tpu_custom_call" | custom-call | tf_op jit(solution)/shard_map/next_kernel/pallas_call | solution.py:504
  137.5 2.7 %collective-permute-start.8 = (f32[3,2,64,128]{3,2,1,0:T(8,128)S(1)}, f32[3,2,64,128]{3,2,1,0:T(8,128)S(1)}, u32[]{:S(2)}, u32[]{:S(2)}) collective-permute-start(f32[3,2,64,128]{3,2,1,0:T(8,128)S(1)} %get-tuple-element.45), channel_id=1, source_target_pairs={{0,32},{1,33},{2,34},{3,35},{4,36},{5,37},{6,38},{7,39},{8,40},{9,... | collective-permute-start | bytes 589832 | tf_op jit(solution)/shard_map/ppermute | solution.py:524
  140.2 1.9 collective-permute-start.9
  142.8 4.4 %collective-permute-done.9.from_below = f32[3,2,64,128]{3,2,1,0:T(8,128)S(1)} collective-permute-done((f32[3,2,64,128]{3,2,1,0:T(8,128)S(1)}, f32[3,2,64,128]{3,2,1,0:T(8,128)S(1)}, u32[]{:S(2)}, u32[]{:S(2)}) %collective-permute-start.9) | collective-permute-done | bytes 196640 | tf_op jit(solution)/shard_map/ppermute | solution.py:524
  147.4 3.0 %collective-permute-start.10 = (f32[3,64,128]{2,1,0:T(8,128)S(1)}, f32[3,64,128]{2,1,0:T(8,128)S(1)}, u32[]{:S(2)}, u32[]{:S(2)}) collective-permute-start(f32[3,64,128]{2,1,0:T(8,128)S(1)} %get-tuple-element.48), channel_id=1, source_target_pairs={{0,1},{1,2},{2,3},{3,4},{4,5},{5,6},{6,7},{7,8},{8,9},{9,10},{10,1... | collective-permute-start | bytes 294920 | tf_op jit(solution)/shard_map/ppermute | solution.py:524
  150.4 1.3 collective-permute-start.11
  152.0 3.7 %collective-permute-done.11.from_right = f32[3,64,128]{2,1,0:T(8,128)S(1)} collective-permute-done((f32[3,64,128]{2,1,0:T(8,128)S(1)}, f32[3,64,128]{2,1,0:T(8,128)S(1)}, u32[]{:S(2)}, u32[]{:S(2)}) %collective-permute-start.11) | collective-permute-done | bytes 98336 | tf_op jit(solution)/shard_map/ppermute | solution.py:524
  155.8 2.9 %merge_kernel.1 = (f32[16,2,4,8,128]{4,3,2,1,0:T(8,128)S(1)}, f32[2,128,128]{2,1,0:T(8,128)S(1)}) custom-call(s32[80,2]{1,0:T(8,128)S(1)} %get-tuple-element.34.near, f32[3,128,128]{2,1,0:T(8,128)S(1)} %get-tuple-element.47.tile, f32[3,64,128]{2,1,0:T(8,128)S(1)} %collective-permute-done.10.from_left, f32[3,64,128]{2,1,0:T(8,128)S(1)} %collective-permute-done.11.from_right, ...), custom_call_target="tpu_custom_call" | custom-call | tf_op jit(solution)/shard_map/merge_kernel/pallas_call | solution.py:504
  158.7 17.5 %all_to_all.32.parts = f32[32,4,8,128]{3,2,1,0:T(8,128)S(1)} all-to-all(f32[32,4,8,128]{3,2,1,0:T(8,128)S(1)} %bitcast.18), channel_id=1, replica_groups=mesh['yl'=2,'x'=4,'c'=2,'yh'=4,'zh'=4,'zl'=2] {'yl','x','c','zl'}, dimensions={0} | all-to-all | bytes 1048576 | tf_op jit(solution)/shard_map/all_to_all | solution.py:528
  176.3 22.2 %all_to_all.33.parts = f32[16,4,8,128]{3,2,1,0:T(8,128)S(1)} all-to-all(f32[16,4,8,128]{3,2,1,0:T(8,128)S(1)} %reduce_kernel.3), channel_id=1, replica_groups=mesh['yl'=2,'x'=4,'c'=2,'yh'=4,'zh'=4,'zl'=2] {'yh','zh'}, dimensions={0} | all-to-all | bytes 524288 | tf_op jit(solution)/shard_map/all_to_all | solution.py:528
  199.1 16.0 %all_to_all.34 = f32[32,3,8,128]{3,2,1,0:T(8,128)S(1)} all-to-all(f32[32,3,8,128]{3,2,1,0:T(8,128)S(1)} %strip_kernel.3), channel_id=1, replica_groups=mesh['yl'=2,'x'=4,'c'=2,'yh'=4,'zh'=4,'zl'=2] {'yl','x','c','zl'}, dimensions={0} | all-to-all | bytes 786432 | tf_op jit(solution)/shard_map/all_to_all | solution.py:528
  (39 shorter events, 9.9 us)
Async XLA Ops:
  1.4 0.9 copy-start.7
  2.3 22.4 %copy-start.2 = (f32[2,2,128,128]{3,2,1,0:T(8,128)S(1)}, f32[2,2,128,128]{3,2,1,0:T(8,128)}, u32[]{:S(2)}) copy-start(f32[2,2,128,128]{3,2,1,0:T(8,128)} %probe.7) | copy-start | bytes 786436
  3.0 10.7 %collective-permute-start.1 = (f32[2,72,128]{2,1,0:T(8,128)S(1)}, f32[2,72,128]{2,1,0:T(8,128)S(1)}, u32[]{:S(2)}, u32[]{:S(2)}) collective-permute-start(f32[2,72,128]{2,1,0:T(8,128)S(1)} %get-tuple-element.30), channel_id=1, source_target_pairs={{32,0},{33,1},{34,2},{35,3},{36,4},{37,5},{38,6},{39,7},{40,8},{41... | collective-permute-start | bytes 221192 | tf_op jit(solution)/shard_map/ppermute | solution.py:524
  11.8 3.3 %collective-permute-start = (f32[2,72,128]{2,1,0:T(8,128)S(1)}, f32[2,72,128]{2,1,0:T(8,128)S(1)}, u32[]{:S(2)}, u32[]{:S(2)}) collective-permute-start(f32[2,72,128]{2,1,0:T(8,128)S(1)} %get-tuple-element.29.mine), channel_id=1, source_target_pairs={{0,32},{1,33},{2,34},{3,35},{4,36},{5,37},{6,38},{7,39},{8,40},{9,... | collective-permute-start | bytes 221192 | tf_op jit(solution)/shard_map/ppermute | solution.py:524
  15.1 0.9 copy-start.8
  16.0 8.6 %copy-start.9 = (f32[2,128,128]{2,1,0:T(8,128)S(1)}, f32[2,128,128]{2,1,0:T(8,128)}, u32[]{:S(2)}) copy-start(f32[2,128,128]{2,1,0:T(8,128)} %own.5) | copy-start | bytes 393220
  16.1 4.6 %collective-permute-start.2 = (f32[2,136,128]{2,1,0:T(8,128)S(1)}, f32[2,136,128]{2,1,0:T(8,128)S(1)}, u32[]{:S(2)}, u32[]{:S(2)}) collective-permute-start(f32[2,136,128]{2,1,0:T(8,128)S(1)} %get-tuple-element.31), channel_id=1, source_target_pairs={{0,1},{1,2},{2,3},{3,4},{4,5},{5,6},{6,7},{7,8},{8,9},{9,10},{10,1... | collective-permute-start | bytes 417800 | tf_op jit(solution)/shard_map/ppermute | solution.py:524
  17.5 7.2 %collective-permute-start.3 = (f32[2,136,128]{2,1,0:T(8,128)S(1)}, f32[2,136,128]{2,1,0:T(8,128)S(1)}, u32[]{:S(2)}, u32[]{:S(2)}) collective-permute-start(f32[2,136,128]{2,1,0:T(8,128)S(1)} %get-tuple-element.33), channel_id=1, source_target_pairs={{1,0},{2,1},{3,2},{4,3},{5,4},{6,5},{7,6},{8,7},{9,8},{10,9},{11,1... | collective-permute-start | bytes 417800 | tf_op jit(solution)/shard_map/ppermute | solution.py:524
  24.7 1.2 copy-start
  25.9 1.0 copy-start.3
  26.9 1.0 copy-start.5
  34.4 8.1 %collective-permute-start.5 = (f32[2,2,128,128]{3,2,1,0:T(8,128)S(1)}, f32[2,2,128,128]{3,2,1,0:T(8,128)S(1)}, u32[]{:S(2)}, u32[]{:S(2)}) collective-permute-start(f32[2,2,128,128]{3,2,1,0:T(8,128)S(1)} %get-tuple-element.35.top), channel_id=1, source_target_pairs={{32,0},{33,1},{34,2},{35,3},{36,4},{37,5},{38,6},{39,7},{40,8},{41... | collective-permute-start | bytes 786440 | tf_op jit(solution)/shard_map/ppermute | solution.py:524
  37.1 6.6 %collective-permute-start.4 = (f32[2,2,128,128]{3,2,1,0:T(8,128)S(1)}, f32[2,2,128,128]{3,2,1,0:T(8,128)S(1)}, u32[]{:S(2)}, u32[]{:S(2)}) collective-permute-start(f32[2,2,128,128]{3,2,1,0:T(8,128)S(1)} %get-tuple-element.36.bottom), channel_id=1, source_target_pairs={{0,32},{1,33},{2,34},{3,35},{4,36},{5,37},{6,38},{7,39},{8,40},{9,... | collective-permute-start | bytes 786440 | tf_op jit(solution)/shard_map/ppermute | solution.py:524
  43.7 9.4 %collective-permute-start.7 = (f32[2,2,128,128]{3,2,1,0:T(8,128)S(1)}, f32[2,2,128,128]{3,2,1,0:T(8,128)S(1)}, u32[]{:S(2)}, u32[]{:S(2)}) collective-permute-start(f32[2,2,128,128]{3,2,1,0:T(8,128)S(1)} %get-tuple-element.37.left), channel_id=1, source_target_pairs={{1,0},{2,1},{3,2},{4,3},{5,4},{6,5},{7,6},{8,7},{9,8},{10,9},{11,1... | collective-permute-start | bytes 786440 | tf_op jit(solution)/shard_map/ppermute | solution.py:524
  45.0 8.1 %collective-permute-start.6 = (f32[2,2,128,128]{3,2,1,0:T(8,128)S(1)}, f32[2,2,128,128]{3,2,1,0:T(8,128)S(1)}, u32[]{:S(2)}, u32[]{:S(2)}) collective-permute-start(f32[2,2,128,128]{3,2,1,0:T(8,128)S(1)} %get-tuple-element.38.right), channel_id=1, source_target_pairs={{0,1},{1,2},{2,3},{3,4},{4,5},{5,6},{6,7},{7,8},{8,9},{9,10},{10,1... | collective-permute-start | bytes 786440 | tf_op jit(solution)/shard_map/ppermute | solution.py:524
  79.1 51.5 %copy-start.1 = (f32[1,1,2,8,128,128]{5,4,3,2,1,0:T(8,128)S(1)}, f32[1,1,2,8,128,128]{5,4,3,2,1,0:T(8,128)}, u32[]{:S(2)}) copy-start(f32[1,1,2,8,128,128]{5,4,3,2,1,0:T(8,128)} %measured.3) | copy-start | bytes 3145732
  79.1 34.7 %all-to-all-start.1 = ((f32[16,4,8,128]{3,2,1,0:T(8,128)}), f32[16,4,8,128]{3,2,1,0:T(8,128)S(1)}, u32[]{:S(2)}, u32[]{:S(2)}) async-start(f32[16,4,8,128]{3,2,1,0:T(8,128)} %reduce_kernel.2), calls=%async_computation.1 | async-start | bytes 524288 | tf_op jit(solution)/shard_map/all_to_all | solution.py:528
  114.4 16.1 %copy-start.4 = (bf16[256,768]{1,0:T(8,128)(2,1)S(1)}, bf16[256,768]{1,0:T(8,128)(2,1)}, u32[]{:S(2)}) copy-start(bf16[256,768]{1,0:T(8,128)(2,1)} %constant.44.clone.left3) | copy-start | bytes 1179652
  114.4 16.1 %copy-start.6 = (bf16[768,256]{1,0:T(8,128)(2,1)S(1)}, bf16[768,256]{1,0:T(8,128)(2,1)}, u32[]{:S(2)}) copy-start(bf16[768,256]{1,0:T(8,128)(2,1)} %constant.43.clone.right3) | copy-start | bytes 1179652
  137.5 5.3 %collective-permute-start.8 = (f32[3,2,64,128]{3,2,1,0:T(8,128)S(1)}, f32[3,2,64,128]{3,2,1,0:T(8,128)S(1)}, u32[]{:S(2)}, u32[]{:S(2)}) collective-permute-start(f32[3,2,64,128]{3,2,1,0:T(8,128)S(1)} %get-tuple-element.45), channel_id=1, source_target_pairs={{0,32},{1,33},{2,34},{3,35},{4,36},{5,37},{6,38},{7,39},{8,40},{9,... | collective-permute-start | bytes 589832 | tf_op jit(solution)/shard_map/ppermute | solution.py:524
  140.2 7.0 %collective-permute-start.9 = (f32[3,2,64,128]{3,2,1,0:T(8,128)S(1)}, f32[3,2,64,128]{3,2,1,0:T(8,128)S(1)}, u32[]{:S(2)}, u32[]{:S(2)}) collective-permute-start(f32[3,2,64,128]{3,2,1,0:T(8,128)S(1)} %get-tuple-element.46), channel_id=1, source_target_pairs={{32,0},{33,1},{34,2},{35,3},{36,4},{37,5},{38,6},{39,7},{40,8},{41... | collective-permute-start | bytes 589832 | tf_op jit(solution)/shard_map/ppermute | solution.py:524
  147.4 4.6 %collective-permute-start.10 = (f32[3,64,128]{2,1,0:T(8,128)S(1)}, f32[3,64,128]{2,1,0:T(8,128)S(1)}, u32[]{:S(2)}, u32[]{:S(2)}) collective-permute-start(f32[3,64,128]{2,1,0:T(8,128)S(1)} %get-tuple-element.48), channel_id=1, source_target_pairs={{0,1},{1,2},{2,3},{3,4},{4,5},{5,6},{6,7},{7,8},{8,9},{9,10},{10,1... | collective-permute-start | bytes 294920 | tf_op jit(solution)/shard_map/ppermute | solution.py:524
  150.4 5.4 %collective-permute-start.11 = (f32[3,64,128]{2,1,0:T(8,128)S(1)}, f32[3,64,128]{2,1,0:T(8,128)S(1)}, u32[]{:S(2)}, u32[]{:S(2)}) collective-permute-start(f32[3,64,128]{2,1,0:T(8,128)S(1)} %get-tuple-element.49), channel_id=1, source_target_pairs={{1,0},{2,1},{3,2},{4,3},{5,4},{6,5},{7,6},{8,7},{9,8},{10,9},{11,1... | collective-permute-start | bytes 294920 | tf_op jit(solution)/shard_map/ppermute | solution.py:524

commit v5 on v4

--- a/solution.py
+++ b/solution.py
@@ -13,12 +13,11 @@
 HALF = 64
 MODES = 2
 COUNT = 8
-GROUP = 8
 ROW = ("yl", "x", "c")
 COL = ("yh", "zh", "zl")
 ALL = ROW + COL
 SCATTER = ROW + ("zl",)
-REST = ("yh", "zh")
+REST = ("zh", "yh")
 MARK = 1024
 LIST_STEP = 4
 LIST_SIZE = 9 * COUNT + 8
@@ -135,21 +134,32 @@
             store(c, 1, rows, jnp.where(low, mine, right))
 
 
-def send_kernel(offsets, own, to_below, to_above):
+def send_kernel(offsets, own, tile, to_below, to_above, sems):
+    strip = pl.ds(0, HALF)
+    copies = [
+        pltpu.make_async_copy(source, target, sems.at[k])
+        for k, (source, target) in enumerate((
+            (own.at[:, pl.ds(HALF, HALF)], to_below.at[:, strip]),
+            (own.at[:, strip], to_above.at[:, strip]),
+            (own, tile),
+        ))
+    ]
+    for copy in copies:
+        copy.start()
     line = lax.broadcasted_iota(jnp.int32, (TILES, SIZE), 0)
     lane = lax.broadcasted_iota(jnp.int32, (TILES, SIZE), 1)
     code = jnp.zeros((TILES, SIZE), jnp.int32)
-    batches, count, _ = offsets.shape
+    batches, _, count = offsets.shape
     for b in range(batches):
         for k in range(count):
             for d in range(2):
-                code = jnp.where(lane == (b * count + k) * 2 + d, offsets[b, k, d] + MARK, code)
+                code = jnp.where(lane == (b * 2 + d) * count + k, offsets[b, d, k] + MARK, code)
     code = jnp.where(line == 0, code, 0).astype(F32)
     for c in range(2):
-        to_below[c, :HALF] = own[c, HALF:]
-        to_above[c, :HALF] = own[c, :HALF]
         to_below[c, HALF:] = code
         to_above[c, HALF:] = code
+    for copy in copies:
+        copy.wait()
 
 
 def pack_kernel(above, own, below, mine, to_left, to_right, codes):
@@ -171,68 +181,89 @@
     return sum(probe[c, m] * probe[c, m] for c in range(2) for m in range(MODES))
 
 
-def sweep(batch, offsets, padded, probe, measured, right3, left3, sums, accum):
+class Staged:
+    def __init__(self, batch, measured, right3, left3, places, sems):
+        sources = (right3, left3, measured.at[0, 0, batch])
+        self.places = places
+        self.copies = [pltpu.make_async_copy(a, b, sems.at[k]) for k, (a, b) in enumerate(zip(sources, places))]
+        for copy in self.copies:
+            copy.start()
+
+    def take(self, k):
+        self.copies[k].wait()
+        return self.places[k]
+
+
+def staging():
+    return [
+        pltpu.VMEM((6 * SIZE, 2 * SIZE), BF16),
+        pltpu.VMEM((2 * SIZE, 6 * SIZE), BF16),
+        pltpu.VMEM((COUNT, SIZE, SIZE), F32),
+        pltpu.SemaphoreType.DMA((3,)),
+    ]
+
+
+def sweep(batch, offsets, padded, probe, staged, sums, accum):
     accum[...] = jnp.zeros_like(accum)
-    sums[...] = jnp.zeros_like(sums)
+    wins = []
+    fields = []
+    for j in range(COUNT):
+        row, col = offsets[batch, 0, j] + HALF, offsets[batch, 1, j] + HALF
+        wr = window(padded, (0,), row, col)
+        wi = window(padded, (1,), row, col)
+        wins.append((row, col, wr, wi))
+        for m in range(MODES):
+            pr, pi = probe[0, m], probe[1, m]
+            fields.append((pr * wr - pi * wi, pr * wi + pi * wr))
+    tr = staged.take(0)[...]
+    waves = right_transform(fields, tr)
+    tl = staged.take(1)[...]
+    waves = left_transform(waves, tl)
+    measured = staged.take(2)
+    back = []
+    for j in range(COUNT):
+        own = waves[j * MODES : (j + 1) * MODES]
+        intensity = sum(r * r + i * i for r, i in own)
+        ratio = jnp.sqrt(measured[j]) / jnp.maximum(jnp.sqrt(intensity), 0.5) - 1.0
+        back += [(r * ratio, -(i * ratio)) for r, i in own]
+    chis = right_transform(left_transform(back, tl), tr)
     light = power_of(probe) if accum.shape[0] == 3 else None
-    tr = right3[...]
-    tl = left3[...]
-
-    def body(step, carry):
-        wins = []
-        fields = []
-        for g in range(GROUP):
-            j = step * GROUP + g
-            row, col = offsets[batch, j, 0] + HALF, offsets[batch, j, 1] + HALF
-            wr = window(padded, (0,), row, col)
-            wi = window(padded, (1,), row, col)
-            wins.append((row, col, wr, wi))
-            for m in range(MODES):
-                pr, pi = probe[0, m], probe[1, m]
-                fields.append((pr * wr - pi * wi, pr * wi + pi * wr))
-        waves = left_transform(right_transform(fields, tr), tl)
-        back = []
-        for g in range(GROUP):
-            own = waves[g * MODES : (g + 1) * MODES]
-            intensity = sum(r * r + i * i for r, i in own)
-            recorded = measured[0, 0, batch, step * GROUP + g]
-            ratio = jnp.sqrt(recorded) / jnp.maximum(jnp.sqrt(intensity), 0.5) - 1.0
-            back += [(r * ratio, -(i * ratio)) for r, i in own]
-        chis = right_transform(left_transform(back, tl), tr)
-        for g in range(GROUP):
-            row, col, wr, wi = wins[g]
-            cr = jnp.zeros((SIZE, SIZE), F32)
-            ci = jnp.zeros((SIZE, SIZE), F32)
-            for m in range(MODES):
-                xr, xn = chis[g * MODES + m]
-                pr, pi = probe[0, m], probe[1, m]
-                cr += pr * xr - pi * xn
-                ci -= pr * xn + pi * xr
-                sums[m] += wr * xr - wi * xn
-                sums[MODES + m] -= wr * xn + wi * xr
-            sums[2 * MODES] += wr * wr + wi * wi
-            place(accum, 0, row, col, cr)
-            place(accum, 1, row, col, ci)
-            if light is not None:
-                place(accum, 2, row, col, light)
-        return carry
-
-    lax.fori_loop(0, COUNT // GROUP, body, 0)
+    totals = [0.0] * 5
+    for j in range(COUNT):
+        row, col, wr, wi = wins[j]
+        cr = jnp.zeros((SIZE, SIZE), F32)
+        ci = jnp.zeros((SIZE, SIZE), F32)
+        for m in range(MODES):
+            xr, xn = chis[j * MODES + m]
+            pr, pi = probe[0, m], probe[1, m]
+            cr += pr * xr - pi * xn
+            ci -= pr * xn + pi * xr
+            totals[m] = totals[m] + (wr * xr - wi * xn)
+            totals[MODES + m] = totals[MODES + m] - (wr * xn + wi * xr)
+        totals[2 * MODES] = totals[2 * MODES] + (wr * wr + wi * wi)
+        place(accum, 0, row, col, cr)
+        place(accum, 1, row, col, ci)
+        if light is not None:
+            place(accum, 2, row, col, light)
+    for k in range(5):
+        sums[k] = totals[k]
 
 
 def first_kernel(offsets, above, own, below, from_left, from_right, probe, measured, right3, left3,
-                 top, bottom, sums, padded, accum):
+                 top, bottom, sums, padded, accum, *stage):
+    staged = Staged(0, measured, right3, left3, stage[:3], stage[3])
+
     def store(c, h, rows, value):
         padded[c, h, rows] = value
 
     pad_field(above, own, below, from_left, from_right, store)
-    sweep(0, offsets, padded, probe, measured, right3, left3, sums, accum)
+    sweep(0, offsets, padded, probe, staged, sums, accum)
     top[...] = accum[:, :, :SIZE]
     bottom[...] = accum[:, :, SIZE:]
 
 
 def offset_of(others, batch, across, down, j, d):
-    return others[TILES * across + (1, 0, 2)[down], (batch * COUNT + j) * 2 + d] - MARK
+    return others[TILES * across + (1, 0, 2)[down], (batch * 2 + d) * COUNT + j] - MARK
 
 
 def cover_kernel(others, probe, cover, near, light):
@@ -327,7 +358,7 @@
             b1 += jnp.sum(power * (light + 1.0), axis=0, keepdims=True)
     overlap = [jnp.zeros((SIZE, SIZE), F32)] * 2
     for j in range(COUNT):
-        row, col = offsets[0, j, 0] + HALF, offsets[0, j, 1] + HALF
+        row, col = offsets[0, 0, j] + HALF, offsets[0, 1, j] + HALF
         overlap = [overlap[c] + window(product, (c,), row, col) for c in range(2)]
     pack_sums(packed, sums, overlap, a11, b1)
 
@@ -475,10 +506,11 @@
 
 
 def next_kernel(offsets, totals, padded, direction, probe, measured, right3, left3,
-                top, middle, bottom, sums, new_padded, new_probe, accum):
+                top, middle, bottom, sums, new_padded, new_probe, accum, *stage):
+    staged = Staged(1, measured, right3, left3, stage[:3], stage[3])
     step = step_sizes(totals, probe, new_probe)
     new_padded[...] = padded[...] + step * direction[...]
-    sweep(1, offsets, new_padded, new_probe, measured, right3, left3, sums, accum)
+    sweep(1, offsets, new_padded, new_probe, staged, sums, accum)
     top[...] = accum[:, :, :HALF]
     middle[...] = accum[:, :, HALF : HALF + SIZE]
     bottom[...] = accum[:, :, HALF + SIZE :]
@@ -497,10 +529,12 @@
     return jax.ShapeDtypeStruct(dims, F32)
 
 
-def call(kernel, ins, outs, scratch=()):
+def call(kernel, ins, outs, scratch=(), in_hbm=()):
     vmem = pl.BlockSpec(memory_space=pltpu.VMEM)
     smem = pl.BlockSpec(memory_space=pltpu.SMEM)
-    specs = [smem if x.dtype == jnp.int32 else vmem for x in ins]
+    hbm = pl.BlockSpec(memory_space=pltpu.HBM)
+    ins = [pltpu.with_memory_space_constraint(x, pltpu.HBM) if k in in_hbm else x for k, x in enumerate(ins)]
+    specs = [hbm if k in in_hbm else smem if x.dtype == jnp.int32 else vmem for k, x in enumerate(ins)]
     return pl.pallas_call(
         kernel,
         in_specs=specs,
@@ -543,7 +577,7 @@
 
 def per_device(obj, probe, measured, offsets):
     right3, left3 = (jnp.asarray(t) for t in dft_tables())
-    offsets = offsets[0, 0]
+    offsets = jnp.swapaxes(offsets[0, 0], 1, 2)
     r, c, half = (lax.axis_index(axes).astype(jnp.int32) for axes in (ROW, COL, ("zl",)))
     whole = 2 * SIZE
     place_in_group = jnp.stack([r, half])
@@ -556,11 +590,13 @@
 
     strip = shape(2, HALF + TILES, SIZE)
     side = shape(2, SIZE + TILES, SIZE)
-    to_below, to_above = call(send_kernel, [offsets, obj], [strip, strip])
+    tile, to_below, to_above = call(
+        send_kernel, [offsets, obj], [shape(2, SIZE, SIZE), strip, strip],
+        [pltpu.SemaphoreType.DMA((3,))], in_hbm=(1,))
     above = shift(to_below, 1, 0)
     below = shift(to_above, -1, 0)
     to_left, to_right, codes = call(
-        pack_kernel, [above, obj, below, to_below], [side, side, shape(TILES, SIZE)])
+        pack_kernel, [above, tile, below, to_below], [side, side, shape(TILES, SIZE)])
     from_left = shift(to_right, 0, 1)
     from_right = shift(to_left, 0, -1)
     others = jnp.concatenate([from_left[0, SIZE:], codes, from_right[0, SIZE:]], axis=0).astype(jnp.int32)
@@ -574,9 +610,10 @@
 
     top, bottom, sums, padded = call(
         first_kernel,
-        [offsets, above, obj, below, from_left, from_right, probe, measured, right3, left3],
+        [offsets, above, tile, below, from_left, from_right, probe, measured, right3, left3],
         [quads, quads, sums_shape, field],
-        [pltpu.VMEM((2, 2, whole, SIZE), F32)],
+        [pltpu.VMEM((2, 2, whole, SIZE), F32)] + staging(),
+        in_hbm=(7, 8, 9),
     )
     from_above = shift(bottom, 1, 0)
     from_below = shift(top, -1, 0)
@@ -599,18 +636,19 @@
         next_kernel,
         [offsets, totals, padded, direction, probe, measured, right3, left3],
         [edge, shape(3, 2, SIZE, SIZE), edge, sums_shape, field, planes],
-        [pltpu.VMEM((3, 2, whole, SIZE), F32)],
+        [pltpu.VMEM((3, 2, whole, SIZE), F32)] + staging(),
+        in_hbm=(5, 6, 7),
     )
     from_above = shift(bottom, 1, 0)
     from_below = shift(top, -1, 0)
     side = shape(3, HALF, SIZE)
-    tile, left, right = call(
+    middle, left, right = call(
         fold_kernel, [middle, from_above, from_below], [shape(3, SIZE, SIZE), side, side])
     from_left = shift(right, 0, 1)
     from_right = shift(left, 0, -1)
     packed, direction = call(
         merge_kernel,
-        [near, tile, from_left, from_right, padded, sums],
+        [near, middle, from_left, from_right, padded, sums],
         [packed_shape, shape(2, SIZE, SIZE)],
         [pltpu.VMEM((2, 3 * SIZE, SIZE), F32), pltpu.VMEM((2, SIZE, SIZE), F32)],
     )

time: 217 us -> 215 us (level)
  local copies, waits for them, and re-layouts: 5.82 us -> 0.69 us
  Pallas kernels: 25.9 us -> 29.5 us
    unnamed x20 -> x6, local copies, waits for them, and re-layouts: 5.05 us -> 0.69 us
    pallas_call x14, Pallas kernels: 25.9 us -> 29.5 us  [call(): pl.pallas_call(kernel, in_specs=specs, out_specs=[smem if x.dtype == jnp....]
where the time goes in v5:
time: 215 us; the launch traced here: 214 us
  blocking collectives  95.3 us (44%)
  starting transfers between devices  56.1 us (26%)
  waiting for transfers between devices  31.9 us (15%)
  Pallas kernels  29.5 us (14%)
    all_to_all x5, blocking collectives, exchange(): return lax.all_to_all(block, axes, 0, 0, tiled=True)  95.3 us
    ppermute x12, starting transfers between devices, shift(): return lax.ppermute(block, ALL, route)  33.5 us
    pallas_call x14, Pallas kernels, call(): pl.pallas_call(kernel, in_specs=specs, out_specs=[smem if x.dtype == jnp....  29.5 us
    all_to_all x1, starting transfers between devices, exchange(): return lax.all_to_all(block, axes, 0, 0, tiled=True)  22.6 us
    ppermute x12, waiting for transfers between devices, shift(): return lax.ppermute(block, ALL, route)  19.6 us
    all_to_all x1, waiting for transfers between devices, exchange(): return lax.all_to_all(block, axes, 0, 0, tiled=True)  12.3 us
  transfers between devices with their start and end apart: 13, of which 10 were waited for; matrix products, arithmetic and copies ran while one was open for 0% of the time, Pallas kernels for 2%

profile of v5, /device:TPU:1, one launch (start us, length us, event | category | flops | bytes accessed | tf_op | source)
XLA Modules:
  0.0 214.5 jit_solution(950416749321367234)
XLA Ops:
  1.3 1.6 send_kernel.1
  2.9 8.8 %collective-permute-start.1 = (f32[2,72,128]{2,1,0:T(8,128)S(1)}, f32[2,72,128]{2,1,0:T(8,128)S(1)}, u32[]{:S(2)}, u32[]{:S(2)}) collective-permute-start(f32[2,72,128]{2,1,0:T(8,128)S(1)} %get-tuple-element.32), channel_id=1, source_target_pairs={{32,0},{33,1},{34,2},{35,3},{36,4},{37,5},{38,6},{39,7},{40,8},{41... | collective-permute-start | bytes 221192 | tf_op jit(solution)/shard_map/ppermute | solution.py:558
  11.7 1.9 collective-permute-start
  13.6 1.4 collective-permute-done.above
  15.2 1.3 collective-permute-start.2
  16.5 1.3 collective-permute-start.3
  17.8 1.9 collective-permute-done.2.from_left
  19.7 3.9 %collective-permute-done.3.from_right = f32[2,136,128]{2,1,0:T(8,128)S(1)} collective-permute-done((f32[2,136,128]{2,1,0:T(8,128)S(1)}, f32[2,136,128]{2,1,0:T(8,128)S(1)}, u32[]{:S(2)}, u32[]{:S(2)}) %collective-permute-start.3) | collective-permute-done | bytes 139296 | tf_op jit(solution)/shard_map/ppermute | solution.py:558
  23.7 8.4 %first_kernel.1 = (f32[2,2,128,128]{3,2,1,0:T(8,128)S(1)}, f32[2,2,128,128]{3,2,1,0:T(8,128)S(1)}, f32[5,128,128]{2,1,0:T(8,128)S(1)}, f32[2,2,256,128]{3,2,1,0:T(8,128)S(1)}) custom-call(s32[2,2,8]{2,1,0:T(2,128)S(1)} %bitcast.22, f32[2,72,128]{2,1,0:T(8,128)S(1)} %collective-permute-done.above, f32[2,128,128]{2,1,0:T(8,128)S(1)} %get-tuple-element.31.own, ...), custom_call_target="tpu_custom_call" | custom-call | tf_op jit(solution)/shard_map/first_kernel/pallas_call | solution.py:538
  32.0 2.7 %collective-permute-start.5 = (f32[2,2,128,128]{3,2,1,0:T(8,128)S(1)}, f32[2,2,128,128]{3,2,1,0:T(8,128)S(1)}, u32[]{:S(2)}, u32[]{:S(2)}) collective-permute-start(f32[2,2,128,128]{3,2,1,0:T(8,128)S(1)} %get-tuple-element.37.top), channel_id=1, source_target_pairs={{32,0},{33,1},{34,2},{35,3},{36,4},{37,5},{38,6},{39,7},{40,8},{41... | collective-permute-start | bytes 786440 | tf_op jit(solution)/shard_map/ppermute | solution.py:558
  34.7 3.3 %collective-permute-start.4 = (f32[2,2,128,128]{3,2,1,0:T(8,128)S(1)}, f32[2,2,128,128]{3,2,1,0:T(8,128)S(1)}, u32[]{:S(2)}, u32[]{:S(2)}) collective-permute-start(f32[2,2,128,128]{3,2,1,0:T(8,128)S(1)} %get-tuple-element.38.bottom), channel_id=1, source_target_pairs={{0,32},{1,33},{2,34},{3,35},{4,36},{5,37},{6,38},{7,39},{8,40},{9,... | collective-permute-start | bytes 786440 | tf_op jit(solution)/shard_map/ppermute | solution.py:558
  38.1 2.0 collective-permute-done.5.from_below
  40.1 1.2 collective-permute-done.4.from_above
  41.4 1.3 collective-permute-start.7
  42.6 4.0 %collective-permute-start.6 = (f32[2,2,128,128]{3,2,1,0:T(8,128)S(1)}, f32[2,2,128,128]{3,2,1,0:T(8,128)S(1)}, u32[]{:S(2)}, u32[]{:S(2)}) collective-permute-start(f32[2,2,128,128]{3,2,1,0:T(8,128)S(1)} %get-tuple-element.40.right), channel_id=1, source_target_pairs={{0,1},{1,2},{2,3},{3,4},{4,5},{5,6},{6,7},{7,8},{8,9},{9,10},{10,1... | collective-permute-start | bytes 786440 | tf_op jit(solution)/shard_map/ppermute | solution.py:558
  46.7 4.0 %cover_kernel.1 = (f32[2,256,128]{2,1,0:T(8,128)S(1)}, s32[80,2]{1,0:T(8,128)S(1)}) custom-call(s32[24,128]{1,0:T(8,128)S(1)} %maximum_convert_fusion.others, f32[2,2,128,128]{3,2,1,0:T(8,128)S(1)} %copy-done), custom_call_target="tpu_custom_call" | custom-call | tf_op jit(solution)/shard_map/cover_kernel/pallas_call | solution.py:538
  50.7 1.2 wide_merge_kernel.1
  52.0 23.9 %all_to_all.30.parts = f32[32,4,8,128]{3,2,1,0:T(8,128)S(1)} all-to-all(f32[32,4,8,128]{3,2,1,0:T(8,128)S(1)} %bitcast.19), channel_id=1, replica_groups=mesh['yl'=2,'x'=4,'c'=2,'yh'=4,'zh'=4,'zl'=2] {'yl','x','c','zl'}, dimensions={0} | all-to-all | bytes 1048576 | tf_op jit(solution)/shard_map/all_to_all | solution.py:562
  76.7 22.6 %all-to-all-start.1 = ((f32[16,4,8,128]{3,2,1,0:T(8,128)}), f32[16,4,8,128]{3,2,1,0:T(8,128)S(1)}, u32[]{:S(2)}, u32[]{:S(2)}) async-start(f32[16,4,8,128]{3,2,1,0:T(8,128)} %reduce_kernel.2), calls=%async_computation.1 | async-start | bytes 524288 | tf_op jit(solution)/shard_map/all_to_all | solution.py:562
  99.4 12.3 %all-to-all-done.1.parts = f32[16,4,8,128]{3,2,1,0:T(8,128)S(1)} async-done(((f32[16,4,8,128]{3,2,1,0:T(8,128)}), f32[16,4,8,128]{3,2,1,0:T(8,128)S(1)}, u32[]{:S(2)}, u32[]{:S(2)}) %all-to-all-start.1) | async-done | bytes 262176 | tf_op jit(solution)/shard_map/all_to_all | solution.py:562
  112.3 15.5 %all_to_all.31 = f32[32,3,8,128]{3,2,1,0:T(8,128)S(1)} all-to-all(f32[32,3,8,128]{3,2,1,0:T(8,128)S(1)} %strip_kernel.2), channel_id=1, replica_groups=mesh['yl'=2,'x'=4,'c'=2,'yh'=4,'zh'=4,'zl'=2] {'yl','x','c','zl'}, dimensions={0} | all-to-all | bytes 786432 | tf_op jit(solution)/shard_map/all_to_all | solution.py:562
  127.8 8.5 %next_kernel.1 = (f32[3,2,64,128]{3,2,1,0:T(8,128)S(1)}, f32[3,2,128,128]{3,2,1,0:T(8,128)S(1)}, f32[3,2,64,128]{3,2,1,0:T(8,128)S(1)}, f32[5,128,128]{2,1,0:T(8...) custom-call(s32[2,2,8]{2,1,0:T(2,128)S(1)} %bitcast.24, f32[16,2,3,8,128]{4,3,2,1,0:T(8,128)S(1)} %bitcast.17, ...), custom_call_target="tpu_custom_call" | custom-call | tf_op jit(solution)/shard_map/next_kernel/pallas_call | solution.py:538
  136.3 2.7 %collective-permute-start.8 = (f32[3,2,64,128]{3,2,1,0:T(8,128)S(1)}, f32[3,2,64,128]{3,2,1,0:T(8,128)S(1)}, u32[]{:S(2)}, u32[]{:S(2)}) collective-permute-start(f32[3,2,64,128]{3,2,1,0:T(8,128)S(1)} %get-tuple-element.47), channel_id=1, source_target_pairs={{0,32},{1,33},{2,34},{3,35},{4,36},{5,37},{6,38},{7,39},{8,40},{9,... | collective-permute-start | bytes 589832 | tf_op jit(solution)/shard_map/ppermute | solution.py:558
  139.0 1.9 collective-permute-start.9
  141.6 4.4 %collective-permute-done.9.from_below = f32[3,2,64,128]{3,2,1,0:T(8,128)S(1)} collective-permute-done((f32[3,2,64,128]{3,2,1,0:T(8,128)S(1)}, f32[3,2,64,128]{3,2,1,0:T(8,128)S(1)}, u32[]{:S(2)}, u32[]{:S(2)}) %collective-permute-start.9) | collective-permute-done | bytes 196640 | tf_op jit(solution)/shard_map/ppermute | solution.py:558
  146.2 3.0 %collective-permute-start.10 = (f32[3,64,128]{2,1,0:T(8,128)S(1)}, f32[3,64,128]{2,1,0:T(8,128)S(1)}, u32[]{:S(2)}, u32[]{:S(2)}) collective-permute-start(f32[3,64,128]{2,1,0:T(8,128)S(1)} %get-tuple-element.50), channel_id=1, source_target_pairs={{0,1},{1,2},{2,3},{3,4},{4,5},{5,6},{6,7},{7,8},{8,9},{9,10},{10,1... | collective-permute-start | bytes 294920 | tf_op jit(solution)/shard_map/ppermute | solution.py:558
  149.2 1.3 collective-permute-start.11
  150.8 3.7 %collective-permute-done.11.from_right = f32[3,64,128]{2,1,0:T(8,128)S(1)} collective-permute-done((f32[3,64,128]{2,1,0:T(8,128)S(1)}, f32[3,64,128]{2,1,0:T(8,128)S(1)}, u32[]{:S(2)}, u32[]{:S(2)}) %collective-permute-start.11) | collective-permute-done | bytes 98336 | tf_op jit(solution)/shard_map/ppermute | solution.py:558
  154.6 2.3 %merge_kernel.1 = (f32[16,2,4,8,128]{4,3,2,1,0:T(8,128)S(1)}, f32[2,128,128]{2,1,0:T(8,128)S(1)}) custom-call(s32[80,2]{1,0:T(8,128)S(1)} %get-tuple-element.36.near, f32[3,128,128]{2,1,0:T(8,128)S(1)} %get-tuple-element.49.tile, f32[3,64,128]{2,1,0:T(8,128)S(1)} %collective-permute-done.10.from_left, f32[3,64,128]{2,1,0:T(8,128)S(1)} %collective-permute-done.11.from_right, ...), custom_call_target="tpu_custom_call" | custom-call | tf_op jit(solution)/shard_map/merge_kernel/pallas_call | solution.py:538
  156.9 17.2 %all_to_all.32.parts = f32[32,4,8,128]{3,2,1,0:T(8,128)S(1)} all-to-all(f32[32,4,8,128]{3,2,1,0:T(8,128)S(1)} %bitcast.20), channel_id=1, replica_groups=mesh['yl'=2,'x'=4,'c'=2,'yh'=4,'zh'=4,'zl'=2] {'yl','x','c','zl'}, dimensions={0} | all-to-all | bytes 1048576 | tf_op jit(solution)/shard_map/all_to_all | solution.py:562
  174.1 23.2 %all_to_all.33.parts = f32[16,4,8,128]{3,2,1,0:T(8,128)S(1)} all-to-all(f32[16,4,8,128]{3,2,1,0:T(8,128)S(1)} %reduce_kernel.3), channel_id=1, replica_groups=mesh['yl'=2,'x'=4,'c'=2,'yh'=4,'zh'=4,'zl'=2] {'zh','yh'}, dimensions={0} | all-to-all | bytes 524288 | tf_op jit(solution)/shard_map/all_to_all | solution.py:562
  198.0 15.5 %all_to_all.34 = f32[32,3,8,128]{3,2,1,0:T(8,128)S(1)} all-to-all(f32[32,3,8,128]{3,2,1,0:T(8,128)S(1)} %strip_kernel.3), channel_id=1, replica_groups=mesh['yl'=2,'x'=4,'c'=2,'yh'=4,'zh'=4,'zl'=2] {'yl','x','c','zl'}, dimensions={0} | all-to-all | bytes 786432 | tf_op jit(solution)/shard_map/all_to_all | solution.py:562
  (24 shorter events, 5.3 us)
Async XLA Ops:
  0.6 0.7 copy-start.1
  1.3 22.3 %copy-start = (f32[2,2,128,128]{3,2,1,0:T(8,128)S(1)}, f32[2,2,128,128]{3,2,1,0:T(8,128)}, u32[]{:S(2)}) copy-start(f32[2,2,128,128]{3,2,1,0:T(8,128)} %probe.7) | copy-start | bytes 786436
  2.9 10.7 %collective-permute-start.1 = (f32[2,72,128]{2,1,0:T(8,128)S(1)}, f32[2,72,128]{2,1,0:T(8,128)S(1)}, u32[]{:S(2)}, u32[]{:S(2)}) collective-permute-start(f32[2,72,128]{2,1,0:T(8,128)S(1)} %get-tuple-element.32), channel_id=1, source_target_pairs={{32,0},{33,1},{34,2},{35,3},{36,4},{37,5},{38,6},{39,7},{40,8},{41... | collective-permute-start | bytes 221192 | tf_op jit(solution)/shard_map/ppermute | solution.py:558
  11.7 3.3 %collective-permute-start = (f32[2,72,128]{2,1,0:T(8,128)S(1)}, f32[2,72,128]{2,1,0:T(8,128)S(1)}, u32[]{:S(2)}, u32[]{:S(2)}) collective-permute-start(f32[2,72,128]{2,1,0:T(8,128)S(1)} %get-tuple-element.30.mine), channel_id=1, source_target_pairs={{0,32},{1,33},{2,34},{3,35},{4,36},{5,37},{6,38},{7,39},{8,40},{9,... | collective-permute-start | bytes 221192 | tf_op jit(solution)/shard_map/ppermute | solution.py:558
  15.2 4.6 %collective-permute-start.2 = (f32[2,136,128]{2,1,0:T(8,128)S(1)}, f32[2,136,128]{2,1,0:T(8,128)S(1)}, u32[]{:S(2)}, u32[]{:S(2)}) collective-permute-start(f32[2,136,128]{2,1,0:T(8,128)S(1)} %get-tuple-element.33), channel_id=1, source_target_pairs={{0,1},{1,2},{2,3},{3,4},{4,5},{5,6},{6,7},{7,8},{8,9},{9,10},{10,1... | collective-permute-start | bytes 417800 | tf_op jit(solution)/shard_map/ppermute | solution.py:558
  16.5 7.2 %collective-permute-start.3 = (f32[2,136,128]{2,1,0:T(8,128)S(1)}, f32[2,136,128]{2,1,0:T(8,128)S(1)}, u32[]{:S(2)}, u32[]{:S(2)}) collective-permute-start(f32[2,136,128]{2,1,0:T(8,128)S(1)} %get-tuple-element.35), channel_id=1, source_target_pairs={{1,0},{2,1},{3,2},{4,3},{5,4},{6,5},{7,6},{8,7},{9,8},{10,9},{11,1... | collective-permute-start | bytes 417800 | tf_op jit(solution)/shard_map/ppermute | solution.py:558
  17.8 5.9 %copy-start.2 = (s32[1,1,2,8,2]{3,4,2,1,0:T(2,128)S(1)}, s32[1,1,2,8,2]{3,4,2,1,0:T(2,128)}, u32[]{:S(2)}) copy-start(s32[1,1,2,8,2]{3,4,2,1,0:T(2,128)} %param.9) | copy-start | bytes 388
  32.0 8.1 %collective-permute-start.5 = (f32[2,2,128,128]{3,2,1,0:T(8,128)S(1)}, f32[2,2,128,128]{3,2,1,0:T(8,128)S(1)}, u32[]{:S(2)}, u32[]{:S(2)}) collective-permute-start(f32[2,2,128,128]{3,2,1,0:T(8,128)S(1)} %get-tuple-element.37.top), channel_id=1, source_target_pairs={{32,0},{33,1},{34,2},{35,3},{36,4},{37,5},{38,6},{39,7},{40,8},{41... | collective-permute-start | bytes 786440 | tf_op jit(solution)/shard_map/ppermute | solution.py:558
  34.7 6.6 %collective-permute-start.4 = (f32[2,2,128,128]{3,2,1,0:T(8,128)S(1)}, f32[2,2,128,128]{3,2,1,0:T(8,128)S(1)}, u32[]{:S(2)}, u32[]{:S(2)}) collective-permute-start(f32[2,2,128,128]{3,2,1,0:T(8,128)S(1)} %get-tuple-element.38.bottom), channel_id=1, source_target_pairs={{0,32},{1,33},{2,34},{3,35},{4,36},{5,37},{6,38},{7,39},{8,40},{9,... | collective-permute-start | bytes 786440 | tf_op jit(solution)/shard_map/ppermute | solution.py:558
  41.4 9.4 %collective-permute-start.7 = (f32[2,2,128,128]{3,2,1,0:T(8,128)S(1)}, f32[2,2,128,128]{3,2,1,0:T(8,128)S(1)}, u32[]{:S(2)}, u32[]{:S(2)}) collective-permute-start(f32[2,2,128,128]{3,2,1,0:T(8,128)S(1)} %get-tuple-element.39.left), channel_id=1, source_target_pairs={{1,0},{2,1},{3,2},{4,3},{5,4},{6,5},{7,6},{8,7},{9,8},{10,9},{11,1... | collective-permute-start | bytes 786440 | tf_op jit(solution)/shard_map/ppermute | solution.py:558
  42.6 8.1 %collective-permute-start.6 = (f32[2,2,128,128]{3,2,1,0:T(8,128)S(1)}, f32[2,2,128,128]{3,2,1,0:T(8,128)S(1)}, u32[]{:S(2)}, u32[]{:S(2)}) collective-permute-start(f32[2,2,128,128]{3,2,1,0:T(8,128)S(1)} %get-tuple-element.40.right), channel_id=1, source_target_pairs={{0,1},{1,2},{2,3},{3,4},{4,5},{5,6},{6,7},{7,8},{8,9},{9,10},{10,1... | collective-permute-start | bytes 786440 | tf_op jit(solution)/shard_map/ppermute | solution.py:558
  76.7 35.0 %all-to-all-start.1 = ((f32[16,4,8,128]{3,2,1,0:T(8,128)}), f32[16,4,8,128]{3,2,1,0:T(8,128)S(1)}, u32[]{:S(2)}, u32[]{:S(2)}) async-start(f32[16,4,8,128]{3,2,1,0:T(8,128)} %reduce_kernel.2), calls=%async_computation.1 | async-start | bytes 524288 | tf_op jit(solution)/shard_map/all_to_all | solution.py:562
  136.3 5.3 %collective-permute-start.8 = (f32[3,2,64,128]{3,2,1,0:T(8,128)S(1)}, f32[3,2,64,128]{3,2,1,0:T(8,128)S(1)}, u32[]{:S(2)}, u32[]{:S(2)}) collective-permute-start(f32[3,2,64,128]{3,2,1,0:T(8,128)S(1)} %get-tuple-element.47), channel_id=1, source_target_pairs={{0,32},{1,33},{2,34},{3,35},{4,36},{5,37},{6,38},{7,39},{8,40},{9,... | collective-permute-start | bytes 589832 | tf_op jit(solution)/shard_map/ppermute | solution.py:558
  139.0 7.0 %collective-permute-start.9 = (f32[3,2,64,128]{3,2,1,0:T(8,128)S(1)}, f32[3,2,64,128]{3,2,1,0:T(8,128)S(1)}, u32[]{:S(2)}, u32[]{:S(2)}) collective-permute-start(f32[3,2,64,128]{3,2,1,0:T(8,128)S(1)} %get-tuple-element.48), channel_id=1, source_target_pairs={{32,0},{33,1},{34,2},{35,3},{36,4},{37,5},{38,6},{39,7},{40,8},{41... | collective-permute-start | bytes 589832 | tf_op jit(solution)/shard_map/ppermute | solution.py:558
  146.2 4.6 %collective-permute-start.10 = (f32[3,64,128]{2,1,0:T(8,128)S(1)}, f32[3,64,128]{2,1,0:T(8,128)S(1)}, u32[]{:S(2)}, u32[]{:S(2)}) collective-permute-start(f32[3,64,128]{2,1,0:T(8,128)S(1)} %get-tuple-element.50), channel_id=1, source_target_pairs={{0,1},{1,2},{2,3},{3,4},{4,5},{5,6},{6,7},{7,8},{8,9},{9,10},{10,1... | collective-permute-start | bytes 294920 | tf_op jit(solution)/shard_map/ppermute | solution.py:558
  149.2 5.4 %collective-permute-start.11 = (f32[3,64,128]{2,1,0:T(8,128)S(1)}, f32[3,64,128]{2,1,0:T(8,128)S(1)}, u32[]{:S(2)}, u32[]{:S(2)}) collective-permute-start(f32[3,64,128]{2,1,0:T(8,128)S(1)} %get-tuple-element.51), channel_id=1, source_target_pairs={{1,0},{2,1},{3,2},{4,3},{5,4},{6,5},{7,6},{8,7},{9,8},{10,9},{11,1... | collective-permute-start | bytes 294920 | tf_op jit(solution)/shard_map/ppermute | solution.py:558

commit v6 on v5

--- a/solution.py
+++ b/solution.py
@@ -181,52 +181,39 @@
     return sum(probe[c, m] * probe[c, m] for c in range(2) for m in range(MODES))
 
 
-class Staged:
-    def __init__(self, batch, measured, right3, left3, places, sems):
-        sources = (right3, left3, measured.at[0, 0, batch])
-        self.places = places
-        self.copies = [pltpu.make_async_copy(a, b, sems.at[k]) for k, (a, b) in enumerate(zip(sources, places))]
-        for copy in self.copies:
-            copy.start()
-
-    def take(self, k):
-        self.copies[k].wait()
-        return self.places[k]
-
-
-def staging():
-    return [
-        pltpu.VMEM((6 * SIZE, 2 * SIZE), BF16),
-        pltpu.VMEM((2 * SIZE, 6 * SIZE), BF16),
-        pltpu.VMEM((COUNT, SIZE, SIZE), F32),
-        pltpu.SemaphoreType.DMA((3,)),
-    ]
-
-
-def sweep(batch, offsets, padded, probe, staged, sums, accum):
+def stage_kernel(codes, *refs):
+    count = (len(refs) - 1) // 2
+    sems = refs[-1]
+    copies = [pltpu.make_async_copy(refs[k], refs[count + k], sems.at[k]) for k in range(count)]
+    for copy in copies:
+        copy.start()
+    for copy in copies:
+        copy.wait()
+
+
+def sweep(batch, offsets, padded, probe, measured, right3, left3, sums, accum):
     accum[...] = jnp.zeros_like(accum)
+    tr = right3[...]
+    tl = left3[...]
     wins = []
-    fields = []
+    waves = []
     for j in range(COUNT):
         row, col = offsets[batch, 0, j] + HALF, offsets[batch, 1, j] + HALF
         wr = window(padded, (0,), row, col)
         wi = window(padded, (1,), row, col)
         wins.append((row, col, wr, wi))
+        fields = []
         for m in range(MODES):
             pr, pi = probe[0, m], probe[1, m]
             fields.append((pr * wr - pi * wi, pr * wi + pi * wr))
-    tr = staged.take(0)[...]
-    waves = right_transform(fields, tr)
-    tl = staged.take(1)[...]
-    waves = left_transform(waves, tl)
-    measured = staged.take(2)
-    back = []
+        waves.append(right_transform(fields, tr))
+    waves = [left_transform(fields, tl) for fields in waves]
+    chis = []
     for j in range(COUNT):
-        own = waves[j * MODES : (j + 1) * MODES]
-        intensity = sum(r * r + i * i for r, i in own)
-        ratio = jnp.sqrt(measured[j]) / jnp.maximum(jnp.sqrt(intensity), 0.5) - 1.0
-        back += [(r * ratio, -(i * ratio)) for r, i in own]
-    chis = right_transform(left_transform(back, tl), tr)
+        intensity = sum(r * r + i * i for r, i in waves[j])
+        ratio = jnp.sqrt(measured[0, 0, batch, j]) / jnp.maximum(jnp.sqrt(intensity), 0.5) - 1.0
+        chis.append(left_transform([(r * ratio, -(i * ratio)) for r, i in waves[j]], tl))
+    chis = [right_transform(fields, tr) for fields in chis]
     light = power_of(probe) if accum.shape[0] == 3 else None
     totals = [0.0] * 5
     for j in range(COUNT):
@@ -234,7 +221,7 @@
         cr = jnp.zeros((SIZE, SIZE), F32)
         ci = jnp.zeros((SIZE, SIZE), F32)
         for m in range(MODES):
-            xr, xn = chis[j * MODES + m]
+            xr, xn = chis[j][m]
             pr, pi = probe[0, m], probe[1, m]
             cr += pr * xr - pi * xn
             ci -= pr * xn + pi * xr
@@ -250,14 +237,12 @@
 
 
 def first_kernel(offsets, above, own, below, from_left, from_right, probe, measured, right3, left3,
-                 top, bottom, sums, padded, accum, *stage):
-    staged = Staged(0, measured, right3, left3, stage[:3], stage[3])
-
+                 top, bottom, sums, padded, accum):
     def store(c, h, rows, value):
         padded[c, h, rows] = value
 
     pad_field(above, own, below, from_left, from_right, store)
-    sweep(0, offsets, padded, probe, staged, sums, accum)
+    sweep(0, offsets, padded, probe, measured, right3, left3, sums, accum)
     top[...] = accum[:, :, :SIZE]
     bottom[...] = accum[:, :, SIZE:]
 
@@ -506,11 +491,10 @@
 
 
 def next_kernel(offsets, totals, padded, direction, probe, measured, right3, left3,
-                top, middle, bottom, sums, new_padded, new_probe, accum, *stage):
-    staged = Staged(1, measured, right3, left3, stage[:3], stage[3])
+                top, middle, bottom, sums, new_padded, new_probe, accum):
     step = step_sizes(totals, probe, new_probe)
     new_padded[...] = padded[...] + step * direction[...]
-    sweep(1, offsets, new_padded, new_probe, staged, sums, accum)
+    sweep(1, offsets, new_padded, new_probe, measured, right3, left3, sums, accum)
     top[...] = accum[:, :, :HALF]
     middle[...] = accum[:, :, HALF : HALF + SIZE]
     bottom[...] = accum[:, :, HALF + SIZE :]
@@ -599,6 +583,10 @@
         pack_kernel, [above, tile, below, to_below], [side, side, shape(TILES, SIZE)])
     from_left = shift(to_right, 0, 1)
     from_right = shift(to_left, 0, -1)
+    staged = [measured, right3, left3]
+    measured, right3, left3 = call(
+        stage_kernel, [codes, *staged], [jax.ShapeDtypeStruct(x.shape, x.dtype) for x in staged],
+        [pltpu.SemaphoreType.DMA((len(staged),))], in_hbm=(1, 2, 3))
     others = jnp.concatenate([from_left[0, SIZE:], codes, from_right[0, SIZE:]], axis=0).astype(jnp.int32)
 
     field = shape(2, 2, whole, SIZE)
@@ -612,8 +600,7 @@
         first_kernel,
         [offsets, above, tile, below, from_left, from_right, probe, measured, right3, left3],
         [quads, quads, sums_shape, field],
-        [pltpu.VMEM((2, 2, whole, SIZE), F32)] + staging(),
-        in_hbm=(7, 8, 9),
+        [pltpu.VMEM((2, 2, whole, SIZE), F32)],
     )
     from_above = shift(bottom, 1, 0)
     from_below = shift(top, -1, 0)
@@ -636,8 +623,7 @@
         next_kernel,
         [offsets, totals, padded, direction, probe, measured, right3, left3],
         [edge, shape(3, 2, SIZE, SIZE), edge, sums_shape, field, planes],
-        [pltpu.VMEM((3, 2, whole, SIZE), F32)] + staging(),
-        in_hbm=(5, 6, 7),
+        [pltpu.VMEM((3, 2, whole, SIZE), F32)],
     )
     from_above = shift(bottom, 1, 0)
     from_below = shift(top, -1, 0)

time: 215 us -> 209 us (0.972)
  Pallas kernels: 29.5 us -> 25.6 us
    pallas_call x14 -> x15, Pallas kernels: 29.5 us -> 25.6 us  [call(): pl.pallas_call(kernel, in_specs=specs, out_specs=[smem if x.dtype == jnp....]
  transfers between devices with their start and end apart: 13 -> 13, of which waited for: 10 -> 10; matrix products, arithmetic and copies ran while one was open for 0% -> 0% of each run, Pallas kernels for 2% -> 3%
where the time goes in v6:
time: 209 us
  blocking collectives  93.9 us (45%)
  starting transfers between devices  56.2 us (27%)
  waiting for transfers between devices  30.4 us (15%)
  Pallas kernels  25.6 us (12%)
    all_to_all x5, blocking collectives, exchange(): return lax.all_to_all(block, axes, 0, 0, tiled=True)  93.9 us
    ppermute x12, starting transfers between devices, shift(): return lax.ppermute(block, ALL, route)  33.5 us
    pallas_call x15, Pallas kernels, call(): pl.pallas_call(kernel, in_specs=specs, out_specs=[smem if x.dtype == jnp....  25.6 us
    all_to_all x1, starting transfers between devices, exchange(): return lax.all_to_all(block, axes, 0, 0, tiled=True)  22.6 us
    ppermute x12, waiting for transfers between devices, shift(): return lax.ppermute(block, ALL, route)  18.1 us
    all_to_all x1, waiting for transfers between devices, exchange(): return lax.all_to_all(block, axes, 0, 0, tiled=True)  12.3 us
  transfers between devices with their start and end apart: 13, of which 10 were waited for; matrix products, arithmetic and copies ran while one was open for 0% of the time, Pallas kernels for 3%

profile of v6, /device:TPU:1, one launch (start us, length us, event | category | flops | bytes accessed | tf_op | source)
XLA Modules:
  0.0 208.5 jit_solution(15363643736407226413)
XLA Ops:
  1.3 1.6 send_kernel.1
  2.9 8.8 %collective-permute-start.1 = (f32[2,72,128]{2,1,0:T(8,128)S(1)}, f32[2,72,128]{2,1,0:T(8,128)S(1)}, u32[]{:S(2)}, u32[]{:S(2)}) collective-permute-start(f32[2,72,128]{2,1,0:T(8,128)S(1)} %get-tuple-element.35), channel_id=1, source_target_pairs={{32,0},{33,1},{34,2},{35,3},{36,4},{37,5},{38,6},{39,7},{40,8},{41... | collective-permute-start | bytes 221192 | tf_op jit(solution)/shard_map/ppermute | solution.py:542
  11.7 1.9 collective-permute-start
  13.6 1.4 collective-permute-done.above
  15.1 1.3 collective-permute-start.2
  16.5 1.3 collective-permute-start.3
  17.8 1.5 stage_kernel.1
  19.7 3.9 %collective-permute-done.3.from_right = f32[2,136,128]{2,1,0:T(8,128)S(1)} collective-permute-done((f32[2,136,128]{2,1,0:T(8,128)S(1)}, f32[2,136,128]{2,1,0:T(8,128)S(1)}, u32[]{:S(2)}, u32[]{:S(2)}) %collective-permute-start.3) | collective-permute-done | bytes 139296 | tf_op jit(solution)/shard_map/ppermute | solution.py:542
  24.3 5.1 %first_kernel.1 = (f32[2,2,128,128]{3,2,1,0:T(8,128)S(1)}, f32[2,2,128,128]{3,2,1,0:T(8,128)S(1)}, f32[5,128,128]{2,1,0:T(8,128)S(1)}, f32[2,2,256,128]{3,2,1,0:T(8,128)S(1)}) custom-call(s32[2,2,8]{2,1,0:T(2,128)S(1)} %bitcast.22, f32[2,72,128]{2,1,0:T(8,128)S(1)} %collective-permute-done.above, f32[2,128,128]{2,1,0:T(8,128)S(1)} %get-tuple-element.34.own, ...), custom_call_target="tpu_custom_call" | custom-call | tf_op jit(solution)/shard_map/first_kernel/pallas_call | solution.py:522
  29.5 2.7 %collective-permute-start.5 = (f32[2,2,128,128]{3,2,1,0:T(8,128)S(1)}, f32[2,2,128,128]{3,2,1,0:T(8,128)S(1)}, u32[]{:S(2)}, u32[]{:S(2)}) collective-permute-start(f32[2,2,128,128]{3,2,1,0:T(8,128)S(1)} %get-tuple-element.43.top), channel_id=1, source_target_pairs={{32,0},{33,1},{34,2},{35,3},{36,4},{37,5},{38,6},{39,7},{40,8},{41... | collective-permute-start | bytes 786440 | tf_op jit(solution)/shard_map/ppermute | solution.py:542
  32.2 3.3 %collective-permute-start.4 = (f32[2,2,128,128]{3,2,1,0:T(8,128)S(1)}, f32[2,2,128,128]{3,2,1,0:T(8,128)S(1)}, u32[]{:S(2)}, u32[]{:S(2)}) collective-permute-start(f32[2,2,128,128]{3,2,1,0:T(8,128)S(1)} %get-tuple-element.44.bottom), channel_id=1, source_target_pairs={{0,32},{1,33},{2,34},{3,35},{4,36},{5,37},{6,38},{7,39},{8,40},{9,... | collective-permute-start | bytes 786440 | tf_op jit(solution)/shard_map/ppermute | solution.py:542
  35.6 2.0 collective-permute-done.5.from_below
  37.6 1.2 collective-permute-done.4.from_above
  38.8 1.3 collective-permute-start.7
  40.1 4.0 %collective-permute-start.6 = (f32[2,2,128,128]{3,2,1,0:T(8,128)S(1)}, f32[2,2,128,128]{3,2,1,0:T(8,128)S(1)}, u32[]{:S(2)}, u32[]{:S(2)}) collective-permute-start(f32[2,2,128,128]{3,2,1,0:T(8,128)S(1)} %get-tuple-element.46.right), channel_id=1, source_target_pairs={{0,1},{1,2},{2,3},{3,4},{4,5},{5,6},{6,7},{7,8},{8,9},{9,10},{10,1... | collective-permute-start | bytes 786440 | tf_op jit(solution)/shard_map/ppermute | solution.py:542
  44.2 4.0 %cover_kernel.1 = (f32[2,256,128]{2,1,0:T(8,128)S(1)}, s32[80,2]{1,0:T(8,128)S(1)}) custom-call(s32[24,128]{1,0:T(8,128)S(1)} %maximum_convert_fusion.others, f32[2,2,128,128]{3,2,1,0:T(8,128)S(1)} %copy-done), custom_call_target="tpu_custom_call" | custom-call | tf_op jit(solution)/shard_map/cover_kernel/pallas_call | solution.py:522
  48.2 1.2 wide_merge_kernel.1
  49.5 23.9 %all_to_all.30.parts = f32[32,4,8,128]{3,2,1,0:T(8,128)S(1)} all-to-all(f32[32,4,8,128]{3,2,1,0:T(8,128)S(1)} %bitcast.19), channel_id=1, replica_groups=mesh['yl'=2,'x'=4,'c'=2,'yh'=4,'zh'=4,'zl'=2] {'yl','x','c','zl'}, dimensions={0} | all-to-all | bytes 1048576 | tf_op jit(solution)/shard_map/all_to_all | solution.py:546
  74.1 22.6 %all-to-all-start.1 = ((f32[16,4,8,128]{3,2,1,0:T(8,128)}), f32[16,4,8,128]{3,2,1,0:T(8,128)S(1)}, u32[]{:S(2)}, u32[]{:S(2)}) async-start(f32[16,4,8,128]{3,2,1,0:T(8,128)} %reduce_kernel.2), calls=%async_computation.1 | async-start | bytes 524288 | tf_op jit(solution)/shard_map/all_to_all | solution.py:546
  96.8 12.3 %all-to-all-done.1.parts = f32[16,4,8,128]{3,2,1,0:T(8,128)S(1)} async-done(((f32[16,4,8,128]{3,2,1,0:T(8,128)}), f32[16,4,8,128]{3,2,1,0:T(8,128)S(1)}, u32[]{:S(2)}, u32[]{:S(2)}) %all-to-all-start.1) | async-done | bytes 262176 | tf_op jit(solution)/shard_map/all_to_all | solution.py:546
  109.8 15.5 %all_to_all.31 = f32[32,3,8,128]{3,2,1,0:T(8,128)S(1)} all-to-all(f32[32,3,8,128]{3,2,1,0:T(8,128)S(1)} %strip_kernel.2), channel_id=1, replica_groups=mesh['yl'=2,'x'=4,'c'=2,'yh'=4,'zh'=4,'zl'=2] {'yl','x','c','zl'}, dimensions={0} | all-to-all | bytes 786432 | tf_op jit(solution)/shard_map/all_to_all | solution.py:546
  125.3 5.5 %next_kernel.1 = (f32[3,2,64,128]{3,2,1,0:T(8,128)S(1)}, f32[3,2,128,128]{3,2,1,0:T(8,128)S(1)}, f32[3,2,64,128]{3,2,1,0:T(8,128)S(1)}, f32[5,128,128]{2,1,0:T(8...) custom-call(s32[2,2,8]{2,1,0:T(2,128)S(1)} %bitcast.24, f32[16,2,3,8,128]{4,3,2,1,0:T(8,128)S(1)} %bitcast.17, ...), custom_call_target="tpu_custom_call" | custom-call | tf_op jit(solution)/shard_map/next_kernel/pallas_call | solution.py:522
  130.7 2.7 %collective-permute-start.8 = (f32[3,2,64,128]{3,2,1,0:T(8,128)S(1)}, f32[3,2,64,128]{3,2,1,0:T(8,128)S(1)}, u32[]{:S(2)}, u32[]{:S(2)}) collective-permute-start(f32[3,2,64,128]{3,2,1,0:T(8,128)S(1)} %get-tuple-element.53), channel_id=1, source_target_pairs={{0,32},{1,33},{2,34},{3,35},{4,36},{5,37},{6,38},{7,39},{8,40},{9,... | collective-permute-start | bytes 589832 | tf_op jit(solution)/shard_map/ppermute | solution.py:542
  133.5 1.9 collective-permute-start.9
  136.1 4.4 %collective-permute-done.9.from_below = f32[3,2,64,128]{3,2,1,0:T(8,128)S(1)} collective-permute-done((f32[3,2,64,128]{3,2,1,0:T(8,128)S(1)}, f32[3,2,64,128]{3,2,1,0:T(8,128)S(1)}, u32[]{:S(2)}, u32[]{:S(2)}) %collective-permute-start.9) | collective-permute-done | bytes 196640 | tf_op jit(solution)/shard_map/ppermute | solution.py:542
  140.7 3.0 %collective-permute-start.10 = (f32[3,64,128]{2,1,0:T(8,128)S(1)}, f32[3,64,128]{2,1,0:T(8,128)S(1)}, u32[]{:S(2)}, u32[]{:S(2)}) collective-permute-start(f32[3,64,128]{2,1,0:T(8,128)S(1)} %get-tuple-element.56), channel_id=1, source_target_pairs={{0,1},{1,2},{2,3},{3,4},{4,5},{5,6},{6,7},{7,8},{8,9},{9,10},{10,1... | collective-permute-start | bytes 294920 | tf_op jit(solution)/shard_map/ppermute | solution.py:542
  143.7 1.3 collective-permute-start.11
  145.3 3.7 %collective-permute-done.11.from_right = f32[3,64,128]{2,1,0:T(8,128)S(1)} collective-permute-done((f32[3,64,128]{2,1,0:T(8,128)S(1)}, f32[3,64,128]{2,1,0:T(8,128)S(1)}, u32[]{:S(2)}, u32[]{:S(2)}) %collective-permute-start.11) | collective-permute-done | bytes 98336 | tf_op jit(solution)/shard_map/ppermute | solution.py:542
  149.0 3.1 %merge_kernel.1 = (f32[16,2,4,8,128]{4,3,2,1,0:T(8,128)S(1)}, f32[2,128,128]{2,1,0:T(8,128)S(1)}) custom-call(s32[80,2]{1,0:T(8,128)S(1)} %get-tuple-element.39.near, f32[3,128,128]{2,1,0:T(8,128)S(1)} %get-tuple-element.55.tile, f32[3,64,128]{2,1,0:T(8,128)S(1)} %collective-permute-done.10.from_left, f32[3,64,128]{2,1,0:T(8,128)S(1)} %collective-permute-done.11.from_right, ...), custom_call_target="tpu_custom_call" | custom-call | tf_op jit(solution)/shard_map/merge_kernel/pallas_call | solution.py:522
  152.2 16.4 %all_to_all.32.parts = f32[32,4,8,128]{3,2,1,0:T(8,128)S(1)} all-to-all(f32[32,4,8,128]{3,2,1,0:T(8,128)S(1)} %bitcast.20), channel_id=1, replica_groups=mesh['yl'=2,'x'=4,'c'=2,'yh'=4,'zh'=4,'zl'=2] {'yl','x','c','zl'}, dimensions={0} | all-to-all | bytes 1048576 | tf_op jit(solution)/shard_map/all_to_all | solution.py:546
  168.6 22.8 %all_to_all.33.parts = f32[16,4,8,128]{3,2,1,0:T(8,128)S(1)} all-to-all(f32[16,4,8,128]{3,2,1,0:T(8,128)S(1)} %reduce_kernel.3), channel_id=1, replica_groups=mesh['yl'=2,'x'=4,'c'=2,'yh'=4,'zh'=4,'zl'=2] {'zh','yh'}, dimensions={0} | all-to-all | bytes 524288 | tf_op jit(solution)/shard_map/all_to_all | solution.py:546
  192.0 15.5 %all_to_all.34 = f32[32,3,8,128]{3,2,1,0:T(8,128)S(1)} all-to-all(f32[32,3,8,128]{3,2,1,0:T(8,128)S(1)} %strip_kernel.3), channel_id=1, replica_groups=mesh['yl'=2,'x'=4,'c'=2,'yh'=4,'zh'=4,'zl'=2] {'yl','x','c','zl'}, dimensions={0} | all-to-all | bytes 786432 | tf_op jit(solution)/shard_map/all_to_all | solution.py:546
  (25 shorter events, 6.4 us)
Async XLA Ops:
  0.6 0.7 copy-start.1
  2.9 10.7 %collective-permute-start.1 = (f32[2,72,128]{2,1,0:T(8,128)S(1)}, f32[2,72,128]{2,1,0:T(8,128)S(1)}, u32[]{:S(2)}, u32[]{:S(2)}) collective-permute-start(f32[2,72,128]{2,1,0:T(8,128)S(1)} %get-tuple-element.35), channel_id=1, source_target_pairs={{32,0},{33,1},{34,2},{35,3},{36,4},{37,5},{38,6},{39,7},{40,8},{41... | collective-permute-start | bytes 221192 | tf_op jit(solution)/shard_map/ppermute | solution.py:542
  11.7 3.3 %collective-permute-start = (f32[2,72,128]{2,1,0:T(8,128)S(1)}, f32[2,72,128]{2,1,0:T(8,128)S(1)}, u32[]{:S(2)}, u32[]{:S(2)}) collective-permute-start(f32[2,72,128]{2,1,0:T(8,128)S(1)} %get-tuple-element.33.mine), channel_id=1, source_target_pairs={{0,32},{1,33},{2,34},{3,35},{4,36},{5,37},{6,38},{7,39},{8,40},{9,... | collective-permute-start | bytes 221192 | tf_op jit(solution)/shard_map/ppermute | solution.py:542
  15.1 4.6 %collective-permute-start.2 = (f32[2,136,128]{2,1,0:T(8,128)S(1)}, f32[2,136,128]{2,1,0:T(8,128)S(1)}, u32[]{:S(2)}, u32[]{:S(2)}) collective-permute-start(f32[2,136,128]{2,1,0:T(8,128)S(1)} %get-tuple-element.36), channel_id=1, source_target_pairs={{0,1},{1,2},{2,3},{3,4},{4,5},{5,6},{6,7},{7,8},{8,9},{9,10},{10,1... | collective-permute-start | bytes 417800 | tf_op jit(solution)/shard_map/ppermute | solution.py:542
  16.5 7.2 %collective-permute-start.3 = (f32[2,136,128]{2,1,0:T(8,128)S(1)}, f32[2,136,128]{2,1,0:T(8,128)S(1)}, u32[]{:S(2)}, u32[]{:S(2)}) collective-permute-start(f32[2,136,128]{2,1,0:T(8,128)S(1)} %get-tuple-element.38), channel_id=1, source_target_pairs={{1,0},{2,1},{3,2},{4,3},{5,4},{6,5},{7,6},{8,7},{9,8},{10,9},{11,1... | collective-permute-start | bytes 417800 | tf_op jit(solution)/shard_map/ppermute | solution.py:542
  17.8 5.9 %copy-start = (f32[2,2,128,128]{3,2,1,0:T(8,128)S(1)}, f32[2,2,128,128]{3,2,1,0:T(8,128)}, u32[]{:S(2)}) copy-start(f32[2,2,128,128]{3,2,1,0:T(8,128)} %probe.7) | copy-start | bytes 786436
  23.7 0.7 copy-start.2
  29.5 8.1 %collective-permute-start.5 = (f32[2,2,128,128]{3,2,1,0:T(8,128)S(1)}, f32[2,2,128,128]{3,2,1,0:T(8,128)S(1)}, u32[]{:S(2)}, u32[]{:S(2)}) collective-permute-start(f32[2,2,128,128]{3,2,1,0:T(8,128)S(1)} %get-tuple-element.43.top), channel_id=1, source_target_pairs={{32,0},{33,1},{34,2},{35,3},{36,4},{37,5},{38,6},{39,7},{40,8},{41... | collective-permute-start | bytes 786440 | tf_op jit(solution)/shard_map/ppermute | solution.py:542
  32.2 6.6 %collective-permute-start.4 = (f32[2,2,128,128]{3,2,1,0:T(8,128)S(1)}, f32[2,2,128,128]{3,2,1,0:T(8,128)S(1)}, u32[]{:S(2)}, u32[]{:S(2)}) collective-permute-start(f32[2,2,128,128]{3,2,1,0:T(8,128)S(1)} %get-tuple-element.44.bottom), channel_id=1, source_target_pairs={{0,32},{1,33},{2,34},{3,35},{4,36},{5,37},{6,38},{7,39},{8,40},{9,... | collective-permute-start | bytes 786440 | tf_op jit(solution)/shard_map/ppermute | solution.py:542
  38.8 9.4 %collective-permute-start.7 = (f32[2,2,128,128]{3,2,1,0:T(8,128)S(1)}, f32[2,2,128,128]{3,2,1,0:T(8,128)S(1)}, u32[]{:S(2)}, u32[]{:S(2)}) collective-permute-start(f32[2,2,128,128]{3,2,1,0:T(8,128)S(1)} %get-tuple-element.45.left), channel_id=1, source_target_pairs={{1,0},{2,1},{3,2},{4,3},{5,4},{6,5},{7,6},{8,7},{9,8},{10,9},{11,1... | collective-permute-start | bytes 786440 | tf_op jit(solution)/shard_map/ppermute | solution.py:542
  40.1 8.1 %collective-permute-start.6 = (f32[2,2,128,128]{3,2,1,0:T(8,128)S(1)}, f32[2,2,128,128]{3,2,1,0:T(8,128)S(1)}, u32[]{:S(2)}, u32[]{:S(2)}) collective-permute-start(f32[2,2,128,128]{3,2,1,0:T(8,128)S(1)} %get-tuple-element.46.right), channel_id=1, source_target_pairs={{0,1},{1,2},{2,3},{3,4},{4,5},{5,6},{6,7},{7,8},{8,9},{9,10},{10,1... | collective-permute-start | bytes 786440 | tf_op jit(solution)/shard_map/ppermute | solution.py:542
  74.1 35.0 %all-to-all-start.1 = ((f32[16,4,8,128]{3,2,1,0:T(8,128)}), f32[16,4,8,128]{3,2,1,0:T(8,128)S(1)}, u32[]{:S(2)}, u32[]{:S(2)}) async-start(f32[16,4,8,128]{3,2,1,0:T(8,128)} %reduce_kernel.2), calls=%async_computation.1 | async-start | bytes 524288 | tf_op jit(solution)/shard_map/all_to_all | solution.py:546
  130.7 5.3 %collective-permute-start.8 = (f32[3,2,64,128]{3,2,1,0:T(8,128)S(1)}, f32[3,2,64,128]{3,2,1,0:T(8,128)S(1)}, u32[]{:S(2)}, u32[]{:S(2)}) collective-permute-start(f32[3,2,64,128]{3,2,1,0:T(8,128)S(1)} %get-tuple-element.53), channel_id=1, source_target_pairs={{0,32},{1,33},{2,34},{3,35},{4,36},{5,37},{6,38},{7,39},{8,40},{9,... | collective-permute-start | bytes 589832 | tf_op jit(solution)/shard_map/ppermute | solution.py:542
  133.5 7.0 %collective-permute-start.9 = (f32[3,2,64,128]{3,2,1,0:T(8,128)S(1)}, f32[3,2,64,128]{3,2,1,0:T(8,128)S(1)}, u32[]{:S(2)}, u32[]{:S(2)}) collective-permute-start(f32[3,2,64,128]{3,2,1,0:T(8,128)S(1)} %get-tuple-element.54), channel_id=1, source_target_pairs={{32,0},{33,1},{34,2},{35,3},{36,4},{37,5},{38,6},{39,7},{40,8},{41... | collective-permute-start | bytes 589832 | tf_op jit(solution)/shard_map/ppermute | solution.py:542
  140.7 4.6 %collective-permute-start.10 = (f32[3,64,128]{2,1,0:T(8,128)S(1)}, f32[3,64,128]{2,1,0:T(8,128)S(1)}, u32[]{:S(2)}, u32[]{:S(2)}) collective-permute-start(f32[3,64,128]{2,1,0:T(8,128)S(1)} %get-tuple-element.56), channel_id=1, source_target_pairs={{0,1},{1,2},{2,3},{3,4},{4,5},{5,6},{6,7},{7,8},{8,9},{9,10},{10,1... | collective-permute-start | bytes 294920 | tf_op jit(solution)/shard_map/ppermute | solution.py:542
  143.7 5.4 %collective-permute-start.11 = (f32[3,64,128]{2,1,0:T(8,128)S(1)}, f32[3,64,128]{2,1,0:T(8,128)S(1)}, u32[]{:S(2)}, u32[]{:S(2)}) collective-permute-start(f32[3,64,128]{2,1,0:T(8,128)S(1)} %get-tuple-element.57), channel_id=1, source_target_pairs={{1,0},{2,1},{3,2},{4,3},{5,4},{6,5},{7,6},{8,7},{9,8},{10,9},{11,1... | collective-permute-start | bytes 294920 | tf_op jit(solution)/shard_map/ppermute | solution.py:542

commit v7 on v6

--- a/solution.py
+++ b/solution.py
@@ -134,8 +134,10 @@
             store(c, 1, rows, jnp.where(low, mine, right))
 
 
-def send_kernel(offsets, own, tile, to_below, to_above, sems):
+def send_kernel(raw, own, tile, to_below, to_above, offsets, sems):
     strip = pl.ds(0, HALF)
+    first = pltpu.make_async_copy(raw, offsets, sems.at[3])
+    first.start()
     copies = [
         pltpu.make_async_copy(source, target, sems.at[k])
         for k, (source, target) in enumerate((
@@ -149,6 +151,7 @@
     line = lax.broadcasted_iota(jnp.int32, (TILES, SIZE), 0)
     lane = lax.broadcasted_iota(jnp.int32, (TILES, SIZE), 1)
     code = jnp.zeros((TILES, SIZE), jnp.int32)
+    first.wait()
     batches, _, count = offsets.shape
     for b in range(batches):
         for k in range(count):
@@ -214,7 +217,6 @@
         ratio = jnp.sqrt(measured[0, 0, batch, j]) / jnp.maximum(jnp.sqrt(intensity), 0.5) - 1.0
         chis.append(left_transform([(r * ratio, -(i * ratio)) for r, i in waves[j]], tl))
     chis = [right_transform(fields, tr) for fields in chis]
-    light = power_of(probe) if accum.shape[0] == 3 else None
     totals = [0.0] * 5
     for j in range(COUNT):
         row, col, wr, wi = wins[j]
@@ -230,8 +232,6 @@
         totals[2 * MODES] = totals[2 * MODES] + (wr * wr + wi * wi)
         place(accum, 0, row, col, cr)
         place(accum, 1, row, col, ci)
-        if light is not None:
-            place(accum, 2, row, col, light)
     for k in range(5):
         sums[k] = totals[k]
 
@@ -350,7 +350,7 @@
 
 def fold_kernel(middle, from_above, from_below, tile, left, right):
     low = low_lanes(HALF)
-    for k in range(3):
+    for k in range(2):
         upper = [middle[k, h, :HALF] + from_above[k, h] for h in range(2)]
         lower = [middle[k, h, HALF:] + from_below[k, h] for h in range(2)]
         tile[k, :HALF] = join(low, *upper)
@@ -359,25 +359,51 @@
         right[k] = pack_high(low, upper[1], lower[1])
 
 
-def merge_kernel(near, tile, from_left, from_right, padded, sums,
+def tile_cover_kernel(near, probe, cover, light):
+    none = jnp.zeros((SIZE, SIZE), F32)
+    light[:SIZE] = none
+    light[SIZE : 2 * SIZE] = power_of(probe)
+    light[2 * SIZE :] = none
+    cover[...] = none
+    lane = lanes()
+
+    def body(step, carry):
+        total = 0.0
+        for g in range(LIST_STEP):
+            down, across = near[step * LIST_STEP + g, 0], near[step * LIST_STEP + g, 1]
+            source = lane - across
+            valid = (source >= 0) & (source < SIZE)
+            moved = pltpu.roll(light[pl.ds(SIZE - down, SIZE)], lax.rem(2 * SIZE + across, SIZE), 1)
+            total = total + jnp.where(valid, moved, 0.0)
+        cover[...] += total
+        return carry
+
+    lax.fori_loop(0, lax.div(near[LIST_SIZE - 1, 0] + LIST_STEP - 1, LIST_STEP), body, 0)
+
+
+def merge_kernel(near, tile, from_left, from_right, cover, padded, sums,
                  packed, direction, product, overlap):
     low = low_lanes(HALF)
     lane = lanes()
     a11 = jnp.zeros((1, SIZE), F32)
     b1 = jnp.zeros((1, SIZE), F32)
-    product[...] = jnp.zeros_like(product)
+    for c in range(2):
+        product[c, :SIZE] = jnp.zeros((SIZE, SIZE), F32)
+        product[c, 2 * SIZE :] = jnp.zeros((SIZE, SIZE), F32)
+        overlap[c] = jnp.zeros((SIZE, SIZE), F32)
     for v in range(2):
         rows = slice(HALF * v, HALF * (v + 1))
         full = []
-        for k in range(3):
+        for k in range(2):
             left, right = from_left[k], from_right[k]
             if v == 0:
                 right = pltpu.roll(right, HALF, 1)
             else:
                 left = pltpu.roll(left, HALF, 1)
             full.append(tile[k, rows] + jnp.where(low, left, right))
-        gr, gi, cover = full
-        inverse = 1.0 / (cover + 1.0)
+        gr, gi = full
+        light = cover[rows]
+        inverse = 1.0 / (light + 1.0)
         dr = gr * inverse
         di = gi * inverse
         direction[0, rows] = dr
@@ -389,9 +415,8 @@
         product[0, inner] = dr * pr + di * pi
         product[1, inner] = dr * pi - di * pr
         power = dr * dr + di * di
-        a11 += jnp.sum(power * cover, axis=0, keepdims=True)
-        b1 += jnp.sum(power * (cover + 1.0), axis=0, keepdims=True)
-    overlap[...] = jnp.zeros_like(overlap)
+        a11 += jnp.sum(power * light, axis=0, keepdims=True)
+        b1 += jnp.sum(power * (light + 1.0), axis=0, keepdims=True)
 
     def body(step, carry):
         total = [0.0, 0.0]
@@ -574,9 +599,10 @@
 
     strip = shape(2, HALF + TILES, SIZE)
     side = shape(2, SIZE + TILES, SIZE)
-    tile, to_below, to_above = call(
-        send_kernel, [offsets, obj], [shape(2, SIZE, SIZE), strip, strip],
-        [pltpu.SemaphoreType.DMA((3,))], in_hbm=(1,))
+    tile, to_below, to_above, offsets = call(
+        send_kernel, [offsets, obj],
+        [shape(2, SIZE, SIZE), strip, strip, jax.ShapeDtypeStruct(offsets.shape, jnp.int32)],
+        [pltpu.SemaphoreType.DMA((4,))], in_hbm=(0, 1))
     above = shift(to_below, 1, 0)
     below = shift(to_above, -1, 0)
     to_left, to_right, codes = call(
@@ -590,7 +616,7 @@
     others = jnp.concatenate([from_left[0, SIZE:], codes, from_right[0, SIZE:]], axis=0).astype(jnp.int32)
 
     field = shape(2, 2, whole, SIZE)
-    edge = shape(3, 2, HALF, SIZE)
+    edge = shape(2, 2, HALF, SIZE)
     quads = shape(2, 2, SIZE, SIZE)
     planes = shape(2, MODES, SIZE, SIZE)
     sums_shape = shape(5, SIZE, SIZE)
@@ -622,19 +648,21 @@
     top, middle, bottom, sums, padded, probe = call(
         next_kernel,
         [offsets, totals, padded, direction, probe, measured, right3, left3],
-        [edge, shape(3, 2, SIZE, SIZE), edge, sums_shape, field, planes],
-        [pltpu.VMEM((3, 2, whole, SIZE), F32)],
+        [edge, quads, edge, sums_shape, field, planes],
+        [pltpu.VMEM((2, 2, whole, SIZE), F32)],
     )
     from_above = shift(bottom, 1, 0)
     from_below = shift(top, -1, 0)
-    side = shape(3, HALF, SIZE)
+    side = shape(2, HALF, SIZE)
+    (cover,) = call(
+        tile_cover_kernel, [near, probe], [shape(SIZE, SIZE)], [pltpu.VMEM((3 * SIZE, SIZE), F32)])
     middle, left, right = call(
-        fold_kernel, [middle, from_above, from_below], [shape(3, SIZE, SIZE), side, side])
+        fold_kernel, [middle, from_above, from_below], [shape(2, SIZE, SIZE), side, side])
     from_left = shift(right, 0, 1)
     from_right = shift(left, 0, -1)
     packed, direction = call(
         merge_kernel,
-        [near, middle, from_left, from_right, padded, sums],
+        [near, middle, from_left, from_right, cover, padded, sums],
         [packed_shape, shape(2, SIZE, SIZE)],
         [pltpu.VMEM((2, 3 * SIZE, SIZE), F32), pltpu.VMEM((2, SIZE, SIZE), F32)],
     )

time: 209 us -> 207 us (level)
  waiting for transfers between devices: 30.4 us -> 27.1 us
    ppermute x12, waiting for transfers between devices: 18.1 us -> 14.8 us  [shift(): return lax.ppermute(block, ALL, route)]
    pallas_call x15 -> x16, Pallas kernels: 25.6 us -> 27.4 us  [call(): pl.pallas_call(kernel, in_specs=specs, out_specs=[smem if x.dtype == jnp....]
  transfers between devices with their start and end apart: 13 -> 13, of which waited for: 10 -> 8; matrix products, arithmetic and copies ran while one was open for 0% -> 0% of each run, Pallas kernels for 3% -> 4%
where the time goes in v7:
time: 207 us; the launch traced here: 206 us
  blocking collectives  94.6 us (46%)
  starting transfers between devices  56.1 us (27%)
  Pallas kernels  27.4 us (13%)
  waiting for transfers between devices  27.1 us (13%)
    all_to_all x5, blocking collectives, exchange(): return lax.all_to_all(block, axes, 0, 0, tiled=True)  94.6 us
    ppermute x12, starting transfers between devices, shift(): return lax.ppermute(block, ALL, route)  33.5 us
    pallas_call x16, Pallas kernels, call(): pl.pallas_call(kernel, in_specs=specs, out_specs=[smem if x.dtype == jnp....  27.4 us
    all_to_all x1, starting transfers between devices, exchange(): return lax.all_to_all(block, axes, 0, 0, tiled=True)  22.6 us
    ppermute x12, waiting for transfers between devices, shift(): return lax.ppermute(block, ALL, route)  14.8 us
    all_to_all x1, waiting for transfers between devices, exchange(): return lax.all_to_all(block, axes, 0, 0, tiled=True)  12.3 us
  transfers between devices with their start and end apart: 13, of which 8 were waited for; matrix products, arithmetic and copies ran while one was open for 0% of the time, Pallas kernels for 4%

profile of v7, /device:TPU:1, one launch (start us, length us, event | category | flops | bytes accessed | tf_op | source)
XLA Modules:
  0.0 206.4 jit_solution(109544666271500783)
XLA Ops:
  0.6 1.6 send_kernel.1
  2.3 8.8 %collective-permute-start.1 = (f32[2,72,128]{2,1,0:T(8,128)S(1)}, f32[2,72,128]{2,1,0:T(8,128)S(1)}, u32[]{:S(2)}, u32[]{:S(2)}) collective-permute-start(f32[2,72,128]{2,1,0:T(8,128)S(1)} %get-tuple-element.36), channel_id=1, source_target_pairs={{32,0},{33,1},{34,2},{35,3},{36,4},{37,5},{38,6},{39,7},{40,8},{41... | collective-permute-start | bytes 221192 | tf_op jit(solution)/shard_map/ppermute | solution.py:567
  11.1 1.9 collective-permute-start
  13.0 1.4 collective-permute-done.above
  14.5 1.3 collective-permute-start.2
  15.8 1.3 collective-permute-start.3
  17.2 1.5 stage_kernel.1
  19.1 3.9 %collective-permute-done.3.from_right = f32[2,136,128]{2,1,0:T(8,128)S(1)} collective-permute-done((f32[2,136,128]{2,1,0:T(8,128)S(1)}, f32[2,136,128]{2,1,0:T(8,128)S(1)}, u32[]{:S(2)}, u32[]{:S(2)}) %collective-permute-start.3) | collective-permute-done | bytes 139296 | tf_op jit(solution)/shard_map/ppermute | solution.py:567
  23.0 5.2 %first_kernel.1 = (f32[2,2,128,128]{3,2,1,0:T(8,128)S(1)}, f32[2,2,128,128]{3,2,1,0:T(8,128)S(1)}, f32[5,128,128]{2,1,0:T(8,128)S(1)}, f32[2,2,256,128]{3,2,1,0:T(8,128)S(1)}) custom-call(s32[2,2,8]{2,1,0:T(2,128)S(1)} %get-tuple-element.41.offsets, f32[2,72,128]{2,1,0:T(8,128)S(1)} %collective-permute-done.above, f32[2,128,128]{2,1,0:T(8,128)S(1)} %get-tuple-element.35.own, ...), custom_call_target="tpu_custom_call" | custom-call | tf_op jit(solution)/shard_map/first_kernel/pallas_call | solution.py:547
  28.2 2.7 %collective-permute-start.5 = (f32[2,2,128,128]{3,2,1,0:T(8,128)S(1)}, f32[2,2,128,128]{3,2,1,0:T(8,128)S(1)}, u32[]{:S(2)}, u32[]{:S(2)}) collective-permute-start(f32[2,2,128,128]{3,2,1,0:T(8,128)S(1)} %get-tuple-element.45.top), channel_id=1, source_target_pairs={{32,0},{33,1},{34,2},{35,3},{36,4},{37,5},{38,6},{39,7},{40,8},{41... | collective-permute-start | bytes 786440 | tf_op jit(solution)/shard_map/ppermute | solution.py:567
  30.9 3.3 %collective-permute-start.4 = (f32[2,2,128,128]{3,2,1,0:T(8,128)S(1)}, f32[2,2,128,128]{3,2,1,0:T(8,128)S(1)}, u32[]{:S(2)}, u32[]{:S(2)}) collective-permute-start(f32[2,2,128,128]{3,2,1,0:T(8,128)S(1)} %get-tuple-element.46.bottom), channel_id=1, source_target_pairs={{0,32},{1,33},{2,34},{3,35},{4,36},{5,37},{6,38},{7,39},{8,40},{9,... | collective-permute-start | bytes 786440 | tf_op jit(solution)/shard_map/ppermute | solution.py:567
  34.3 2.0 collective-permute-done.5.from_below
  37.5 1.3 collective-permute-start.7
  38.8 4.0 %collective-permute-start.6 = (f32[2,2,128,128]{3,2,1,0:T(8,128)S(1)}, f32[2,2,128,128]{3,2,1,0:T(8,128)S(1)}, u32[]{:S(2)}, u32[]{:S(2)}) collective-permute-start(f32[2,2,128,128]{3,2,1,0:T(8,128)S(1)} %get-tuple-element.48.right), channel_id=1, source_target_pairs={{0,1},{1,2},{2,3},{3,4},{4,5},{5,6},{6,7},{7,8},{8,9},{9,10},{10,1... | collective-permute-start | bytes 786440 | tf_op jit(solution)/shard_map/ppermute | solution.py:567
  42.9 4.0 %cover_kernel.1 = (f32[2,256,128]{2,1,0:T(8,128)S(1)}, s32[80,2]{1,0:T(8,128)S(1)}) custom-call(s32[24,128]{1,0:T(8,128)S(1)} %maximum_convert_fusion.others, f32[2,2,128,128]{3,2,1,0:T(8,128)S(1)} %copy-done), custom_call_target="tpu_custom_call" | custom-call | tf_op jit(solution)/shard_map/cover_kernel/pallas_call | solution.py:547
  46.9 1.2 wide_merge_kernel.1
  48.2 23.9 %all_to_all.30.parts = f32[32,4,8,128]{3,2,1,0:T(8,128)S(1)} all-to-all(f32[32,4,8,128]{3,2,1,0:T(8,128)S(1)} %bitcast.19), channel_id=1, replica_groups=mesh['yl'=2,'x'=4,'c'=2,'yh'=4,'zh'=4,'zl'=2] {'yl','x','c','zl'}, dimensions={0} | all-to-all | bytes 1048576 | tf_op jit(solution)/shard_map/all_to_all | solution.py:571
  72.8 22.6 %all-to-all-start.1 = ((f32[16,4,8,128]{3,2,1,0:T(8,128)}), f32[16,4,8,128]{3,2,1,0:T(8,128)S(1)}, u32[]{:S(2)}, u32[]{:S(2)}) async-start(f32[16,4,8,128]{3,2,1,0:T(8,128)} %reduce_kernel.2), calls=%async_computation.1 | async-start | bytes 524288 | tf_op jit(solution)/shard_map/all_to_all | solution.py:571
  95.5 12.3 %all-to-all-done.1.parts = f32[16,4,8,128]{3,2,1,0:T(8,128)S(1)} async-done(((f32[16,4,8,128]{3,2,1,0:T(8,128)}), f32[16,4,8,128]{3,2,1,0:T(8,128)S(1)}, u32[]{:S(2)}, u32[]{:S(2)}) %all-to-all-start.1) | async-done | bytes 262176 | tf_op jit(solution)/shard_map/all_to_all | solution.py:571
  108.5 15.5 %all_to_all.31 = f32[32,3,8,128]{3,2,1,0:T(8,128)S(1)} all-to-all(f32[32,3,8,128]{3,2,1,0:T(8,128)S(1)} %strip_kernel.2), channel_id=1, replica_groups=mesh['yl'=2,'x'=4,'c'=2,'yh'=4,'zh'=4,'zl'=2] {'yl','x','c','zl'}, dimensions={0} | all-to-all | bytes 786432 | tf_op jit(solution)/shard_map/all_to_all | solution.py:571
  124.0 5.3 %next_kernel.1 = (f32[2,2,64,128]{3,2,1,0:T(8,128)S(1)}, f32[2,2,128,128]{3,2,1,0:T(8,128)S(1)}, f32[2,2,64,128]{3,2,1,0:T(8,128)S(1)}, f32[5,128,128]{2,1,0:T(8...) custom-call(s32[2,2,8]{2,1,0:T(2,128)S(1)} %get-tuple-element.41.offsets, ...), custom_call_target="tpu_custom_call" | custom-call | tf_op jit(solution)/shard_map/next_kernel/pallas_call | solution.py:547
  129.2 2.8 %collective-permute-start.8 = (f32[2,2,64,128]{3,2,1,0:T(8,128)S(1)}, f32[2,2,64,128]{3,2,1,0:T(8,128)S(1)}, u32[]{:S(2)}, u32[]{:S(2)}) collective-permute-start(f32[2,2,64,128]{3,2,1,0:T(8,128)S(1)} %get-tuple-element.55), channel_id=1, source_target_pairs={{0,32},{1,33},{2,34},{3,35},{4,36},{5,37},{6,38},{7,39},{8,40},{9,... | collective-permute-start | bytes 393224 | tf_op jit(solution)/shard_map/ppermute | solution.py:567
  132.0 1.9 collective-permute-start.9
  134.0 4.3 %collective-permute-done.9.from_below = f32[2,2,64,128]{3,2,1,0:T(8,128)S(1)} collective-permute-done((f32[2,2,64,128]{3,2,1,0:T(8,128)S(1)}, f32[2,2,64,128]{3,2,1,0:T(8,128)S(1)}, u32[]{:S(2)}, u32[]{:S(2)}) %collective-permute-start.9) | collective-permute-done | bytes 131104 | tf_op jit(solution)/shard_map/ppermute | solution.py:567
  138.5 3.0 %collective-permute-start.10 = (f32[2,64,128]{2,1,0:T(8,128)S(1)}, f32[2,64,128]{2,1,0:T(8,128)S(1)}, u32[]{:S(2)}, u32[]{:S(2)}) collective-permute-start(f32[2,64,128]{2,1,0:T(8,128)S(1)} %get-tuple-element.58), channel_id=1, source_target_pairs={{0,1},{1,2},{2,3},{3,4},{4,5},{5,6},{6,7},{7,8},{8,9},{9,10},{10,1... | collective-permute-start | bytes 196616 | tf_op jit(solution)/shard_map/ppermute | solution.py:567
  141.4 1.3 collective-permute-start.11
  142.7 2.2 %tile_cover_kernel.1.cover = f32[128,128]{1,0:T(8,128)S(1)} custom-call(s32[80,2]{1,0:T(8,128)S(1)} %get-tuple-element.40.near, f32[2,2,128,128]{3,2,1,0:T(8,128)S(1)} %get-tuple-element.60.probe), custom_call_target="tpu_custom_call" | custom-call | tf_op jit(solution)/shard_map/tile_cover_kernel/pallas_call | solution.py:547
  144.9 1.5 collective-permute-done.11.from_right
  146.4 2.9 %merge_kernel.1 = (f32[16,2,4,8,128]{4,3,2,1,0:T(8,128)S(1)}, f32[2,128,128]{2,1,0:T(8,128)S(1)}) custom-call(s32[80,2]{1,0:T(8,128)S(1)} %get-tuple-element.40.near, f32[2,128,128]{2,1,0:T(8,128)S(1)} %get-tuple-element.57.tile, f32[2,64,128]{2,1,0:T(8,128)S(1)} %collective-permute-done.10.from_left, f32[2,64,128]{2,1,0:T(8,128)S(1)} %collective-permute-done.11.from_right, ...), custom_call_target="tpu_custom_call" | custom-call | tf_op jit(solution)/shard_map/merge_kernel/pallas_call | solution.py:547
  149.4 16.8 %all_to_all.32.parts = f32[32,4,8,128]{3,2,1,0:T(8,128)S(1)} all-to-all(f32[32,4,8,128]{3,2,1,0:T(8,128)S(1)} %bitcast.20), channel_id=1, replica_groups=mesh['yl'=2,'x'=4,'c'=2,'yh'=4,'zh'=4,'zl'=2] {'yl','x','c','zl'}, dimensions={0} | all-to-all | bytes 1048576 | tf_op jit(solution)/shard_map/all_to_all | solution.py:571
  166.2 23.0 %all_to_all.33.parts = f32[16,4,8,128]{3,2,1,0:T(8,128)S(1)} all-to-all(f32[16,4,8,128]{3,2,1,0:T(8,128)S(1)} %reduce_kernel.3), channel_id=1, replica_groups=mesh['yl'=2,'x'=4,'c'=2,'yh'=4,'zh'=4,'zl'=2] {'zh','yh'}, dimensions={0} | all-to-all | bytes 524288 | tf_op jit(solution)/shard_map/all_to_all | solution.py:571
  189.9 15.5 %all_to_all.34 = f32[32,3,8,128]{3,2,1,0:T(8,128)S(1)} all-to-all(f32[32,3,8,128]{3,2,1,0:T(8,128)S(1)} %strip_kernel.3), channel_id=1, replica_groups=mesh['yl'=2,'x'=4,'c'=2,'yh'=4,'zh'=4,'zl'=2] {'yl','x','c','zl'}, dimensions={0} | all-to-all | bytes 786432 | tf_op jit(solution)/shard_map/all_to_all | solution.py:571
  (22 shorter events, 5.2 us)
Async XLA Ops:
  2.3 10.7 %collective-permute-start.1 = (f32[2,72,128]{2,1,0:T(8,128)S(1)}, f32[2,72,128]{2,1,0:T(8,128)S(1)}, u32[]{:S(2)}, u32[]{:S(2)}) collective-permute-start(f32[2,72,128]{2,1,0:T(8,128)S(1)} %get-tuple-element.36), channel_id=1, source_target_pairs={{32,0},{33,1},{34,2},{35,3},{36,4},{37,5},{38,6},{39,7},{40,8},{41... | collective-permute-start | bytes 221192 | tf_op jit(solution)/shard_map/ppermute | solution.py:567
  11.1 3.3 %collective-permute-start = (f32[2,72,128]{2,1,0:T(8,128)S(1)}, f32[2,72,128]{2,1,0:T(8,128)S(1)}, u32[]{:S(2)}, u32[]{:S(2)}) collective-permute-start(f32[2,72,128]{2,1,0:T(8,128)S(1)} %get-tuple-element.34.mine), channel_id=1, source_target_pairs={{0,32},{1,33},{2,34},{3,35},{4,36},{5,37},{6,38},{7,39},{8,40},{9,... | collective-permute-start | bytes 221192 | tf_op jit(solution)/shard_map/ppermute | solution.py:567
  14.5 4.6 %collective-permute-start.2 = (f32[2,136,128]{2,1,0:T(8,128)S(1)}, f32[2,136,128]{2,1,0:T(8,128)S(1)}, u32[]{:S(2)}, u32[]{:S(2)}) collective-permute-start(f32[2,136,128]{2,1,0:T(8,128)S(1)} %get-tuple-element.37), channel_id=1, source_target_pairs={{0,1},{1,2},{2,3},{3,4},{4,5},{5,6},{6,7},{7,8},{8,9},{9,10},{10,1... | collective-permute-start | bytes 417800 | tf_op jit(solution)/shard_map/ppermute | solution.py:567
  15.8 7.2 %collective-permute-start.3 = (f32[2,136,128]{2,1,0:T(8,128)S(1)}, f32[2,136,128]{2,1,0:T(8,128)S(1)}, u32[]{:S(2)}, u32[]{:S(2)}) collective-permute-start(f32[2,136,128]{2,1,0:T(8,128)S(1)} %get-tuple-element.39), channel_id=1, source_target_pairs={{1,0},{2,1},{3,2},{4,3},{5,4},{6,5},{7,6},{8,7},{9,8},{10,9},{11,1... | collective-permute-start | bytes 417800 | tf_op jit(solution)/shard_map/ppermute | solution.py:567
  17.2 5.9 %copy-start = (f32[2,2,128,128]{3,2,1,0:T(8,128)S(1)}, f32[2,2,128,128]{3,2,1,0:T(8,128)}, u32[]{:S(2)}) copy-start(f32[2,2,128,128]{3,2,1,0:T(8,128)} %probe.7) | copy-start | bytes 786436
  28.2 8.1 %collective-permute-start.5 = (f32[2,2,128,128]{3,2,1,0:T(8,128)S(1)}, f32[2,2,128,128]{3,2,1,0:T(8,128)S(1)}, u32[]{:S(2)}, u32[]{:S(2)}) collective-permute-start(f32[2,2,128,128]{3,2,1,0:T(8,128)S(1)} %get-tuple-element.45.top), channel_id=1, source_target_pairs={{32,0},{33,1},{34,2},{35,3},{36,4},{37,5},{38,6},{39,7},{40,8},{41... | collective-permute-start | bytes 786440 | tf_op jit(solution)/shard_map/ppermute | solution.py:567
  30.9 6.6 %collective-permute-start.4 = (f32[2,2,128,128]{3,2,1,0:T(8,128)S(1)}, f32[2,2,128,128]{3,2,1,0:T(8,128)S(1)}, u32[]{:S(2)}, u32[]{:S(2)}) collective-permute-start(f32[2,2,128,128]{3,2,1,0:T(8,128)S(1)} %get-tuple-element.46.bottom), channel_id=1, source_target_pairs={{0,32},{1,33},{2,34},{3,35},{4,36},{5,37},{6,38},{7,39},{8,40},{9,... | collective-permute-start | bytes 786440 | tf_op jit(solution)/shard_map/ppermute | solution.py:567
  37.5 9.4 %collective-permute-start.7 = (f32[2,2,128,128]{3,2,1,0:T(8,128)S(1)}, f32[2,2,128,128]{3,2,1,0:T(8,128)S(1)}, u32[]{:S(2)}, u32[]{:S(2)}) collective-permute-start(f32[2,2,128,128]{3,2,1,0:T(8,128)S(1)} %get-tuple-element.47.left), channel_id=1, source_target_pairs={{1,0},{2,1},{3,2},{4,3},{5,4},{6,5},{7,6},{8,7},{9,8},{10,9},{11,1... | collective-permute-start | bytes 786440 | tf_op jit(solution)/shard_map/ppermute | solution.py:567
  38.8 8.1 %collective-permute-start.6 = (f32[2,2,128,128]{3,2,1,0:T(8,128)S(1)}, f32[2,2,128,128]{3,2,1,0:T(8,128)S(1)}, u32[]{:S(2)}, u32[]{:S(2)}) collective-permute-start(f32[2,2,128,128]{3,2,1,0:T(8,128)S(1)} %get-tuple-element.48.right), channel_id=1, source_target_pairs={{0,1},{1,2},{2,3},{3,4},{4,5},{5,6},{6,7},{7,8},{8,9},{9,10},{10,1... | collective-permute-start | bytes 786440 | tf_op jit(solution)/shard_map/ppermute | solution.py:567
  72.8 35.0 %all-to-all-start.1 = ((f32[16,4,8,128]{3,2,1,0:T(8,128)}), f32[16,4,8,128]{3,2,1,0:T(8,128)S(1)}, u32[]{:S(2)}, u32[]{:S(2)}) async-start(f32[16,4,8,128]{3,2,1,0:T(8,128)} %reduce_kernel.2), calls=%async_computation.1 | async-start | bytes 524288 | tf_op jit(solution)/shard_map/all_to_all | solution.py:571
  129.2 4.7 %collective-permute-start.8 = (f32[2,2,64,128]{3,2,1,0:T(8,128)S(1)}, f32[2,2,64,128]{3,2,1,0:T(8,128)S(1)}, u32[]{:S(2)}, u32[]{:S(2)}) collective-permute-start(f32[2,2,64,128]{3,2,1,0:T(8,128)S(1)} %get-tuple-element.55), channel_id=1, source_target_pairs={{0,32},{1,33},{2,34},{3,35},{4,36},{5,37},{6,38},{7,39},{8,40},{9,... | collective-permute-start | bytes 393224 | tf_op jit(solution)/shard_map/ppermute | solution.py:567
  132.0 6.3 %collective-permute-start.9 = (f32[2,2,64,128]{3,2,1,0:T(8,128)S(1)}, f32[2,2,64,128]{3,2,1,0:T(8,128)S(1)}, u32[]{:S(2)}, u32[]{:S(2)}) collective-permute-start(f32[2,2,64,128]{3,2,1,0:T(8,128)S(1)} %get-tuple-element.56), channel_id=1, source_target_pairs={{32,0},{33,1},{34,2},{35,3},{36,4},{37,5},{38,6},{39,7},{40,8},{41... | collective-permute-start | bytes 393224 | tf_op jit(solution)/shard_map/ppermute | solution.py:567
  138.5 6.5 %collective-permute-start.10 = (f32[2,64,128]{2,1,0:T(8,128)S(1)}, f32[2,64,128]{2,1,0:T(8,128)S(1)}, u32[]{:S(2)}, u32[]{:S(2)}) collective-permute-start(f32[2,64,128]{2,1,0:T(8,128)S(1)} %get-tuple-element.58), channel_id=1, source_target_pairs={{0,1},{1,2},{2,3},{3,4},{4,5},{5,6},{6,7},{7,8},{8,9},{9,10},{10,1... | collective-permute-start | bytes 196616 | tf_op jit(solution)/shard_map/ppermute | solution.py:567
  141.4 5.0 %collective-permute-start.11 = (f32[2,64,128]{2,1,0:T(8,128)S(1)}, f32[2,64,128]{2,1,0:T(8,128)S(1)}, u32[]{:S(2)}, u32[]{:S(2)}) collective-permute-start(f32[2,64,128]{2,1,0:T(8,128)S(1)} %get-tuple-element.59), channel_id=1, source_target_pairs={{1,0},{2,1},{3,2},{4,3},{5,4},{6,5},{7,6},{8,7},{9,8},{10,9},{11,1... | collective-permute-start | bytes 196616 | tf_op jit(solution)/shard_map/ppermute | solution.py:567

commit v8 on v7

--- a/solution.py
+++ b/solution.py
@@ -1,3 +1,4 @@
+import itertools
 import math
 from functools import partial
 
@@ -117,13 +118,23 @@
     return (line >= row_low) & (line < row_high) & (lane >= col_low) & (lane < col_high)
 
 
-def pad_field(above, own, below, from_left, from_right, store):
+def evens():
+    return tuple(lax.axis_index(axis) == 0 for axis in (ROW[-1], COL[-1]))
+
+
+def sides(even, first, second):
+    return jnp.where(even, second, first), jnp.where(even, first, second)
+
+
+def pad_field(rows_in, own, cols_in, store):
     low = low_lanes(HALF)
-    for c in range(2):
-        strips = (above[c, :HALF], own[c, :HALF], own[c, HALF:], below[c, :HALF])
+    even_row, even_col = evens()
+    for c in range(2):
+        above, below = sides(even_row, *(x[c, :HALF] for x in rows_in))
+        strips = (above, own[c, :HALF], own[c, HALF:], below)
         for k in range(4):
             half = slice(HALF * (k % 2), HALF * (k % 2 + 1))
-            left, right = from_left[c, half], from_right[c, half]
+            left, right = sides(even_col, *(x[c, half] for x in cols_in))
             if k < 2:
                 right = pltpu.roll(right, HALF, 1)
             else:
@@ -134,15 +145,17 @@
             store(c, 1, rows, jnp.where(low, mine, right))
 
 
-def send_kernel(raw, own, tile, to_below, to_above, offsets, sems):
+def send_kernel(raw, own, tile, row_out0, row_out1, offsets, sems):
     strip = pl.ds(0, HALF)
+    even_row, _ = evens()
+    starts = [pl.multiple_of(jnp.where(even_row == (k == 0), HALF, 0), HALF) for k in range(2)]
     first = pltpu.make_async_copy(raw, offsets, sems.at[3])
     first.start()
     copies = [
         pltpu.make_async_copy(source, target, sems.at[k])
         for k, (source, target) in enumerate((
-            (own.at[:, pl.ds(HALF, HALF)], to_below.at[:, strip]),
-            (own.at[:, strip], to_above.at[:, strip]),
+            (own.at[:, pl.ds(starts[0], HALF)], row_out0.at[:, strip]),
+            (own.at[:, pl.ds(starts[1], HALF)], row_out1.at[:, strip]),
             (own, tile),
         ))
     ]
@@ -159,24 +172,29 @@
                 code = jnp.where(lane == (b * 2 + d) * count + k, offsets[b, d, k] + MARK, code)
     code = jnp.where(line == 0, code, 0).astype(F32)
     for c in range(2):
-        to_below[c, HALF:] = code
-        to_above[c, HALF:] = code
+        row_out0[c, HALF:] = code
+        row_out1[c, HALF:] = code
     for copy in copies:
         copy.wait()
 
 
-def pack_kernel(above, own, below, mine, to_left, to_right, codes):
+def pack_kernel(row_in0, row_in1, own, mine, col_out0, col_out1, codes):
     low = low_lanes(HALF)
-    for c in range(2):
-        strips = (above[c, :HALF], own[c, :HALF], own[c, HALF:], below[c, :HALF])
+    even_row, even_col = evens()
+    for c in range(2):
+        above, below = sides(even_row, row_in0[c, :HALF], row_in1[c, :HALF])
+        strips = (above, own[c, :HALF], own[c, HALF:], below)
         for k in range(2):
             rows = slice(HALF * k, HALF * (k + 1))
-            to_left[c, rows] = pack_low(low, strips[k], strips[k + 2])
-            to_right[c, rows] = pack_high(low, strips[k], strips[k + 2])
-    code = mine[0, HALF:] + pltpu.roll(above[0, HALF:], 1, 0) + pltpu.roll(below[0, HALF:], 2, 0)
-    for c in range(2):
-        to_left[c, SIZE:] = code
-        to_right[c, SIZE:] = code
+            to_left = pack_low(low, strips[k], strips[k + 2])
+            to_right = pack_high(low, strips[k], strips[k + 2])
+            col_out0[c, rows] = jnp.where(even_col, to_right, to_left)
+            col_out1[c, rows] = jnp.where(even_col, to_left, to_right)
+    above, below = sides(even_row, row_in0[0, HALF:], row_in1[0, HALF:])
+    code = mine[0, HALF:] + pltpu.roll(above, 1, 0) + pltpu.roll(below, 2, 0)
+    for c in range(2):
+        col_out0[c, SIZE:] = code
+        col_out1[c, SIZE:] = code
     codes[...] = code
 
 
@@ -236,19 +254,25 @@
         sums[k] = totals[k]
 
 
-def first_kernel(offsets, above, own, below, from_left, from_right, probe, measured, right3, left3,
-                 top, bottom, sums, padded, accum):
+def first_kernel(offsets, row_in0, row_in1, own, col_in0, col_in1, probe, measured, right3, left3,
+                 row_out0, row_out1, sums, padded, accum):
     def store(c, h, rows, value):
         padded[c, h, rows] = value
 
-    pad_field(above, own, below, from_left, from_right, store)
+    pad_field((row_in0, row_in1), own, (col_in0, col_in1), store)
     sweep(0, offsets, padded, probe, measured, right3, left3, sums, accum)
-    top[...] = accum[:, :, :SIZE]
-    bottom[...] = accum[:, :, SIZE:]
+    even_row, _ = evens()
+    for c in range(2):
+        for h in range(2):
+            top, bottom = accum[c, h, :SIZE], accum[c, h, SIZE:]
+            row_out0[c, h] = jnp.where(even_row, bottom, top)
+            row_out1[c, h] = jnp.where(even_row, top, bottom)
 
 
 def offset_of(others, batch, across, down, j, d):
-    return others[TILES * across + (1, 0, 2)[down], (batch * 2 + d) * COUNT + j] - MARK
+    _, even_col = evens()
+    tile = jnp.where(even_col, 2 - across, across)
+    return others[TILES * tile + (1, 0, 2)[down], (batch * 2 + d) * COUNT + j] - MARK
 
 
 def cover_kernel(others, probe, cover, near, light):
@@ -290,10 +314,18 @@
     near[LIST_SIZE - 1, 0] = count
 
 
-def wide_fold_kernel(top, bottom, from_above, from_below, left, right):
-    for v, own, other in ((0, top, from_above), (1, bottom, from_below)):
-        left[v] = own[:, 0] + other[:, 0]
-        right[v] = own[:, 1] + other[:, 1]
+def wide_fold_kernel(row_out0, row_out1, row_in0, row_in1, col_out0, col_out1):
+    even_row, even_col = evens()
+    for c in range(2):
+        top, bottom = [], []
+        for h in range(2):
+            upper, lower = sides(
+                even_row, row_out0[c, h] + row_in0[c, h], row_out1[c, h] + row_in1[c, h])
+            top.append(upper)
+            bottom.append(lower)
+        for v, (left, right) in enumerate((top, bottom)):
+            col_out0[v, c] = jnp.where(even_col, right, left)
+            col_out1[v, c] = jnp.where(even_col, left, right)
 
 
 def pack_planes(packed, planes):
@@ -318,19 +350,20 @@
     pack_planes(packed, [sums[k] for k in range(5)] + [numbers] + list(overlap))
 
 
-def wide_merge_kernel(edges, offsets, left, right, from_left, from_right, cover, padded, sums,
+def wide_merge_kernel(edges, offsets, col_out0, col_out1, col_in0, col_in1, cover, padded, sums,
                       packed, direction, product):
     limits = bounds(edges)
+    _, even_col = evens()
     a11 = jnp.zeros((1, SIZE), F32)
     b1 = jnp.zeros((1, SIZE), F32)
     for v in range(2):
         rows = slice(v * SIZE, (v + 1) * SIZE)
         mine_rows = lax.broadcasted_iota(jnp.int32, (SIZE, SIZE), 0) + v * SIZE
+        totals = [sides(even_col, col_out0[v, c] + col_in0[v, c], col_out1[v, c] + col_in1[v, c]) for c in range(2)]
         for h in range(2):
-            own, other = ((left, from_left), (right, from_right))[h]
             light = cover[h, rows]
             inverse = jnp.where(inside(limits, v * SIZE, h * SIZE), 1.0 / (light + 1.0), 0.0)
-            dr, di = ((own[v, c] + other[v, c]) * inverse for c in range(2))
+            dr, di = (totals[c][h] * inverse for c in range(2))
             direction[0, h, rows] = dr
             direction[1, h, rows] = di
             pr, pi = padded[0, h, rows], padded[1, h, rows]
@@ -348,15 +381,21 @@
     pack_sums(packed, sums, overlap, a11, b1)
 
 
-def fold_kernel(middle, from_above, from_below, tile, left, right):
+def fold_kernel(middle, row_in0, row_in1, tile, col_out0, col_out1):
     low = low_lanes(HALF)
+    even_row, even_col = evens()
     for k in range(2):
-        upper = [middle[k, h, :HALF] + from_above[k, h] for h in range(2)]
-        lower = [middle[k, h, HALF:] + from_below[k, h] for h in range(2)]
+        upper, lower = [], []
+        for h in range(2):
+            above, below = sides(even_row, row_in0[k, h], row_in1[k, h])
+            upper.append(middle[k, h, :HALF] + above)
+            lower.append(middle[k, h, HALF:] + below)
         tile[k, :HALF] = join(low, *upper)
         tile[k, HALF:] = join(low, *lower)
-        left[k] = pack_low(low, upper[0], lower[0])
-        right[k] = pack_high(low, upper[1], lower[1])
+        to_left = pack_low(low, upper[0], lower[0])
+        to_right = pack_high(low, upper[1], lower[1])
+        col_out0[k] = jnp.where(even_col, to_right, to_left)
+        col_out1[k] = jnp.where(even_col, to_left, to_right)
 
 
 def tile_cover_kernel(near, probe, cover, light):
@@ -381,10 +420,11 @@
     lax.fori_loop(0, lax.div(near[LIST_SIZE - 1, 0] + LIST_STEP - 1, LIST_STEP), body, 0)
 
 
-def merge_kernel(near, tile, from_left, from_right, cover, padded, sums,
+def merge_kernel(near, tile, col_in0, col_in1, cover, padded, sums,
                  packed, direction, product, overlap):
     low = low_lanes(HALF)
     lane = lanes()
+    _, even_col = evens()
     a11 = jnp.zeros((1, SIZE), F32)
     b1 = jnp.zeros((1, SIZE), F32)
     for c in range(2):
@@ -395,7 +435,7 @@
         rows = slice(HALF * v, HALF * (v + 1))
         full = []
         for k in range(2):
-            left, right = from_left[k], from_right[k]
+            left, right = sides(even_col, col_in0[k], col_in1[k])
             if v == 0:
                 right = pltpu.roll(right, HALF, 1)
             else:
@@ -516,13 +556,17 @@
 
 
 def next_kernel(offsets, totals, padded, direction, probe, measured, right3, left3,
-                top, middle, bottom, sums, new_padded, new_probe, accum):
+                row_out0, middle, row_out1, sums, new_padded, new_probe, accum):
     step = step_sizes(totals, probe, new_probe)
     new_padded[...] = padded[...] + step * direction[...]
     sweep(1, offsets, new_padded, new_probe, measured, right3, left3, sums, accum)
-    top[...] = accum[:, :, :HALF]
     middle[...] = accum[:, :, HALF : HALF + SIZE]
-    bottom[...] = accum[:, :, HALF + SIZE :]
+    even_row, _ = evens()
+    for c in range(2):
+        for h in range(2):
+            top, bottom = accum[c, h, :HALF], accum[c, h, HALF + SIZE :]
+            row_out0[c, h] = jnp.where(even_row, bottom, top)
+            row_out1[c, h] = jnp.where(even_row, top, bottom)
 
 
 def last_kernel(totals, padded, direction, probe, new_obj, new_probe, gradient):
@@ -555,16 +599,18 @@
     )(*ins)
 
 
-def shift(block, rows, cols):
-    n_row = math.prod(lax.axis_size(a) for a in ROW)
-    n_col = math.prod(lax.axis_size(a) for a in COL)
-    route = [
-        (r * n_col + c, (r + rows) * n_col + c + cols)
-        for r in range(n_row)
-        for c in range(n_col)
-        if 0 <= r + rows < n_row and 0 <= c + cols < n_col
-    ]
-    return lax.ppermute(block, ALL, route)
+def swap(blocks, along):
+    counts = size_of(ROW), size_of(COL)
+    taken = []
+    for k, block in enumerate(blocks):
+        route = []
+        for here in itertools.product(*(range(n) for n in counts)):
+            there = list(here)
+            there[along] += 1 if here[along] % 2 == k else -1
+            if 0 <= there[along] < counts[along]:
+                route.append((here[0] * counts[1] + here[1], there[0] * counts[1] + there[1]))
+        taken.append(lax.ppermute(block, ALL, route))
+    return taken
 
 
 def exchange(block, axes):
@@ -599,21 +645,19 @@
 
     strip = shape(2, HALF + TILES, SIZE)
     side = shape(2, SIZE + TILES, SIZE)
-    tile, to_below, to_above, offsets = call(
+    tile, *row_out, offsets = call(
         send_kernel, [offsets, obj],
         [shape(2, SIZE, SIZE), strip, strip, jax.ShapeDtypeStruct(offsets.shape, jnp.int32)],
         [pltpu.SemaphoreType.DMA((4,))], in_hbm=(0, 1))
-    above = shift(to_below, 1, 0)
-    below = shift(to_above, -1, 0)
-    to_left, to_right, codes = call(
-        pack_kernel, [above, tile, below, to_below], [side, side, shape(TILES, SIZE)])
-    from_left = shift(to_right, 0, 1)
-    from_right = shift(to_left, 0, -1)
+    row_in = swap(row_out, 0)
+    *col_out, codes = call(
+        pack_kernel, [*row_in, tile, row_out[0]], [side, side, shape(TILES, SIZE)])
+    col_in = swap(col_out, 1)
     staged = [measured, right3, left3]
     measured, right3, left3 = call(
         stage_kernel, [codes, *staged], [jax.ShapeDtypeStruct(x.shape, x.dtype) for x in staged],
         [pltpu.SemaphoreType.DMA((len(staged),))], in_hbm=(1, 2, 3))
-    others = jnp.concatenate([from_left[0, SIZE:], codes, from_right[0, SIZE:]], axis=0).astype(jnp.int32)
+    others = jnp.concatenate([col_in[0][0, SIZE:], codes, col_in[1][0, SIZE:]], axis=0).astype(jnp.int32)
 
     field = shape(2, 2, whole, SIZE)
     edge = shape(2, 2, HALF, SIZE)
@@ -622,47 +666,43 @@
     sums_shape = shape(5, SIZE, SIZE)
     packed_shape = shape(SIZE // TILES, 2, 4, TILES, SIZE)
 
-    top, bottom, sums, padded = call(
+    *row_out, sums, padded = call(
         first_kernel,
-        [offsets, above, tile, below, from_left, from_right, probe, measured, right3, left3],
+        [offsets, *row_in, tile, *col_in, probe, measured, right3, left3],
         [quads, quads, sums_shape, field],
         [pltpu.VMEM((2, 2, whole, SIZE), F32)],
     )
-    from_above = shift(bottom, 1, 0)
-    from_below = shift(top, -1, 0)
+    row_in = swap(row_out, 0)
     cover, near = call(
         cover_kernel, [others, probe],
         [shape(2, whole, SIZE), jax.ShapeDtypeStruct((LIST_SIZE, 2), jnp.int32)],
         [pltpu.VMEM((3 * SIZE, SIZE), F32)])
-    left, right = call(wide_fold_kernel, [top, bottom, from_above, from_below], [quads, quads])
-    from_left = shift(right, 0, 1)
-    from_right = shift(left, 0, -1)
+    col_out = call(wide_fold_kernel, [*row_out, *row_in], [quads, quads])
+    col_in = swap(col_out, 1)
     packed, direction = call(
         wide_merge_kernel,
-        [edges, offsets, left, right, from_left, from_right, cover, padded, sums],
+        [edges, offsets, *col_out, *col_in, cover, padded, sums],
         [packed_shape, field],
         [pltpu.VMEM((2, 2, whole, SIZE), F32)],
     )
     totals = reduce_all(packed, probe, place_in_group)
 
-    top, middle, bottom, sums, padded, probe = call(
+    row_out0, middle, row_out1, sums, padded, probe = call(
         next_kernel,
         [offsets, totals, padded, direction, probe, measured, right3, left3],
         [edge, quads, edge, sums_shape, field, planes],
         [pltpu.VMEM((2, 2, whole, SIZE), F32)],
     )
-    from_above = shift(bottom, 1, 0)
-    from_below = shift(top, -1, 0)
+    row_in = swap((row_out0, row_out1), 0)
     side = shape(2, HALF, SIZE)
     (cover,) = call(
         tile_cover_kernel, [near, probe], [shape(SIZE, SIZE)], [pltpu.VMEM((3 * SIZE, SIZE), F32)])
-    middle, left, right = call(
-        fold_kernel, [middle, from_above, from_below], [shape(2, SIZE, SIZE), side, side])
-    from_left = shift(right, 0, 1)
-    from_right = shift(left, 0, -1)
+    middle, *col_out = call(
+        fold_kernel, [middle, *row_in], [shape(2, SIZE, SIZE), side, side])
+    col_in = swap(col_out, 1)
     packed, direction = call(
         merge_kernel,
-        [near, middle, from_left, from_right, cover, padded, sums],
+        [near, middle, *col_in, cover, padded, sums],
         [packed_shape, shape(2, SIZE, SIZE)],
         [pltpu.VMEM((2, 3 * SIZE, SIZE), F32), pltpu.VMEM((2, SIZE, SIZE), F32)],
     )

time: 207 us -> 201 us (0.971)
  starting transfers between devices: 56.1 us -> 49 us
    all_to_all x1, starting transfers between devices: 22.6 us -> 17.1 us  [exchange(): return lax.all_to_all(block, axes, 0, 0, tiled=True)]
  transfers between devices with their start and end apart: 13 -> 13, of which waited for: 8 -> 5; matrix products, arithmetic and copies ran while one was open for 0% -> 0% of each run, Pallas kernels for 4% -> 4%
where the time goes in v8:
time: 201 us; the launch traced here: 200 us
  blocking collectives  96.3 us (48%)
  starting transfers between devices  49 us (24%)
  Pallas kernels  27.6 us (14%)
  waiting for transfers between devices  26.2 us (13%)
    all_to_all x5, blocking collectives, exchange(): return lax.all_to_all(block, axes, 0, 0, tiled=True)  96.3 us
    ppermute x12, starting transfers between devices, swap(): taken.append(lax.ppermute(block, ALL, route))  31.9 us
    pallas_call x16, Pallas kernels, call(): pl.pallas_call(kernel, in_specs=specs, out_specs=[smem if x.dtype == jnp....  27.6 us
    all_to_all x1, starting transfers between devices, exchange(): return lax.all_to_all(block, axes, 0, 0, tiled=True)  17.1 us
    ppermute x12, waiting for transfers between devices, swap(): taken.append(lax.ppermute(block, ALL, route))  13.9 us
    all_to_all x1, waiting for transfers between devices, exchange(): return lax.all_to_all(block, axes, 0, 0, tiled=True)  12.3 us
  transfers between devices with their start and end apart: 13, of which 5 were waited for; matrix products, arithmetic and copies ran while one was open for 0% of the time, Pallas kernels for 4%

profile of v8, /device:TPU:1, one launch (start us, length us, event | category | flops | bytes accessed | tf_op | source)
XLA Modules:
  0.0 200.2 jit_solution(623222996797251853)
XLA Ops:
  0.6 1.7 send_kernel.1
  2.3 4.5 %collective-permute-start.1 = (f32[2,72,128]{2,1,0:T(8,128)S(1)}, f32[2,72,128]{2,1,0:T(8,128)S(1)}, u32[]{:S(2)}, u32[]{:S(2)}) collective-permute-start(f32[2,72,128]{2,1,0:T(8,128)S(1)} %get-tuple-element.35), channel_id=1, source_target_pairs={{32,64},{33,65},{34,66},{35,67},{36,68},{37,69},{38,70},{39,71},{4... | collective-permute-start | bytes 221192 | tf_op jit(solution)/shard_map/ppermute | solution.py:612
  6.8 4.9 %collective-permute-start = (f32[2,72,128]{2,1,0:T(8,128)S(1)}, f32[2,72,128]{2,1,0:T(8,128)S(1)}, u32[]{:S(2)}, u32[]{:S(2)}) collective-permute-start(f32[2,72,128]{2,1,0:T(8,128)S(1)} %get-tuple-element.34.mine), channel_id=1, source_target_pairs={{0,32},{1,33},{2,34},{3,35},{4,36},{5,37},{6,38},{7,39},{8,40},{9,... | collective-permute-start | bytes 221192 | tf_op jit(solution)/shard_map/ppermute | solution.py:612
  11.8 0.9 collective-permute-done.row_in0
  12.8 1.9 collective-permute-start.2
  14.7 0.7 collective-permute-start.3
  15.4 1.5 stage_kernel.1
  17.0 2.6 %collective-permute-done.2.col_in0 = f32[2,136,128]{2,1,0:T(8,128)S(1)} collective-permute-done((f32[2,136,128]{2,1,0:T(8,128)S(1)}, f32[2,136,128]{2,1,0:T(8,128)S(1)}, u32[]{:S(2)}, u32[]{:S(2)}) %collective-permute-start.2) | collective-permute-done | bytes 139296 | tf_op jit(solution)/shard_map/ppermute | solution.py:612
  19.6 5.2 %first_kernel.1 = (f32[2,2,128,128]{3,2,1,0:T(8,128)S(1)}, f32[2,2,128,128]{3,2,1,0:T(8,128)S(1)}, f32[5,128,128]{2,1,0:T(8,128)S(1)}, f32[2,2,256,128]{3,2,1,0:T(8,128)S(1)}) custom-call(s32[2,2,8]{2,1,0:T(2,128)S(1)} %get-tuple-element.41.offsets, f32[2,72,128]{2,1,0:T(8,128)S(1)} %collective-permute-done.row_in0, ...), custom_call_target="tpu_custom_call" | custom-call | tf_op jit(solution)/shard_map/first_kernel/pallas_call | solution.py:591
  24.8 3.1 %collective-permute-start.4 = (f32[2,2,128,128]{3,2,1,0:T(8,128)S(1)}, f32[2,2,128,128]{3,2,1,0:T(8,128)S(1)}, u32[]{:S(2)}, u32[]{:S(2)}) collective-permute-start(f32[2,2,128,128]{3,2,1,0:T(8,128)S(1)} %get-tuple-element.45.row_out0), channel_id=1, source_target_pairs={{0,32},{1,33},{2,34},{3,35},{4,36},{5,37},{6,38},{7,39},{8,40},{9,... | collective-permute-start | bytes 786440 | tf_op jit(solution)/shard_map/ppermute | solution.py:612
  27.8 1.9 collective-permute-start.5
  29.9 5.7 %collective-permute-done.5.row_in1 = f32[2,2,128,128]{3,2,1,0:T(8,128)S(1)} collective-permute-done((f32[2,2,128,128]{3,2,1,0:T(8,128)S(1)}, f32[2,2,128,128]{3,2,1,0:T(8,128)S(1)}, u32[]{:S(2)}, u32[]{:S(2)}) %collective-permute-start.5) | collective-permute-done | bytes 262176 | tf_op jit(solution)/shard_map/ppermute | solution.py:612
  35.6 6.2 %collective-permute-start.6 = (f32[2,2,128,128]{3,2,1,0:T(8,128)S(1)}, f32[2,2,128,128]{3,2,1,0:T(8,128)S(1)}, u32[]{:S(2)}, u32[]{:S(2)}) collective-permute-start(f32[2,2,128,128]{3,2,1,0:T(8,128)S(1)} %get-tuple-element.47.col_out0), channel_id=1, source_target_pairs={{0,1},{1,0},{2,3},{3,2},{4,5},{5,4},{6,7},{7,6},{8,9},{9,8},{10,11... | collective-permute-start | bytes 786440 | tf_op jit(solution)/shard_map/ppermute | solution.py:612
  41.9 0.7 collective-permute-start.7
  42.6 4.0 %cover_kernel.1 = (f32[2,256,128]{2,1,0:T(8,128)S(1)}, s32[80,2]{1,0:T(8,128)S(1)}) custom-call(s32[24,128]{1,0:T(8,128)S(1)} %maximum_convert_fusion.others, f32[2,2,128,128]{3,2,1,0:T(8,128)S(1)} %copy-done), custom_call_target="tpu_custom_call" | custom-call | tf_op jit(solution)/shard_map/cover_kernel/pallas_call | solution.py:591
  46.7 1.3 wide_merge_kernel.1
  47.9 26.7 %all_to_all.30.parts = f32[32,4,8,128]{3,2,1,0:T(8,128)S(1)} all-to-all(f32[32,4,8,128]{3,2,1,0:T(8,128)S(1)} %bitcast.19), channel_id=1, replica_groups=mesh['yl'=2,'x'=4,'c'=2,'yh'=4,'zh'=4,'zl'=2] {'yl','x','c','zl'}, dimensions={0} | all-to-all | bytes 1048576 | tf_op jit(solution)/shard_map/all_to_all | solution.py:617
  74.6 0.8 reduce_kernel.2
  75.4 17.1 %all-to-all-start.1 = ((f32[16,4,8,128]{3,2,1,0:T(8,128)}), f32[16,4,8,128]{3,2,1,0:T(8,128)S(1)}, u32[]{:S(2)}, u32[]{:S(2)}) async-start(f32[16,4,8,128]{3,2,1,0:T(8,128)} %reduce_kernel.2), calls=%async_computation.1 | async-start | bytes 524288 | tf_op jit(solution)/shard_map/all_to_all | solution.py:617
  92.6 12.3 %all-to-all-done.1.parts = f32[16,4,8,128]{3,2,1,0:T(8,128)S(1)} async-done(((f32[16,4,8,128]{3,2,1,0:T(8,128)}), f32[16,4,8,128]{3,2,1,0:T(8,128)S(1)}, u32[]{:S(2)}, u32[]{:S(2)}) %all-to-all-start.1) | async-done | bytes 262176 | tf_op jit(solution)/shard_map/all_to_all | solution.py:617
  105.6 15.5 %all_to_all.31 = f32[32,3,8,128]{3,2,1,0:T(8,128)S(1)} all-to-all(f32[32,3,8,128]{3,2,1,0:T(8,128)S(1)} %strip_kernel.2), channel_id=1, replica_groups=mesh['yl'=2,'x'=4,'c'=2,'yh'=4,'zh'=4,'zl'=2] {'yl','x','c','zl'}, dimensions={0} | all-to-all | bytes 786432 | tf_op jit(solution)/shard_map/all_to_all | solution.py:617
  121.0 5.3 %next_kernel.1 = (f32[2,2,64,128]{3,2,1,0:T(8,128)S(1)}, f32[2,2,128,128]{3,2,1,0:T(8,128)S(1)}, f32[2,2,64,128]{3,2,1,0:T(8,128)S(1)}, f32[5,128,128]{2,1,0:T(8...) custom-call(s32[2,2,8]{2,1,0:T(2,128)S(1)} %get-tuple-element.41.offsets, ...), custom_call_target="tpu_custom_call" | custom-call | tf_op jit(solution)/shard_map/next_kernel/pallas_call | solution.py:591
  126.3 3.1 %collective-permute-start.8 = (f32[2,2,64,128]{3,2,1,0:T(8,128)S(1)}, f32[2,2,64,128]{3,2,1,0:T(8,128)S(1)}, u32[]{:S(2)}, u32[]{:S(2)}) collective-permute-start(f32[2,2,64,128]{3,2,1,0:T(8,128)S(1)} %get-tuple-element.55), channel_id=1, source_target_pairs={{0,32},{1,33},{2,34},{3,35},{4,36},{5,37},{6,38},{7,39},{8,40},{9,... | collective-permute-start | bytes 393224 | tf_op jit(solution)/shard_map/ppermute | solution.py:612
  129.4 1.9 collective-permute-start.9
  131.4 4.6 %collective-permute-done.9.row_in1 = f32[2,2,64,128]{3,2,1,0:T(8,128)S(1)} collective-permute-done((f32[2,2,64,128]{3,2,1,0:T(8,128)S(1)}, f32[2,2,64,128]{3,2,1,0:T(8,128)S(1)}, u32[]{:S(2)}, u32[]{:S(2)}) %collective-permute-start.9) | collective-permute-done | bytes 131104 | tf_op jit(solution)/shard_map/ppermute | solution.py:612
  136.2 2.3 %collective-permute-start.10 = (f32[2,64,128]{2,1,0:T(8,128)S(1)}, f32[2,64,128]{2,1,0:T(8,128)S(1)}, u32[]{:S(2)}, u32[]{:S(2)}) collective-permute-start(f32[2,64,128]{2,1,0:T(8,128)S(1)} %get-tuple-element.58), channel_id=1, source_target_pairs={{0,1},{1,0},{2,3},{3,2},{4,5},{5,4},{6,7},{7,6},{8,9},{9,8},{10,11... | collective-permute-start | bytes 196616 | tf_op jit(solution)/shard_map/ppermute | solution.py:612
  139.1 2.2 %tile_cover_kernel.1.cover = f32[128,128]{1,0:T(8,128)S(1)} custom-call(s32[80,2]{1,0:T(8,128)S(1)} %get-tuple-element.40.near, f32[2,2,128,128]{3,2,1,0:T(8,128)S(1)} %get-tuple-element.60.probe), custom_call_target="tpu_custom_call" | custom-call | tf_op jit(solution)/shard_map/tile_cover_kernel/pallas_call | solution.py:591
  141.4 2.9 %merge_kernel.1 = (f32[16,2,4,8,128]{4,3,2,1,0:T(8,128)S(1)}, f32[2,128,128]{2,1,0:T(8,128)S(1)}) custom-call(s32[80,2]{1,0:T(8,128)S(1)} %get-tuple-element.40.near, f32[2,128,128]{2,1,0:T(8,128)S(1)} %get-tuple-element.57.tile, f32[2,64,128]{2,1,0:T(8,128)S(1)} %collective-permute-done.10.col_in0, f32[2,64,128]{2,1,0:T(8,128)S(1)} %collective-permute-done.11.col_in1, ...), custom_call_target="tpu_custom_call" | custom-call | tf_op jit(solution)/shard_map/merge_kernel/pallas_call | solution.py:591
  144.3 18.8 %all_to_all.32.parts = f32[32,4,8,128]{3,2,1,0:T(8,128)S(1)} all-to-all(f32[32,4,8,128]{3,2,1,0:T(8,128)S(1)} %bitcast.20), channel_id=1, replica_groups=mesh['yl'=2,'x'=4,'c'=2,'yh'=4,'zh'=4,'zl'=2] {'yl','x','c','zl'}, dimensions={0} | all-to-all | bytes 1048576 | tf_op jit(solution)/shard_map/all_to_all | solution.py:617
  163.2 19.8 %all_to_all.33.parts = f32[16,4,8,128]{3,2,1,0:T(8,128)S(1)} all-to-all(f32[16,4,8,128]{3,2,1,0:T(8,128)S(1)} %reduce_kernel.3), channel_id=1, replica_groups=mesh['yl'=2,'x'=4,'c'=2,'yh'=4,'zh'=4,'zl'=2] {'zh','yh'}, dimensions={0} | all-to-all | bytes 524288 | tf_op jit(solution)/shard_map/all_to_all | solution.py:617
  183.7 15.5 %all_to_all.34 = f32[32,3,8,128]{3,2,1,0:T(8,128)S(1)} all-to-all(f32[32,3,8,128]{3,2,1,0:T(8,128)S(1)} %strip_kernel.3), channel_id=1, replica_groups=mesh['yl'=2,'x'=4,'c'=2,'yh'=4,'zh'=4,'zl'=2] {'yl','x','c','zl'}, dimensions={0} | all-to-all | bytes 786432 | tf_op jit(solution)/shard_map/all_to_all | solution.py:617
  199.1 1.0 last_kernel.1
  (22 shorter events, 2.6 us)
Async XLA Ops:
  2.3 9.5 %collective-permute-start.1 = (f32[2,72,128]{2,1,0:T(8,128)S(1)}, f32[2,72,128]{2,1,0:T(8,128)S(1)}, u32[]{:S(2)}, u32[]{:S(2)}) collective-permute-start(f32[2,72,128]{2,1,0:T(8,128)S(1)} %get-tuple-element.35), channel_id=1, source_target_pairs={{32,64},{33,65},{34,66},{35,67},{36,68},{37,69},{38,70},{39,71},{4... | collective-permute-start | bytes 221192 | tf_op jit(solution)/shard_map/ppermute | solution.py:612
  6.8 5.8 %collective-permute-start = (f32[2,72,128]{2,1,0:T(8,128)S(1)}, f32[2,72,128]{2,1,0:T(8,128)S(1)}, u32[]{:S(2)}, u32[]{:S(2)}) collective-permute-start(f32[2,72,128]{2,1,0:T(8,128)S(1)} %get-tuple-element.34.mine), channel_id=1, source_target_pairs={{0,32},{1,33},{2,34},{3,35},{4,36},{5,37},{6,38},{7,39},{8,40},{9,... | collective-permute-start | bytes 221192 | tf_op jit(solution)/shard_map/ppermute | solution.py:612
  12.8 6.8 %collective-permute-start.2 = (f32[2,136,128]{2,1,0:T(8,128)S(1)}, f32[2,136,128]{2,1,0:T(8,128)S(1)}, u32[]{:S(2)}, u32[]{:S(2)}) collective-permute-start(f32[2,136,128]{2,1,0:T(8,128)S(1)} %get-tuple-element.37), channel_id=1, source_target_pairs={{0,1},{1,0},{2,3},{3,2},{4,5},{5,4},{6,7},{7,6},{8,9},{9,8},{10,11... | collective-permute-start | bytes 417800 | tf_op jit(solution)/shard_map/ppermute | solution.py:612
  14.7 4.9 %collective-permute-start.3 = (f32[2,136,128]{2,1,0:T(8,128)S(1)}, f32[2,136,128]{2,1,0:T(8,128)S(1)}, u32[]{:S(2)}, u32[]{:S(2)}) collective-permute-start(f32[2,136,128]{2,1,0:T(8,128)S(1)} %get-tuple-element.39), channel_id=1, source_target_pairs={{1,2},{2,1},{3,4},{4,3},{5,6},{6,5},{7,8},{8,7},{9,10},{10,9},{11,... | collective-permute-start | bytes 417800 | tf_op jit(solution)/shard_map/ppermute | solution.py:612
  15.4 4.2 %copy-start = (f32[2,2,128,128]{3,2,1,0:T(8,128)S(1)}, f32[2,2,128,128]{3,2,1,0:T(8,128)}, u32[]{:S(2)}) copy-start(f32[2,2,128,128]{3,2,1,0:T(8,128)} %probe.7) | copy-start | bytes 786436
  24.8 5.1 %collective-permute-start.4 = (f32[2,2,128,128]{3,2,1,0:T(8,128)S(1)}, f32[2,2,128,128]{3,2,1,0:T(8,128)S(1)}, u32[]{:S(2)}, u32[]{:S(2)}) collective-permute-start(f32[2,2,128,128]{3,2,1,0:T(8,128)S(1)} %get-tuple-element.45.row_out0), channel_id=1, source_target_pairs={{0,32},{1,33},{2,34},{3,35},{4,36},{5,37},{6,38},{7,39},{8,40},{9,... | collective-permute-start | bytes 786440 | tf_op jit(solution)/shard_map/ppermute | solution.py:612
  27.8 7.7 %collective-permute-start.5 = (f32[2,2,128,128]{3,2,1,0:T(8,128)S(1)}, f32[2,2,128,128]{3,2,1,0:T(8,128)S(1)}, u32[]{:S(2)}, u32[]{:S(2)}) collective-permute-start(f32[2,2,128,128]{3,2,1,0:T(8,128)S(1)} %get-tuple-element.46.row_out1), channel_id=1, source_target_pairs={{32,64},{33,65},{34,66},{35,67},{36,68},{37,69},{38,70},{39,71},{4... | collective-permute-start | bytes 786440 | tf_op jit(solution)/shard_map/ppermute | solution.py:612
  35.6 11.0 %collective-permute-start.6 = (f32[2,2,128,128]{3,2,1,0:T(8,128)S(1)}, f32[2,2,128,128]{3,2,1,0:T(8,128)S(1)}, u32[]{:S(2)}, u32[]{:S(2)}) collective-permute-start(f32[2,2,128,128]{3,2,1,0:T(8,128)S(1)} %get-tuple-element.47.col_out0), channel_id=1, source_target_pairs={{0,1},{1,0},{2,3},{3,2},{4,5},{5,4},{6,7},{7,6},{8,9},{9,8},{10,11... | collective-permute-start | bytes 786440 | tf_op jit(solution)/shard_map/ppermute | solution.py:612
  41.9 4.8 %collective-permute-start.7 = (f32[2,2,128,128]{3,2,1,0:T(8,128)S(1)}, f32[2,2,128,128]{3,2,1,0:T(8,128)S(1)}, u32[]{:S(2)}, u32[]{:S(2)}) collective-permute-start(f32[2,2,128,128]{3,2,1,0:T(8,128)S(1)} %get-tuple-element.48.col_out1), channel_id=1, source_target_pairs={{1,2},{2,1},{3,4},{4,3},{5,6},{6,5},{7,8},{8,7},{9,10},{10,9},{11,... | collective-permute-start | bytes 786440 | tf_op jit(solution)/shard_map/ppermute | solution.py:612
  75.4 29.5 %all-to-all-start.1 = ((f32[16,4,8,128]{3,2,1,0:T(8,128)}), f32[16,4,8,128]{3,2,1,0:T(8,128)S(1)}, u32[]{:S(2)}, u32[]{:S(2)}) async-start(f32[16,4,8,128]{3,2,1,0:T(8,128)} %reduce_kernel.2), calls=%async_computation.1 | async-start | bytes 524288 | tf_op jit(solution)/shard_map/all_to_all | solution.py:617
  126.3 5.0 %collective-permute-start.8 = (f32[2,2,64,128]{3,2,1,0:T(8,128)S(1)}, f32[2,2,64,128]{3,2,1,0:T(8,128)S(1)}, u32[]{:S(2)}, u32[]{:S(2)}) collective-permute-start(f32[2,2,64,128]{3,2,1,0:T(8,128)S(1)} %get-tuple-element.55), channel_id=1, source_target_pairs={{0,32},{1,33},{2,34},{3,35},{4,36},{5,37},{6,38},{7,39},{8,40},{9,... | collective-permute-start | bytes 393224 | tf_op jit(solution)/shard_map/ppermute | solution.py:612
  129.4 6.6 %collective-permute-start.9 = (f32[2,2,64,128]{3,2,1,0:T(8,128)S(1)}, f32[2,2,64,128]{3,2,1,0:T(8,128)S(1)}, u32[]{:S(2)}, u32[]{:S(2)}) collective-permute-start(f32[2,2,64,128]{3,2,1,0:T(8,128)S(1)} %get-tuple-element.56), channel_id=1, source_target_pairs={{32,64},{33,65},{34,66},{35,67},{36,68},{37,69},{38,70},{39,71},{4... | collective-permute-start | bytes 393224 | tf_op jit(solution)/shard_map/ppermute | solution.py:612
  136.2 5.2 %collective-permute-start.10 = (f32[2,64,128]{2,1,0:T(8,128)S(1)}, f32[2,64,128]{2,1,0:T(8,128)S(1)}, u32[]{:S(2)}, u32[]{:S(2)}) collective-permute-start(f32[2,64,128]{2,1,0:T(8,128)S(1)} %get-tuple-element.58), channel_id=1, source_target_pairs={{0,1},{1,0},{2,3},{3,2},{4,5},{5,4},{6,7},{7,6},{8,9},{9,8},{10,11... | collective-permute-start | bytes 196616 | tf_op jit(solution)/shard_map/ppermute | solution.py:612
  138.5 2.9 %collective-permute-start.11 = (f32[2,64,128]{2,1,0:T(8,128)S(1)}, f32[2,64,128]{2,1,0:T(8,128)S(1)}, u32[]{:S(2)}, u32[]{:S(2)}) collective-permute-start(f32[2,64,128]{2,1,0:T(8,128)S(1)} %get-tuple-element.59), channel_id=1, source_target_pairs={{1,2},{2,1},{3,4},{4,3},{5,6},{6,5},{7,8},{8,7},{9,10},{10,9},{11,... | collective-permute-start | bytes 196616 | tf_op jit(solution)/shard_map/ppermute | solution.py:612

commit v9 on v8

--- a/solution.py
+++ b/solution.py
@@ -118,23 +118,23 @@
     return (line >= row_low) & (line < row_high) & (lane >= col_low) & (lane < col_high)
 
 
-def evens():
-    return tuple(lax.axis_index(axis) == 0 for axis in (ROW[-1], COL[-1]))
-
-
-def sides(even, first, second):
-    return jnp.where(even, second, first), jnp.where(even, first, second)
+def odds():
+    return tuple(lax.axis_index(axis) == 1 for axis in (ROW[-1], COL[-1]))
+
+
+def sides(odd, first, second):
+    return jnp.where(odd, second, first), jnp.where(odd, first, second)
 
 
 def pad_field(rows_in, own, cols_in, store):
     low = low_lanes(HALF)
-    even_row, even_col = evens()
-    for c in range(2):
-        above, below = sides(even_row, *(x[c, :HALF] for x in rows_in))
+    odd_row, odd_col = odds()
+    for c in range(2):
+        above, below = sides(odd_row, *(x[c, :HALF] for x in rows_in))
         strips = (above, own[c, :HALF], own[c, HALF:], below)
         for k in range(4):
             half = slice(HALF * (k % 2), HALF * (k % 2 + 1))
-            left, right = sides(even_col, *(x[c, half] for x in cols_in))
+            left, right = sides(odd_col, *(x[c, half] for x in cols_in))
             if k < 2:
                 right = pltpu.roll(right, HALF, 1)
             else:
@@ -147,8 +147,8 @@
 
 def send_kernel(raw, own, tile, row_out0, row_out1, offsets, sems):
     strip = pl.ds(0, HALF)
-    even_row, _ = evens()
-    starts = [pl.multiple_of(jnp.where(even_row == (k == 0), HALF, 0), HALF) for k in range(2)]
+    odd_row, _ = odds()
+    starts = [pl.multiple_of(jnp.where(odd_row == (k == 0), HALF, 0), HALF) for k in range(2)]
     first = pltpu.make_async_copy(raw, offsets, sems.at[3])
     first.start()
     copies = [
@@ -180,17 +180,17 @@
 
 def pack_kernel(row_in0, row_in1, own, mine, col_out0, col_out1, codes):
     low = low_lanes(HALF)
-    even_row, even_col = evens()
-    for c in range(2):
-        above, below = sides(even_row, row_in0[c, :HALF], row_in1[c, :HALF])
+    odd_row, odd_col = odds()
+    for c in range(2):
+        above, below = sides(odd_row, row_in0[c, :HALF], row_in1[c, :HALF])
         strips = (above, own[c, :HALF], own[c, HALF:], below)
         for k in range(2):
             rows = slice(HALF * k, HALF * (k + 1))
             to_left = pack_low(low, strips[k], strips[k + 2])
             to_right = pack_high(low, strips[k], strips[k + 2])
-            col_out0[c, rows] = jnp.where(even_col, to_right, to_left)
-            col_out1[c, rows] = jnp.where(even_col, to_left, to_right)
-    above, below = sides(even_row, row_in0[0, HALF:], row_in1[0, HALF:])
+            col_out0[c, rows] = jnp.where(odd_col, to_right, to_left)
+            col_out1[c, rows] = jnp.where(odd_col, to_left, to_right)
+    above, below = sides(odd_row, row_in0[0, HALF:], row_in1[0, HALF:])
     code = mine[0, HALF:] + pltpu.roll(above, 1, 0) + pltpu.roll(below, 2, 0)
     for c in range(2):
         col_out0[c, SIZE:] = code
@@ -261,17 +261,17 @@
 
     pad_field((row_in0, row_in1), own, (col_in0, col_in1), store)
     sweep(0, offsets, padded, probe, measured, right3, left3, sums, accum)
-    even_row, _ = evens()
+    odd_row, _ = odds()
     for c in range(2):
         for h in range(2):
             top, bottom = accum[c, h, :SIZE], accum[c, h, SIZE:]
-            row_out0[c, h] = jnp.where(even_row, bottom, top)
-            row_out1[c, h] = jnp.where(even_row, top, bottom)
+            row_out0[c, h] = jnp.where(odd_row, bottom, top)
+            row_out1[c, h] = jnp.where(odd_row, top, bottom)
 
 
 def offset_of(others, batch, across, down, j, d):
-    _, even_col = evens()
-    tile = jnp.where(even_col, 2 - across, across)
+    _, odd_col = odds()
+    tile = jnp.where(odd_col, 2 - across, across)
     return others[TILES * tile + (1, 0, 2)[down], (batch * 2 + d) * COUNT + j] - MARK
 
 
@@ -315,17 +315,17 @@
 
 
 def wide_fold_kernel(row_out0, row_out1, row_in0, row_in1, col_out0, col_out1):
-    even_row, even_col = evens()
+    odd_row, odd_col = odds()
     for c in range(2):
         top, bottom = [], []
         for h in range(2):
             upper, lower = sides(
-                even_row, row_out0[c, h] + row_in0[c, h], row_out1[c, h] + row_in1[c, h])
+                odd_row, row_out0[c, h] + row_in0[c, h], row_out1[c, h] + row_in1[c, h])
             top.append(upper)
             bottom.append(lower)
         for v, (left, right) in enumerate((top, bottom)):
-            col_out0[v, c] = jnp.where(even_col, right, left)
-            col_out1[v, c] = jnp.where(even_col, left, right)
+            col_out0[v, c] = jnp.where(odd_col, right, left)
+            col_out1[v, c] = jnp.where(odd_col, left, right)
 
 
 def pack_planes(packed, planes):
@@ -353,13 +353,13 @@
 def wide_merge_kernel(edges, offsets, col_out0, col_out1, col_in0, col_in1, cover, padded, sums,
                       packed, direction, product):
     limits = bounds(edges)
-    _, even_col = evens()
+    _, odd_col = odds()
     a11 = jnp.zeros((1, SIZE), F32)
     b1 = jnp.zeros((1, SIZE), F32)
     for v in range(2):
         rows = slice(v * SIZE, (v + 1) * SIZE)
         mine_rows = lax.broadcasted_iota(jnp.int32, (SIZE, SIZE), 0) + v * SIZE
-        totals = [sides(even_col, col_out0[v, c] + col_in0[v, c], col_out1[v, c] + col_in1[v, c]) for c in range(2)]
+        totals = [sides(odd_col, col_out0[v, c] + col_in0[v, c], col_out1[v, c] + col_in1[v, c]) for c in range(2)]
         for h in range(2):
             light = cover[h, rows]
             inverse = jnp.where(inside(limits, v * SIZE, h * SIZE), 1.0 / (light + 1.0), 0.0)
@@ -383,19 +383,19 @@
 
 def fold_kernel(middle, row_in0, row_in1, tile, col_out0, col_out1):
     low = low_lanes(HALF)
-    even_row, even_col = evens()
+    odd_row, odd_col = odds()
     for k in range(2):
         upper, lower = [], []
         for h in range(2):
-            above, below = sides(even_row, row_in0[k, h], row_in1[k, h])
+            above, below = sides(odd_row, row_in0[k, h], row_in1[k, h])
             upper.append(middle[k, h, :HALF] + above)
             lower.append(middle[k, h, HALF:] + below)
         tile[k, :HALF] = join(low, *upper)
         tile[k, HALF:] = join(low, *lower)
         to_left = pack_low(low, upper[0], lower[0])
         to_right = pack_high(low, upper[1], lower[1])
-        col_out0[k] = jnp.where(even_col, to_right, to_left)
-        col_out1[k] = jnp.where(even_col, to_left, to_right)
+        col_out0[k] = jnp.where(odd_col, to_right, to_left)
+        col_out1[k] = jnp.where(odd_col, to_left, to_right)
 
 
 def tile_cover_kernel(near, probe, cover, light):
@@ -424,7 +424,7 @@
                  packed, direction, product, overlap):
     low = low_lanes(HALF)
     lane = lanes()
-    _, even_col = evens()
+    _, odd_col = odds()
     a11 = jnp.zeros((1, SIZE), F32)
     b1 = jnp.zeros((1, SIZE), F32)
     for c in range(2):
@@ -435,7 +435,7 @@
         rows = slice(HALF * v, HALF * (v + 1))
         full = []
         for k in range(2):
-            left, right = sides(even_col, col_in0[k], col_in1[k])
+            left, right = sides(odd_col, col_in0[k], col_in1[k])
             if v == 0:
                 right = pltpu.roll(right, HALF, 1)
             else:
@@ -561,12 +561,12 @@
     new_padded[...] = padded[...] + step * direction[...]
     sweep(1, offsets, new_padded, new_probe, measured, right3, left3, sums, accum)
     middle[...] = accum[:, :, HALF : HALF + SIZE]
-    even_row, _ = evens()
+    odd_row, _ = odds()
     for c in range(2):
         for h in range(2):
             top, bottom = accum[c, h, :HALF], accum[c, h, HALF + SIZE :]
-            row_out0[c, h] = jnp.where(even_row, bottom, top)
-            row_out1[c, h] = jnp.where(even_row, top, bottom)
+            row_out0[c, h] = jnp.where(odd_row, bottom, top)
+            row_out1[c, h] = jnp.where(odd_row, top, bottom)
 
 
 def last_kernel(totals, padded, direction, probe, new_obj, new_probe, gradient):
@@ -606,7 +606,7 @@
         route = []
         for here in itertools.product(*(range(n) for n in counts)):
             there = list(here)
-            there[along] += 1 if here[along] % 2 == k else -1
+            there[along] += 1 if here[along] % 2 != k else -1
             if 0 <= there[along] < counts[along]:
                 route.append((here[0] * counts[1] + here[1], there[0] * counts[1] + there[1]))
         taken.append(lax.ppermute(block, ALL, route))
@@ -651,7 +651,7 @@
         [pltpu.SemaphoreType.DMA((4,))], in_hbm=(0, 1))
     row_in = swap(row_out, 0)
     *col_out, codes = call(
-        pack_kernel, [*row_in, tile, row_out[0]], [side, side, shape(TILES, SIZE)])
+        pack_kernel, [*row_in, tile, row_out[1]], [side, side, shape(TILES, SIZE)])
     col_in = swap(col_out, 1)
     staged = [measured, right3, left3]
     measured, right3, left3 = call(

time: 201 us -> 192 us (0.955)
  blocking collectives: 96.3 us -> 85.9 us
  starting transfers between devices: 49 us -> 55.2 us
  waiting for transfers between devices: 26.2 us -> 21.9 us
    all_to_all x5, blocking collectives: 96.3 us -> 85.9 us  [exchange(): return lax.all_to_all(block, axes, 0, 0, tiled=True)]
    ppermute x12, starting transfers between devices: 31.9 us -> 39.1 us  [swap(): taken.append(lax.ppermute(block, ALL, route))]
    ppermute x12, waiting for transfers between devices: 13.9 us -> 9.6 us  [swap(): taken.append(lax.ppermute(block, ALL, route))]
  transfers between devices with their start and end apart: 13 -> 13, of which waited for: 5 -> 7; matrix products, arithmetic and copies ran while one was open for 0% -> 0% of each run, Pallas kernels for 4% -> 4%
where the time goes in v9:
time: 192 us; the launch traced here: 191 us
  blocking collectives  85.9 us (45%)
  starting transfers between devices  55.2 us (29%)
  Pallas kernels  27.2 us (14%)
  waiting for transfers between devices  21.9 us (11%)
    all_to_all x5, blocking collectives, exchange(): return lax.all_to_all(block, axes, 0, 0, tiled=True)  85.9 us
    ppermute x12, starting transfers between devices, swap(): taken.append(lax.ppermute(block, ALL, route))  39.1 us
    pallas_call x16, Pallas kernels, call(): pl.pallas_call(kernel, in_specs=specs, out_specs=[smem if x.dtype == jnp....  27.2 us
    all_to_all x1, starting transfers between devices, exchange(): return lax.all_to_all(block, axes, 0, 0, tiled=True)  16 us
    all_to_all x1, waiting for transfers between devices, exchange(): return lax.all_to_all(block, axes, 0, 0, tiled=True)  12.3 us
    ppermute x12, waiting for transfers between devices, swap(): taken.append(lax.ppermute(block, ALL, route))  9.6 us
  transfers between devices with their start and end apart: 13, of which 7 were waited for; matrix products, arithmetic and copies ran while one was open for 0% of the time, Pallas kernels for 4%

profile of v9, /device:TPU:1, one launch (start us, length us, event | category | flops | bytes accessed | tf_op | source)
XLA Modules:
  0.0 191.3 jit_solution(14648307607405903791)
XLA Ops:
  0.6 1.7 send_kernel.1
  2.3 4.5 %collective-permute-start = (f32[2,72,128]{2,1,0:T(8,128)S(1)}, f32[2,72,128]{2,1,0:T(8,128)S(1)}, u32[]{:S(2)}, u32[]{:S(2)}) collective-permute-start(f32[2,72,128]{2,1,0:T(8,128)S(1)} %get-tuple-element.34), channel_id=1, source_target_pairs={{32,64},{33,65},{34,66},{35,67},{36,68},{37,69},{38,70},{39,71},{4... | collective-permute-start | bytes 221192 | tf_op jit(solution)/shard_map/ppermute | solution.py:612
  6.8 4.9 %collective-permute-start.1 = (f32[2,72,128]{2,1,0:T(8,128)S(1)}, f32[2,72,128]{2,1,0:T(8,128)S(1)}, u32[]{:S(2)}, u32[]{:S(2)}) collective-permute-start(f32[2,72,128]{2,1,0:T(8,128)S(1)} %get-tuple-element.35.mine), channel_id=1, source_target_pairs={{0,32},{1,33},{2,34},{3,35},{4,36},{5,37},{6,38},{7,39},{8,40},{9,... | collective-permute-start | bytes 221192 | tf_op jit(solution)/shard_map/ppermute | solution.py:612
  11.8 0.9 collective-permute-done.1.row_in1
  13.5 4.7 %collective-permute-start.3 = (f32[2,136,128]{2,1,0:T(8,128)S(1)}, f32[2,136,128]{2,1,0:T(8,128)S(1)}, u32[]{:S(2)}, u32[]{:S(2)}) collective-permute-start(f32[2,136,128]{2,1,0:T(8,128)S(1)} %get-tuple-element.39), channel_id=1, source_target_pairs={{0,1},{1,0},{2,3},{3,2},{4,5},{5,4},{6,7},{7,6},{8,9},{9,8},{10,11... | collective-permute-start | bytes 417800 | tf_op jit(solution)/shard_map/ppermute | solution.py:612
  18.2 1.5 stage_kernel.1
  19.7 2.1 %collective-permute-done.3.col_in1 = f32[2,136,128]{2,1,0:T(8,128)S(1)} collective-permute-done((f32[2,136,128]{2,1,0:T(8,128)S(1)}, f32[2,136,128]{2,1,0:T(8,128)S(1)}, u32[]{:S(2)}, u32[]{:S(2)}) %collective-permute-start.3) | collective-permute-done | bytes 139296 | tf_op jit(solution)/shard_map/ppermute | solution.py:612
  21.8 5.2 %first_kernel.1 = (f32[2,2,128,128]{3,2,1,0:T(8,128)S(1)}, f32[2,2,128,128]{3,2,1,0:T(8,128)S(1)}, f32[5,128,128]{2,1,0:T(8,128)S(1)}, f32[2,2,256,128]{3,2,1,0:T(8,128)S(1)}) custom-call(s32[2,2,8]{2,1,0:T(2,128)S(1)} %get-tuple-element.41.offsets, f32[2,72,128]{2,1,0:T(8,128)S(1)} %collective-permute-done.row_in0, ...), custom_call_target="tpu_custom_call" | custom-call | tf_op jit(solution)/shard_map/first_kernel/pallas_call | solution.py:591
  27.0 4.0 %collective-permute-start.4 = (f32[2,2,128,128]{3,2,1,0:T(8,128)S(1)}, f32[2,2,128,128]{3,2,1,0:T(8,128)S(1)}, u32[]{:S(2)}, u32[]{:S(2)}) collective-permute-start(f32[2,2,128,128]{3,2,1,0:T(8,128)S(1)} %get-tuple-element.45.row_out0), channel_id=1, source_target_pairs={{32,64},{33,65},{34,66},{35,67},{36,68},{37,69},{38,70},{39,71},{4... | collective-permute-start | bytes 786440 | tf_op jit(solution)/shard_map/ppermute | solution.py:612
  30.9 1.9 %collective-permute-start.5 = (f32[2,2,128,128]{3,2,1,0:T(8,128)S(1)}, f32[2,2,128,128]{3,2,1,0:T(8,128)S(1)}, u32[]{:S(2)}, u32[]{:S(2)}) collective-permute-start(f32[2,2,128,128]{3,2,1,0:T(8,128)S(1)} %get-tuple-element.46.row_out1), channel_id=1, source_target_pairs={{0,32},{1,33},{2,34},{3,35},{4,36},{5,37},{6,38},{7,39},{8,40},{9,... | collective-permute-start | bytes 786440 | tf_op jit(solution)/shard_map/ppermute | solution.py:612
  33.0 2.0 %collective-permute-done.4.row_in0 = f32[2,2,128,128]{3,2,1,0:T(8,128)S(1)} collective-permute-done((f32[2,2,128,128]{3,2,1,0:T(8,128)S(1)}, f32[2,2,128,128]{3,2,1,0:T(8,128)S(1)}, u32[]{:S(2)}, u32[]{:S(2)}) %collective-permute-start.4) | collective-permute-done | bytes 262176 | tf_op jit(solution)/shard_map/ppermute | solution.py:612
  35.1 0.7 collective-permute-start.6
  35.8 8.5 %collective-permute-start.7 = (f32[2,2,128,128]{3,2,1,0:T(8,128)S(1)}, f32[2,2,128,128]{3,2,1,0:T(8,128)S(1)}, u32[]{:S(2)}, u32[]{:S(2)}) collective-permute-start(f32[2,2,128,128]{3,2,1,0:T(8,128)S(1)} %get-tuple-element.48.col_out1), channel_id=1, source_target_pairs={{0,1},{1,0},{2,3},{3,2},{4,5},{5,4},{6,7},{7,6},{8,9},{9,8},{10,11... | collective-permute-start | bytes 786440 | tf_op jit(solution)/shard_map/ppermute | solution.py:612
  44.3 4.0 %cover_kernel.1 = (f32[2,256,128]{2,1,0:T(8,128)S(1)}, s32[80,2]{1,0:T(8,128)S(1)}) custom-call(s32[24,128]{1,0:T(8,128)S(1)} %maximum_convert_fusion.others, f32[2,2,128,128]{3,2,1,0:T(8,128)S(1)} %copy-done), custom_call_target="tpu_custom_call" | custom-call | tf_op jit(solution)/shard_map/cover_kernel/pallas_call | solution.py:591
  48.4 2.7 %collective-permute-done.7.col_in1 = f32[2,2,128,128]{3,2,1,0:T(8,128)S(1)} collective-permute-done((f32[2,2,128,128]{3,2,1,0:T(8,128)S(1)}, f32[2,2,128,128]{3,2,1,0:T(8,128)S(1)}, u32[]{:S(2)}, u32[]{:S(2)}) %collective-permute-start.7) | collective-permute-done | bytes 262176 | tf_op jit(solution)/shard_map/ppermute | solution.py:612
  51.1 1.3 wide_merge_kernel.1
  52.4 17.1 %all_to_all.30.parts = f32[32,4,8,128]{3,2,1,0:T(8,128)S(1)} all-to-all(f32[32,4,8,128]{3,2,1,0:T(8,128)S(1)} %bitcast.19), channel_id=1, replica_groups=mesh['yl'=2,'x'=4,'c'=2,'yh'=4,'zh'=4,'zl'=2] {'yl','x','c','zl'}, dimensions={0} | all-to-all | bytes 1048576 | tf_op jit(solution)/shard_map/all_to_all | solution.py:617
  69.5 0.8 reduce_kernel.2
  70.3 16.0 %all-to-all-start.1 = ((f32[16,4,8,128]{3,2,1,0:T(8,128)}), f32[16,4,8,128]{3,2,1,0:T(8,128)S(1)}, u32[]{:S(2)}, u32[]{:S(2)}) async-start(f32[16,4,8,128]{3,2,1,0:T(8,128)} %reduce_kernel.2), calls=%async_computation.1 | async-start | bytes 524288 | tf_op jit(solution)/shard_map/all_to_all | solution.py:617
  86.4 12.3 %all-to-all-done.1.parts = f32[16,4,8,128]{3,2,1,0:T(8,128)S(1)} async-done(((f32[16,4,8,128]{3,2,1,0:T(8,128)}), f32[16,4,8,128]{3,2,1,0:T(8,128)S(1)}, u32[]{:S(2)}, u32[]{:S(2)}) %all-to-all-start.1) | async-done | bytes 262176 | tf_op jit(solution)/shard_map/all_to_all | solution.py:617
  99.3 15.5 %all_to_all.31 = f32[32,3,8,128]{3,2,1,0:T(8,128)S(1)} all-to-all(f32[32,3,8,128]{3,2,1,0:T(8,128)S(1)} %strip_kernel.2), channel_id=1, replica_groups=mesh['yl'=2,'x'=4,'c'=2,'yh'=4,'zh'=4,'zl'=2] {'yl','x','c','zl'}, dimensions={0} | all-to-all | bytes 786432 | tf_op jit(solution)/shard_map/all_to_all | solution.py:617
  114.8 5.3 %next_kernel.1 = (f32[2,2,64,128]{3,2,1,0:T(8,128)S(1)}, f32[2,2,128,128]{3,2,1,0:T(8,128)S(1)}, f32[2,2,64,128]{3,2,1,0:T(8,128)S(1)}, f32[5,128,128]{2,1,0:T(8...) custom-call(s32[2,2,8]{2,1,0:T(2,128)S(1)} %get-tuple-element.41.offsets, ...), custom_call_target="tpu_custom_call" | custom-call | tf_op jit(solution)/shard_map/next_kernel/pallas_call | solution.py:591
  120.1 2.7 %collective-permute-start.8 = (f32[2,2,64,128]{3,2,1,0:T(8,128)S(1)}, f32[2,2,64,128]{3,2,1,0:T(8,128)S(1)}, u32[]{:S(2)}, u32[]{:S(2)}) collective-permute-start(f32[2,2,64,128]{3,2,1,0:T(8,128)S(1)} %get-tuple-element.55), channel_id=1, source_target_pairs={{32,64},{33,65},{34,66},{35,67},{36,68},{37,69},{38,70},{39,71},{4... | collective-permute-start | bytes 393224 | tf_op jit(solution)/shard_map/ppermute | solution.py:612
  122.8 1.9 %collective-permute-start.9 = (f32[2,2,64,128]{3,2,1,0:T(8,128)S(1)}, f32[2,2,64,128]{3,2,1,0:T(8,128)S(1)}, u32[]{:S(2)}, u32[]{:S(2)}) collective-permute-start(f32[2,2,64,128]{3,2,1,0:T(8,128)S(1)} %get-tuple-element.56), channel_id=1, source_target_pairs={{0,32},{1,33},{2,34},{3,35},{4,36},{5,37},{6,38},{7,39},{8,40},{9,... | collective-permute-start | bytes 393224 | tf_op jit(solution)/shard_map/ppermute | solution.py:612
  124.8 1.6 collective-permute-done.8.row_in0
  127.3 3.9 %collective-permute-start.11 = (f32[2,64,128]{2,1,0:T(8,128)S(1)}, f32[2,64,128]{2,1,0:T(8,128)S(1)}, u32[]{:S(2)}, u32[]{:S(2)}) collective-permute-start(f32[2,64,128]{2,1,0:T(8,128)S(1)} %get-tuple-element.59), channel_id=1, source_target_pairs={{0,1},{1,0},{2,3},{3,2},{4,5},{5,4},{6,7},{7,6},{8,9},{9,8},{10,11... | collective-permute-start | bytes 196616 | tf_op jit(solution)/shard_map/ppermute | solution.py:612
  131.2 2.1 %tile_cover_kernel.1.cover = f32[128,128]{1,0:T(8,128)S(1)} custom-call(s32[80,2]{1,0:T(8,128)S(1)} %get-tuple-element.40.near, f32[2,2,128,128]{3,2,1,0:T(8,128)S(1)} %get-tuple-element.60.probe), custom_call_target="tpu_custom_call" | custom-call | tf_op jit(solution)/shard_map/tile_cover_kernel/pallas_call | solution.py:591
  133.5 2.7 %merge_kernel.1 = (f32[16,2,4,8,128]{4,3,2,1,0:T(8,128)S(1)}, f32[2,128,128]{2,1,0:T(8,128)S(1)}) custom-call(s32[80,2]{1,0:T(8,128)S(1)} %get-tuple-element.40.near, f32[2,128,128]{2,1,0:T(8,128)S(1)} %get-tuple-element.57.tile, f32[2,64,128]{2,1,0:T(8,128)S(1)} %collective-permute-done.10.col_in0, f32[2,64,128]{2,1,0:T(8,128)S(1)} %collective-permute-done.11.col_in1, ...), custom_call_target="tpu_custom_call" | custom-call | tf_op jit(solution)/shard_map/merge_kernel/pallas_call | solution.py:591
  136.2 18.3 %all_to_all.32.parts = f32[32,4,8,128]{3,2,1,0:T(8,128)S(1)} all-to-all(f32[32,4,8,128]{3,2,1,0:T(8,128)S(1)} %bitcast.20), channel_id=1, replica_groups=mesh['yl'=2,'x'=4,'c'=2,'yh'=4,'zh'=4,'zl'=2] {'yl','x','c','zl'}, dimensions={0} | all-to-all | bytes 1048576 | tf_op jit(solution)/shard_map/all_to_all | solution.py:617
  154.6 19.5 %all_to_all.33.parts = f32[16,4,8,128]{3,2,1,0:T(8,128)S(1)} all-to-all(f32[16,4,8,128]{3,2,1,0:T(8,128)S(1)} %reduce_kernel.3), channel_id=1, replica_groups=mesh['yl'=2,'x'=4,'c'=2,'yh'=4,'zh'=4,'zl'=2] {'zh','yh'}, dimensions={0} | all-to-all | bytes 524288 | tf_op jit(solution)/shard_map/all_to_all | solution.py:617
  174.8 15.5 %all_to_all.34 = f32[32,3,8,128]{3,2,1,0:T(8,128)S(1)} all-to-all(f32[32,3,8,128]{3,2,1,0:T(8,128)S(1)} %strip_kernel.3), channel_id=1, replica_groups=mesh['yl'=2,'x'=4,'c'=2,'yh'=4,'zh'=4,'zl'=2] {'yl','x','c','zl'}, dimensions={0} | all-to-all | bytes 786432 | tf_op jit(solution)/shard_map/all_to_all | solution.py:617
  190.3 1.0 last_kernel.1
  (22 shorter events, 3.5 us)
Async XLA Ops:
  2.3 9.5 %collective-permute-start = (f32[2,72,128]{2,1,0:T(8,128)S(1)}, f32[2,72,128]{2,1,0:T(8,128)S(1)}, u32[]{:S(2)}, u32[]{:S(2)}) collective-permute-start(f32[2,72,128]{2,1,0:T(8,128)S(1)} %get-tuple-element.34), channel_id=1, source_target_pairs={{32,64},{33,65},{34,66},{35,67},{36,68},{37,69},{38,70},{39,71},{4... | collective-permute-start | bytes 221192 | tf_op jit(solution)/shard_map/ppermute | solution.py:612
  6.8 5.8 %collective-permute-start.1 = (f32[2,72,128]{2,1,0:T(8,128)S(1)}, f32[2,72,128]{2,1,0:T(8,128)S(1)}, u32[]{:S(2)}, u32[]{:S(2)}) collective-permute-start(f32[2,72,128]{2,1,0:T(8,128)S(1)} %get-tuple-element.35.mine), channel_id=1, source_target_pairs={{0,32},{1,33},{2,34},{3,35},{4,36},{5,37},{6,38},{7,39},{8,40},{9,... | collective-permute-start | bytes 221192 | tf_op jit(solution)/shard_map/ppermute | solution.py:612
  12.8 6.9 %collective-permute-start.2 = (f32[2,136,128]{2,1,0:T(8,128)S(1)}, f32[2,136,128]{2,1,0:T(8,128)S(1)}, u32[]{:S(2)}, u32[]{:S(2)}) collective-permute-start(f32[2,136,128]{2,1,0:T(8,128)S(1)} %get-tuple-element.37), channel_id=1, source_target_pairs={{1,2},{2,1},{3,4},{4,3},{5,6},{6,5},{7,8},{8,7},{9,10},{10,9},{11,... | collective-permute-start | bytes 417800 | tf_op jit(solution)/shard_map/ppermute | solution.py:612
  13.5 8.3 %collective-permute-start.3 = (f32[2,136,128]{2,1,0:T(8,128)S(1)}, f32[2,136,128]{2,1,0:T(8,128)S(1)}, u32[]{:S(2)}, u32[]{:S(2)}) collective-permute-start(f32[2,136,128]{2,1,0:T(8,128)S(1)} %get-tuple-element.39), channel_id=1, source_target_pairs={{0,1},{1,0},{2,3},{3,2},{4,5},{5,4},{6,7},{7,6},{8,9},{9,8},{10,11... | collective-permute-start | bytes 417800 | tf_op jit(solution)/shard_map/ppermute | solution.py:612
  18.2 3.6 %copy-start = (f32[2,2,128,128]{3,2,1,0:T(8,128)S(1)}, f32[2,2,128,128]{3,2,1,0:T(8,128)}, u32[]{:S(2)}) copy-start(f32[2,2,128,128]{3,2,1,0:T(8,128)} %probe.7) | copy-start | bytes 786436
  27.0 8.0 %collective-permute-start.4 = (f32[2,2,128,128]{3,2,1,0:T(8,128)S(1)}, f32[2,2,128,128]{3,2,1,0:T(8,128)S(1)}, u32[]{:S(2)}, u32[]{:S(2)}) collective-permute-start(f32[2,2,128,128]{3,2,1,0:T(8,128)S(1)} %get-tuple-element.45.row_out0), channel_id=1, source_target_pairs={{32,64},{33,65},{34,66},{35,67},{36,68},{37,69},{38,70},{39,71},{4... | collective-permute-start | bytes 786440 | tf_op jit(solution)/shard_map/ppermute | solution.py:612
  30.9 4.0 %collective-permute-start.5 = (f32[2,2,128,128]{3,2,1,0:T(8,128)S(1)}, f32[2,2,128,128]{3,2,1,0:T(8,128)S(1)}, u32[]{:S(2)}, u32[]{:S(2)}) collective-permute-start(f32[2,2,128,128]{3,2,1,0:T(8,128)S(1)} %get-tuple-element.46.row_out1), channel_id=1, source_target_pairs={{0,32},{1,33},{2,34},{3,35},{4,36},{5,37},{6,38},{7,39},{8,40},{9,... | collective-permute-start | bytes 786440 | tf_op jit(solution)/shard_map/ppermute | solution.py:612
  35.1 13.3 %collective-permute-start.6 = (f32[2,2,128,128]{3,2,1,0:T(8,128)S(1)}, f32[2,2,128,128]{3,2,1,0:T(8,128)S(1)}, u32[]{:S(2)}, u32[]{:S(2)}) collective-permute-start(f32[2,2,128,128]{3,2,1,0:T(8,128)S(1)} %get-tuple-element.47.col_out0), channel_id=1, source_target_pairs={{1,2},{2,1},{3,4},{4,3},{5,6},{6,5},{7,8},{8,7},{9,10},{10,9},{11,... | collective-permute-start | bytes 786440 | tf_op jit(solution)/shard_map/ppermute | solution.py:612
  35.8 15.4 %collective-permute-start.7 = (f32[2,2,128,128]{3,2,1,0:T(8,128)S(1)}, f32[2,2,128,128]{3,2,1,0:T(8,128)S(1)}, u32[]{:S(2)}, u32[]{:S(2)}) collective-permute-start(f32[2,2,128,128]{3,2,1,0:T(8,128)S(1)} %get-tuple-element.48.col_out1), channel_id=1, source_target_pairs={{0,1},{1,0},{2,3},{3,2},{4,5},{5,4},{6,7},{7,6},{8,9},{9,8},{10,11... | collective-permute-start | bytes 786440 | tf_op jit(solution)/shard_map/ppermute | solution.py:612
  70.3 28.4 %all-to-all-start.1 = ((f32[16,4,8,128]{3,2,1,0:T(8,128)}), f32[16,4,8,128]{3,2,1,0:T(8,128)S(1)}, u32[]{:S(2)}, u32[]{:S(2)}) async-start(f32[16,4,8,128]{3,2,1,0:T(8,128)} %reduce_kernel.2), calls=%async_computation.1 | async-start | bytes 524288 | tf_op jit(solution)/shard_map/all_to_all | solution.py:617
  120.1 6.3 %collective-permute-start.8 = (f32[2,2,64,128]{3,2,1,0:T(8,128)S(1)}, f32[2,2,64,128]{3,2,1,0:T(8,128)S(1)}, u32[]{:S(2)}, u32[]{:S(2)}) collective-permute-start(f32[2,2,64,128]{3,2,1,0:T(8,128)S(1)} %get-tuple-element.55), channel_id=1, source_target_pairs={{32,64},{33,65},{34,66},{35,67},{36,68},{37,69},{38,70},{39,71},{4... | collective-permute-start | bytes 393224 | tf_op jit(solution)/shard_map/ppermute | solution.py:612
  122.8 3.6 %collective-permute-start.9 = (f32[2,2,64,128]{3,2,1,0:T(8,128)S(1)}, f32[2,2,64,128]{3,2,1,0:T(8,128)S(1)}, u32[]{:S(2)}, u32[]{:S(2)}) collective-permute-start(f32[2,2,64,128]{3,2,1,0:T(8,128)S(1)} %get-tuple-element.56), channel_id=1, source_target_pairs={{0,32},{1,33},{2,34},{3,35},{4,36},{5,37},{6,38},{7,39},{8,40},{9,... | collective-permute-start | bytes 393224 | tf_op jit(solution)/shard_map/ppermute | solution.py:612
  126.6 6.7 %collective-permute-start.10 = (f32[2,64,128]{2,1,0:T(8,128)S(1)}, f32[2,64,128]{2,1,0:T(8,128)S(1)}, u32[]{:S(2)}, u32[]{:S(2)}) collective-permute-start(f32[2,64,128]{2,1,0:T(8,128)S(1)} %get-tuple-element.58), channel_id=1, source_target_pairs={{1,2},{2,1},{3,4},{4,3},{5,6},{6,5},{7,8},{8,7},{9,10},{10,9},{11,... | collective-permute-start | bytes 196616 | tf_op jit(solution)/shard_map/ppermute | solution.py:612
  127.3 6.3 %collective-permute-start.11 = (f32[2,64,128]{2,1,0:T(8,128)S(1)}, f32[2,64,128]{2,1,0:T(8,128)S(1)}, u32[]{:S(2)}, u32[]{:S(2)}) collective-permute-start(f32[2,64,128]{2,1,0:T(8,128)S(1)} %get-tuple-element.59), channel_id=1, source_target_pairs={{0,1},{1,0},{2,3},{3,2},{4,5},{5,4},{6,7},{7,6},{8,9},{9,8},{10,11... | collective-permute-start | bytes 196616 | tf_op jit(solution)/shard_map/ppermute | solution.py:612

commit v10 on v9

--- a/solution.py
+++ b/solution.py
@@ -17,7 +17,7 @@
 ROW = ("yl", "x", "c")
 COL = ("yh", "zh", "zl")
 ALL = ROW + COL
-SCATTER = ROW + ("zl",)
+SCATTER = ("x", "c", "yl", "zl")
 REST = ("zh", "yh")
 MARK = 1024
 LIST_STEP = 4
@@ -126,83 +126,66 @@
     return jnp.where(odd, second, first), jnp.where(odd, first, second)
 
 
-def pad_field(rows_in, own, cols_in, store):
-    low = low_lanes(HALF)
-    odd_row, odd_col = odds()
-    for c in range(2):
-        above, below = sides(odd_row, *(x[c, :HALF] for x in rows_in))
-        strips = (above, own[c, :HALF], own[c, HALF:], below)
-        for k in range(4):
-            half = slice(HALF * (k % 2), HALF * (k % 2 + 1))
-            left, right = sides(odd_col, *(x[c, half] for x in cols_in))
-            if k < 2:
-                right = pltpu.roll(right, HALF, 1)
-            else:
-                left = pltpu.roll(left, HALF, 1)
-            mine = pltpu.roll(strips[k], HALF, 1)
-            rows = slice(HALF * k, HALF * (k + 1))
-            store(c, 0, rows, jnp.where(low, left, mine))
-            store(c, 1, rows, jnp.where(low, mine, right))
-
-
-def send_kernel(raw, own, tile, row_out0, row_out1, offsets, sems):
-    strip = pl.ds(0, HALF)
-    odd_row, _ = odds()
-    starts = [pl.multiple_of(jnp.where(odd_row == (k == 0), HALF, 0), HALF) for k in range(2)]
-    first = pltpu.make_async_copy(raw, offsets, sems.at[3])
-    first.start()
+def send_kernel(raw, own, tile, col_out0, col_out1, offsets, sems):
     copies = [
         pltpu.make_async_copy(source, target, sems.at[k])
-        for k, (source, target) in enumerate((
-            (own.at[:, pl.ds(starts[0], HALF)], row_out0.at[:, strip]),
-            (own.at[:, pl.ds(starts[1], HALF)], row_out1.at[:, strip]),
-            (own, tile),
-        ))
+        for k, (source, target) in enumerate(((raw, offsets), (own, tile)))
     ]
     for copy in copies:
         copy.start()
     line = lax.broadcasted_iota(jnp.int32, (TILES, SIZE), 0)
     lane = lax.broadcasted_iota(jnp.int32, (TILES, SIZE), 1)
     code = jnp.zeros((TILES, SIZE), jnp.int32)
-    first.wait()
+    copies[0].wait()
     batches, _, count = offsets.shape
     for b in range(batches):
         for k in range(count):
             for d in range(2):
                 code = jnp.where(lane == (b * 2 + d) * count + k, offsets[b, d, k] + MARK, code)
     code = jnp.where(line == 0, code, 0).astype(F32)
-    for c in range(2):
-        row_out0[c, HALF:] = code
-        row_out1[c, HALF:] = code
-    for copy in copies:
-        copy.wait()
-
-
-def pack_kernel(row_in0, row_in1, own, mine, col_out0, col_out1, codes):
+    copies[1].wait()
+    low = low_lanes(HALF)
+    _, odd_col = odds()
+    for c in range(2):
+        upper, lower = tile[c, :HALF], tile[c, HALF:]
+        to_left = pack_low(low, upper, lower)
+        to_right = pack_high(low, upper, lower)
+        col_out0[c, :HALF] = jnp.where(odd_col, to_right, to_left)
+        col_out1[c, :HALF] = jnp.where(odd_col, to_left, to_right)
+        col_out0[c, HALF:] = code
+        col_out1[c, HALF:] = code
+
+
+def spread_kernel(col_in0, col_in1, tile, mine, staged, middle, row_out0, row_out1, codes):
     low = low_lanes(HALF)
     odd_row, odd_col = odds()
-    for c in range(2):
-        above, below = sides(odd_row, row_in0[c, :HALF], row_in1[c, :HALF])
-        strips = (above, own[c, :HALF], own[c, HALF:], below)
+    left, right = sides(odd_col, col_in0[0, HALF:], col_in1[0, HALF:])
+    code = mine[0, HALF:] + pltpu.roll(left, 1, 0) + pltpu.roll(right, 2, 0)
+    codes[...] = code
+    for c in range(2):
+        left, right = sides(odd_col, col_in0[c, :HALF], col_in1[c, :HALF])
+        ends = []
         for k in range(2):
             rows = slice(HALF * k, HALF * (k + 1))
-            to_left = pack_low(low, strips[k], strips[k + 2])
-            to_right = pack_high(low, strips[k], strips[k + 2])
-            col_out0[c, rows] = jnp.where(odd_col, to_right, to_left)
-            col_out1[c, rows] = jnp.where(odd_col, to_left, to_right)
-    above, below = sides(odd_row, row_in0[0, HALF:], row_in1[0, HALF:])
-    code = mine[0, HALF:] + pltpu.roll(above, 1, 0) + pltpu.roll(below, 2, 0)
-    for c in range(2):
-        col_out0[c, SIZE:] = code
-        col_out1[c, SIZE:] = code
-    codes[...] = code
+            own = pltpu.roll(tile[c, rows], HALF, 1)
+            first = jnp.where(low, left if k == 0 else pltpu.roll(left, HALF, 1), own)
+            second = jnp.where(low, own, right if k == 1 else pltpu.roll(right, HALF, 1))
+            middle[c, 0, rows] = first
+            middle[c, 1, rows] = second
+            ends.append((first, second))
+        for h in range(2):
+            top, bottom = ends[0][h], ends[1][h]
+            row_out0[c, h, :HALF] = jnp.where(odd_row, bottom, top)
+            row_out1[c, h, :HALF] = jnp.where(odd_row, top, bottom)
+            row_out0[c, h, HALF:] = code
+            row_out1[c, h, HALF:] = code
 
 
 def power_of(probe):
     return sum(probe[c, m] * probe[c, m] for c in range(2) for m in range(MODES))
 
 
-def stage_kernel(codes, *refs):
+def stage_kernel(tile, *refs):
     count = (len(refs) - 1) // 2
     sems = refs[-1]
     copies = [pltpu.make_async_copy(refs[k], refs[count + k], sems.at[k]) for k in range(count)]
@@ -254,14 +237,16 @@
         sums[k] = totals[k]
 
 
-def first_kernel(offsets, row_in0, row_in1, own, col_in0, col_in1, probe, measured, right3, left3,
+def first_kernel(offsets, row_in0, row_in1, middle, probe, measured, right3, left3,
                  row_out0, row_out1, sums, padded, accum):
-    def store(c, h, rows, value):
-        padded[c, h, rows] = value
-
-    pad_field((row_in0, row_in1), own, (col_in0, col_in1), store)
+    odd_row, _ = odds()
+    for c in range(2):
+        for h in range(2):
+            above, below = sides(odd_row, row_in0[c, h, :HALF], row_in1[c, h, :HALF])
+            padded[c, h, :HALF] = above
+            padded[c, h, HALF : HALF + SIZE] = middle[c, h]
+            padded[c, h, HALF + SIZE :] = below
     sweep(0, offsets, padded, probe, measured, right3, left3, sums, accum)
-    odd_row, _ = odds()
     for c in range(2):
         for h in range(2):
             top, bottom = accum[c, h, :SIZE], accum[c, h, SIZE:]
@@ -270,9 +255,9 @@
 
 
 def offset_of(others, batch, across, down, j, d):
-    _, odd_col = odds()
-    tile = jnp.where(odd_col, 2 - across, across)
-    return others[TILES * tile + (1, 0, 2)[down], (batch * 2 + d) * COUNT + j] - MARK
+    odd_row, _ = odds()
+    tile = jnp.where(odd_row, 2 - down, down)
+    return others[TILES * tile + (1, 0, 2)[across], (batch * 2 + d) * COUNT + j] - MARK
 
 
 def cover_kernel(others, probe, cover, near, light):
@@ -381,7 +366,7 @@
     pack_sums(packed, sums, overlap, a11, b1)
 
 
-def fold_kernel(middle, row_in0, row_in1, tile, col_out0, col_out1):
+def fold_kernel(middle, row_in0, row_in1, cover, tile, col_out0, col_out1):
     low = low_lanes(HALF)
     odd_row, odd_col = odds()
     for k in range(2):
@@ -635,7 +620,7 @@
     offsets = jnp.swapaxes(offsets[0, 0], 1, 2)
     r, c, half = (lax.axis_index(axes).astype(jnp.int32) for axes in (ROW, COL, ("zl",)))
     whole = 2 * SIZE
-    place_in_group = jnp.stack([r, half])
+    place_in_group = jnp.stack([lax.axis_index(SCATTER[:-1]).astype(jnp.int32), half])
     edges = jnp.stack([
         jnp.where(r == 0, HALF, 0),
         jnp.where(r == size_of(ROW) - 1, whole - HALF, whole),
@@ -644,31 +629,31 @@
     ]).astype(jnp.int32)
 
     strip = shape(2, HALF + TILES, SIZE)
-    side = shape(2, SIZE + TILES, SIZE)
-    tile, *row_out, offsets = call(
+    rows_strip = shape(2, 2, HALF + TILES, SIZE)
+    quads = shape(2, 2, SIZE, SIZE)
+    tile, *col_out, offsets = call(
         send_kernel, [offsets, obj],
         [shape(2, SIZE, SIZE), strip, strip, jax.ShapeDtypeStruct(offsets.shape, jnp.int32)],
-        [pltpu.SemaphoreType.DMA((4,))], in_hbm=(0, 1))
-    row_in = swap(row_out, 0)
-    *col_out, codes = call(
-        pack_kernel, [*row_in, tile, row_out[1]], [side, side, shape(TILES, SIZE)])
+        [pltpu.SemaphoreType.DMA((2,))], in_hbm=(0, 1))
     col_in = swap(col_out, 1)
     staged = [measured, right3, left3]
     measured, right3, left3 = call(
-        stage_kernel, [codes, *staged], [jax.ShapeDtypeStruct(x.shape, x.dtype) for x in staged],
+        stage_kernel, [tile, *staged], [jax.ShapeDtypeStruct(x.shape, x.dtype) for x in staged],
         [pltpu.SemaphoreType.DMA((len(staged),))], in_hbm=(1, 2, 3))
-    others = jnp.concatenate([col_in[0][0, SIZE:], codes, col_in[1][0, SIZE:]], axis=0).astype(jnp.int32)
+    middle, *row_out, codes = call(
+        spread_kernel, [*col_in, tile, col_out[1], right3], [quads, rows_strip, rows_strip, shape(TILES, SIZE)])
+    row_in = swap(row_out, 0)
+    others = jnp.concatenate([row_in[0][0, 0, HALF:], codes, row_in[1][0, 0, HALF:]], axis=0).astype(jnp.int32)
 
     field = shape(2, 2, whole, SIZE)
     edge = shape(2, 2, HALF, SIZE)
-    quads = shape(2, 2, SIZE, SIZE)
     planes = shape(2, MODES, SIZE, SIZE)
     sums_shape = shape(5, SIZE, SIZE)
     packed_shape = shape(SIZE // TILES, 2, 4, TILES, SIZE)
 
     *row_out, sums, padded = call(
         first_kernel,
-        [offsets, *row_in, tile, *col_in, probe, measured, right3, left3],
+        [offsets, *row_in, middle, probe, measured, right3, left3],
         [quads, quads, sums_shape, field],
         [pltpu.VMEM((2, 2, whole, SIZE), F32)],
     )
@@ -698,7 +683,7 @@
     (cover,) = call(
         tile_cover_kernel, [near, probe], [shape(SIZE, SIZE)], [pltpu.VMEM((3 * SIZE, SIZE), F32)])
     middle, *col_out = call(
-        fold_kernel, [middle, *row_in], [shape(2, SIZE, SIZE), side, side])
+        fold_kernel, [middle, *row_in, cover], [shape(2, SIZE, SIZE), side, side])
     col_in = swap(col_out, 1)
     packed, direction = call(
         merge_kernel,

time: 192 us -> 190 us (0.990)
    ppermute x12, waiting for transfers between devices: 9.6 us -> 7.67 us  [swap(): taken.append(lax.ppermute(block, ALL, route))]
where the time goes in v10:
time: 190 us; the launch traced here: 189 us
  blocking collectives  84.6 us (45%)
  starting transfers between devices  55.3 us (29%)
  Pallas kernels  27.2 us (14%)
  waiting for transfers between devices  21 us (11%)
    all_to_all x5, blocking collectives, exchange(): return lax.all_to_all(block, axes, 0, 0, tiled=True)  84.6 us
    ppermute x12, starting transfers between devices, swap(): taken.append(lax.ppermute(block, ALL, route))  40.1 us
    pallas_call x16, Pallas kernels, call(): pl.pallas_call(kernel, in_specs=specs, out_specs=[smem if x.dtype == jnp....  27.2 us
    all_to_all x1, starting transfers between devices, exchange(): return lax.all_to_all(block, axes, 0, 0, tiled=True)  15.3 us
    all_to_all x1, waiting for transfers between devices, exchange(): return lax.all_to_all(block, axes, 0, 0, tiled=True)  13.4 us
    ppermute x12, waiting for transfers between devices, swap(): taken.append(lax.ppermute(block, ALL, route))  7.67 us
  transfers between devices with their start and end apart: 13, of which 7 were waited for; matrix products, arithmetic and copies ran while one was open for 0% of the time, Pallas kernels for 4%

profile of v10, /device:TPU:1, one launch (start us, length us, event | category | flops | bytes accessed | tf_op | source)
XLA Modules:
  0.0 189.3 jit_solution(1160443882677833644)
XLA Ops:
  0.6 1.5 send_kernel.1
  2.2 0.7 collective-permute-start
  2.9 8.2 %collective-permute-start.1 = (f32[2,72,128]{2,1,0:T(8,128)S(1)}, f32[2,72,128]{2,1,0:T(8,128)S(1)}, u32[]{:S(2)}, u32[]{:S(2)}) collective-permute-start(f32[2,72,128]{2,1,0:T(8,128)S(1)} %get-tuple-element.36.mine), channel_id=1, source_target_pairs={{0,1},{1,0},{2,3},{3,2},{4,5},{5,4},{6,7},{7,6},{8,9},{9,8},{10,11... | collective-permute-start | bytes 221192 | tf_op jit(solution)/shard_map/ppermute | solution.py:597
  11.0 1.5 stage_kernel.1
  12.9 4.8 %collective-permute-start.2 = (f32[2,2,72,128]{3,2,1,0:T(8,128)S(1)}, f32[2,2,72,128]{3,2,1,0:T(8,128)S(1)}, u32[]{:S(2)}, u32[]{:S(2)}) collective-permute-start(f32[2,2,72,128]{3,2,1,0:T(8,128)S(1)} %get-tuple-element.39), channel_id=1, source_target_pairs={{32,64},{33,65},{34,66},{35,67},{36,68},{37,69},{38,70},{39,71},{4... | collective-permute-start | bytes 442376 | tf_op jit(solution)/shard_map/ppermute | solution.py:597
  17.7 1.9 %collective-permute-start.3 = (f32[2,2,72,128]{3,2,1,0:T(8,128)S(1)}, f32[2,2,72,128]{3,2,1,0:T(8,128)S(1)}, u32[]{:S(2)}, u32[]{:S(2)}) collective-permute-start(f32[2,2,72,128]{3,2,1,0:T(8,128)S(1)} %get-tuple-element.41), channel_id=1, source_target_pairs={{0,32},{1,33},{2,34},{3,35},{4,36},{5,37},{6,38},{7,39},{8,40},{9,... | collective-permute-start | bytes 442376 | tf_op jit(solution)/shard_map/ppermute | solution.py:597
  19.7 0.8 collective-permute-done.2.row_in0
  21.0 5.0 %first_kernel.1 = (f32[2,2,128,128]{3,2,1,0:T(8,128)S(1)}, f32[2,2,128,128]{3,2,1,0:T(8,128)S(1)}, f32[5,128,128]{2,1,0:T(8,128)S(1)}, f32[2,2,256,128]{3,2,1,0:T(8,128)S(1)}) custom-call(s32[2,2,8]{2,1,0:T(2,128)S(1)} %get-tuple-element.43.offsets, f32[2,2,72,128]{3,2,1,0:T(8,128)S(1)} %collective-permute-done.2.row_in0, ...), custom_call_target="tpu_custom_call" | custom-call | tf_op jit(solution)/shard_map/first_kernel/pallas_call | solution.py:576
  26.0 3.2 %collective-permute-start.4 = (f32[2,2,128,128]{3,2,1,0:T(8,128)S(1)}, f32[2,2,128,128]{3,2,1,0:T(8,128)S(1)}, u32[]{:S(2)}, u32[]{:S(2)}) collective-permute-start(f32[2,2,128,128]{3,2,1,0:T(8,128)S(1)} %get-tuple-element.47.row_out0), channel_id=1, source_target_pairs={{32,64},{33,65},{34,66},{35,67},{36,68},{37,69},{38,70},{39,71},{4... | collective-permute-start | bytes 786440 | tf_op jit(solution)/shard_map/ppermute | solution.py:597
  29.2 1.9 %collective-permute-start.5 = (f32[2,2,128,128]{3,2,1,0:T(8,128)S(1)}, f32[2,2,128,128]{3,2,1,0:T(8,128)S(1)}, u32[]{:S(2)}, u32[]{:S(2)}) collective-permute-start(f32[2,2,128,128]{3,2,1,0:T(8,128)S(1)} %get-tuple-element.48.row_out1), channel_id=1, source_target_pairs={{0,32},{1,33},{2,34},{3,35},{4,36},{5,37},{6,38},{7,39},{8,40},{9,... | collective-permute-start | bytes 786440 | tf_op jit(solution)/shard_map/ppermute | solution.py:597
  31.2 2.5 %collective-permute-done.4.row_in0 = f32[2,2,128,128]{3,2,1,0:T(8,128)S(1)} collective-permute-done((f32[2,2,128,128]{3,2,1,0:T(8,128)S(1)}, f32[2,2,128,128]{3,2,1,0:T(8,128)S(1)}, u32[]{:S(2)}, u32[]{:S(2)}) %collective-permute-start.4) | collective-permute-done | bytes 262176 | tf_op jit(solution)/shard_map/ppermute | solution.py:597
  33.8 0.7 collective-permute-start.6
  34.5 8.5 %collective-permute-start.7 = (f32[2,2,128,128]{3,2,1,0:T(8,128)S(1)}, f32[2,2,128,128]{3,2,1,0:T(8,128)S(1)}, u32[]{:S(2)}, u32[]{:S(2)}) collective-permute-start(f32[2,2,128,128]{3,2,1,0:T(8,128)S(1)} %get-tuple-element.50.col_out1), channel_id=1, source_target_pairs={{0,1},{1,0},{2,3},{3,2},{4,5},{5,4},{6,7},{7,6},{8,9},{9,8},{10,11... | collective-permute-start | bytes 786440 | tf_op jit(solution)/shard_map/ppermute | solution.py:597
  43.0 4.0 %cover_kernel.1 = (f32[2,256,128]{2,1,0:T(8,128)S(1)}, s32[80,2]{1,0:T(8,128)S(1)}) custom-call(s32[24,128]{1,0:T(8,128)S(1)} %maximum_convert_fusion.others, f32[2,2,128,128]{3,2,1,0:T(8,128)S(1)} %copy-done), custom_call_target="tpu_custom_call" | custom-call | tf_op jit(solution)/shard_map/cover_kernel/pallas_call | solution.py:576
  47.1 2.0 %collective-permute-done.7.col_in1 = f32[2,2,128,128]{3,2,1,0:T(8,128)S(1)} collective-permute-done((f32[2,2,128,128]{3,2,1,0:T(8,128)S(1)}, f32[2,2,128,128]{3,2,1,0:T(8,128)S(1)}, u32[]{:S(2)}, u32[]{:S(2)}) %collective-permute-start.7) | collective-permute-done | bytes 262176 | tf_op jit(solution)/shard_map/ppermute | solution.py:597
  49.1 1.3 wide_merge_kernel.1
  50.3 17.9 %all_to_all.30.parts = f32[32,4,8,128]{3,2,1,0:T(8,128)S(1)} all-to-all(f32[32,4,8,128]{3,2,1,0:T(8,128)S(1)} %bitcast.19), channel_id=1, replica_groups=mesh['yl'=2,'x'=4,'c'=2,'yh'=4,'zh'=4,'zl'=2] {'x','c','yl','zl'}, dimensions={0} | all-to-all | bytes 1048576 | tf_op jit(solution)/shard_map/all_to_all | solution.py:602
  68.2 0.8 reduce_kernel.2
  69.0 15.3 %all-to-all-start.1 = ((f32[16,4,8,128]{3,2,1,0:T(8,128)}), f32[16,4,8,128]{3,2,1,0:T(8,128)S(1)}, u32[]{:S(2)}, u32[]{:S(2)}) async-start(f32[16,4,8,128]{3,2,1,0:T(8,128)} %reduce_kernel.2), calls=%async_computation.1 | async-start | bytes 524288 | tf_op jit(solution)/shard_map/all_to_all | solution.py:602
  84.4 13.4 %all-to-all-done.1.parts = f32[16,4,8,128]{3,2,1,0:T(8,128)S(1)} async-done(((f32[16,4,8,128]{3,2,1,0:T(8,128)}), f32[16,4,8,128]{3,2,1,0:T(8,128)S(1)}, u32[]{:S(2)}, u32[]{:S(2)}) %all-to-all-start.1) | async-done | bytes 262176 | tf_op jit(solution)/shard_map/all_to_all | solution.py:602
  98.4 14.2 %all_to_all.31 = f32[32,3,8,128]{3,2,1,0:T(8,128)S(1)} all-to-all(f32[32,3,8,128]{3,2,1,0:T(8,128)S(1)} %strip_kernel.2), channel_id=1, replica_groups=mesh['yl'=2,'x'=4,'c'=2,'yh'=4,'zh'=4,'zl'=2] {'x','c','yl','zl'}, dimensions={0} | all-to-all | bytes 786432 | tf_op jit(solution)/shard_map/all_to_all | solution.py:602
  112.6 5.3 %next_kernel.1 = (f32[2,2,64,128]{3,2,1,0:T(8,128)S(1)}, f32[2,2,128,128]{3,2,1,0:T(8,128)S(1)}, f32[2,2,64,128]{3,2,1,0:T(8,128)S(1)}, f32[5,128,128]{2,1,0:T(8...) custom-call(s32[2,2,8]{2,1,0:T(2,128)S(1)} %get-tuple-element.43.offsets, ...), custom_call_target="tpu_custom_call" | custom-call | tf_op jit(solution)/shard_map/next_kernel/pallas_call | solution.py:576
  117.9 3.6 %collective-permute-start.8 = (f32[2,2,64,128]{3,2,1,0:T(8,128)S(1)}, f32[2,2,64,128]{3,2,1,0:T(8,128)S(1)}, u32[]{:S(2)}, u32[]{:S(2)}) collective-permute-start(f32[2,2,64,128]{3,2,1,0:T(8,128)S(1)} %get-tuple-element.57), channel_id=1, source_target_pairs={{32,64},{33,65},{34,66},{35,67},{36,68},{37,69},{38,70},{39,71},{4... | collective-permute-start | bytes 393224 | tf_op jit(solution)/shard_map/ppermute | solution.py:597
  121.5 1.9 %collective-permute-start.9 = (f32[2,2,64,128]{3,2,1,0:T(8,128)S(1)}, f32[2,2,64,128]{3,2,1,0:T(8,128)S(1)}, u32[]{:S(2)}, u32[]{:S(2)}) collective-permute-start(f32[2,2,64,128]{3,2,1,0:T(8,128)S(1)} %get-tuple-element.58), channel_id=1, source_target_pairs={{0,32},{1,33},{2,34},{3,35},{4,36},{5,37},{6,38},{7,39},{8,40},{9,... | collective-permute-start | bytes 393224 | tf_op jit(solution)/shard_map/ppermute | solution.py:597
  123.4 2.2 %tile_cover_kernel.1.cover = f32[128,128]{1,0:T(8,128)S(1)} custom-call(s32[80,2]{1,0:T(8,128)S(1)} %get-tuple-element.42.near, f32[2,2,128,128]{3,2,1,0:T(8,128)S(1)} %get-tuple-element.59.probe), custom_call_target="tpu_custom_call" | custom-call | tf_op jit(solution)/shard_map/tile_cover_kernel/pallas_call | solution.py:576
  126.5 4.0 %collective-permute-start.11 = (f32[2,64,128]{2,1,0:T(8,128)S(1)}, f32[2,64,128]{2,1,0:T(8,128)S(1)}, u32[]{:S(2)}, u32[]{:S(2)}) collective-permute-start(f32[2,64,128]{2,1,0:T(8,128)S(1)} %get-tuple-element.62), channel_id=1, source_target_pairs={{0,1},{1,0},{2,3},{3,2},{4,5},{5,4},{6,7},{7,6},{8,9},{9,8},{10,11... | collective-permute-start | bytes 196616 | tf_op jit(solution)/shard_map/ppermute | solution.py:597
  130.5 1.6 collective-permute-done.11.col_in1
  132.1 2.9 %merge_kernel.1 = (f32[16,2,4,8,128]{4,3,2,1,0:T(8,128)S(1)}, f32[2,128,128]{2,1,0:T(8,128)S(1)}) custom-call(s32[80,2]{1,0:T(8,128)S(1)} %get-tuple-element.42.near, f32[2,128,128]{2,1,0:T(8,128)S(1)} %get-tuple-element.60.tile, f32[2,64,128]{2,1,0:T(8,128)S(1)} %collective-permute-done.10.col_in0, f32[2,64,128]{2,1,0:T(8,128)S(1)} %collective-permute-done.11.col_in1, ...), custom_call_target="tpu_custom_call" | custom-call | tf_op jit(solution)/shard_map/merge_kernel/pallas_call | solution.py:576
  135.1 17.6 %all_to_all.32.parts = f32[32,4,8,128]{3,2,1,0:T(8,128)S(1)} all-to-all(f32[32,4,8,128]{3,2,1,0:T(8,128)S(1)} %bitcast.20), channel_id=1, replica_groups=mesh['yl'=2,'x'=4,'c'=2,'yh'=4,'zh'=4,'zl'=2] {'x','c','yl','zl'}, dimensions={0} | all-to-all | bytes 1048576 | tf_op jit(solution)/shard_map/all_to_all | solution.py:602
  152.8 20.7 %all_to_all.33.parts = f32[16,4,8,128]{3,2,1,0:T(8,128)S(1)} all-to-all(f32[16,4,8,128]{3,2,1,0:T(8,128)S(1)} %reduce_kernel.3), channel_id=1, replica_groups=mesh['yl'=2,'x'=4,'c'=2,'yh'=4,'zh'=4,'zl'=2] {'zh','yh'}, dimensions={0} | all-to-all | bytes 524288 | tf_op jit(solution)/shard_map/all_to_all | solution.py:602
  174.1 14.2 %all_to_all.34 = f32[32,3,8,128]{3,2,1,0:T(8,128)S(1)} all-to-all(f32[32,3,8,128]{3,2,1,0:T(8,128)S(1)} %strip_kernel.3), channel_id=1, replica_groups=mesh['yl'=2,'x'=4,'c'=2,'yh'=4,'zh'=4,'zl'=2] {'x','c','yl','zl'}, dimensions={0} | all-to-all | bytes 786432 | tf_op jit(solution)/shard_map/all_to_all | solution.py:602
  188.3 1.0 last_kernel.1
  (22 shorter events, 3.3 us)
Async XLA Ops:
  2.2 10.3 %collective-permute-start = (f32[2,72,128]{2,1,0:T(8,128)S(1)}, f32[2,72,128]{2,1,0:T(8,128)S(1)}, u32[]{:S(2)}, u32[]{:S(2)}) collective-permute-start(f32[2,72,128]{2,1,0:T(8,128)S(1)} %get-tuple-element.35), channel_id=1, source_target_pairs={{1,2},{2,1},{3,4},{4,3},{5,6},{6,5},{7,8},{8,7},{9,10},{10,9},{11,... | collective-permute-start | bytes 221192 | tf_op jit(solution)/shard_map/ppermute | solution.py:597
  2.9 9.9 %collective-permute-start.1 = (f32[2,72,128]{2,1,0:T(8,128)S(1)}, f32[2,72,128]{2,1,0:T(8,128)S(1)}, u32[]{:S(2)}, u32[]{:S(2)}) collective-permute-start(f32[2,72,128]{2,1,0:T(8,128)S(1)} %get-tuple-element.36.mine), channel_id=1, source_target_pairs={{0,1},{1,0},{2,3},{3,2},{4,5},{5,4},{6,7},{7,6},{8,9},{9,8},{10,11... | collective-permute-start | bytes 221192 | tf_op jit(solution)/shard_map/ppermute | solution.py:597
  12.8 8.2 %copy-start = (f32[2,2,128,128]{3,2,1,0:T(8,128)S(1)}, f32[2,2,128,128]{3,2,1,0:T(8,128)}, u32[]{:S(2)}) copy-start(f32[2,2,128,128]{3,2,1,0:T(8,128)} %probe.7) | copy-start | bytes 786436
  12.9 7.6 %collective-permute-start.2 = (f32[2,2,72,128]{3,2,1,0:T(8,128)S(1)}, f32[2,2,72,128]{3,2,1,0:T(8,128)S(1)}, u32[]{:S(2)}, u32[]{:S(2)}) collective-permute-start(f32[2,2,72,128]{3,2,1,0:T(8,128)S(1)} %get-tuple-element.39), channel_id=1, source_target_pairs={{32,64},{33,65},{34,66},{35,67},{36,68},{37,69},{38,70},{39,71},{4... | collective-permute-start | bytes 442376 | tf_op jit(solution)/shard_map/ppermute | solution.py:597
  17.7 3.3 %collective-permute-start.3 = (f32[2,2,72,128]{3,2,1,0:T(8,128)S(1)}, f32[2,2,72,128]{3,2,1,0:T(8,128)S(1)}, u32[]{:S(2)}, u32[]{:S(2)}) collective-permute-start(f32[2,2,72,128]{3,2,1,0:T(8,128)S(1)} %get-tuple-element.41), channel_id=1, source_target_pairs={{0,32},{1,33},{2,34},{3,35},{4,36},{5,37},{6,38},{7,39},{8,40},{9,... | collective-permute-start | bytes 442376 | tf_op jit(solution)/shard_map/ppermute | solution.py:597
  26.0 7.7 %collective-permute-start.4 = (f32[2,2,128,128]{3,2,1,0:T(8,128)S(1)}, f32[2,2,128,128]{3,2,1,0:T(8,128)S(1)}, u32[]{:S(2)}, u32[]{:S(2)}) collective-permute-start(f32[2,2,128,128]{3,2,1,0:T(8,128)S(1)} %get-tuple-element.47.row_out0), channel_id=1, source_target_pairs={{32,64},{33,65},{34,66},{35,67},{36,68},{37,69},{38,70},{39,71},{4... | collective-permute-start | bytes 786440 | tf_op jit(solution)/shard_map/ppermute | solution.py:597
  29.2 4.5 %collective-permute-start.5 = (f32[2,2,128,128]{3,2,1,0:T(8,128)S(1)}, f32[2,2,128,128]{3,2,1,0:T(8,128)S(1)}, u32[]{:S(2)}, u32[]{:S(2)}) collective-permute-start(f32[2,2,128,128]{3,2,1,0:T(8,128)S(1)} %get-tuple-element.48.row_out1), channel_id=1, source_target_pairs={{0,32},{1,33},{2,34},{3,35},{4,36},{5,37},{6,38},{7,39},{8,40},{9,... | collective-permute-start | bytes 786440 | tf_op jit(solution)/shard_map/ppermute | solution.py:597
  33.8 13.3 %collective-permute-start.6 = (f32[2,2,128,128]{3,2,1,0:T(8,128)S(1)}, f32[2,2,128,128]{3,2,1,0:T(8,128)S(1)}, u32[]{:S(2)}, u32[]{:S(2)}) collective-permute-start(f32[2,2,128,128]{3,2,1,0:T(8,128)S(1)} %get-tuple-element.49.col_out0), channel_id=1, source_target_pairs={{1,2},{2,1},{3,4},{4,3},{5,6},{6,5},{7,8},{8,7},{9,10},{10,9},{11,... | collective-permute-start | bytes 786440 | tf_op jit(solution)/shard_map/ppermute | solution.py:597
  34.5 14.6 %collective-permute-start.7 = (f32[2,2,128,128]{3,2,1,0:T(8,128)S(1)}, f32[2,2,128,128]{3,2,1,0:T(8,128)S(1)}, u32[]{:S(2)}, u32[]{:S(2)}) collective-permute-start(f32[2,2,128,128]{3,2,1,0:T(8,128)S(1)} %get-tuple-element.50.col_out1), channel_id=1, source_target_pairs={{0,1},{1,0},{2,3},{3,2},{4,5},{5,4},{6,7},{7,6},{8,9},{9,8},{10,11... | collective-permute-start | bytes 786440 | tf_op jit(solution)/shard_map/ppermute | solution.py:597
  69.0 28.7 %all-to-all-start.1 = ((f32[16,4,8,128]{3,2,1,0:T(8,128)}), f32[16,4,8,128]{3,2,1,0:T(8,128)S(1)}, u32[]{:S(2)}, u32[]{:S(2)}) async-start(f32[16,4,8,128]{3,2,1,0:T(8,128)} %reduce_kernel.2), calls=%async_computation.1 | async-start | bytes 524288 | tf_op jit(solution)/shard_map/all_to_all | solution.py:602
  117.9 7.7 %collective-permute-start.8 = (f32[2,2,64,128]{3,2,1,0:T(8,128)S(1)}, f32[2,2,64,128]{3,2,1,0:T(8,128)S(1)}, u32[]{:S(2)}, u32[]{:S(2)}) collective-permute-start(f32[2,2,64,128]{3,2,1,0:T(8,128)S(1)} %get-tuple-element.57), channel_id=1, source_target_pairs={{32,64},{33,65},{34,66},{35,67},{36,68},{37,69},{38,70},{39,71},{4... | collective-permute-start | bytes 393224 | tf_op jit(solution)/shard_map/ppermute | solution.py:597
  121.5 4.2 %collective-permute-start.9 = (f32[2,2,64,128]{3,2,1,0:T(8,128)S(1)}, f32[2,2,64,128]{3,2,1,0:T(8,128)S(1)}, u32[]{:S(2)}, u32[]{:S(2)}) collective-permute-start(f32[2,2,64,128]{3,2,1,0:T(8,128)S(1)} %get-tuple-element.58), channel_id=1, source_target_pairs={{0,32},{1,33},{2,34},{3,35},{4,36},{5,37},{6,38},{7,39},{8,40},{9,... | collective-permute-start | bytes 393224 | tf_op jit(solution)/shard_map/ppermute | solution.py:597
  125.8 4.7 %collective-permute-start.10 = (f32[2,64,128]{2,1,0:T(8,128)S(1)}, f32[2,64,128]{2,1,0:T(8,128)S(1)}, u32[]{:S(2)}, u32[]{:S(2)}) collective-permute-start(f32[2,64,128]{2,1,0:T(8,128)S(1)} %get-tuple-element.61), channel_id=1, source_target_pairs={{1,2},{2,1},{3,4},{4,3},{5,6},{6,5},{7,8},{8,7},{9,10},{10,9},{11,... | collective-permute-start | bytes 196616 | tf_op jit(solution)/shard_map/ppermute | solution.py:597
  126.5 5.7 %collective-permute-start.11 = (f32[2,64,128]{2,1,0:T(8,128)S(1)}, f32[2,64,128]{2,1,0:T(8,128)S(1)}, u32[]{:S(2)}, u32[]{:S(2)}) collective-permute-start(f32[2,64,128]{2,1,0:T(8,128)S(1)} %get-tuple-element.62), channel_id=1, source_target_pairs={{0,1},{1,0},{2,3},{3,2},{4,5},{5,4},{6,7},{7,6},{8,9},{9,8},{10,11... | collective-permute-start | bytes 196616 | tf_op jit(solution)/shard_map/ppermute | solution.py:597

commit v11 on v10

--- a/solution.py
+++ b/solution.py
@@ -21,7 +21,7 @@
 REST = ("zh", "yh")
 MARK = 1024
 LIST_STEP = 4
-LIST_SIZE = 9 * COUNT + 8
+LIST_SIZE = 6 * COUNT + 8
 TILES = 8
 VMEM_LIMIT = 16 * 1024 * 1024
 F32 = jnp.float32
@@ -107,8 +107,13 @@
     return lax.broadcasted_iota(jnp.int32, (rows, SIZE), 1) < HALF
 
 
-def bounds(edges):
-    return tuple(edges[k] for k in range(4))
+def bounds():
+    limits = []
+    for axes in (ROW, COL):
+        here = lax.axis_index(axes)
+        limits.append(jnp.where(here == 0, HALF, 0))
+        limits.append(jnp.where(here == size_of(axes) - 1, 2 * SIZE - HALF, 2 * SIZE))
+    return limits
 
 
 def inside(limits, down, across, rows=SIZE):
@@ -283,20 +288,41 @@
         for h in range(2):
             cover[h, v * SIZE : (v + 1) * SIZE] = total[h]
 
-    count = jnp.int32(0)
-    for down in range(3):
-        for across in range(3):
-            for j in range(COUNT):
-                row = offset_of(others, 1, across, down, j, 0) + SIZE * (down - 1)
-                col = offset_of(others, 1, across, down, j, 1) + SIZE * (across - 1)
-                near[count, 0] = row
-                near[count, 1] = col
-                reaches = (jnp.abs(row) < SIZE) & (jnp.abs(col) < SIZE)
-                count += reaches.astype(jnp.int32)
-    for k in range(LIST_STEP):
-        near[count + k, 0] = SIZE
-        near[count + k, 1] = 0
-    near[LIST_SIZE - 1, 0] = count
+    for v in range(2):
+        count = jnp.int32(0)
+        for down in (1, 2 - 2 * v):
+            for across in range(3):
+                for j in range(COUNT):
+                    row = offset_of(others, 1, across, down, j, 0) + SIZE * (down - 1)
+                    col = offset_of(others, 1, across, down, j, 1) + SIZE * (across - 1)
+                    near[v, 0, count] = row
+                    near[v, 1, count] = col
+                    reaches = (jnp.abs(row) < SIZE) & (jnp.abs(col) < SIZE)
+                    count += reaches.astype(jnp.int32)
+        for k in range(LIST_STEP):
+            near[v, 0, count + k] = 0
+            near[v, 1, count + k] = SIZE
+        near[v, 0, LIST_SIZE - 1] = count
+
+
+def listed_sum(near, which, half, planes, sign):
+    lane = lax.broadcasted_iota(jnp.int32, (HALF, SIZE), 1)
+
+    def body(step, totals):
+        totals = list(totals)
+        for g in range(LIST_STEP):
+            down = sign * near[which, 0, step * LIST_STEP + g]
+            across = sign * near[which, 1, step * LIST_STEP + g]
+            turn = lax.rem(2 * SIZE - across, SIZE)
+            source = lane + across
+            valid = (source >= 0) & (source < SIZE)
+            for c, plane in enumerate(planes):
+                moved = pltpu.roll(plane[pl.ds(SIZE + HALF * half + down, HALF)], turn, 1)
+                totals[c] = totals[c] + jnp.where(valid, moved, 0.0)
+        return tuple(totals)
+
+    steps = lax.div(near[which, 0, LIST_SIZE - 1] + LIST_STEP - 1, LIST_STEP)
+    return lax.fori_loop(0, steps, body, (jnp.zeros((HALF, SIZE), F32),) * len(planes))
 
 
 def wide_fold_kernel(row_out0, row_out1, row_in0, row_in1, col_out0, col_out1):
@@ -335,9 +361,9 @@
     pack_planes(packed, [sums[k] for k in range(5)] + [numbers] + list(overlap))
 
 
-def wide_merge_kernel(edges, offsets, col_out0, col_out1, col_in0, col_in1, cover, padded, sums,
+def wide_merge_kernel(offsets, col_out0, col_out1, col_in0, col_in1, cover, padded, sums,
                       packed, direction, product):
-    limits = bounds(edges)
+    limits = bounds()
     _, odd_col = odds()
     a11 = jnp.zeros((1, SIZE), F32)
     b1 = jnp.zeros((1, SIZE), F32)
@@ -384,29 +410,15 @@
 
 
 def tile_cover_kernel(near, probe, cover, light):
-    none = jnp.zeros((SIZE, SIZE), F32)
-    light[:SIZE] = none
+    light[:SIZE] = jnp.zeros((SIZE, SIZE), F32)
     light[SIZE : 2 * SIZE] = power_of(probe)
-    light[2 * SIZE :] = none
-    cover[...] = none
-    lane = lanes()
-
-    def body(step, carry):
-        total = 0.0
-        for g in range(LIST_STEP):
-            down, across = near[step * LIST_STEP + g, 0], near[step * LIST_STEP + g, 1]
-            source = lane - across
-            valid = (source >= 0) & (source < SIZE)
-            moved = pltpu.roll(light[pl.ds(SIZE - down, SIZE)], lax.rem(2 * SIZE + across, SIZE), 1)
-            total = total + jnp.where(valid, moved, 0.0)
-        cover[...] += total
-        return carry
-
-    lax.fori_loop(0, lax.div(near[LIST_SIZE - 1, 0] + LIST_STEP - 1, LIST_STEP), body, 0)
+    light[2 * SIZE :] = jnp.zeros((SIZE, SIZE), F32)
+    for half in range(2):
+        (cover[HALF * half : HALF * (half + 1)],) = listed_sum(near, 1 - half, half, [light], -1)
 
 
 def merge_kernel(near, tile, col_in0, col_in1, cover, padded, sums,
-                 packed, direction, product, overlap):
+                 packed, direction, product):
     low = low_lanes(HALF)
     lane = lanes()
     _, odd_col = odds()
@@ -415,7 +427,6 @@
     for c in range(2):
         product[c, :SIZE] = jnp.zeros((SIZE, SIZE), F32)
         product[c, 2 * SIZE :] = jnp.zeros((SIZE, SIZE), F32)
-        overlap[c] = jnp.zeros((SIZE, SIZE), F32)
     for v in range(2):
         rows = slice(HALF * v, HALF * (v + 1))
         full = []
@@ -443,23 +454,9 @@
         a11 += jnp.sum(power * light, axis=0, keepdims=True)
         b1 += jnp.sum(power * (light + 1.0), axis=0, keepdims=True)
 
-    def body(step, carry):
-        total = [0.0, 0.0]
-        for g in range(LIST_STEP):
-            down, across = near[step * LIST_STEP + g, 0], near[step * LIST_STEP + g, 1]
-            turn = lax.rem(2 * SIZE - across, SIZE)
-            source = lane + across
-            valid = (source >= 0) & (source < SIZE)
-            for c in range(2):
-                moved = pltpu.roll(product[c, pl.ds(SIZE + down, SIZE)], turn, 1)
-                total[c] = total[c] + jnp.where(valid, moved, 0.0)
-        for c in range(2):
-            overlap[c] += total[c]
-        return carry
-
-    lax.fori_loop(0, lax.div(near[LIST_SIZE - 1, 0] + LIST_STEP - 1, LIST_STEP), body, 0)
-
-    pack_sums(packed, sums, (overlap[0], overlap[1]), a11, b1)
+    parts = [listed_sum(near, half, half, [product.at[0], product.at[1]], 1) for half in range(2)]
+    overlap = [jnp.concatenate([parts[0][c], parts[1][c]], axis=0) for c in range(2)]
+    pack_sums(packed, sums, overlap, a11, b1)
 
 
 def add_all(parts):
@@ -475,13 +472,13 @@
         out[k] = total
 
 
-def strip_kernel(place_ref, parts, probe, out):
+def strip_kernel(parts, probe, out):
     total = add_all(parts)
     line = lax.broadcasted_iota(jnp.int32, (TILES, SIZE), 0)
     half = TILES // 2
     upper = line < half
-    first = place_ref[1] == 0
-    rows = pl.ds(pl.multiple_of(place_ref[0] * TILES, TILES), TILES)
+    first = lax.axis_index(SCATTER[-1]) == 0
+    rows = pl.ds(pl.multiple_of(lax.axis_index(SCATTER[:-1]) * TILES, TILES), TILES)
 
     def turned(x):
         return pltpu.roll(x, half, 0)
@@ -606,27 +603,19 @@
     return math.prod(lax.axis_size(a) for a in axes)
 
 
-def reduce_all(packed, probe, place_in_group):
+def reduce_all(packed, probe):
     group, rest = size_of(SCATTER), size_of(REST)
     part = exchange(packed.reshape(group, 4, TILES, SIZE), SCATTER)
     (part,) = call(reduce_kernel, [part], [shape(rest, 4, TILES, SIZE)])
     part = exchange(part, REST)
-    (part,) = call(strip_kernel, [place_in_group, part, probe], [shape(group, 3, TILES, SIZE)])
+    (part,) = call(strip_kernel, [part, probe], [shape(group, 3, TILES, SIZE)])
     return exchange(part, SCATTER).reshape(SIZE // TILES, 2, 3, TILES, SIZE)
 
 
 def per_device(obj, probe, measured, offsets):
     right3, left3 = (jnp.asarray(t) for t in dft_tables())
     offsets = jnp.swapaxes(offsets[0, 0], 1, 2)
-    r, c, half = (lax.axis_index(axes).astype(jnp.int32) for axes in (ROW, COL, ("zl",)))
     whole = 2 * SIZE
-    place_in_group = jnp.stack([lax.axis_index(SCATTER[:-1]).astype(jnp.int32), half])
-    edges = jnp.stack([
-        jnp.where(r == 0, HALF, 0),
-        jnp.where(r == size_of(ROW) - 1, whole - HALF, whole),
-        jnp.where(c == 0, HALF, 0),
-        jnp.where(c == size_of(COL) - 1, whole - HALF, whole),
-    ]).astype(jnp.int32)
 
     strip = shape(2, HALF + TILES, SIZE)
     rows_strip = shape(2, 2, HALF + TILES, SIZE)
@@ -660,17 +649,17 @@
     row_in = swap(row_out, 0)
     cover, near = call(
         cover_kernel, [others, probe],
-        [shape(2, whole, SIZE), jax.ShapeDtypeStruct((LIST_SIZE, 2), jnp.int32)],
+        [shape(2, whole, SIZE), jax.ShapeDtypeStruct((2, 2, LIST_SIZE), jnp.int32)],
         [pltpu.VMEM((3 * SIZE, SIZE), F32)])
     col_out = call(wide_fold_kernel, [*row_out, *row_in], [quads, quads])
     col_in = swap(col_out, 1)
     packed, direction = call(
         wide_merge_kernel,
-        [edges, offsets, *col_out, *col_in, cover, padded, sums],
+        [offsets, *col_out, *col_in, cover, padded, sums],
         [packed_shape, field],
         [pltpu.VMEM((2, 2, whole, SIZE), F32)],
     )
-    totals = reduce_all(packed, probe, place_in_group)
+    totals = reduce_all(packed, probe)
 
     row_out0, middle, row_out1, sums, padded, probe = call(
         next_kernel,
@@ -689,9 +678,9 @@
         merge_kernel,
         [near, middle, *col_in, cover, padded, sums],
         [packed_shape, shape(2, SIZE, SIZE)],
-        [pltpu.VMEM((2, 3 * SIZE, SIZE), F32), pltpu.VMEM((2, SIZE, SIZE), F32)],
+        [pltpu.VMEM((2, 3 * SIZE, SIZE), F32)],
     )
-    totals = reduce_all(packed, probe, place_in_group)
+    totals = reduce_all(packed, probe)
     return tuple(call(
         last_kernel, [totals, padded, direction, probe], [shape(2, SIZE, SIZE), planes, planes]
     ))

time: 190 us -> 188 us (0.989)
  blocking collectives: 84.6 us -> 113 us
  starting transfers between devices: 55.3 us -> 40.2 us
  waiting for transfers between devices: 21 us -> 8.25 us
  Pallas kernels: 27.2 us -> 24.3 us
    all_to_all x5 -> x6, blocking collectives: 84.6 us -> 113 us  [exchange(): return lax.all_to_all(block, axes, 0, 0, tiled=True)]
    all_to_all x1 -> x0, starting transfers between devices: 15.3 us -> none  [exchange(): return lax.all_to_all(block, axes, 0, 0, tiled=True)]
    all_to_all x1 -> x0, waiting for transfers between devices: 13.4 us -> none  [exchange(): return lax.all_to_all(block, axes, 0, 0, tiled=True)]
    pallas_call x16, Pallas kernels: 27.2 us -> 24.3 us  [call(): pl.pallas_call(kernel, in_specs=specs, out_specs=[smem if x.dtype == jnp....]
  transfers between devices with their start and end apart: 13 -> 12, of which waited for: 7 -> 6; matrix products, arithmetic and copies ran while one was open for 0% -> 0% of each run, Pallas kernels for 4% -> 4%
where the time goes in v11:
time: 188 us; the launch traced here: 187 us
  blocking collectives  113 us (60%)
  starting transfers between devices  40.2 us (21%)
  Pallas kernels  24.3 us (13%)
  waiting for transfers between devices  8.25 us (4%)
    all_to_all x6, blocking collectives, exchange(): return lax.all_to_all(block, axes, 0, 0, tiled=True)  113 us
    ppermute x12, starting transfers between devices, swap(): taken.append(lax.ppermute(block, ALL, route))  40.2 us
    pallas_call x16, Pallas kernels, call(): pl.pallas_call(kernel, in_specs=specs, out_specs=[smem if x.dtype == jnp....  24.3 us
    ppermute x12, waiting for transfers between devices, swap(): taken.append(lax.ppermute(block, ALL, route))  8.25 us
  transfers between devices with their start and end apart: 12, of which 6 were waited for; matrix products, arithmetic and copies ran while one was open for 0% of the time, Pallas kernels for 4%

profile of v11, /device:TPU:1, one launch (start us, length us, event | category | flops | bytes accessed | tf_op | source)
XLA Modules:
  0.0 186.9 jit_solution(7061417164029789896)
XLA Ops:
  0.6 1.5 send_kernel.1
  2.2 0.7 collective-permute-start
  2.9 8.2 %collective-permute-start.1 = (f32[2,72,128]{2,1,0:T(8,128)S(1)}, f32[2,72,128]{2,1,0:T(8,128)S(1)}, u32[]{:S(2)}, u32[]{:S(2)}) collective-permute-start(f32[2,72,128]{2,1,0:T(8,128)S(1)} %get-tuple-element.36.mine), channel_id=1, source_target_pairs={{0,1},{1,0},{2,3},{3,2},{4,5},{5,4},{6,7},{7,6},{8,9},{9,8},{10,11... | collective-permute-start | bytes 221192 | tf_op jit(solution)/shard_map/ppermute | solution.py:594
  11.0 1.5 stage_kernel.1
  12.9 4.8 %collective-permute-start.2 = (f32[2,2,72,128]{3,2,1,0:T(8,128)S(1)}, f32[2,2,72,128]{3,2,1,0:T(8,128)S(1)}, u32[]{:S(2)}, u32[]{:S(2)}) collective-permute-start(f32[2,2,72,128]{3,2,1,0:T(8,128)S(1)} %get-tuple-element.39), channel_id=1, source_target_pairs={{32,64},{33,65},{34,66},{35,67},{36,68},{37,69},{38,70},{39,71},{4... | collective-permute-start | bytes 442376 | tf_op jit(solution)/shard_map/ppermute | solution.py:594
  17.7 1.9 %collective-permute-start.3 = (f32[2,2,72,128]{3,2,1,0:T(8,128)S(1)}, f32[2,2,72,128]{3,2,1,0:T(8,128)S(1)}, u32[]{:S(2)}, u32[]{:S(2)}) collective-permute-start(f32[2,2,72,128]{3,2,1,0:T(8,128)S(1)} %get-tuple-element.41), channel_id=1, source_target_pairs={{0,32},{1,33},{2,34},{3,35},{4,36},{5,37},{6,38},{7,39},{8,40},{9,... | collective-permute-start | bytes 442376 | tf_op jit(solution)/shard_map/ppermute | solution.py:594
  19.7 0.9 collective-permute-done.2.row_in0
  20.6 0.5 collective-permute-done.3.row_in1
  21.0 5.3 %first_kernel.1 = (f32[2,2,128,128]{3,2,1,0:T(8,128)S(1)}, f32[2,2,128,128]{3,2,1,0:T(8,128)S(1)}, f32[5,128,128]{2,1,0:T(8,128)S(1)}, f32[2,2,256,128]{3,2,1,0:T(8,128)S(1)}) custom-call(s32[2,2,8]{2,1,0:T(2,128)S(1)} %get-tuple-element.43.offsets, f32[2,2,72,128]{3,2,1,0:T(8,128)S(1)} %collective-permute-done.2.row_in0, ...), custom_call_target="tpu_custom_call" | custom-call | tf_op jit(solution)/shard_map/first_kernel/pallas_call | solution.py:573
  26.3 3.2 %collective-permute-start.4 = (f32[2,2,128,128]{3,2,1,0:T(8,128)S(1)}, f32[2,2,128,128]{3,2,1,0:T(8,128)S(1)}, u32[]{:S(2)}, u32[]{:S(2)}) collective-permute-start(f32[2,2,128,128]{3,2,1,0:T(8,128)S(1)} %get-tuple-element.47.row_out0), channel_id=1, source_target_pairs={{32,64},{33,65},{34,66},{35,67},{36,68},{37,69},{38,70},{39,71},{4... | collective-permute-start | bytes 786440 | tf_op jit(solution)/shard_map/ppermute | solution.py:594
  29.5 1.9 %collective-permute-start.5 = (f32[2,2,128,128]{3,2,1,0:T(8,128)S(1)}, f32[2,2,128,128]{3,2,1,0:T(8,128)S(1)}, u32[]{:S(2)}, u32[]{:S(2)}) collective-permute-start(f32[2,2,128,128]{3,2,1,0:T(8,128)S(1)} %get-tuple-element.48.row_out1), channel_id=1, source_target_pairs={{0,32},{1,33},{2,34},{3,35},{4,36},{5,37},{6,38},{7,39},{8,40},{9,... | collective-permute-start | bytes 786440 | tf_op jit(solution)/shard_map/ppermute | solution.py:594
  31.4 2.6 %collective-permute-done.4.row_in0 = f32[2,2,128,128]{3,2,1,0:T(8,128)S(1)} collective-permute-done((f32[2,2,128,128]{3,2,1,0:T(8,128)S(1)}, f32[2,2,128,128]{3,2,1,0:T(8,128)S(1)}, u32[]{:S(2)}, u32[]{:S(2)}) %collective-permute-start.4) | collective-permute-done | bytes 262176 | tf_op jit(solution)/shard_map/ppermute | solution.py:594
  34.1 0.7 collective-permute-start.6
  34.8 8.5 %collective-permute-start.7 = (f32[2,2,128,128]{3,2,1,0:T(8,128)S(1)}, f32[2,2,128,128]{3,2,1,0:T(8,128)S(1)}, u32[]{:S(2)}, u32[]{:S(2)}) collective-permute-start(f32[2,2,128,128]{3,2,1,0:T(8,128)S(1)} %get-tuple-element.50.col_out1), channel_id=1, source_target_pairs={{0,1},{1,0},{2,3},{3,2},{4,5},{5,4},{6,7},{7,6},{8,9},{9,8},{10,11... | collective-permute-start | bytes 786440 | tf_op jit(solution)/shard_map/ppermute | solution.py:594
  43.3 3.6 %cover_kernel.1 = (f32[2,256,128]{2,1,0:T(8,128)S(1)}, s32[2,2,56]{2,1,0:T(2,128)S(1)}) custom-call(s32[24,128]{1,0:T(8,128)S(1)} %maximum_convert_fusion.others, f32[2,2,128,128]{3,2,1,0:T(8,128)S(1)} %copy-done), custom_call_target="tpu_custom_call" | custom-call | tf_op jit(solution)/shard_map/cover_kernel/pallas_call | solution.py:573
  47.0 2.4 %collective-permute-done.7.col_in1 = f32[2,2,128,128]{3,2,1,0:T(8,128)S(1)} collective-permute-done((f32[2,2,128,128]{3,2,1,0:T(8,128)S(1)}, f32[2,2,128,128]{3,2,1,0:T(8,128)S(1)}, u32[]{:S(2)}, u32[]{:S(2)}) %collective-permute-start.7) | collective-permute-done | bytes 262176 | tf_op jit(solution)/shard_map/ppermute | solution.py:594
  49.4 1.3 wide_merge_kernel.1
  50.7 17.9 %all_to_all.30.parts = f32[32,4,8,128]{3,2,1,0:T(8,128)S(1)} all-to-all(f32[32,4,8,128]{3,2,1,0:T(8,128)S(1)} %bitcast.13), channel_id=1, replica_groups=mesh['yl'=2,'x'=4,'c'=2,'yh'=4,'zh'=4,'zl'=2] {'x','c','yl','zl'}, dimensions={0} | all-to-all | bytes 1048576 | tf_op jit(solution)/shard_map/all_to_all | solution.py:599
  68.6 28.5 %all_to_all.31.parts = f32[16,4,8,128]{3,2,1,0:T(8,128)S(1)} all-to-all(f32[16,4,8,128]{3,2,1,0:T(8,128)S(1)} %reduce_kernel.2), channel_id=1, replica_groups=mesh['yl'=2,'x'=4,'c'=2,'yh'=4,'zh'=4,'zl'=2] {'zh','yh'}, dimensions={0} | all-to-all | bytes 524288 | tf_op jit(solution)/shard_map/all_to_all | solution.py:599
  97.2 14.2 %all_to_all.32 = f32[32,3,8,128]{3,2,1,0:T(8,128)S(1)} all-to-all(f32[32,3,8,128]{3,2,1,0:T(8,128)S(1)} %strip_kernel.2), channel_id=1, replica_groups=mesh['yl'=2,'x'=4,'c'=2,'yh'=4,'zh'=4,'zl'=2] {'x','c','yl','zl'}, dimensions={0} | all-to-all | bytes 786432 | tf_op jit(solution)/shard_map/all_to_all | solution.py:599
  111.5 5.5 %next_kernel.1 = (f32[2,2,64,128]{3,2,1,0:T(8,128)S(1)}, f32[2,2,128,128]{3,2,1,0:T(8,128)S(1)}, f32[2,2,64,128]{3,2,1,0:T(8,128)S(1)}, f32[5,128,128]{2,1,0:T(8...) custom-call(s32[2,2,8]{2,1,0:T(2,128)S(1)} %get-tuple-element.43.offsets, ...), custom_call_target="tpu_custom_call" | custom-call | tf_op jit(solution)/shard_map/next_kernel/pallas_call | solution.py:573
  117.0 3.5 %collective-permute-start.8 = (f32[2,2,64,128]{3,2,1,0:T(8,128)S(1)}, f32[2,2,64,128]{3,2,1,0:T(8,128)S(1)}, u32[]{:S(2)}, u32[]{:S(2)}) collective-permute-start(f32[2,2,64,128]{3,2,1,0:T(8,128)S(1)} %get-tuple-element.57), channel_id=1, source_target_pairs={{32,64},{33,65},{34,66},{35,67},{36,68},{37,69},{38,70},{39,71},{4... | collective-permute-start | bytes 393224 | tf_op jit(solution)/shard_map/ppermute | solution.py:594
  120.5 1.9 %collective-permute-start.9 = (f32[2,2,64,128]{3,2,1,0:T(8,128)S(1)}, f32[2,2,64,128]{3,2,1,0:T(8,128)S(1)}, u32[]{:S(2)}, u32[]{:S(2)}) collective-permute-start(f32[2,2,64,128]{3,2,1,0:T(8,128)S(1)} %get-tuple-element.58), channel_id=1, source_target_pairs={{0,32},{1,33},{2,34},{3,35},{4,36},{5,37},{6,38},{7,39},{8,40},{9,... | collective-permute-start | bytes 393224 | tf_op jit(solution)/shard_map/ppermute | solution.py:594
  122.5 1.7 tile_cover_kernel.1.cover
  124.3 0.7 collective-permute-start.10
  125.0 4.2 %collective-permute-start.11 = (f32[2,64,128]{2,1,0:T(8,128)S(1)}, f32[2,64,128]{2,1,0:T(8,128)S(1)}, u32[]{:S(2)}, u32[]{:S(2)}) collective-permute-start(f32[2,64,128]{2,1,0:T(8,128)S(1)} %get-tuple-element.62), channel_id=1, source_target_pairs={{0,1},{1,0},{2,3},{3,2},{4,5},{5,4},{6,7},{7,6},{8,9},{9,8},{10,11... | collective-permute-start | bytes 196616 | tf_op jit(solution)/shard_map/ppermute | solution.py:594
  129.2 1.6 collective-permute-done.11.col_in1
  130.9 2.2 %merge_kernel.1 = (f32[16,2,4,8,128]{4,3,2,1,0:T(8,128)S(1)}, f32[2,128,128]{2,1,0:T(8,128)S(1)}) custom-call(s32[2,2,56]{2,1,0:T(2,128)S(1)} %get-tuple-element.42.near, f32[2,128,128]{2,1,0:T(8,128)S(1)} %get-tuple-element.60.tile, f32[2,64,128]{2,1,0:T(8,128)S(1)} %collective-permute-done.10.col_in0, f32[2,64,128]{2,1,0:T(8,128)S(1)} %collective-permute-done.11.col_in1, ...), custom_call_target="tpu_custom_call" | custom-call | tf_op jit(solution)/shard_map/merge_kernel/pallas_call | solution.py:573
  133.1 17.5 %all_to_all.33.parts = f32[32,4,8,128]{3,2,1,0:T(8,128)S(1)} all-to-all(f32[32,4,8,128]{3,2,1,0:T(8,128)S(1)} %bitcast.14), channel_id=1, replica_groups=mesh['yl'=2,'x'=4,'c'=2,'yh'=4,'zh'=4,'zl'=2] {'x','c','yl','zl'}, dimensions={0} | all-to-all | bytes 1048576 | tf_op jit(solution)/shard_map/all_to_all | solution.py:599
  150.7 20.8 %all_to_all.34.parts = f32[16,4,8,128]{3,2,1,0:T(8,128)S(1)} all-to-all(f32[16,4,8,128]{3,2,1,0:T(8,128)S(1)} %reduce_kernel.3), channel_id=1, replica_groups=mesh['yl'=2,'x'=4,'c'=2,'yh'=4,'zh'=4,'zl'=2] {'zh','yh'}, dimensions={0} | all-to-all | bytes 524288 | tf_op jit(solution)/shard_map/all_to_all | solution.py:599
  171.6 14.2 %all_to_all.35 = f32[32,3,8,128]{3,2,1,0:T(8,128)S(1)} all-to-all(f32[32,3,8,128]{3,2,1,0:T(8,128)S(1)} %strip_kernel.3), channel_id=1, replica_groups=mesh['yl'=2,'x'=4,'c'=2,'yh'=4,'zh'=4,'zl'=2] {'x','c','yl','zl'}, dimensions={0} | all-to-all | bytes 786432 | tf_op jit(solution)/shard_map/all_to_all | solution.py:599
  185.9 1.0 last_kernel.1
  (19 shorter events, 1.0 us)
Async XLA Ops:
  2.2 10.3 %collective-permute-start = (f32[2,72,128]{2,1,0:T(8,128)S(1)}, f32[2,72,128]{2,1,0:T(8,128)S(1)}, u32[]{:S(2)}, u32[]{:S(2)}) collective-permute-start(f32[2,72,128]{2,1,0:T(8,128)S(1)} %get-tuple-element.35), channel_id=1, source_target_pairs={{1,2},{2,1},{3,4},{4,3},{5,6},{6,5},{7,8},{8,7},{9,10},{10,9},{11,... | collective-permute-start | bytes 221192 | tf_op jit(solution)/shard_map/ppermute | solution.py:594
  2.9 9.9 %collective-permute-start.1 = (f32[2,72,128]{2,1,0:T(8,128)S(1)}, f32[2,72,128]{2,1,0:T(8,128)S(1)}, u32[]{:S(2)}, u32[]{:S(2)}) collective-permute-start(f32[2,72,128]{2,1,0:T(8,128)S(1)} %get-tuple-element.36.mine), channel_id=1, source_target_pairs={{0,1},{1,0},{2,3},{3,2},{4,5},{5,4},{6,7},{7,6},{8,9},{9,8},{10,11... | collective-permute-start | bytes 221192 | tf_op jit(solution)/shard_map/ppermute | solution.py:594
  12.8 8.2 %copy-start = (f32[2,2,128,128]{3,2,1,0:T(8,128)S(1)}, f32[2,2,128,128]{3,2,1,0:T(8,128)}, u32[]{:S(2)}) copy-start(f32[2,2,128,128]{3,2,1,0:T(8,128)} %probe.7) | copy-start | bytes 786436
  12.9 7.6 %collective-permute-start.2 = (f32[2,2,72,128]{3,2,1,0:T(8,128)S(1)}, f32[2,2,72,128]{3,2,1,0:T(8,128)S(1)}, u32[]{:S(2)}, u32[]{:S(2)}) collective-permute-start(f32[2,2,72,128]{3,2,1,0:T(8,128)S(1)} %get-tuple-element.39), channel_id=1, source_target_pairs={{32,64},{33,65},{34,66},{35,67},{36,68},{37,69},{38,70},{39,71},{4... | collective-permute-start | bytes 442376 | tf_op jit(solution)/shard_map/ppermute | solution.py:594
  17.7 3.3 %collective-permute-start.3 = (f32[2,2,72,128]{3,2,1,0:T(8,128)S(1)}, f32[2,2,72,128]{3,2,1,0:T(8,128)S(1)}, u32[]{:S(2)}, u32[]{:S(2)}) collective-permute-start(f32[2,2,72,128]{3,2,1,0:T(8,128)S(1)} %get-tuple-element.41), channel_id=1, source_target_pairs={{0,32},{1,33},{2,34},{3,35},{4,36},{5,37},{6,38},{7,39},{8,40},{9,... | collective-permute-start | bytes 442376 | tf_op jit(solution)/shard_map/ppermute | solution.py:594
  26.3 7.7 %collective-permute-start.4 = (f32[2,2,128,128]{3,2,1,0:T(8,128)S(1)}, f32[2,2,128,128]{3,2,1,0:T(8,128)S(1)}, u32[]{:S(2)}, u32[]{:S(2)}) collective-permute-start(f32[2,2,128,128]{3,2,1,0:T(8,128)S(1)} %get-tuple-element.47.row_out0), channel_id=1, source_target_pairs={{32,64},{33,65},{34,66},{35,67},{36,68},{37,69},{38,70},{39,71},{4... | collective-permute-start | bytes 786440 | tf_op jit(solution)/shard_map/ppermute | solution.py:594
  29.5 4.5 %collective-permute-start.5 = (f32[2,2,128,128]{3,2,1,0:T(8,128)S(1)}, f32[2,2,128,128]{3,2,1,0:T(8,128)S(1)}, u32[]{:S(2)}, u32[]{:S(2)}) collective-permute-start(f32[2,2,128,128]{3,2,1,0:T(8,128)S(1)} %get-tuple-element.48.row_out1), channel_id=1, source_target_pairs={{0,32},{1,33},{2,34},{3,35},{4,36},{5,37},{6,38},{7,39},{8,40},{9,... | collective-permute-start | bytes 786440 | tf_op jit(solution)/shard_map/ppermute | solution.py:594
  34.1 12.9 %collective-permute-start.6 = (f32[2,2,128,128]{3,2,1,0:T(8,128)S(1)}, f32[2,2,128,128]{3,2,1,0:T(8,128)S(1)}, u32[]{:S(2)}, u32[]{:S(2)}) collective-permute-start(f32[2,2,128,128]{3,2,1,0:T(8,128)S(1)} %get-tuple-element.49.col_out0), channel_id=1, source_target_pairs={{1,2},{2,1},{3,4},{4,3},{5,6},{6,5},{7,8},{8,7},{9,10},{10,9},{11,... | collective-permute-start | bytes 786440 | tf_op jit(solution)/shard_map/ppermute | solution.py:594
  34.8 14.6 %collective-permute-start.7 = (f32[2,2,128,128]{3,2,1,0:T(8,128)S(1)}, f32[2,2,128,128]{3,2,1,0:T(8,128)S(1)}, u32[]{:S(2)}, u32[]{:S(2)}) collective-permute-start(f32[2,2,128,128]{3,2,1,0:T(8,128)S(1)} %get-tuple-element.50.col_out1), channel_id=1, source_target_pairs={{0,1},{1,0},{2,3},{3,2},{4,5},{5,4},{6,7},{7,6},{8,9},{9,8},{10,11... | collective-permute-start | bytes 786440 | tf_op jit(solution)/shard_map/ppermute | solution.py:594
  117.0 7.1 %collective-permute-start.8 = (f32[2,2,64,128]{3,2,1,0:T(8,128)S(1)}, f32[2,2,64,128]{3,2,1,0:T(8,128)S(1)}, u32[]{:S(2)}, u32[]{:S(2)}) collective-permute-start(f32[2,2,64,128]{3,2,1,0:T(8,128)S(1)} %get-tuple-element.57), channel_id=1, source_target_pairs={{32,64},{33,65},{34,66},{35,67},{36,68},{37,69},{38,70},{39,71},{4... | collective-permute-start | bytes 393224 | tf_op jit(solution)/shard_map/ppermute | solution.py:594
  120.5 3.6 %collective-permute-start.9 = (f32[2,2,64,128]{3,2,1,0:T(8,128)S(1)}, f32[2,2,64,128]{3,2,1,0:T(8,128)S(1)}, u32[]{:S(2)}, u32[]{:S(2)}) collective-permute-start(f32[2,2,64,128]{3,2,1,0:T(8,128)S(1)} %get-tuple-element.58), channel_id=1, source_target_pairs={{0,32},{1,33},{2,34},{3,35},{4,36},{5,37},{6,38},{7,39},{8,40},{9,... | collective-permute-start | bytes 393224 | tf_op jit(solution)/shard_map/ppermute | solution.py:594
  124.3 4.9 %collective-permute-start.10 = (f32[2,64,128]{2,1,0:T(8,128)S(1)}, f32[2,64,128]{2,1,0:T(8,128)S(1)}, u32[]{:S(2)}, u32[]{:S(2)}) collective-permute-start(f32[2,64,128]{2,1,0:T(8,128)S(1)} %get-tuple-element.61), channel_id=1, source_target_pairs={{1,2},{2,1},{3,4},{4,3},{5,6},{6,5},{7,8},{8,7},{9,10},{10,9},{11,... | collective-permute-start | bytes 196616 | tf_op jit(solution)/shard_map/ppermute | solution.py:594
  125.0 5.9 %collective-permute-start.11 = (f32[2,64,128]{2,1,0:T(8,128)S(1)}, f32[2,64,128]{2,1,0:T(8,128)S(1)}, u32[]{:S(2)}, u32[]{:S(2)}) collective-permute-start(f32[2,64,128]{2,1,0:T(8,128)S(1)} %get-tuple-element.62), channel_id=1, source_target_pairs={{0,1},{1,0},{2,3},{3,2},{4,5},{5,4},{6,7},{7,6},{8,9},{9,8},{10,11... | collective-permute-start | bytes 196616 | tf_op jit(solution)/shard_map/ppermute | solution.py:594

commit v12 on v11

--- a/solution.py
+++ b/solution.py
@@ -17,7 +17,7 @@
 ROW = ("yl", "x", "c")
 COL = ("yh", "zh", "zl")
 ALL = ROW + COL
-SCATTER = ("x", "c", "yl", "zl")
+SCATTER = ("c", "x", "yl", "zl")
 REST = ("zh", "yh")
 MARK = 1024
 LIST_STEP = 4
@@ -339,13 +339,21 @@
             col_out1[v, c] = jnp.where(odd_col, left, right)
 
 
-def pack_planes(packed, planes):
-    strips = (SIZE // TILES, TILES, SIZE)
+def pack_planes(keep, give, planes):
+    half = SIZE // TILES // 2
+    strips = (2 * half, TILES, SIZE)
     upper = lax.rem(lax.broadcasted_iota(jnp.int32, (SIZE, SIZE), 0), TILES) < TILES // 2
+    odd, _ = odds()
     for q in range(len(planes) // 2):
         one, two = planes[2 * q], planes[2 * q + 1]
-        packed[:, 0, q] = jnp.where(upper, one, pltpu.roll(two, TILES // 2, 0)).reshape(strips)
-        packed[:, 1, q] = jnp.where(upper, pltpu.roll(one, SIZE - TILES // 2, 0), two).reshape(strips)
+        pieces = (
+            jnp.where(upper, one, pltpu.roll(two, TILES // 2, 0)),
+            jnp.where(upper, pltpu.roll(one, SIZE - TILES // 2, 0), two),
+        )
+        for h, piece in enumerate(pieces):
+            piece = piece.reshape(strips)
+            keep[:, h, q] = jnp.where(odd, piece[half:], piece[:half])
+            give[:, h, q] = jnp.where(odd, piece[:half], piece[half:])
 
 
 def unpack_planes(packed, q):
@@ -355,14 +363,14 @@
             jnp.where(upper, pltpu.roll(one, SIZE - TILES // 2, 0), two))
 
 
-def pack_sums(packed, sums, overlap, a11, b1):
+def pack_sums(keep, give, sums, overlap, a11, b1):
     turn = lax.rem(lax.broadcasted_iota(jnp.int32, (SIZE, SIZE), 0), TILES // 2)
     numbers = jnp.where(turn == 0, a11, jnp.where(turn == 1, b1, 0.0))
-    pack_planes(packed, [sums[k] for k in range(5)] + [numbers] + list(overlap))
+    pack_planes(keep, give, [sums[k] for k in range(5)] + [numbers] + list(overlap))
 
 
 def wide_merge_kernel(offsets, col_out0, col_out1, col_in0, col_in1, cover, padded, sums,
-                      packed, direction, product):
+                      keep, give, direction, product):
     limits = bounds()
     _, odd_col = odds()
     a11 = jnp.zeros((1, SIZE), F32)
@@ -389,7 +397,7 @@
     for j in range(COUNT):
         row, col = offsets[0, 0, j] + HALF, offsets[0, 1, j] + HALF
         overlap = [overlap[c] + window(product, (c,), row, col) for c in range(2)]
-    pack_sums(packed, sums, overlap, a11, b1)
+    pack_sums(keep, give, sums, overlap, a11, b1)
 
 
 def fold_kernel(middle, row_in0, row_in1, cover, tile, col_out0, col_out1):
@@ -418,7 +426,7 @@
 
 
 def merge_kernel(near, tile, col_in0, col_in1, cover, padded, sums,
-                 packed, direction, product):
+                 keep, give, direction, product):
     low = low_lanes(HALF)
     lane = lanes()
     _, odd_col = odds()
@@ -456,7 +464,7 @@
 
     parts = [listed_sum(near, half, half, [product.at[0], product.at[1]], 1) for half in range(2)]
     overlap = [jnp.concatenate([parts[0][c], parts[1][c]], axis=0) for c in range(2)]
-    pack_sums(packed, sums, overlap, a11, b1)
+    pack_sums(keep, give, sums, overlap, a11, b1)
 
 
 def add_all(parts):
@@ -464,6 +472,10 @@
     for k in range(1, parts.shape[0]):
         total = total + parts[k]
     return total
+
+
+def pair_kernel(keep, taken, out):
+    out[...] = keep[...] + taken[...]
 
 
 def reduce_kernel(parts, out):
@@ -603,9 +615,12 @@
     return math.prod(lax.axis_size(a) for a in axes)
 
 
-def reduce_all(packed, probe):
+def reduce_all(keep, give, probe):
     group, rest = size_of(SCATTER), size_of(REST)
-    part = exchange(packed.reshape(group, 4, TILES, SIZE), SCATTER)
+    pairs = [(0, 1), (1, 0)]
+    taken = lax.ppermute(give, SCATTER[0], pairs)
+    (part,) = call(pair_kernel, [keep, taken], [shape(*keep.shape)])
+    part = exchange(part.reshape(group // 2, 4, TILES, SIZE), SCATTER[1:])
     (part,) = call(reduce_kernel, [part], [shape(rest, 4, TILES, SIZE)])
     part = exchange(part, REST)
     (part,) = call(strip_kernel, [part, probe], [shape(group, 3, TILES, SIZE)])
@@ -638,7 +653,7 @@
     edge = shape(2, 2, HALF, SIZE)
     planes = shape(2, MODES, SIZE, SIZE)
     sums_shape = shape(5, SIZE, SIZE)
-    packed_shape = shape(SIZE // TILES, 2, 4, TILES, SIZE)
+    strips = [shape(SIZE // TILES // 2, 2, 4, TILES, SIZE)] * 2
 
     *row_out, sums, padded = call(
         first_kernel,
@@ -653,13 +668,13 @@
         [pltpu.VMEM((3 * SIZE, SIZE), F32)])
     col_out = call(wide_fold_kernel, [*row_out, *row_in], [quads, quads])
     col_in = swap(col_out, 1)
-    packed, direction = call(
+    keep, give, direction = call(
         wide_merge_kernel,
         [offsets, *col_out, *col_in, cover, padded, sums],
-        [packed_shape, field],
+        [*strips, field],
         [pltpu.VMEM((2, 2, whole, SIZE), F32)],
     )
-    totals = reduce_all(packed, probe)
+    totals = reduce_all(keep, give, probe)
 
     row_out0, middle, row_out1, sums, padded, probe = call(
         next_kernel,
@@ -674,13 +689,13 @@
     middle, *col_out = call(
         fold_kernel, [middle, *row_in, cover], [shape(2, SIZE, SIZE), side, side])
     col_in = swap(col_out, 1)
-    packed, direction = call(
+    keep, give, direction = call(
         merge_kernel,
         [near, middle, *col_in, cover, padded, sums],
-        [packed_shape, shape(2, SIZE, SIZE)],
+        [*strips, shape(2, SIZE, SIZE)],
         [pltpu.VMEM((2, 3 * SIZE, SIZE), F32)],
     )
-    totals = reduce_all(packed, probe)
+    totals = reduce_all(keep, give, probe)
     return tuple(call(
         last_kernel, [totals, padded, direction, probe], [shape(2, SIZE, SIZE), planes, planes]
     ))

time: 188 us -> 187 us (level)
  blocking collectives: 113 us -> 106 us
  starting transfers between devices: 40.2 us -> 44.9 us
  waiting for transfers between devices: 8.25 us -> 11 us
    all_to_all x6, blocking collectives: 113 us -> 106 us  [exchange(): return lax.all_to_all(block, axes, 0, 0, tiled=True)]
    ppermute x0 -> x2, starting transfers between devices: none -> 5.11 us  [reduce_all(): taken = lax.ppermute(give, SCATTER[0], pairs)]
    ppermute x0 -> x2, waiting for transfers between devices: none -> 2.34 us  [reduce_all(): taken = lax.ppermute(give, SCATTER[0], pairs)]
    pallas_call x16 -> x18, Pallas kernels: 24.3 us -> 24 us  [call(): pl.pallas_call(kernel, in_specs=specs, out_specs=[smem if x.dtype == jnp....]
  transfers between devices with their start and end apart: 12 -> 14, of which waited for: 6 -> 8; matrix products, arithmetic and copies ran while one was open for 0% -> 0% of each run, Pallas kernels for 4% -> 4%
where the time goes in v12:
time: 187 us; the launch traced here: 186 us
  blocking collectives  106 us (57%)
  starting transfers between devices  44.9 us (24%)
  Pallas kernels  24 us (13%)
  waiting for transfers between devices  11 us (6%)
    all_to_all x6, blocking collectives, exchange(): return lax.all_to_all(block, axes, 0, 0, tiled=True)  106 us
    ppermute x12, starting transfers between devices, swap(): taken.append(lax.ppermute(block, ALL, route))  39.8 us
    pallas_call x18, Pallas kernels, call(): pl.pallas_call(kernel, in_specs=specs, out_specs=[smem if x.dtype == jnp....  24 us
    ppermute x12, waiting for transfers between devices, swap(): taken.append(lax.ppermute(block, ALL, route))  8.63 us
    ppermute x2, starting transfers between devices, reduce_all(): taken = lax.ppermute(give, SCATTER[0], pairs)  5.11 us
  transfers between devices with their start and end apart: 14, of which 8 were waited for; matrix products, arithmetic and copies ran while one was open for 0% of the time, Pallas kernels for 4%

profile of v12, /device:TPU:1, one launch (start us, length us, event | category | flops | bytes accessed | tf_op | source)
XLA Modules:
  0.0 186.4 jit_solution(7334175878099250957)
XLA Ops:
  0.6 1.5 send_kernel.1
  2.9 8.2 %collective-permute-start.1 = (f32[2,72,128]{2,1,0:T(8,128)S(1)}, f32[2,72,128]{2,1,0:T(8,128)S(1)}, u32[]{:S(2)}, u32[]{:S(2)}) collective-permute-start(f32[2,72,128]{2,1,0:T(8,128)S(1)} %get-tuple-element.38.mine), channel_id=1, source_target_pairs={{0,1},{1,0},{2,3},{3,2},{4,5},{5,4},{6,7},{7,6},{8,9},{9,8},{10,11... | collective-permute-start | bytes 221192 | tf_op jit(solution)/shard_map/ppermute | solution.py:606
  11.0 1.5 stage_kernel.1
  12.9 4.8 %collective-permute-start.2 = (f32[2,2,72,128]{3,2,1,0:T(8,128)S(1)}, f32[2,2,72,128]{3,2,1,0:T(8,128)S(1)}, u32[]{:S(2)}, u32[]{:S(2)}) collective-permute-start(f32[2,2,72,128]{3,2,1,0:T(8,128)S(1)} %get-tuple-element.41), channel_id=1, source_target_pairs={{32,64},{33,65},{34,66},{35,67},{36,68},{37,69},{38,70},{39,71},{4... | collective-permute-start | bytes 442376 | tf_op jit(solution)/shard_map/ppermute | solution.py:606
  17.7 1.9 %collective-permute-start.3 = (f32[2,2,72,128]{3,2,1,0:T(8,128)S(1)}, f32[2,2,72,128]{3,2,1,0:T(8,128)S(1)}, u32[]{:S(2)}, u32[]{:S(2)}) collective-permute-start(f32[2,2,72,128]{3,2,1,0:T(8,128)S(1)} %get-tuple-element.43), channel_id=1, source_target_pairs={{0,32},{1,33},{2,34},{3,35},{4,36},{5,37},{6,38},{7,39},{8,40},{9,... | collective-permute-start | bytes 442376 | tf_op jit(solution)/shard_map/ppermute | solution.py:606
  19.7 0.9 collective-permute-done.2.row_in0
  21.0 5.2 %first_kernel.1 = (f32[2,2,128,128]{3,2,1,0:T(8,128)S(1)}, f32[2,2,128,128]{3,2,1,0:T(8,128)S(1)}, f32[5,128,128]{2,1,0:T(8,128)S(1)}, f32[2,2,256,128]{3,2,1,0:T(8,128)S(1)}) custom-call(s32[2,2,8]{2,1,0:T(2,128)S(1)} %get-tuple-element.45.offsets, f32[2,2,72,128]{3,2,1,0:T(8,128)S(1)} %collective-permute-done.2.row_in0, ...), custom_call_target="tpu_custom_call" | custom-call | tf_op jit(solution)/shard_map/first_kernel/pallas_call | solution.py:585
  26.3 3.2 %collective-permute-start.4 = (f32[2,2,128,128]{3,2,1,0:T(8,128)S(1)}, f32[2,2,128,128]{3,2,1,0:T(8,128)S(1)}, u32[]{:S(2)}, u32[]{:S(2)}) collective-permute-start(f32[2,2,128,128]{3,2,1,0:T(8,128)S(1)} %get-tuple-element.49.row_out0), channel_id=1, source_target_pairs={{32,64},{33,65},{34,66},{35,67},{36,68},{37,69},{38,70},{39,71},{4... | collective-permute-start | bytes 786440 | tf_op jit(solution)/shard_map/ppermute | solution.py:606
  29.5 1.9 %collective-permute-start.5 = (f32[2,2,128,128]{3,2,1,0:T(8,128)S(1)}, f32[2,2,128,128]{3,2,1,0:T(8,128)S(1)}, u32[]{:S(2)}, u32[]{:S(2)}) collective-permute-start(f32[2,2,128,128]{3,2,1,0:T(8,128)S(1)} %get-tuple-element.50.row_out1), channel_id=1, source_target_pairs={{0,32},{1,33},{2,34},{3,35},{4,36},{5,37},{6,38},{7,39},{8,40},{9,... | collective-permute-start | bytes 786440 | tf_op jit(solution)/shard_map/ppermute | solution.py:606
  31.4 2.5 %collective-permute-done.4.row_in0 = f32[2,2,128,128]{3,2,1,0:T(8,128)S(1)} collective-permute-done((f32[2,2,128,128]{3,2,1,0:T(8,128)S(1)}, f32[2,2,128,128]{3,2,1,0:T(8,128)S(1)}, u32[]{:S(2)}, u32[]{:S(2)}) %collective-permute-start.4) | collective-permute-done | bytes 262176 | tf_op jit(solution)/shard_map/ppermute | solution.py:606
  34.7 8.5 %collective-permute-start.7 = (f32[2,2,128,128]{3,2,1,0:T(8,128)S(1)}, f32[2,2,128,128]{3,2,1,0:T(8,128)S(1)}, u32[]{:S(2)}, u32[]{:S(2)}) collective-permute-start(f32[2,2,128,128]{3,2,1,0:T(8,128)S(1)} %get-tuple-element.52.col_out1), channel_id=1, source_target_pairs={{0,1},{1,0},{2,3},{3,2},{4,5},{5,4},{6,7},{7,6},{8,9},{9,8},{10,11... | collective-permute-start | bytes 786440 | tf_op jit(solution)/shard_map/ppermute | solution.py:606
  43.3 3.6 %cover_kernel.1 = (f32[2,256,128]{2,1,0:T(8,128)S(1)}, s32[2,2,56]{2,1,0:T(2,128)S(1)}) custom-call(s32[24,128]{1,0:T(8,128)S(1)} %maximum_convert_fusion.others, f32[2,2,128,128]{3,2,1,0:T(8,128)S(1)} %copy-done), custom_call_target="tpu_custom_call" | custom-call | tf_op jit(solution)/shard_map/cover_kernel/pallas_call | solution.py:585
  46.9 2.4 %collective-permute-done.7.col_in1 = f32[2,2,128,128]{3,2,1,0:T(8,128)S(1)} collective-permute-done((f32[2,2,128,128]{3,2,1,0:T(8,128)S(1)}, f32[2,2,128,128]{3,2,1,0:T(8,128)S(1)}, u32[]{:S(2)}, u32[]{:S(2)}) %collective-permute-start.7) | collective-permute-done | bytes 262176 | tf_op jit(solution)/shard_map/ppermute | solution.py:606
  49.4 1.3 wide_merge_kernel.1
  50.7 2.2 %collective-permute-start.8 = (f32[8,2,4,8,128]{4,3,2,1,0:T(8,128)S(1)}, f32[8,2,4,8,128]{4,3,2,1,0:T(8,128)S(1)}, u32[]{:S(2)}, u32[]{:S(2)}) collective-permute-start(f32[8,2,4,8,128]{4,3,2,1,0:T(8,128)S(1)} %get-tuple-element.57), channel_id=1, source_target_pairs={{0,32},{32,0},{1,33},{33,1},{2,34},{34,2},{3,35},{35,3},{4,36},{36... | collective-permute-start | bytes 786440 | tf_op jit(solution)/shard_map/ppermute | solution.py:621
  52.9 1.2 collective-permute-done.8.taken
  54.1 14.1 %all_to_all.30.parts = f32[16,4,8,128]{3,2,1,0:T(8,128)S(1)} all-to-all(f32[16,4,8,128]{3,2,1,0:T(8,128)S(1)} %bitcast.13), channel_id=1, replica_groups=mesh['yl'=2,'x'=4,'c'=2,'yh'=4,'zh'=4,'zl'=2] {'x','yl','zl'}, dimensions={0} | all-to-all | bytes 524288 | tf_op jit(solution)/shard_map/all_to_all | solution.py:611
  68.3 27.2 %all_to_all.31.parts = f32[16,4,8,128]{3,2,1,0:T(8,128)S(1)} all-to-all(f32[16,4,8,128]{3,2,1,0:T(8,128)S(1)} %reduce_kernel.2), channel_id=1, replica_groups=mesh['yl'=2,'x'=4,'c'=2,'yh'=4,'zh'=4,'zl'=2] {'zh','yh'}, dimensions={0} | all-to-all | bytes 524288 | tf_op jit(solution)/shard_map/all_to_all | solution.py:611
  95.6 15.9 %all_to_all.32 = f32[32,3,8,128]{3,2,1,0:T(8,128)S(1)} all-to-all(f32[32,3,8,128]{3,2,1,0:T(8,128)S(1)} %strip_kernel.2), channel_id=1, replica_groups=mesh['yl'=2,'x'=4,'c'=2,'yh'=4,'zh'=4,'zl'=2] {'c','x','yl','zl'}, dimensions={0} | all-to-all | bytes 786432 | tf_op jit(solution)/shard_map/all_to_all | solution.py:611
  111.6 5.5 %next_kernel.1 = (f32[2,2,64,128]{3,2,1,0:T(8,128)S(1)}, f32[2,2,128,128]{3,2,1,0:T(8,128)S(1)}, f32[2,2,64,128]{3,2,1,0:T(8,128)S(1)}, f32[5,128,128]{2,1,0:T(8...) custom-call(s32[2,2,8]{2,1,0:T(2,128)S(1)} %get-tuple-element.45.offsets, ...), custom_call_target="tpu_custom_call" | custom-call | tf_op jit(solution)/shard_map/next_kernel/pallas_call | solution.py:585
  117.1 3.2 %collective-permute-start.9 = (f32[2,2,64,128]{3,2,1,0:T(8,128)S(1)}, f32[2,2,64,128]{3,2,1,0:T(8,128)S(1)}, u32[]{:S(2)}, u32[]{:S(2)}) collective-permute-start(f32[2,2,64,128]{3,2,1,0:T(8,128)S(1)} %get-tuple-element.60), channel_id=1, source_target_pairs={{32,64},{33,65},{34,66},{35,67},{36,68},{37,69},{38,70},{39,71},{4... | collective-permute-start | bytes 393224 | tf_op jit(solution)/shard_map/ppermute | solution.py:606
  120.3 1.9 %collective-permute-start.10 = (f32[2,2,64,128]{3,2,1,0:T(8,128)S(1)}, f32[2,2,64,128]{3,2,1,0:T(8,128)S(1)}, u32[]{:S(2)}, u32[]{:S(2)}) collective-permute-start(f32[2,2,64,128]{3,2,1,0:T(8,128)S(1)} %get-tuple-element.61), channel_id=1, source_target_pairs={{0,32},{1,33},{2,34},{3,35},{4,36},{5,37},{6,38},{7,39},{8,40},{9,... | collective-permute-start | bytes 393224 | tf_op jit(solution)/shard_map/ppermute | solution.py:606
  122.3 1.5 tile_cover_kernel.1.cover
  124.7 4.1 %collective-permute-start.12 = (f32[2,64,128]{2,1,0:T(8,128)S(1)}, f32[2,64,128]{2,1,0:T(8,128)S(1)}, u32[]{:S(2)}, u32[]{:S(2)}) collective-permute-start(f32[2,64,128]{2,1,0:T(8,128)S(1)} %get-tuple-element.65), channel_id=1, source_target_pairs={{0,1},{1,0},{2,3},{3,2},{4,5},{5,4},{6,7},{7,6},{8,9},{9,8},{10,11... | collective-permute-start | bytes 196616 | tf_op jit(solution)/shard_map/ppermute | solution.py:606
  128.8 2.0 %collective-permute-done.12.col_in1 = f32[2,64,128]{2,1,0:T(8,128)S(1)} collective-permute-done((f32[2,64,128]{2,1,0:T(8,128)S(1)}, f32[2,64,128]{2,1,0:T(8,128)S(1)}, u32[]{:S(2)}, u32[]{:S(2)}) %collective-permute-start.12) | collective-permute-done | bytes 65568 | tf_op jit(solution)/shard_map/ppermute | solution.py:606
  130.8 2.1 %merge_kernel.1 = (f32[8,2,4,8,128]{4,3,2,1,0:T(8,128)S(1)}, f32[8,2,4,8,128]{4,3,2,1,0:T(8,128)S(1)}, f32[2,128,128]{2,1,0:T(8,128)S(1)}) custom-call(s32[2,2,56]{2,1,0:T(2,128)S(1)} %get-tuple-element.44.near, f32[2,128,128]{2,1,0:T(8,128)S(1)} %get-tuple-element.63.tile, f32[2,64,128]{2,1,0:T(8,128)S(1)} %collective-permute-done.11.col_in0, ...), custom_call_target="tpu_custom_call" | custom-call | tf_op jit(solution)/shard_map/merge_kernel/pallas_call | solution.py:585
  132.9 2.9 %collective-permute-start.13 = (f32[8,2,4,8,128]{4,3,2,1,0:T(8,128)S(1)}, f32[8,2,4,8,128]{4,3,2,1,0:T(8,128)S(1)}, u32[]{:S(2)}, u32[]{:S(2)}) collective-permute-start(f32[8,2,4,8,128]{4,3,2,1,0:T(8,128)S(1)} %get-tuple-element.69), channel_id=1, source_target_pairs={{0,32},{32,0},{1,33},{33,1},{2,34},{34,2},{3,35},{35,3},{4,36},{36... | collective-permute-start | bytes 786440 | tf_op jit(solution)/shard_map/ppermute | solution.py:621
  135.8 1.1 collective-permute-done.13.taken
  137.0 12.8 %all_to_all.33.parts = f32[16,4,8,128]{3,2,1,0:T(8,128)S(1)} all-to-all(f32[16,4,8,128]{3,2,1,0:T(8,128)S(1)} %bitcast.14), channel_id=1, replica_groups=mesh['yl'=2,'x'=4,'c'=2,'yh'=4,'zh'=4,'zl'=2] {'x','yl','zl'}, dimensions={0} | all-to-all | bytes 524288 | tf_op jit(solution)/shard_map/all_to_all | solution.py:611
  149.8 19.5 %all_to_all.34.parts = f32[16,4,8,128]{3,2,1,0:T(8,128)S(1)} all-to-all(f32[16,4,8,128]{3,2,1,0:T(8,128)S(1)} %reduce_kernel.3), channel_id=1, replica_groups=mesh['yl'=2,'x'=4,'c'=2,'yh'=4,'zh'=4,'zl'=2] {'zh','yh'}, dimensions={0} | all-to-all | bytes 524288 | tf_op jit(solution)/shard_map/all_to_all | solution.py:611
  169.5 15.9 %all_to_all.35 = f32[32,3,8,128]{3,2,1,0:T(8,128)S(1)} all-to-all(f32[32,3,8,128]{3,2,1,0:T(8,128)S(1)} %strip_kernel.3), channel_id=1, replica_groups=mesh['yl'=2,'x'=4,'c'=2,'yh'=4,'zh'=4,'zl'=2] {'c','x','yl','zl'}, dimensions={0} | all-to-all | bytes 786432 | tf_op jit(solution)/shard_map/all_to_all | solution.py:611
  185.4 1.0 last_kernel.1
  (25 shorter events, 3.4 us)
Async XLA Ops:
  2.2 10.3 %collective-permute-start = (f32[2,72,128]{2,1,0:T(8,128)S(1)}, f32[2,72,128]{2,1,0:T(8,128)S(1)}, u32[]{:S(2)}, u32[]{:S(2)}) collective-permute-start(f32[2,72,128]{2,1,0:T(8,128)S(1)} %get-tuple-element.37), channel_id=1, source_target_pairs={{1,2},{2,1},{3,4},{4,3},{5,6},{6,5},{7,8},{8,7},{9,10},{10,9},{11,... | collective-permute-start | bytes 221192 | tf_op jit(solution)/shard_map/ppermute | solution.py:606
  2.9 9.9 %collective-permute-start.1 = (f32[2,72,128]{2,1,0:T(8,128)S(1)}, f32[2,72,128]{2,1,0:T(8,128)S(1)}, u32[]{:S(2)}, u32[]{:S(2)}) collective-permute-start(f32[2,72,128]{2,1,0:T(8,128)S(1)} %get-tuple-element.38.mine), channel_id=1, source_target_pairs={{0,1},{1,0},{2,3},{3,2},{4,5},{5,4},{6,7},{7,6},{8,9},{9,8},{10,11... | collective-permute-start | bytes 221192 | tf_op jit(solution)/shard_map/ppermute | solution.py:606
  12.8 8.2 %copy-start = (f32[2,2,128,128]{3,2,1,0:T(8,128)S(1)}, f32[2,2,128,128]{3,2,1,0:T(8,128)}, u32[]{:S(2)}) copy-start(f32[2,2,128,128]{3,2,1,0:T(8,128)} %probe.7) | copy-start | bytes 786436
  12.9 7.6 %collective-permute-start.2 = (f32[2,2,72,128]{3,2,1,0:T(8,128)S(1)}, f32[2,2,72,128]{3,2,1,0:T(8,128)S(1)}, u32[]{:S(2)}, u32[]{:S(2)}) collective-permute-start(f32[2,2,72,128]{3,2,1,0:T(8,128)S(1)} %get-tuple-element.41), channel_id=1, source_target_pairs={{32,64},{33,65},{34,66},{35,67},{36,68},{37,69},{38,70},{39,71},{4... | collective-permute-start | bytes 442376 | tf_op jit(solution)/shard_map/ppermute | solution.py:606
  17.7 3.3 %collective-permute-start.3 = (f32[2,2,72,128]{3,2,1,0:T(8,128)S(1)}, f32[2,2,72,128]{3,2,1,0:T(8,128)S(1)}, u32[]{:S(2)}, u32[]{:S(2)}) collective-permute-start(f32[2,2,72,128]{3,2,1,0:T(8,128)S(1)} %get-tuple-element.43), channel_id=1, source_target_pairs={{0,32},{1,33},{2,34},{3,35},{4,36},{5,37},{6,38},{7,39},{8,40},{9,... | collective-permute-start | bytes 442376 | tf_op jit(solution)/shard_map/ppermute | solution.py:606
  26.3 7.7 %collective-permute-start.4 = (f32[2,2,128,128]{3,2,1,0:T(8,128)S(1)}, f32[2,2,128,128]{3,2,1,0:T(8,128)S(1)}, u32[]{:S(2)}, u32[]{:S(2)}) collective-permute-start(f32[2,2,128,128]{3,2,1,0:T(8,128)S(1)} %get-tuple-element.49.row_out0), channel_id=1, source_target_pairs={{32,64},{33,65},{34,66},{35,67},{36,68},{37,69},{38,70},{39,71},{4... | collective-permute-start | bytes 786440 | tf_op jit(solution)/shard_map/ppermute | solution.py:606
  29.5 4.5 %collective-permute-start.5 = (f32[2,2,128,128]{3,2,1,0:T(8,128)S(1)}, f32[2,2,128,128]{3,2,1,0:T(8,128)S(1)}, u32[]{:S(2)}, u32[]{:S(2)}) collective-permute-start(f32[2,2,128,128]{3,2,1,0:T(8,128)S(1)} %get-tuple-element.50.row_out1), channel_id=1, source_target_pairs={{0,32},{1,33},{2,34},{3,35},{4,36},{5,37},{6,38},{7,39},{8,40},{9,... | collective-permute-start | bytes 786440 | tf_op jit(solution)/shard_map/ppermute | solution.py:606
  34.1 12.9 %collective-permute-start.6 = (f32[2,2,128,128]{3,2,1,0:T(8,128)S(1)}, f32[2,2,128,128]{3,2,1,0:T(8,128)S(1)}, u32[]{:S(2)}, u32[]{:S(2)}) collective-permute-start(f32[2,2,128,128]{3,2,1,0:T(8,128)S(1)} %get-tuple-element.51.col_out0), channel_id=1, source_target_pairs={{1,2},{2,1},{3,4},{4,3},{5,6},{6,5},{7,8},{8,7},{9,10},{10,9},{11,... | collective-permute-start | bytes 786440 | tf_op jit(solution)/shard_map/ppermute | solution.py:606
  34.7 14.7 %collective-permute-start.7 = (f32[2,2,128,128]{3,2,1,0:T(8,128)S(1)}, f32[2,2,128,128]{3,2,1,0:T(8,128)S(1)}, u32[]{:S(2)}, u32[]{:S(2)}) collective-permute-start(f32[2,2,128,128]{3,2,1,0:T(8,128)S(1)} %get-tuple-element.52.col_out1), channel_id=1, source_target_pairs={{0,1},{1,0},{2,3},{3,2},{4,5},{5,4},{6,7},{7,6},{8,9},{9,8},{10,11... | collective-permute-start | bytes 786440 | tf_op jit(solution)/shard_map/ppermute | solution.py:606
  50.7 3.4 %collective-permute-start.8 = (f32[8,2,4,8,128]{4,3,2,1,0:T(8,128)S(1)}, f32[8,2,4,8,128]{4,3,2,1,0:T(8,128)S(1)}, u32[]{:S(2)}, u32[]{:S(2)}) collective-permute-start(f32[8,2,4,8,128]{4,3,2,1,0:T(8,128)S(1)} %get-tuple-element.57), channel_id=1, source_target_pairs={{0,32},{32,0},{1,33},{33,1},{2,34},{34,2},{3,35},{35,3},{4,36},{36... | collective-permute-start | bytes 786440 | tf_op jit(solution)/shard_map/ppermute | solution.py:621
  117.1 6.7 %collective-permute-start.9 = (f32[2,2,64,128]{3,2,1,0:T(8,128)S(1)}, f32[2,2,64,128]{3,2,1,0:T(8,128)S(1)}, u32[]{:S(2)}, u32[]{:S(2)}) collective-permute-start(f32[2,2,64,128]{3,2,1,0:T(8,128)S(1)} %get-tuple-element.60), channel_id=1, source_target_pairs={{32,64},{33,65},{34,66},{35,67},{36,68},{37,69},{38,70},{39,71},{4... | collective-permute-start | bytes 393224 | tf_op jit(solution)/shard_map/ppermute | solution.py:606
  120.3 3.5 %collective-permute-start.10 = (f32[2,2,64,128]{3,2,1,0:T(8,128)S(1)}, f32[2,2,64,128]{3,2,1,0:T(8,128)S(1)}, u32[]{:S(2)}, u32[]{:S(2)}) collective-permute-start(f32[2,2,64,128]{3,2,1,0:T(8,128)S(1)} %get-tuple-element.61), channel_id=1, source_target_pairs={{0,32},{1,33},{2,34},{3,35},{4,36},{5,37},{6,38},{7,39},{8,40},{9,... | collective-permute-start | bytes 393224 | tf_op jit(solution)/shard_map/ppermute | solution.py:606
  124.0 4.8 %collective-permute-start.11 = (f32[2,64,128]{2,1,0:T(8,128)S(1)}, f32[2,64,128]{2,1,0:T(8,128)S(1)}, u32[]{:S(2)}, u32[]{:S(2)}) collective-permute-start(f32[2,64,128]{2,1,0:T(8,128)S(1)} %get-tuple-element.64), channel_id=1, source_target_pairs={{1,2},{2,1},{3,4},{4,3},{5,6},{6,5},{7,8},{8,7},{9,10},{10,9},{11,... | collective-permute-start | bytes 196616 | tf_op jit(solution)/shard_map/ppermute | solution.py:606
  124.7 6.1 %collective-permute-start.12 = (f32[2,64,128]{2,1,0:T(8,128)S(1)}, f32[2,64,128]{2,1,0:T(8,128)S(1)}, u32[]{:S(2)}, u32[]{:S(2)}) collective-permute-start(f32[2,64,128]{2,1,0:T(8,128)S(1)} %get-tuple-element.65), channel_id=1, source_target_pairs={{0,1},{1,0},{2,3},{3,2},{4,5},{5,4},{6,7},{7,6},{8,9},{9,8},{10,11... | collective-permute-start | bytes 196616 | tf_op jit(solution)/shard_map/ppermute | solution.py:606
  132.9 4.0 %collective-permute-start.13 = (f32[8,2,4,8,128]{4,3,2,1,0:T(8,128)S(1)}, f32[8,2,4,8,128]{4,3,2,1,0:T(8,128)S(1)}, u32[]{:S(2)}, u32[]{:S(2)}) collective-permute-start(f32[8,2,4,8,128]{4,3,2,1,0:T(8,128)S(1)} %get-tuple-element.69), channel_id=1, source_target_pairs={{0,32},{32,0},{1,33},{33,1},{2,34},{34,2},{3,35},{35,3},{4,36},{36... | collective-permute-start | bytes 786440 | tf_op jit(solution)/shard_map/ppermute | solution.py:621
